TPU v7x, 128 devices: a whole 4x4x4 slice. The times are simulated.
128 devices in a mesh: gx: 8 (over x, core), gy: 16 (over y, z).
Axes of the slice: x: 4, y: 4, z: 4, core: 2. Of those that a mesh axis runs over, the one named last changes fastest.
Arguments:
- state_prior: float32 [16, 16, 128, 1024], P(None, None, 'gy', 'gx'), may hold values from 0.1 to 3.6, as said below
- conductivity: float32 [16, 128, 1024], P(None, 'gy', 'gx'), may hold values from 0.25 to 1
- heat_input: bfloat16 [16, 16384, 128], P(None, ('gx', 'gy')), may hold values from 0.19921875 to 2
- owner_tile: int32 [16384, 1], P(('gx', 'gy')), may hold values from 0 to 127; in each aligned block of 128 rows (0 to 127, 128 to 255, ...) at most 2 rows name the same one
- voxel_list: int32 [16384, 128], P(('gx', 'gy')), may hold values from 0 to 2047
- pixel_cell: int32 [65536], P(('gx', 'gy')), may hold values from 0 to 1023
- observed: float32 [65536], P(('gx', 'gy')), may hold values from -6 to 6
- pixel_variance: float32 [65536], P(('gx', 'gy')), may hold values from 0.1 to 10
- pixel_noise: float32 [16, 65536], P(None, ('gx', 'gy')), may hold values from -6 to 6
Outputs:
- analysis: float32 [16, 16, 128, 1024], P(None, None, 'gy', 'gx')
Inputs may be any that keep to these rules, and one draw needn't show every extreme that they name: `state_prior`: positive temperatures. `owner_tile`: in the rows of one device no tile is named more than 2 times. `voxel_list`: indices into the two top layers of the owner tile, flattened over layer, width cell and length cell. `pixel_cell`: indices into the top layer of the pixel's tile, flattened over width cell and length cell.
All inputs are finite; a program needn't handle non-finite values.
Results may differ from a plain program's by a relative error of at most 0.00055.
Values may be sent and summed in bfloat16 or wider, within the bound.
No kernel may reach another device: no remote copies, remote signals or barrier semaphores. Data moves between devices by JAX's collectives and lax.ppermute only.
A program may use at most 128 MiB of HBM per device.

v0:
```python
import jax
import jax.numpy as jnp
from jax import lax
from jax.sharding import PartitionSpec as P

SUBSTEPS = 6
CAP = 2


cool_rate = 0.1
stable_share = 0.9


def padded_2(block, sides, width):
    for axis, dim in sides:
        count = lax.axis_size(axis)
        forward = [(i, i + 1) for i in range(count - 1)]
        backward = [(target, source) for source, target in forward]
        low = lax.ppermute(
            lax.slice_in_dim(block, block.shape[dim] - width, None, axis=dim), axis, forward
        )
        high = lax.ppermute(lax.slice_in_dim(block, 0, width, axis=dim), axis, backward)
        block = jnp.concatenate([low, block, high], axis=dim)
    return block


def advance(padded, conduct, time_step):
    centre = padded[..., 1:-1, 1:-1]
    inner_k = conduct[..., 1:-1, 1:-1]
    lateral = 0.5 * (inner_k + conduct[..., 2:, 1:-1]) * (padded[..., 2:, 1:-1] - centre)
    lateral = lateral + 0.5 * (inner_k + conduct[..., :-2, 1:-1]) * (
        padded[..., :-2, 1:-1] - centre
    )
    lateral = lateral + 0.5 * (inner_k + conduct[..., 1:-1, 2:]) * (padded[..., 1:-1, 2:] - centre)
    lateral = lateral + 0.5 * (inner_k + conduct[..., 1:-1, :-2]) * (
        padded[..., 1:-1, :-2] - centre
    )
    vertical_flux = (
        0.5
        * (inner_k[..., 1:, :, :] + inner_k[..., :-1, :, :])
        * (centre[..., 1:, :, :] - centre[..., :-1, :, :])
    )
    zero_face = jnp.zeros_like(vertical_flux[..., :1, :, :])
    vertical = jnp.concatenate([vertical_flux, zero_face], axis=-3) - jnp.concatenate(
        [zero_face, vertical_flux], axis=-3
    )
    cooling = jnp.concatenate(
        [cool_rate * centre[..., :1, :, :], jnp.zeros_like(centre[..., 1:, :, :])], axis=-3
    )
    return centre + time_step * (lateral + vertical - cooling)


def peak_step(field_now, conductivity):
    local_peak = jnp.max(conductivity[None] * (1.0 + 0.25 * field_now * field_now))
    global_peak = lax.pmax(local_peak, ("gx", "gy"))
    return stable_share / (6.0 * global_peak + cool_rate)


def on_device(
    state_prior,
    conductivity,
    heat_input,
    owner_tile,
    voxel_list,
    pixel_cell,
    observed,
    pixel_variance,
    pixel_noise,
):
    members, layers, width_cells, length_cells = state_prior.shape
    face_cells = heat_input.shape[2]
    tiles_x = lax.axis_size("gx")
    tiles_y = lax.axis_size("gy")
    owners = tiles_x * tiles_y
    target_tile = owner_tile[:, 0]
    owner_table = (target_tile[:, None] == jnp.arange(owners, dtype=jnp.int32)[None, :]).astype(
        jnp.int32
    )
    earlier = jnp.cumsum(owner_table, axis=0) - owner_table
    slot_rank = jnp.sum(earlier * owner_table, axis=1)
    slot_place = target_tile * CAP + slot_rank
    outgoing = (
        jnp.zeros((members, owners * CAP, face_cells), jnp.bfloat16)
        .at[:, slot_place]
        .set(heat_input)
    )
    cells_out = (
        jnp.zeros((1, owners * CAP, face_cells), jnp.int32).at[:, slot_place].set(voxel_list[None])
    )
    incoming, cells_in = (
        lax.all_to_all(
            outgoing.reshape(members, owners, CAP, face_cells),
            ("gx", "gy"),
            split_axis=1,
            concat_axis=1,
            tiled=True,
        ),
        lax.all_to_all(
            cells_out.reshape(1, owners, CAP, face_cells),
            ("gx", "gy"),
            split_axis=1,
            concat_axis=1,
            tiled=True,
        ),
    )
    flat_state = (
        state_prior.reshape(members, -1)
        .at[:, cells_in.reshape(-1)]
        .add(incoming.reshape(members, -1).astype(jnp.float32))
    )
    field_now = flat_state.reshape(state_prior.shape)
    coef_pad = padded_2(conductivity.astype(jnp.bfloat16), (("gx", 2), ("gy", 1)), 1).astype(
        conductivity.dtype
    )
    for substep in range(SUBSTEPS):
        time_step = peak_step(field_now, conductivity)
        padded = padded_2(field_now, (("gx", 3), ("gy", 2)), 1)
        field_now = advance(padded, coef_pad[None] * (1.0 + 0.25 * padded * padded), time_step)
    surface = field_now[:, 0].reshape(members, -1)
    seen = surface[:, pixel_cell]
    spread = seen - jnp.mean(seen, axis=0, keepdims=True)
    innovation = observed[None, :] + pixel_noise * jnp.sqrt(pixel_variance)[None, :] - seen
    weighted = spread / pixel_variance[None, :]
    cross = jnp.dot(weighted, spread.T, precision=lax.Precision.HIGHEST)
    target_sum = jnp.dot(weighted, innovation.T, precision=lax.Precision.HIGHEST)
    cross, target_sum = lax.psum((cross, target_sum), ("gx", "gy"))
    system = cross + (members - 1) * jnp.eye(members, dtype=jnp.float32)
    factor = jnp.linalg.cholesky(system)
    halfway = lax.linalg.triangular_solve(factor, target_sum, left_side=True, lower=True)
    weights = lax.linalg.triangular_solve(
        factor, halfway, left_side=True, lower=True, transpose_a=True
    )
    flat_field = field_now.reshape(members, -1)
    anomalies = flat_field - jnp.mean(flat_field, axis=0, keepdims=True)
    analysis = flat_field + jnp.einsum(
        "kc,km->mc", anomalies, weights, precision=lax.Precision.HIGHEST
    )
    return analysis.reshape(field_now.shape)


def solution(mesh):
    in_specs = (
        P(None, None, "gy", "gx"),
        P(None, "gy", "gx"),
        P(None, ("gx", "gy"), None),
        P(("gx", "gy"), None),
        P(("gx", "gy"), None),
        P(("gx", "gy")),
        P(("gx", "gy")),
        P(("gx", "gy")),
        P(None, ("gx", "gy")),
    )
    out_specs = P(None, None, "gy", "gx")
    return jax.shard_map(
        on_device, mesh=mesh, in_specs=in_specs, out_specs=out_specs, check_vma=False
    )
```

profile of v0, /device:TPU:1, one launch (start us, length us, event | category | flops | bytes accessed | tf_op | source)
XLA Modules:
  0.0 944.2 jit_solution(10993576198664131948)
XLA Ops:
  4.2 11.5 %all-to-all-start = ((s32[1,128,2,128]{3,2,0,1:T(2,128)}), s32[1,128,2,128]{3,2,0,1:T(2,128)S(1)}, u32[]{:S(2)}, u32[]{:S(2)}) async-start(s32[1,128,2,128]{3,2,0,1:T(2,128)} %bitcast.5), calls=%async_computation | async-start | bytes 262144 | tf_op jit(solution)/shard_map/all_to_all | solution.py:98
  16.7 3.0 collective-permute-start.1
  19.6 2.6 collective-permute-start
  23.1 6.0 copy.494
  30.6 13.2 %scatter_fusion = bf16[16,256,128]{2,0,1:T(8,128)(2,1)} fusion(bf16[16,256,128]{2,0,1:T(8,128)(2,1)} %broadcast_in_dim.11, s32[128]{0:T(128)S(1)} %fusion.182, bf16[128,16,128]{2,1,0:T(8,128)(2,1)S(1)} %copy.496), kind=kCustom, calls=%fused_computation.2 | custom fusion | bytes 1573376 | tf_op jit(solution)/shard_map/scatter | solution.py:85
  45.2 4.0 collective-permute-start.2
  49.2 11.6 %all-to-all-start.1 = ((bf16[16,128,2,128]{3,0,2,1:T(8,128)(2,1)}), bf16[16,128,2,128]{3,0,2,1:T(8,128)(2,1)S(1)}, u32[]{:S(2)}, u32[]{:S(2)}) async-start(bf16[16,128,2,128]{3,0,2,1:T(8,128)(2,1)} %bitcast.9), calls=%async_computation.1 | async-start | bytes 2097152 | tf_op jit(solution)/shard_map/all_to_all | solution.py:91
  60.9 18.8 %all-to-all-done.1 = bf16[16,128,2,128]{3,0,2,1:T(8,128)(2,1)S(1)} async-done(((bf16[16,128,2,128]{3,0,2,1:T(8,128)(2,1)}), bf16[16,128,2,128]{3,0,2,1:T(8,128)(2,1)S(1)}, u32[]{:S(2)}, u32[]{:S(2)}) %all-to-all-start.1) | async-done | bytes 1048608 | tf_op jit(solution)/shard_map/all_to_all | solution.py:91
  79.7 7.6 copy.497
  87.3 163.1 %scatter_fusion.1 = f32[16,16384]{0,1:T(8,128)} fusion(f32[16,16384]{0,1:T(8,128)} %bitcast.56, s32[32768]{0:T(1024)S(1)} %bitcast.63, f32[32768,16]{1,0:T(8,128)} %bitcast.59), kind=kCustom, calls=%fused_computation.3 | custom fusion | flops 524288 | bytes 6422528 | tf_op jit(solution)/shard_map/scatter-add | solution.py:109
  250.4 5.1 copy.498
  257.0 41.6 %collective-permute-start.5 = (f32[16,16,8,1]{1,2,3,0:T(8,128)S(1)}, f32[16,16,8,1]{1,2,3,0:T(8,128)S(1)}, u32[]{:S(2)}, u32[]{:S(2)}) collective-permute-start(f32[16,16,8,1]{1,2,3,0:T(8,128)S(1)} %copy.557), channel_id=1, source_target_pairs={{16,0},{32,16},{48,32},{64,48},{80,64},{96,80},{112,96},{17,1},{33... | collective-permute-start | bytes 24584 | tf_op jit(solution)/shard_map/ppermute | solution.py:22
  299.3 2.6 collective-permute-start.4
  302.9 63.3 %pmax.42 = f32[]{:T(128)} all-reduce(f32[]{:T(128)} %fusion.15), channel_id=1, replica_groups=mesh['gx'=8,'gy'=16] {'gx','gy'}, use_global_device_ids=true, to_apply=%region_6.7 | all-reduce | flops 1 | bytes 8 | tf_op jit(solution)/shard_map/pmax | solution.py:55
  366.2 5.2 copy.517
  375.2 4.5 collective-permute-start.6
  379.8 3.0 collective-permute-done.7
  385.3 5.0 fusion.18
  391.5 4.0 collective-permute-start.9
  396.9 1.9 collective-permute-start.8
  398.8 67.2 %pmax.43 = f32[]{:T(128)} all-reduce(f32[]{:T(128)} %get-tuple-element.17), channel_id=1, replica_groups=mesh['gx'=8,'gy'=16] {'gx','gy'}, use_global_device_ids=true, to_apply=%region_8.9 | all-reduce | flops 1 | bytes 8 | tf_op jit(solution)/shard_map/pmax | solution.py:55
  470.7 4.0 collective-permute-start.10
  474.7 3.4 collective-permute-done.11
  480.7 5.0 fusion.21
  486.8 4.0 collective-permute-start.13
  494.2 67.9 %pmax.44 = f32[]{:T(128)} all-reduce(f32[]{:T(128)} %get-tuple-element.15), channel_id=1, replica_groups=mesh['gx'=8,'gy'=16] {'gx','gy'}, use_global_device_ids=true, to_apply=%region_10.11 | all-reduce | flops 1 | bytes 8 | tf_op jit(solution)/shard_map/pmax | solution.py:55
  566.8 4.0 collective-permute-start.14
  570.8 3.7 collective-permute-done.15
  577.1 5.0 fusion.24
  583.2 3.7 collective-permute-start.17
  588.4 1.9 collective-permute-start.16
  590.4 67.5 %pmax.45 = f32[]{:T(128)} all-reduce(f32[]{:T(128)} %get-tuple-element.13), channel_id=1, replica_groups=mesh['gx'=8,'gy'=16] {'gx','gy'}, use_global_device_ids=true, to_apply=%region_12.13 | all-reduce | flops 1 | bytes 8 | tf_op jit(solution)/shard_map/pmax | solution.py:55
  662.5 4.2 collective-permute-start.18
  666.8 3.4 collective-permute-done.19
  672.7 5.0 fusion.27
  678.8 3.9 collective-permute-start.21
  686.1 67.7 %pmax.46 = f32[]{:T(128)} all-reduce(f32[]{:T(128)} %get-tuple-element.11), channel_id=1, replica_groups=mesh['gx'=8,'gy'=16] {'gx','gy'}, use_global_device_ids=true, to_apply=%region_14.15 | all-reduce | flops 1 | bytes 8 | tf_op jit(solution)/shard_map/pmax | solution.py:55
  758.4 4.0 collective-permute-start.22
  762.5 3.6 collective-permute-done.23
  768.6 5.0 fusion.30
  774.7 3.9 collective-permute-start.25
  779.4 1.9 collective-permute-start.24
  781.4 67.4 %pmax.47 = f32[]{:T(128)} all-reduce(f32[]{:T(128)} %get-tuple-element.9), channel_id=1, replica_groups=mesh['gx'=8,'gy'=16] {'gx','gy'}, use_global_device_ids=true, to_apply=%region_16.17 | all-reduce | flops 1 | bytes 8 | tf_op jit(solution)/shard_map/pmax | solution.py:55
  852.7 4.0 collective-permute-start.26
  856.8 3.4 collective-permute-done.27
  862.7 2.9 fusion.183
  867.9 68.2 %all-reduce.18 = (f32[16,16]{1,0:T(8,128)S(1)}, f32[16,16]{1,0:T(8,128)S(1)}) all-reduce(f32[16,16]{1,0:T(8,128)S(1)} %fusion.163, f32[16,16]{1,0:T(8,128)S(1)} %fusion.166), channel_id=1, replica_groups=mesh['gx'=8,'gy'=16] {'gx','gy'}, use_global_device_ids=true, to_apply=%region_21.22 | all-reduce | flops 512 | bytes 4096 | tf_op jit(solution)/shard_map/psum | solution.py:126
  940.6 2.0 fusion.12
  (146 shorter events, 74.0 us)
Async XLA Ops:
  4.2 45.0 %all-to-all-start = ((s32[1,128,2,128]{3,2,0,1:T(2,128)}), s32[1,128,2,128]{3,2,0,1:T(2,128)S(1)}, u32[]{:S(2)}, u32[]{:S(2)}) async-start(s32[1,128,2,128]{3,2,0,1:T(2,128)} %bitcast.5), calls=%async_computation | async-start | bytes 262144 | tf_op jit(solution)/shard_map/all_to_all | solution.py:98
  16.7 27.1 %collective-permute-start.1 = (bf16[16,8,1]{2,0,1:T(8,128)(2,1)S(1)}, bf16[16,8,1]{2,0,1:T(8,128)(2,1)S(1)}, u32[]{:S(2)}, u32[]{:S(2)}) collective-permute-start(bf16[16,8,1]{2,0,1:T(8,128)(2,1)S(1)} %get-tuple-element.46), channel_id=1, source_target_pairs={{16,0},{32,16},{48,32},{64,48},{80,64},{96,80},{112,96},{17,1},{33... | collective-permute-start | bytes 776 | tf_op jit(solution)/shard_map/ppermute | solution.py:22
  19.6 24.1 %collective-permute-start = (bf16[16,8,1]{2,0,1:T(8,128)(2,1)S(1)}, bf16[16,8,1]{2,0,1:T(8,128)(2,1)S(1)}, u32[]{:S(2)}, u32[]{:S(2)}) collective-permute-start(bf16[16,8,1]{2,0,1:T(8,128)(2,1)S(1)} %get-tuple-element.45), channel_id=1, source_target_pairs={{0,16},{16,32},{32,48},{48,64},{64,80},{80,96},{96,112},{1,17},{17... | collective-permute-start | bytes 776 | tf_op jit(solution)/shard_map/ppermute | solution.py:19
  23.1 6.1 copy-start.6
  43.9 258.9 %collective-permute-start.3 = (bf16[16,1,130]{2,0,1:T(8,128)(2,1)S(1)}, bf16[16,1,130]{2,0,1:T(8,128)(2,1)S(1)}, u32[]{:S(2)}, u32[]{:S(2)}) collective-permute-start(bf16[16,1,130]{2,0,1:T(8,128)(2,1)S(1)} %get-tuple-element.44), channel_id=1, source_target_pairs={{1,0},{2,1},{3,2},{4,3},{5,4},{6,5},{7,6},{8,7},{9,8},{10,9},{11,1... | collective-permute-start | bytes 12488 | tf_op jit(solution)/shard_map/ppermute | solution.py:22
  45.2 257.6 %collective-permute-start.2 = (bf16[16,1,130]{2,0,1:T(8,128)(2,1)S(1)}, bf16[16,1,130]{2,0,1:T(8,128)(2,1)S(1)}, u32[]{:S(2)}, u32[]{:S(2)}) collective-permute-start(bf16[16,1,130]{2,0,1:T(8,128)(2,1)S(1)} %get-tuple-element.43), channel_id=1, source_target_pairs={{0,1},{1,2},{2,3},{3,4},{4,5},{5,6},{6,7},{7,8},{8,9},{9,10},{10,1... | collective-permute-start | bytes 12488 | tf_op jit(solution)/shard_map/ppermute | solution.py:19
  49.2 30.5 %all-to-all-start.1 = ((bf16[16,128,2,128]{3,0,2,1:T(8,128)(2,1)}), bf16[16,128,2,128]{3,0,2,1:T(8,128)(2,1)S(1)}, u32[]{:S(2)}, u32[]{:S(2)}) async-start(bf16[16,128,2,128]{3,0,2,1:T(8,128)(2,1)} %bitcast.9), calls=%async_computation.1 | async-start | bytes 2097152 | tf_op jit(solution)/shard_map/all_to_all | solution.py:91
  250.4 51.5 %copy-start.5 = (f32[16,8,128]{2,1,0:T(8,128)S(1)}, f32[16,8,128]{2,1,0:T(8,128)}, u32[]{:S(2)}) copy-start(f32[16,8,128]{2,1,0:T(8,128)} %param.10) | copy-start | bytes 196612
  257.0 115.0 %collective-permute-start.5 = (f32[16,16,8,1]{1,2,3,0:T(8,128)S(1)}, f32[16,16,8,1]{1,2,3,0:T(8,128)S(1)}, u32[]{:S(2)}, u32[]{:S(2)}) collective-permute-start(f32[16,16,8,1]{1,2,3,0:T(8,128)S(1)} %copy.557), channel_id=1, source_target_pairs={{16,0},{32,16},{48,32},{64,48},{80,64},{96,80},{112,96},{17,1},{33... | collective-permute-start | bytes 24584 | tf_op jit(solution)/shard_map/ppermute | solution.py:22
  299.3 73.5 %collective-permute-start.4 = (f32[16,16,8,1]{1,2,3,0:T(8,128)}, f32[16,16,8,1]{1,2,3,0:T(8,128)S(1)}, u32[]{:S(2)}, u32[]{:S(2)}) collective-permute-start(f32[16,16,8,1]{1,2,3,0:T(8,128)} %copy.556), channel_id=1, source_target_pairs={{0,16},{16,32},{32,48},{48,64},{64,80},{80,96},{96,112},{1,17},{17... | collective-permute-start | bytes 24584 | tf_op jit(solution)/shard_map/ppermute | solution.py:19
  373.6 11.0 %copy-start.1 = (f32[16,16,8,1]{3,1,2,0:T(8,128)}, f32[16,16,8,1]{3,1,2,0:T(8,128)S(1)}, u32[]{:S(2)}) copy-start(f32[16,16,8,1]{3,1,2,0:T(8,128)S(1)} %copy.503) | copy-start | bytes 24580
  373.9 8.9 collective-permute-start.7
  375.2 8.5 collective-permute-start.6
  391.5 75.1 %collective-permute-start.9 = (f32[16,16,8,1]{1,2,3,0:T(8,128)S(1)}, f32[16,16,8,1]{1,2,3,0:T(8,128)S(1)}, u32[]{:S(2)}, u32[]{:S(2)}) collective-permute-start(f32[16,16,8,1]{1,2,3,0:T(8,128)S(1)} %copy.520), channel_id=1, source_target_pairs={{16,0},{32,16},{48,32},{64,48},{80,64},{96,80},{112,96},{17,1},{33... | collective-permute-start | bytes 24584 | tf_op jit(solution)/shard_map/ppermute | solution.py:22
  396.9 70.6 %collective-permute-start.8 = (f32[16,16,8,1]{1,2,3,0:T(8,128)}, f32[16,16,8,1]{1,2,3,0:T(8,128)}, u32[]{:S(2)}, u32[]{:S(2)}) collective-permute-start(f32[16,16,8,1]{1,2,3,0:T(8,128)} %copy.519), channel_id=1, source_target_pairs={{0,16},{16,32},{32,48},{48,64},{64,80},{80,96},{96,112},{1,17},{17... | collective-permute-start | bytes 24584 | tf_op jit(solution)/shard_map/ppermute | solution.py:19
  469.1 10.9 %copy-start.2 = (f32[16,16,8,1]{3,1,2,0:T(8,128)}, f32[16,16,8,1]{3,1,2,0:T(8,128)S(1)}, u32[]{:S(2)}) copy-start(f32[16,16,8,1]{3,1,2,0:T(8,128)S(1)} %copy.521) | copy-start | bytes 24580
  469.4 8.8 collective-permute-start.11
  470.7 8.4 collective-permute-start.10
  486.8 75.9 %collective-permute-start.13 = (f32[16,16,8,1]{1,2,3,0:T(8,128)S(1)}, f32[16,16,8,1]{1,2,3,0:T(8,128)S(1)}, u32[]{:S(2)}, u32[]{:S(2)}) collective-permute-start(f32[16,16,8,1]{1,2,3,0:T(8,128)S(1)} %copy.526), channel_id=1, source_target_pairs={{16,0},{32,16},{48,32},{64,48},{80,64},{96,80},{112,96},{17,1},{33... | collective-permute-start | bytes 24584 | tf_op jit(solution)/shard_map/ppermute | solution.py:22
  492.3 71.2 %collective-permute-start.12 = (f32[16,16,8,1]{1,2,3,0:T(8,128)}, f32[16,16,8,1]{1,2,3,0:T(8,128)}, u32[]{:S(2)}, u32[]{:S(2)}) collective-permute-start(f32[16,16,8,1]{1,2,3,0:T(8,128)} %copy.525), channel_id=1, source_target_pairs={{0,16},{16,32},{32,48},{48,64},{64,80},{80,96},{96,112},{1,17},{17... | collective-permute-start | bytes 24584 | tf_op jit(solution)/shard_map/ppermute | solution.py:19
  565.2 11.2 %copy-start.3 = (f32[16,16,8,1]{3,1,2,0:T(8,128)}, f32[16,16,8,1]{3,1,2,0:T(8,128)S(1)}, u32[]{:S(2)}) copy-start(f32[16,16,8,1]{3,1,2,0:T(8,128)S(1)} %copy.527) | copy-start | bytes 24580
  565.5 9.1 collective-permute-start.15
  566.8 8.7 collective-permute-start.14
  583.2 75.2 %collective-permute-start.17 = (f32[16,16,8,1]{1,2,3,0:T(8,128)S(1)}, f32[16,16,8,1]{1,2,3,0:T(8,128)S(1)}, u32[]{:S(2)}, u32[]{:S(2)}) collective-permute-start(f32[16,16,8,1]{1,2,3,0:T(8,128)S(1)} %copy.532), channel_id=1, source_target_pairs={{16,0},{32,16},{48,32},{64,48},{80,64},{96,80},{112,96},{17,1},{33... | collective-permute-start | bytes 24584 | tf_op jit(solution)/shard_map/ppermute | solution.py:22
  588.4 70.9 %collective-permute-start.16 = (f32[16,16,8,1]{1,2,3,0:T(8,128)}, f32[16,16,8,1]{1,2,3,0:T(8,128)}, u32[]{:S(2)}, u32[]{:S(2)}) collective-permute-start(f32[16,16,8,1]{1,2,3,0:T(8,128)} %copy.531), channel_id=1, source_target_pairs={{0,16},{16,32},{32,48},{48,64},{64,80},{80,96},{96,112},{1,17},{17... | collective-permute-start | bytes 24584 | tf_op jit(solution)/shard_map/ppermute | solution.py:19
  660.9 11.0 %copy-start.4 = (f32[16,16,8,1]{3,1,2,0:T(8,128)}, f32[16,16,8,1]{3,1,2,0:T(8,128)S(1)}, u32[]{:S(2)}) copy-start(f32[16,16,8,1]{3,1,2,0:T(8,128)S(1)} %copy.533) | copy-start | bytes 24580
  661.2 9.0 collective-permute-start.19
  662.5 8.5 collective-permute-start.18
  677.7 8.4 copy-start.7
  678.8 75.5 %collective-permute-start.21 = (f32[16,16,8,1]{1,2,3,0:T(8,128)S(1)}, f32[16,16,8,1]{1,2,3,0:T(8,128)S(1)}, u32[]{:S(2)}, u32[]{:S(2)}) collective-permute-start(f32[16,16,8,1]{1,2,3,0:T(8,128)S(1)} %copy.538), channel_id=1, source_target_pairs={{16,0},{32,16},{48,32},{64,48},{80,64},{96,80},{112,96},{17,1},{33... | collective-permute-start | bytes 24584 | tf_op jit(solution)/shard_map/ppermute | solution.py:22
  684.2 71.0 %collective-permute-start.20 = (f32[16,16,8,1]{1,2,3,0:T(8,128)}, f32[16,16,8,1]{1,2,3,0:T(8,128)}, u32[]{:S(2)}, u32[]{:S(2)}) collective-permute-start(f32[16,16,8,1]{1,2,3,0:T(8,128)} %copy.537), channel_id=1, source_target_pairs={{0,16},{16,32},{32,48},{48,64},{64,80},{80,96},{96,112},{1,17},{17... | collective-permute-start | bytes 24584 | tf_op jit(solution)/shard_map/ppermute | solution.py:19
  756.8 11.0 %copy-start = (f32[16,16,8,1]{3,1,2,0:T(8,128)}, f32[16,16,8,1]{3,1,2,0:T(8,128)S(1)}, u32[]{:S(2)}) copy-start(f32[16,16,8,1]{3,1,2,0:T(8,128)S(1)} %copy.539) | copy-start | bytes 24580
  757.1 8.9 collective-permute-start.23
  758.4 8.5 collective-permute-start.22
  773.5 7.8 copy-start.8
  774.7 74.8 %collective-permute-start.25 = (f32[16,16,8,1]{1,2,3,0:T(8,128)S(1)}, f32[16,16,8,1]{1,2,3,0:T(8,128)S(1)}, u32[]{:S(2)}, u32[]{:S(2)}) collective-permute-start(f32[16,16,8,1]{1,2,3,0:T(8,128)S(1)} %copy.544), channel_id=1, source_target_pairs={{16,0},{32,16},{48,32},{64,48},{80,64},{96,80},{112,96},{17,1},{33... | collective-permute-start | bytes 24584 | tf_op jit(solution)/shard_map/ppermute | solution.py:22
  779.4 70.9 %collective-permute-start.24 = (f32[16,16,8,1]{1,2,3,0:T(8,128)S(1)}, f32[16,16,8,1]{1,2,3,0:T(8,128)S(1)}, u32[]{:S(2)}, u32[]{:S(2)}) collective-permute-start(f32[16,16,8,1]{1,2,3,0:T(8,128)S(1)} %copy.543), channel_id=1, source_target_pairs={{0,16},{16,32},{32,48},{48,64},{64,80},{80,96},{96,112},{1,17},{17... | collective-permute-start | bytes 24584 | tf_op jit(solution)/shard_map/ppermute | solution.py:19
  851.4 8.8 collective-permute-start.27
  852.7 8.4 collective-permute-start.26
  865.6 2.1 copy-start.9
  865.7 2.1 copy-start.10
where the time goes:
time: 953 us; the launch traced here: 944 us
  blocking collectives  469 us (49%)
  other arithmetic  210 us (22%)
  starting transfers between devices  140 us (15%)
  local copies, waits for them, and re-layouts  73 us (8%)
  waiting for transfers between devices  44.6 us (5%)
    pmax x6, blocking collectives, peak_step(): global_peak = lax.pmax(local_peak, ('gx', 'gy'))  401 us
    scatter-add x1, other arithmetic, on_device(): flat_state = state_prior.reshape(members, -1).at[:, cells_in.reshape(-1)]...  163 us
    ppermute x14, starting transfers between devices, padded_2(): lax.ppermute(lax.slice_in_dim(block, 0, width, axis=dim), axis, backward)  73.1 us
    psum x1, blocking collectives, on_device(): cross, target_sum = lax.psum((cross, target_sum), ('gx', 'gy'))  68.2 us
    ppermute x14, starting transfers between devices, padded_2(): lax.ppermute(lax.slice_in_dim(block, block.shape[dim] - width, None, axis...  43.5 us
    reduce_max x6, other arithmetic, peak_step(): jnp.max(conductivity[None] * (1.0 + 0.25 * field_now * field_now))  25.8 us
    ppermute x14, waiting for transfers between devices, padded_2(): lax.ppermute(lax.slice_in_dim(block, 0, width, axis=dim), axis, backward)  20.5 us
  transfers between devices with their start and end apart: 30, of which 13 were waited for; matrix products, arithmetic and copies ran while one was open for 23% of the time, Pallas kernels for 0%

commit v1 on v0

v1 whole, which is shorter than its diff:
```python
import functools

import jax
import jax.numpy as jnp
from jax import lax
from jax.experimental import pallas as pl
from jax.experimental.pallas import tpu as pltpu
from jax.sharding import PartitionSpec as P

SUBSTEPS = 6
CAP = 2
COOL = 0.1
SHARE = 0.9
F32 = jnp.float32
BF16 = jnp.bfloat16
VM = pltpu.VMEM
LIMIT = 48 * 1024 * 1024
NT = (((1,), (1,)), ((), ()))
BOTH = ("gx", "gy")

M, NZ, CY, CX = 16, 16, 8, 128
ROWS = 40


def vspec():
    return pl.BlockSpec(memory_space=pltpu.VMEM)


def params():
    return pltpu.CompilerParams(vmem_limit_bytes=LIMIT)


def lanes():
    return lax.broadcasted_iota(jnp.int32, (CY, CX), 1)


def rows():
    return lax.broadcasted_iota(jnp.int32, (CY, CX), 0)


def pack_kernel(owner, heat, voxel, out, wide, high, low, inverse):
    blocks = owner.shape[0]
    devices = out.shape[0]

    def clear(i, carry):
        inverse[i] = blocks
        return carry

    lax.fori_loop(0, devices * CAP, clear, 0, unroll=16)

    def place(b, carry):
        base = owner[b] * CAP
        base = base + jnp.where(inverse[base] != blocks, 1, 0)
        inverse[base] = b
        return carry

    lax.fori_loop(0, blocks, place, 0, unroll=8)

    def widen(m, carry):
        wide[m, 0:blocks, :] = heat[m].astype(F32)
        wide[m, blocks:, :] = jnp.zeros((8, CX), F32)
        return carry

    lax.fori_loop(0, M, widen, 0)
    cells = voxel[...]
    high[0:blocks, :] = (cells >> 7).astype(F32)
    high[blocks:, :] = jnp.zeros((8, CX), F32)
    low[0:blocks, :] = (cells & 127).astype(F32)
    low[blocks:, :] = jnp.zeros((8, CX), F32)
    row = rows()

    def emit(d, carry):
        first = inverse[d * CAP]
        second = inverse[d * CAP + 1]
        index = jnp.where(
            row == 0,
            high[pl.ds(first, 1), :],
            jnp.where(
                row == 1,
                high[pl.ds(second, 1), :],
                jnp.where(
                    row == 2,
                    low[pl.ds(first, 1), :],
                    jnp.where(row == 3, low[pl.ds(second, 1), :], 0.0),
                ),
            ),
        )
        chunk = jnp.concatenate(
            [
                wide[:, pl.ds(first, 1), :].reshape(M, CX),
                wide[:, pl.ds(second, 1), :].reshape(M, CX),
                index,
            ],
            axis=0,
        )
        out[d] = chunk.astype(BF16)
        return carry

    lax.fori_loop(0, devices, emit, 0, unroll=4)


def pack(owner, heat, voxel, devices):
    blocks = owner.shape[0]
    return pl.pallas_call(
        pack_kernel,
        out_shape=jax.ShapeDtypeStruct((devices, ROWS, CX), BF16),
        in_specs=[pl.BlockSpec(memory_space=pltpu.SMEM), vspec(), vspec()],
        out_specs=vspec(),
        scratch_shapes=[
            VM((M, blocks + 8, CX), F32),
            VM((blocks + 8, CX), F32),
            VM((blocks + 8, CX), F32),
            pltpu.SMEM((devices * CAP,), jnp.int32),
        ],
        compiler_params=params(),
        name="pack",
    )(owner, heat, voxel)


def pack_columns(field):
    lane = lanes()
    packed = jnp.zeros((CY, CX), F32)
    for z in range(NZ):
        packed = jnp.where((lane >> 1) == z, pltpu.roll(field[z], 2 * z + 1, axis=1), packed)
    return packed


def coef_kernel(conduct, half, eighth, cols, lo, hi):
    base = conduct[...]
    half[...] = 0.5 * base
    eighth[...] = 0.125 * base
    packed = pack_columns([0.5 * conduct[z] for z in range(NZ)])
    packed = packed + pltpu.roll(packed, 32, axis=1)
    cols[...] = packed + pltpu.roll(packed, 64, axis=1)
    for z0 in (0, 8):
        lo[z0 : z0 + 8, :] = 0.5 * conduct[z0 : z0 + 8, 0, :]
        hi[z0 : z0 + 8, :] = 0.5 * conduct[z0 : z0 + 8, CY - 1, :]


def coefs(conduct):
    whole = jax.ShapeDtypeStruct((NZ, CY, CX), F32)
    row = jax.ShapeDtypeStruct((NZ, CX), F32)
    return pl.pallas_call(
        coef_kernel,
        out_shape=[whole, whole, jax.ShapeDtypeStruct((CY, CX), F32), row, row],
        in_specs=[vspec()],
        out_specs=[vspec()] * 5,
        compiler_params=params(),
        name="coefs",
    )(conduct)


def finish_member(m, new, field, cols, lo, hi):
    lane = lanes()
    packed = pltpu.roll(pack_columns(new), 32 * (m % 4), axis=1)
    held = cols[m // 4]
    cols[m // 4] = jnp.where((lane >> 5) == m % 4, packed, held)
    for z0 in (0, 8):
        lo[m, z0 : z0 + 8, :] = field[m, z0 : z0 + 8, 0, :]
        hi[m, z0 : z0 + 8, :] = field[m, z0 : z0 + 8, CY - 1, :]


def spread_peak(peak, out):
    row = jnp.max(peak, axis=0, keepdims=True)
    for d in range(out.shape[0]):
        out[d] = row


EDGE_SHAPES = [
    jax.ShapeDtypeStruct((M, NZ, CY, CX), F32),
    jax.ShapeDtypeStruct((M // 4, CY, CX), F32),
    jax.ShapeDtypeStruct((M, NZ, CX), F32),
    jax.ShapeDtypeStruct((M, NZ, CX), F32),
]


def deposit_kernel(incoming, state, half, eighth, field, cols, lo, hi, peaks, total):
    sources = incoming.shape[0]
    group = 4
    place = lax.broadcasted_iota(jnp.int32, (CX, CX), 0).astype(F32).astype(BF16)
    zero = jnp.zeros((M, CX), BF16)
    total[...] = jnp.zeros_like(total)

    def one(g, carry):
        left = []
        right = []
        for s in range(group):
            source = g * group + s
            index = incoming[source, 32:40, :].astype(F32)
            for slot in range(CAP):
                heat = incoming[source, slot * M : (slot + 1) * M, :]
                layer = jnp.broadcast_to(index[slot : slot + 1, :], (M, CX)).astype(BF16)
                cell = jnp.broadcast_to(index[2 + slot : 3 + slot, :], (CX, CX)).astype(BF16)
                left.append(
                    jnp.concatenate(
                        [jnp.where(layer == h, heat, zero) for h in range(2 * CY)], axis=0
                    )
                )
                right.append(jnp.where(place == cell, 1.0, 0.0).astype(BF16))
        total[...] += lax.dot_general(
            jnp.concatenate(left, axis=1),
            jnp.concatenate(right, axis=1),
            NT,
            preferred_element_type=F32,
        )
        return carry

    lax.fori_loop(0, sources // group, one, 0)

    def member(m, peak):
        new = []
        for z in range(NZ):
            value = state[m, z]
            if z < 2:
                value = value + total[pl.ds(z * CY * M + m, CY, stride=M), :]
            field[m, z] = value
            peak = jnp.maximum(peak, half[z] + eighth[z] * (value * value))
            new.append(value)
        finish_member(m, new, field, cols, lo, hi)
        return peak

    peak = lax.fori_loop(0, M, member, jnp.zeros((CY, CX), F32))
    spread_peak(peak, peaks)


def deposit(incoming, state, half, eighth):
    devices = incoming.shape[0]
    return pl.pallas_call(
        deposit_kernel,
        out_shape=EDGE_SHAPES + [jax.ShapeDtypeStruct((devices, 1, CX), F32)],
        in_specs=[vspec()] * 4,
        out_specs=[vspec()] * 5,
        scratch_shapes=[VM((2 * CY * M, CX), F32)],
        compiler_params=params(),
        name="deposit",
    )(incoming, state, half, eighth)


def substep_kernel(
    last,
    field, cols, lo, hi,
    from_left, from_right, from_low, from_high,
    peaks,
    half, eighth, cols_k, lo_k, hi_k,
    left_k, right_k, low_k, high_k,
    *rest,
):
    if last:
        weight, data, out, sums, side, border, flat, flat_data = rest
    else:
        out, out_cols, out_lo, out_hi, out_peaks, side, border = rest
    lane = lanes()
    row = rows()
    even = (lane & 1) == 0
    edge_lane = (lane == 0) | (lane == CX - 1)
    not_last_lane = lane != CX - 1
    not_last_row = row != CY - 1

    peak = peaks[0]
    for d in range(1, peaks.shape[0]):
        peak = jnp.maximum(peak, peaks[d])
    peak = 2.0 * jnp.max(peak, axis=1, keepdims=True)
    step = jnp.broadcast_to(SHARE / (6.0 * peak + COOL), (CY, CX))

    own_k = cols_k[...]
    next_k = jnp.where(even, pltpu.roll(right_k[...], CX - 1, axis=1), pltpu.roll(left_k[...], 1, axis=1))
    for q in range(M // 4):
        own = cols[q]
        near = jnp.where(
            even, pltpu.roll(from_right[q], CX - 1, axis=1), pltpu.roll(from_left[q], 1, axis=1)
        )
        both = own_k * (1.0 + 0.25 * (own * own)) + next_k * (1.0 + 0.25 * (near * near))
        side[q] = both * (near - own)
    border[...] = jnp.zeros_like(border)

    def member(m, peak):
        for z0 in (0, 8):
            at = slice(z0, z0 + 8)
            for own_ref, near_ref, own_c, near_c, where in (
                (lo, from_low, lo_k, low_k, 0),
                (hi, from_high, hi_k, high_k, CY - 1),
            ):
                own = own_ref[m, at, :]
                near = near_ref[m, at, :]
                both = own_c[at, :] * (1.0 + 0.25 * (own * own)) + near_c[at, :] * (
                    1.0 + 0.25 * (near * near)
                )
                border[at, where, :] = both * (near - own)
        beside = pltpu.roll(side[m // 4], (CX - 32 * (m % 4)) % CX, axis=1)
        new = []
        u = field[m, 0]
        h = half[0] + eighth[0] * (u * u)
        flux_up = COOL * u
        for z in range(NZ):
            if z < NZ - 1:
                u_next = field[m, z + 1]
                h_next = half[z + 1] + eighth[z + 1] * (u_next * u_next)
                flux_down = (h + h_next) * (u_next - u)
            flux = (h + pltpu.roll(h, CX - 1, axis=1)) * (pltpu.roll(u, CX - 1, axis=1) - u)
            flux = jnp.where(not_last_lane, flux, 0.0)
            change = flux - pltpu.roll(flux, 1, axis=1)
            flux = (h + pltpu.roll(h, CY - 1, axis=0)) * (pltpu.roll(u, CY - 1, axis=0) - u)
            flux = jnp.where(not_last_row, flux, 0.0)
            change = change + (flux - pltpu.roll(flux, 1, axis=0))
            change = change + border[z]
            change = change + jnp.where(edge_lane, pltpu.roll(beside, CX - 1 - 2 * z, axis=1), 0.0)
            change = change - flux_up
            if z < NZ - 1:
                change = change + flux_down
            value = u + step * change
            out[m, z] = value
            if not last:
                peak = jnp.maximum(peak, half[z] + eighth[z] * (value * value))
                new.append(value)
            if z < NZ - 1:
                u, h, flux_up = u_next, h_next, flux_down
        if not last:
            finish_member(m, new, out, out_cols, out_lo, out_hi)
        return peak

    peak = lax.fori_loop(0, M, member, jnp.zeros((CY, CX), F32))
    if not last:
        spread_peak(peak, out_peaks)
        return

    grams = jnp.zeros((M, 2 * M), F32)
    for y in range(CY):
        for m in range(M):
            flat[m : m + 1, :] = out[m, 0, y : y + 1, :]
            flat_data[m : m + 1, :] = data[m, y : y + 1, :]
        seen = flat[...]
        w = weight[y : y + 1, :]
        spread = seen - jnp.mean(seen, axis=0, keepdims=True)
        both = jnp.concatenate([spread * w, flat_data[...] - seen * w], axis=0)
        grams = grams + lax.dot_general(
            spread, both, NT, precision=lax.Precision.HIGHEST, preferred_element_type=F32
        )
    grams = jnp.concatenate([grams, jnp.zeros((M, CX - 2 * M), F32)], axis=1)
    pair = grams[0:8] + pltpu.roll(grams[8:16], 32, axis=1)
    pair = jnp.where(lane < 64, pair, 0.0)
    quad = pair + pltpu.roll(pltpu.roll(pair, 64, axis=1), 4, axis=0)
    quad = quad[0:4]
    for d in range(sums.shape[0]):
        sums[d] = quad


def substep(field, edges, halos, peaks, coef, coef_halos, pixels=None):
    last = pixels is not None
    devices = peaks.shape[0]
    operands = [field, *edges, *halos, peaks, *coef, *coef_halos]
    scratch = [VM((M // 4, CY, CX), F32), VM((NZ, CY, CX), F32)]
    if last:
        operands += list(pixels)
        out_shape = [EDGE_SHAPES[0], jax.ShapeDtypeStruct((devices, 4, CX), F32)]
        scratch += [VM((M, CX), F32), VM((M, CX), F32)]
    else:
        out_shape = EDGE_SHAPES + [jax.ShapeDtypeStruct((devices, 1, CX), F32)]
    return pl.pallas_call(
        functools.partial(substep_kernel, last),
        out_shape=out_shape,
        in_specs=[vspec()] * len(operands),
        out_specs=[vspec()] * len(out_shape),
        scratch_shapes=scratch,
        compiler_params=params(),
        name="substep_last" if last else "substep",
    )(*operands)


def pixel_kernel(cell, observed, variance, noise, weight, data):
    pixels = cell.shape[1]
    place = cell[...]
    var = variance[...]
    inverse = 1.0 / var
    values = (observed[...] + noise[...] * jnp.sqrt(var)) * inverse
    stack = jnp.concatenate([values, jnp.broadcast_to(inverse, (8, pixels))], axis=0)
    width = place >> 7
    hot = jnp.where(
        lax.broadcasted_iota(jnp.int32, (CX, pixels), 0) == (place & 127), 1.0, 0.0
    ).astype(F32)
    for y in range(CY):
        part = lax.dot_general(
            jnp.where(width == y, stack, 0.0),
            hot,
            NT,
            precision=lax.Precision.HIGHEST,
            preferred_element_type=F32,
        )
        weight[y : y + 1, :] = part[M : M + 1, :]
        for m in range(M):
            data[m, y : y + 1, :] = part[m : m + 1, :]


def pixel_sums(cell, observed, variance, noise):
    return pl.pallas_call(
        pixel_kernel,
        out_shape=[
            jax.ShapeDtypeStruct((CY, CX), F32),
            jax.ShapeDtypeStruct((M, CY, CX), F32),
        ],
        in_specs=[vspec()] * 4,
        out_specs=[vspec()] * 2,
        compiler_params=params(),
        name="pixels",
    )(cell, observed, variance, noise)


def update_kernel(sums, field, out, weights):
    quad = sums[0]
    for d in range(1, sums.shape[0]):
        quad = quad + sums[d]
    lane = lanes()
    row = rows()
    quad = jnp.concatenate([quad, jnp.zeros_like(quad)], axis=0)
    pair = jnp.where(row < 4, quad, pltpu.roll(pltpu.roll(quad, 64, axis=1), 4, axis=0))
    system = jnp.concatenate([pair, pltpu.roll(pair, CX - 32, axis=1)], axis=0)
    tall = lax.broadcasted_iota(jnp.int32, (M, CX), 0)
    wide = lax.broadcasted_iota(jnp.int32, (M, CX), 1)
    system = jnp.where(tall == wide, system + (M - 1.0), system)
    for i in range(M):
        pivot = system[i : i + 1, :]
        pivot = pivot / pivot[:, i : i + 1]
        factor = jnp.where(tall == i, 0.0, jnp.broadcast_to(system[:, i : i + 1], (M, CX)))
        system = jnp.where(tall == i, pivot, system - factor * pivot)
    system = system - jnp.mean(system, axis=0, keepdims=True)
    for m in range(M):
        weights[m] = jnp.broadcast_to(system[:, M + m : M + m + 1], (M, CX))

    def layer(z, carry):
        prior = [field[k, z] for k in range(M)]
        for m in range(M):
            value = prior[m]
            for k in range(M):
                value = value + weights[m, k : k + 1, :] * prior[k]
            out[m, z] = value
        return carry

    lax.fori_loop(0, NZ, layer, 0)


def update(sums, field):
    return pl.pallas_call(
        update_kernel,
        out_shape=jax.ShapeDtypeStruct((M, NZ, CY, CX), F32),
        in_specs=[vspec()] * 2,
        out_specs=vspec(),
        scratch_shapes=[VM((M, M, CX), F32)],
        compiler_params=params(),
        name="update",
    )(sums, field)


def exchange(parts):
    return lax.all_to_all(parts, BOTH, split_axis=0, concat_axis=0, tiled=True)


def neighbours(to_right, to_left, to_high, to_low):
    def move(part, axis, ahead):
        count = lax.axis_size(axis)
        pairs = [(i, i + 1) if ahead else (i + 1, i) for i in range(count - 1)]
        return lax.ppermute(part, axis, pairs)

    return (
        move(to_right, "gx", True),
        move(to_left, "gx", False),
        move(to_high, "gy", True),
        move(to_low, "gy", False),
    )


def on_device(
    state_prior,
    conductivity,
    heat_input,
    owner_tile,
    voxel_list,
    pixel_cell,
    observed,
    pixel_variance,
    pixel_noise,
):
    devices = lax.axis_size("gx") * lax.axis_size("gy")
    pixels = pixel_cell.shape[0]
    outgoing = pack(owner_tile.reshape(-1), heat_input, voxel_list, devices)
    incoming = exchange(outgoing)
    half, eighth, cols_k, lo_k, hi_k = coefs(conductivity)
    coef = (half, eighth, cols_k, lo_k, hi_k)
    coef_halos = neighbours(cols_k, cols_k, hi_k, lo_k)
    seen = pixel_sums(
        pixel_cell.reshape(1, pixels),
        observed.reshape(1, pixels),
        pixel_variance.reshape(1, pixels),
        pixel_noise,
    )
    field, cols, lo, hi, peaks = deposit(incoming, state_prior, half, eighth)
    for s in range(SUBSTEPS):
        halos = neighbours(cols, cols, hi, lo)
        peaks = exchange(peaks)
        if s < SUBSTEPS - 1:
            field, cols, lo, hi, peaks = substep(
                field, (cols, lo, hi), halos, peaks, coef, coef_halos
            )
        else:
            field, sums = substep(field, (cols, lo, hi), halos, peaks, coef, coef_halos, seen)
    return update(exchange(sums), field)


def solution(mesh):
    in_specs = (
        P(None, None, "gy", "gx"),
        P(None, "gy", "gx"),
        P(None, BOTH, None),
        P(BOTH, None),
        P(BOTH, None),
        P(BOTH),
        P(BOTH),
        P(BOTH),
        P(None, BOTH),
    )
    out_specs = P(None, None, "gy", "gx")
    return jax.shard_map(
        on_device, mesh=mesh, in_specs=in_specs, out_specs=out_specs, check_vma=False
    )
```

time: 953 us -> 267 us (0.28)
  blocking collectives: 469 us -> 19.2 us
  other arithmetic: 210 us -> 0 us
  local copies, waits for them, and re-layouts: 73 us -> 4.56 us
  Pallas kernels: 0 us -> 60.3 us
    pmax x6 -> x0, blocking collectives: 401 us -> none  [peak_step(): global_peak = lax.pmax(local_peak, ('gx', 'gy'))]
    scatter-add x1 -> x0, other arithmetic: 163 us -> none  [on_device(): flat_state = state_prior.reshape(members, -1).at[:, cells_in.reshape(-1)]...]
    psum x1 -> x0, blocking collectives: 68.2 us -> none  [on_device(): cross, target_sum = lax.psum((cross, target_sum), ('gx', 'gy'))]
    pallas_call x0 -> x11, Pallas kernels: none -> 60.3 us  [the longest x6 36 us: substep(): pl.pallas_call(functools.partial(substep_kernel, last), out_shape=out_sha...]
    ppermute x28, starting transfers between devices: 117 us -> 67.3 us  [move(): return lax.ppermute(part, axis, pairs)]
    all_to_all x2 -> x7, starting transfers between devices: 23.1 us -> 71 us  [exchange(): return lax.all_to_all(parts, BOTH, split_axis=0, concat_axis=0, tiled=True)]
    reduce_max x6 -> x0, other arithmetic: 25.8 us -> none  [peak_step(): jnp.max(conductivity[None] * (1.0 + 0.25 * field_now * field_now))]
    all_to_all x0 -> x1, blocking collectives: none -> 19.2 us  [exchange(): return lax.all_to_all(parts, BOTH, split_axis=0, concat_axis=0, tiled=True)]
  transfers between devices with their start and end apart: 30 -> 35, of which waited for: 13 -> 12; matrix products, arithmetic and copies ran while one was open for 23% -> 0% of each run, Pallas kernels for 0% -> 1%
where the time goes in v1:
time: 267 us; the launch traced here: 266 us
  starting transfers between devices  138 us (52%)
  Pallas kernels  60.3 us (23%)
  waiting for transfers between devices  42.6 us (16%)
  blocking collectives  19.2 us (7%)
  local copies, waits for them, and re-layouts  4.56 us (2%)
    all_to_all x7, starting transfers between devices, exchange(): return lax.all_to_all(parts, BOTH, split_axis=0, concat_axis=0, tiled=True)  71 us
    ppermute x28, starting transfers between devices, move(): return lax.ppermute(part, axis, pairs)  67.3 us
    pallas_call x6, Pallas kernels, substep(): pl.pallas_call(functools.partial(substep_kernel, last), out_shape=out_sha...  36 us
    all_to_all x7, waiting for transfers between devices, exchange(): return lax.all_to_all(parts, BOTH, split_axis=0, concat_axis=0, tiled=True)  24.2 us
    all_to_all x1, blocking collectives, exchange(): return lax.all_to_all(parts, BOTH, split_axis=0, concat_axis=0, tiled=True)  19.2 us
    ppermute x28, waiting for transfers between devices, move(): return lax.ppermute(part, axis, pairs)  18.4 us
    pallas_call x1, Pallas kernels, deposit(): pl.pallas_call(deposit_kernel, out_shape=EDGE_SHAPES + [jax.ShapeDtypeStr...  13.9 us
  transfers between devices with their start and end apart: 35, of which 12 were waited for; matrix products, arithmetic and copies ran while one was open for 0% of the time, Pallas kernels for 1%

profile of v1, /device:TPU:1, one launch (start us, length us, event | category | flops | bytes accessed | tf_op | source)
XLA Modules:
  0.0 265.6 jit_solution(18089687276717124949)
XLA Ops:
  2.5 4.4 %pack.1 = bf16[128,40,128]{2,1,0:T(8,128)(2,1)} custom-call(s32[128]{0:T(128)S(1)} %bitcast.7, bf16[16,128,128]{2,1,0:T(8,128)(2,1)S(1)} %copy-done.1, s32[128,128]{1,0:T(8,128)S(1)} %copy-done.5), custom_call_target="tpu_custom_call" | custom-call | tf_op jit(solution)/shard_map/pack/pallas_call | solution.py:104
  7.0 11.5 %all-to-all-start = ((bf16[128,40,128]{2,1,0:T(8,128)(2,1)}), bf16[128,40,128]{2,1,0:T(8,128)(2,1)S(1)}, u32[]{:S(2)}, u32[]{:S(2)}) async-start(bf16[128,40,128]{2,1,0:T(8,128)(2,1)} %pack.1), calls=%async_computation | async-start | bytes 2621440 | tf_op jit(solution)/shard_map/all_to_all | solution.py:453
  18.7 21.1 %all-to-all-done.incoming = bf16[128,40,128]{2,1,0:T(8,128)(2,1)S(1)} async-done(((bf16[128,40,128]{2,1,0:T(8,128)(2,1)}), bf16[128,40,128]{2,1,0:T(8,128)(2,1)S(1)}, u32[]{:S(2)}, u32[]{:S(2)}) %all-to-all-start) | async-done | bytes 1310752 | tf_op jit(solution)/shard_map/all_to_all | solution.py:453
  39.8 13.9 %deposit.1 = (f32[16,16,8,128]{3,2,1,0:T(8,128)S(1)}, f32[4,8,128]{2,1,0:T(8,128)S(1)}, f32[16,16,128]{2,1,0:T(8,128)}, f32[16,16,128]{2,1,0:T(8,128)}, f32[128,1,128]{2,1,0:T(1,128)S(1)}) custom-call(bf16[128,40,128]{2,1,0:T(8,128)(2,1)S(1)} %all-to-all-done.incoming, f32[16,16,8,128]{3,2,1,0:T(8,128)S(1)} %copy-done, ...), custom_call_target="tpu_custom_call" | custom-call | tf_op jit(solution)/shard_map/deposit/pallas_call | solution.py:228
  54.4 2.5 collective-permute-start.2
  58.2 8.4 %all-to-all-start.1 = ((f32[128,1,128]{2,1,0:T(1,128)}), f32[128,1,128]{2,1,0:T(1,128)S(1)}, u32[]{:S(2)}, u32[]{:S(2)}) async-start(f32[128,1,128]{2,1,0:T(1,128)} %copy-done.7), calls=%async_computation.1 | async-start | bytes 131072 | tf_op jit(solution)/shard_map/all_to_all | solution.py:453
  66.6 3.5 %collective-permute-start.4 = (f32[8,128]{1,0:T(8,128)}, f32[8,128]{1,0:T(8,128)S(1)}, u32[]{:S(2)}, u32[]{:S(2)}) collective-permute-start(f32[8,128]{1,0:T(8,128)} %copy-done.2), channel_id=1, source_target_pairs={{0,16},{16,32},{32,48},{48,64},{64,80},{80,96},{96,112},{1,17},{17... | collective-permute-start | bytes 12296 | tf_op jit(solution)/shard_map/ppermute | solution.py:460
  70.2 1.9 collective-permute-start.5
  72.1 3.2 %collective-permute-start.6 = (f32[16,128]{1,0:T(8,128)S(1)}, f32[16,128]{1,0:T(8,128)S(1)}, u32[]{:S(2)}, u32[]{:S(2)}) collective-permute-start(f32[16,128]{1,0:T(8,128)S(1)} %get-tuple-element.53.hi_k), channel_id=1, source_target_pairs={{0,1},{1,2},{2,3},{3,4},{4,5},{5,6},{6,7},{7,8},{8,9},{9,10},{10,1... | collective-permute-start | bytes 24584 | tf_op jit(solution)/shard_map/ppermute | solution.py:460
  75.3 3.9 %collective-permute-start = (f32[4,8,128]{2,1,0:T(8,128)}, f32[4,8,128]{2,1,0:T(8,128)S(1)}, u32[]{:S(2)}, u32[]{:S(2)}) collective-permute-start(f32[4,8,128]{2,1,0:T(8,128)} %copy-done.9), channel_id=1, source_target_pairs={{0,16},{16,32},{32,48},{48,64},{64,80},{80,96},{96,112},{1,17},{17... | collective-permute-start | bytes 49160 | tf_op jit(solution)/shard_map/ppermute | solution.py:460
  79.3 1.9 collective-permute-start.1
  81.2 1.3 collective-permute-start.7
  82.5 3.1 %collective-permute-done.7.high_k = f32[16,128]{1,0:T(8,128)S(1)} collective-permute-done((f32[16,128]{1,0:T(8,128)S(1)}, f32[16,128]{1,0:T(8,128)S(1)}, u32[]{:S(2)}, u32[]{:S(2)}) %collective-permute-start.7) | collective-permute-done | bytes 8224 | tf_op jit(solution)/shard_map/ppermute | solution.py:460
  87.0 7.2 %substep.5 = (f32[16,16,8,128]{3,2,1,0:T(8,128)S(1)}, f32[4,8,128]{2,1,0:T(8,128)S(1)}, f32[16,16,128]{2,1,0:T(8,128)S(1)}, f32[16,16,128]{2,1,0:T(8,128)S(1)}, f32[128,1,128]{2,1,0:T(1,128)}) custom-call(f32[16,16,8,128]{3,2,1,0:T(8,128)S(1)} %get-tuple-element.46.field, f32[4,8,128]{2,1,0:T(8,128)S(1)} %copy-done.10, f32[16,16,128]{2,1,0:T(8,128)} %get-tuple-element.48.lo, ...), custom_call_target="tpu_custom_call" | custom-call | tf_op jit(solution)/shard_map/substep/pallas_call | solution.py:358
  94.2 3.4 %collective-permute-start.10 = (f32[16,16,128]{2,1,0:T(8,128)S(1)}, f32[16,16,128]{2,1,0:T(8,128)S(1)}, u32[]{:S(2)}, u32[]{:S(2)}) collective-permute-start(f32[16,16,128]{2,1,0:T(8,128)S(1)} %get-tuple-element.57.hi), channel_id=1, source_target_pairs={{0,1},{1,2},{2,3},{3,4},{4,5},{5,6},{6,7},{7,8},{8,9},{9,10},{10,1... | collective-permute-start | bytes 393224 | tf_op jit(solution)/shard_map/ppermute | solution.py:460
  97.6 1.3 collective-permute-start.11
  98.9 13.1 %all-to-all-start.2 = ((f32[128,1,128]{2,1,0:T(1,128)}), f32[128,1,128]{2,1,0:T(1,128)S(1)}, u32[]{:S(2)}, u32[]{:S(2)}) async-start(f32[128,1,128]{2,1,0:T(1,128)} %get-tuple-element.58), calls=%async_computation.2 | async-start | bytes 131072 | tf_op jit(solution)/shard_map/all_to_all | solution.py:453
  112.0 3.5 %collective-permute-start.8 = (f32[4,8,128]{2,1,0:T(8,128)S(1)}, f32[4,8,128]{2,1,0:T(8,128)S(1)}, u32[]{:S(2)}, u32[]{:S(2)}) collective-permute-start(f32[4,8,128]{2,1,0:T(8,128)S(1)} %get-tuple-element.55.cols), channel_id=1, source_target_pairs={{0,16},{16,32},{32,48},{48,64},{64,80},{80,96},{96,112},{1,17},{17... | collective-permute-start | bytes 49160 | tf_op jit(solution)/shard_map/ppermute | solution.py:460
  115.5 1.9 collective-permute-start.9
  117.5 3.4 %collective-permute-done.9.from_right = f32[4,8,128]{2,1,0:T(8,128)S(1)} collective-permute-done((f32[4,8,128]{2,1,0:T(8,128)S(1)}, f32[4,8,128]{2,1,0:T(8,128)S(1)}, u32[]{:S(2)}, u32[]{:S(2)}) %collective-permute-start.9) | collective-permute-done | bytes 16416 | tf_op jit(solution)/shard_map/ppermute | solution.py:460
  121.6 6.2 %substep.6 = (f32[16,16,8,128]{3,2,1,0:T(8,128)S(1)}, f32[4,8,128]{2,1,0:T(8,128)S(1)}, f32[16,16,128]{2,1,0:T(8,128)S(1)}, f32[16,16,128]{2,1,0:T(8,128)S(1)}, f32[128,1,128]{2,1,0:T(1,128)}) custom-call(f32[16,16,8,128]{3,2,1,0:T(8,128)S(1)} %get-tuple-element.54.field, f32[4,8,128]{2,1,0:T(8,128)S(1)} %get-tuple-element.55.cols, ...), custom_call_target="tpu_custom_call" | custom-call | tf_op jit(solution)/shard_map/substep/pallas_call | solution.py:358
  127.8 2.6 collective-permute-start.14
  131.7 9.5 %all-to-all-start.3 = ((f32[128,1,128]{2,1,0:T(1,128)}), f32[128,1,128]{2,1,0:T(1,128)S(1)}, u32[]{:S(2)}, u32[]{:S(2)}) async-start(f32[128,1,128]{2,1,0:T(1,128)} %get-tuple-element.63), calls=%async_computation.3 | async-start | bytes 131072 | tf_op jit(solution)/shard_map/all_to_all | solution.py:453
  141.2 3.5 %collective-permute-start.12 = (f32[4,8,128]{2,1,0:T(8,128)S(1)}, f32[4,8,128]{2,1,0:T(8,128)S(1)}, u32[]{:S(2)}, u32[]{:S(2)}) collective-permute-start(f32[4,8,128]{2,1,0:T(8,128)S(1)} %get-tuple-element.60.cols), channel_id=1, source_target_pairs={{0,16},{16,32},{32,48},{48,64},{64,80},{80,96},{96,112},{1,17},{17... | collective-permute-start | bytes 49160 | tf_op jit(solution)/shard_map/ppermute | solution.py:460
  144.7 1.9 collective-permute-start.13
  146.7 3.4 %collective-permute-done.13.from_right = f32[4,8,128]{2,1,0:T(8,128)S(1)} collective-permute-done((f32[4,8,128]{2,1,0:T(8,128)S(1)}, f32[4,8,128]{2,1,0:T(8,128)S(1)}, u32[]{:S(2)}, u32[]{:S(2)}) %collective-permute-start.13) | collective-permute-done | bytes 16416 | tf_op jit(solution)/shard_map/ppermute | solution.py:460
  150.7 6.2 %substep.7 = (f32[16,16,8,128]{3,2,1,0:T(8,128)S(1)}, f32[4,8,128]{2,1,0:T(8,128)S(1)}, f32[16,16,128]{2,1,0:T(8,128)S(1)}, f32[16,16,128]{2,1,0:T(8,128)S(1)}, f32[128,1,128]{2,1,0:T(1,128)}) custom-call(f32[16,16,8,128]{3,2,1,0:T(8,128)S(1)} %get-tuple-element.59.field, f32[4,8,128]{2,1,0:T(8,128)S(1)} %get-tuple-element.60.cols, ...), custom_call_target="tpu_custom_call" | custom-call | tf_op jit(solution)/shard_map/substep/pallas_call | solution.py:358
  156.9 2.6 collective-permute-start.18
  160.9 9.5 %all-to-all-start.4 = ((f32[128,1,128]{2,1,0:T(1,128)}), f32[128,1,128]{2,1,0:T(1,128)S(1)}, u32[]{:S(2)}, u32[]{:S(2)}) async-start(f32[128,1,128]{2,1,0:T(1,128)} %get-tuple-element.68), calls=%async_computation.4 | async-start | bytes 131072 | tf_op jit(solution)/shard_map/all_to_all | solution.py:453
  170.4 3.5 %collective-permute-start.16 = (f32[4,8,128]{2,1,0:T(8,128)S(1)}, f32[4,8,128]{2,1,0:T(8,128)S(1)}, u32[]{:S(2)}, u32[]{:S(2)}) collective-permute-start(f32[4,8,128]{2,1,0:T(8,128)S(1)} %get-tuple-element.65.cols), channel_id=1, source_target_pairs={{0,16},{16,32},{32,48},{48,64},{64,80},{80,96},{96,112},{1,17},{17... | collective-permute-start | bytes 49160 | tf_op jit(solution)/shard_map/ppermute | solution.py:460
  173.9 1.9 collective-permute-start.17
  175.9 3.4 %collective-permute-done.17.from_right = f32[4,8,128]{2,1,0:T(8,128)S(1)} collective-permute-done((f32[4,8,128]{2,1,0:T(8,128)S(1)}, f32[4,8,128]{2,1,0:T(8,128)S(1)}, u32[]{:S(2)}, u32[]{:S(2)}) %collective-permute-start.17) | collective-permute-done | bytes 16416 | tf_op jit(solution)/shard_map/ppermute | solution.py:460
  179.9 6.2 %substep.8 = (f32[16,16,8,128]{3,2,1,0:T(8,128)S(1)}, f32[4,8,128]{2,1,0:T(8,128)S(1)}, f32[16,16,128]{2,1,0:T(8,128)S(1)}, f32[16,16,128]{2,1,0:T(8,128)S(1)}, f32[128,1,128]{2,1,0:T(1,128)}) custom-call(f32[16,16,8,128]{3,2,1,0:T(8,128)S(1)} %get-tuple-element.64.field, f32[4,8,128]{2,1,0:T(8,128)S(1)} %get-tuple-element.65.cols, ...), custom_call_target="tpu_custom_call" | custom-call | tf_op jit(solution)/shard_map/substep/pallas_call | solution.py:358
  186.1 2.8 %collective-permute-start.22 = (f32[16,16,128]{2,1,0:T(8,128)S(1)}, f32[16,16,128]{2,1,0:T(8,128)S(1)}, u32[]{:S(2)}, u32[]{:S(2)}) collective-permute-start(f32[16,16,128]{2,1,0:T(8,128)S(1)} %get-tuple-element.72.hi), channel_id=1, source_target_pairs={{0,1},{1,2},{2,3},{3,4},{4,5},{5,6},{6,7},{7,8},{8,9},{9,10},{10,1... | collective-permute-start | bytes 393224 | tf_op jit(solution)/shard_map/ppermute | solution.py:460
  190.2 9.5 %all-to-all-start.5 = ((f32[128,1,128]{2,1,0:T(1,128)}), f32[128,1,128]{2,1,0:T(1,128)S(1)}, u32[]{:S(2)}, u32[]{:S(2)}) async-start(f32[128,1,128]{2,1,0:T(1,128)} %get-tuple-element.73), calls=%async_computation.5 | async-start | bytes 131072 | tf_op jit(solution)/shard_map/all_to_all | solution.py:453
  199.7 3.5 %collective-permute-start.20 = (f32[4,8,128]{2,1,0:T(8,128)S(1)}, f32[4,8,128]{2,1,0:T(8,128)S(1)}, u32[]{:S(2)}, u32[]{:S(2)}) collective-permute-start(f32[4,8,128]{2,1,0:T(8,128)S(1)} %get-tuple-element.70.cols), channel_id=1, source_target_pairs={{0,16},{16,32},{32,48},{48,64},{64,80},{80,96},{96,112},{1,17},{17... | collective-permute-start | bytes 49160 | tf_op jit(solution)/shard_map/ppermute | solution.py:460
  203.3 1.9 collective-permute-start.21
  205.2 3.4 %collective-permute-done.21.from_right = f32[4,8,128]{2,1,0:T(8,128)S(1)} collective-permute-done((f32[4,8,128]{2,1,0:T(8,128)S(1)}, f32[4,8,128]{2,1,0:T(8,128)S(1)}, u32[]{:S(2)}, u32[]{:S(2)}) %collective-permute-start.21) | collective-permute-done | bytes 16416 | tf_op jit(solution)/shard_map/ppermute | solution.py:460
  209.2 6.2 %substep.9 = (f32[16,16,8,128]{3,2,1,0:T(8,128)S(1)}, f32[4,8,128]{2,1,0:T(8,128)S(1)}, f32[16,16,128]{2,1,0:T(8,128)S(1)}, f32[16,16,128]{2,1,0:T(8,128)S(1)}, f32[128,1,128]{2,1,0:T(1,128)}) custom-call(f32[16,16,8,128]{3,2,1,0:T(8,128)S(1)} %get-tuple-element.69.field, f32[4,8,128]{2,1,0:T(8,128)S(1)} %get-tuple-element.70.cols, ...), custom_call_target="tpu_custom_call" | custom-call | tf_op jit(solution)/shard_map/substep/pallas_call | solution.py:358
  215.4 2.6 collective-permute-start.26
  219.4 9.5 %all-to-all-start.6 = ((f32[128,1,128]{2,1,0:T(1,128)}), f32[128,1,128]{2,1,0:T(1,128)S(1)}, u32[]{:S(2)}, u32[]{:S(2)}) async-start(f32[128,1,128]{2,1,0:T(1,128)} %get-tuple-element.78), calls=%async_computation.6 | async-start | bytes 131072 | tf_op jit(solution)/shard_map/all_to_all | solution.py:453
  228.9 3.5 %collective-permute-start.24 = (f32[4,8,128]{2,1,0:T(8,128)S(1)}, f32[4,8,128]{2,1,0:T(8,128)S(1)}, u32[]{:S(2)}, u32[]{:S(2)}) collective-permute-start(f32[4,8,128]{2,1,0:T(8,128)S(1)} %get-tuple-element.75.cols), channel_id=1, source_target_pairs={{0,16},{16,32},{32,48},{48,64},{64,80},{80,96},{96,112},{1,17},{17... | collective-permute-start | bytes 49160 | tf_op jit(solution)/shard_map/ppermute | solution.py:460
  232.4 1.9 collective-permute-start.25
  234.4 1.7 pixels.1
  236.2 1.6 collective-permute-done.25.from_right
  238.4 3.9 %substep_last.1 = (f32[16,16,8,128]{3,2,1,0:T(8,128)S(1)}, f32[128,4,128]{2,1,0:T(4,128)S(1)}) custom-call(f32[16,16,8,128]{3,2,1,0:T(8,128)S(1)} %get-tuple-element.74.field, f32[4,8,128]{2,1,0:T(8,128)S(1)} %get-tuple-element.75.cols, f32[16,16,128]{2,1,0:T(8,128)S(1)} %get-tuple-element.76.lo, f32[16,16,128]{2,1,0:T(8,128)S(1)} %get-tuple-element.77.hi, ...), custom_call_target="tpu_custom_call" | custom-call | tf_op jit(solution)/shard_map/substep_last/pallas_call | solution.py:358
  242.3 19.2 %all_to_all.40.sums = f32[128,4,128]{2,1,0:T(4,128)S(1)} all-to-all(f32[128,4,128]{2,1,0:T(4,128)S(1)} %get-tuple-element.81), channel_id=1, replica_groups=mesh['gx'=8,'gy'=16] {'gx','gy'}, dimensions={0} | all-to-all | bytes 524288 | tf_op jit(solution)/shard_map/all_to_all | solution.py:453
  261.5 4.0 %update.1 = f32[16,16,8,128]{3,2,1,0:T(8,128)} custom-call(f32[128,4,128]{2,1,0:T(4,128)S(1)} %all_to_all.40.sums, f32[16,16,8,128]{3,2,1,0:T(8,128)S(1)} %get-tuple-element.82.field), custom_call_target="tpu_custom_call" | custom-call | tf_op jit(solution)/shard_map/update/pallas_call | solution.py:441
  (64 shorter events, 14.4 us)
Async XLA Ops:
  0.0 1.0 copy-start.1
  1.0 0.8 copy-start.5
  7.0 11.5 %copy-start.6 = (f32[16,8,128]{2,1,0:T(8,128)S(1)}, f32[16,8,128]{2,1,0:T(8,128)}, u32[]{:S(2)}) copy-start(f32[16,8,128]{2,1,0:T(8,128)} %conduct.1) | copy-start | bytes 196612
  7.0 32.9 %copy-start = (f32[16,16,8,128]{3,2,1,0:T(8,128)S(1)}, f32[16,16,8,128]{3,2,1,0:T(8,128)}, u32[]{:S(2)}) copy-start(f32[16,16,8,128]{3,2,1,0:T(8,128)} %state.1) | copy-start | bytes 3145732
  7.0 32.9 %all-to-all-start = ((bf16[128,40,128]{2,1,0:T(8,128)(2,1)}), bf16[128,40,128]{2,1,0:T(8,128)(2,1)S(1)}, u32[]{:S(2)}, u32[]{:S(2)}) async-start(bf16[128,40,128]{2,1,0:T(8,128)(2,1)} %pack.1), calls=%async_computation | async-start | bytes 2621440 | tf_op jit(solution)/shard_map/all_to_all | solution.py:453
  18.7 21.1 %copy-start.2 = (f32[8,128]{1,0:T(8,128)}, f32[8,128]{1,0:T(8,128)S(1)}, u32[]{:S(2)}) copy-start(f32[8,128]{1,0:T(8,128)S(1)} %get-tuple-element.51.cols_k) | copy-start | bytes 12292
  54.4 3.8 %copy-start.7 = (f32[128,1,128]{2,1,0:T(1,128)}, f32[128,1,128]{2,1,0:T(1,128)S(1)}, u32[]{:S(2)}) copy-start(f32[128,1,128]{2,1,0:T(1,128)S(1)} %get-tuple-element.50) | copy-start | bytes 196612
  54.4 67.2 %copy-start.4 = (f32[8,128]{1,0:T(8,128)S(1)}, f32[8,128]{1,0:T(8,128)}, u32[]{:S(2)}) copy-start(f32[8,128]{1,0:T(8,128)} %copy-done.2) | copy-start | bytes 12292
  54.4 31.3 %collective-permute-start.2 = (f32[16,16,128]{2,1,0:T(8,128)}, f32[16,16,128]{2,1,0:T(8,128)S(1)}, u32[]{:S(2)}, u32[]{:S(2)}) collective-permute-start(f32[16,16,128]{2,1,0:T(8,128)} %get-tuple-element.49.hi), channel_id=1, source_target_pairs={{0,1},{1,2},{2,3},{3,4},{4,5},{5,6},{6,7},{7,8},{8,9},{9,10},{10,1... | collective-permute-start | bytes 393224 | tf_op jit(solution)/shard_map/ppermute | solution.py:460
  56.9 28.7 %collective-permute-start.3 = (f32[16,16,128]{2,1,0:T(8,128)}, f32[16,16,128]{2,1,0:T(8,128)S(1)}, u32[]{:S(2)}, u32[]{:S(2)}) collective-permute-start(f32[16,16,128]{2,1,0:T(8,128)} %get-tuple-element.48.lo), channel_id=1, source_target_pairs={{1,0},{2,1},{3,2},{4,3},{5,4},{6,5},{7,6},{8,7},{9,8},{10,9},{11,1... | collective-permute-start | bytes 393224 | tf_op jit(solution)/shard_map/ppermute | solution.py:460
  58.2 27.4 %all-to-all-start.1 = ((f32[128,1,128]{2,1,0:T(1,128)}), f32[128,1,128]{2,1,0:T(1,128)S(1)}, u32[]{:S(2)}, u32[]{:S(2)}) async-start(f32[128,1,128]{2,1,0:T(1,128)} %copy-done.7), calls=%async_computation.1 | async-start | bytes 131072 | tf_op jit(solution)/shard_map/all_to_all | solution.py:453
  66.6 8.7 %collective-permute-start.4 = (f32[8,128]{1,0:T(8,128)}, f32[8,128]{1,0:T(8,128)S(1)}, u32[]{:S(2)}, u32[]{:S(2)}) collective-permute-start(f32[8,128]{1,0:T(8,128)} %copy-done.2), channel_id=1, source_target_pairs={{0,16},{16,32},{32,48},{48,64},{64,80},{80,96},{96,112},{1,17},{17... | collective-permute-start | bytes 12296 | tf_op jit(solution)/shard_map/ppermute | solution.py:460
  70.2 9.1 %collective-permute-start.5 = (f32[8,128]{1,0:T(8,128)}, f32[8,128]{1,0:T(8,128)S(1)}, u32[]{:S(2)}, u32[]{:S(2)}) collective-permute-start(f32[8,128]{1,0:T(8,128)} %copy-done.2), channel_id=1, source_target_pairs={{16,0},{32,16},{48,32},{64,48},{80,64},{96,80},{112,96},{17,1},{33... | collective-permute-start | bytes 12296 | tf_op jit(solution)/shard_map/ppermute | solution.py:460
  72.1 9.1 %collective-permute-start.6 = (f32[16,128]{1,0:T(8,128)S(1)}, f32[16,128]{1,0:T(8,128)S(1)}, u32[]{:S(2)}, u32[]{:S(2)}) collective-permute-start(f32[16,128]{1,0:T(8,128)S(1)} %get-tuple-element.53.hi_k), channel_id=1, source_target_pairs={{0,1},{1,2},{2,3},{3,4},{4,5},{5,6},{6,7},{7,8},{8,9},{9,10},{10,1... | collective-permute-start | bytes 24584 | tf_op jit(solution)/shard_map/ppermute | solution.py:460
  75.3 10.3 %collective-permute-start = (f32[4,8,128]{2,1,0:T(8,128)}, f32[4,8,128]{2,1,0:T(8,128)S(1)}, u32[]{:S(2)}, u32[]{:S(2)}) collective-permute-start(f32[4,8,128]{2,1,0:T(8,128)} %copy-done.9), channel_id=1, source_target_pairs={{0,16},{16,32},{32,48},{48,64},{64,80},{80,96},{96,112},{1,17},{17... | collective-permute-start | bytes 49160 | tf_op jit(solution)/shard_map/ppermute | solution.py:460
  79.3 6.3 %collective-permute-start.1 = (f32[4,8,128]{2,1,0:T(8,128)}, f32[4,8,128]{2,1,0:T(8,128)S(1)}, u32[]{:S(2)}, u32[]{:S(2)}) collective-permute-start(f32[4,8,128]{2,1,0:T(8,128)} %copy-done.9), channel_id=1, source_target_pairs={{16,0},{32,16},{48,32},{64,48},{80,64},{96,80},{112,96},{17,1},{33... | collective-permute-start | bytes 49160 | tf_op jit(solution)/shard_map/ppermute | solution.py:460
  81.2 4.4 %collective-permute-start.7 = (f32[16,128]{1,0:T(8,128)S(1)}, f32[16,128]{1,0:T(8,128)S(1)}, u32[]{:S(2)}, u32[]{:S(2)}) collective-permute-start(f32[16,128]{1,0:T(8,128)S(1)} %get-tuple-element.52.lo_k), channel_id=1, source_target_pairs={{1,0},{2,1},{3,2},{4,3},{5,4},{6,5},{7,6},{8,7},{9,8},{10,9},{11,1... | collective-permute-start | bytes 24584 | tf_op jit(solution)/shard_map/ppermute | solution.py:460
  85.6 0.7 copy-start.3
  86.3 0.7 copy-start.10
  94.2 27.4 %collective-permute-start.10 = (f32[16,16,128]{2,1,0:T(8,128)S(1)}, f32[16,16,128]{2,1,0:T(8,128)S(1)}, u32[]{:S(2)}, u32[]{:S(2)}) collective-permute-start(f32[16,16,128]{2,1,0:T(8,128)S(1)} %get-tuple-element.57.hi), channel_id=1, source_target_pairs={{0,1},{1,2},{2,3},{3,4},{4,5},{5,6},{6,7},{7,8},{8,9},{9,10},{10,1... | collective-permute-start | bytes 393224 | tf_op jit(solution)/shard_map/ppermute | solution.py:460
  97.6 24.0 %collective-permute-start.11 = (f32[16,16,128]{2,1,0:T(8,128)S(1)}, f32[16,16,128]{2,1,0:T(8,128)S(1)}, u32[]{:S(2)}, u32[]{:S(2)}) collective-permute-start(f32[16,16,128]{2,1,0:T(8,128)S(1)} %get-tuple-element.56.lo), channel_id=1, source_target_pairs={{1,0},{2,1},{3,2},{4,3},{5,4},{6,5},{7,6},{8,7},{9,8},{10,9},{11,1... | collective-permute-start | bytes 393224 | tf_op jit(solution)/shard_map/ppermute | solution.py:460
  98.9 22.7 %all-to-all-start.2 = ((f32[128,1,128]{2,1,0:T(1,128)}), f32[128,1,128]{2,1,0:T(1,128)S(1)}, u32[]{:S(2)}, u32[]{:S(2)}) async-start(f32[128,1,128]{2,1,0:T(1,128)} %get-tuple-element.58), calls=%async_computation.2 | async-start | bytes 131072 | tf_op jit(solution)/shard_map/all_to_all | solution.py:453
  112.0 5.5 %collective-permute-start.8 = (f32[4,8,128]{2,1,0:T(8,128)S(1)}, f32[4,8,128]{2,1,0:T(8,128)S(1)}, u32[]{:S(2)}, u32[]{:S(2)}) collective-permute-start(f32[4,8,128]{2,1,0:T(8,128)S(1)} %get-tuple-element.55.cols), channel_id=1, source_target_pairs={{0,16},{16,32},{32,48},{48,64},{64,80},{80,96},{96,112},{1,17},{17... | collective-permute-start | bytes 49160 | tf_op jit(solution)/shard_map/ppermute | solution.py:460
  115.5 5.4 %collective-permute-start.9 = (f32[4,8,128]{2,1,0:T(8,128)S(1)}, f32[4,8,128]{2,1,0:T(8,128)S(1)}, u32[]{:S(2)}, u32[]{:S(2)}) collective-permute-start(f32[4,8,128]{2,1,0:T(8,128)S(1)} %get-tuple-element.55.cols), channel_id=1, source_target_pairs={{16,0},{32,16},{48,32},{64,48},{80,64},{96,80},{112,96},{17,1},{33... | collective-permute-start | bytes 49160 | tf_op jit(solution)/shard_map/ppermute | solution.py:460
  127.8 22.9 %collective-permute-start.14 = (f32[16,16,128]{2,1,0:T(8,128)S(1)}, f32[16,16,128]{2,1,0:T(8,128)S(1)}, u32[]{:S(2)}, u32[]{:S(2)}) collective-permute-start(f32[16,16,128]{2,1,0:T(8,128)S(1)} %get-tuple-element.62.hi), channel_id=1, source_target_pairs={{0,1},{1,2},{2,3},{3,4},{4,5},{5,6},{6,7},{7,8},{8,9},{9,10},{10,1... | collective-permute-start | bytes 393224 | tf_op jit(solution)/shard_map/ppermute | solution.py:460
  130.4 20.3 %collective-permute-start.15 = (f32[16,16,128]{2,1,0:T(8,128)S(1)}, f32[16,16,128]{2,1,0:T(8,128)S(1)}, u32[]{:S(2)}, u32[]{:S(2)}) collective-permute-start(f32[16,16,128]{2,1,0:T(8,128)S(1)} %get-tuple-element.61.lo), channel_id=1, source_target_pairs={{1,0},{2,1},{3,2},{4,3},{5,4},{6,5},{7,6},{8,7},{9,8},{10,9},{11,1... | collective-permute-start | bytes 393224 | tf_op jit(solution)/shard_map/ppermute | solution.py:460
  131.7 19.0 %all-to-all-start.3 = ((f32[128,1,128]{2,1,0:T(1,128)}), f32[128,1,128]{2,1,0:T(1,128)S(1)}, u32[]{:S(2)}, u32[]{:S(2)}) async-start(f32[128,1,128]{2,1,0:T(1,128)} %get-tuple-element.63), calls=%async_computation.3 | async-start | bytes 131072 | tf_op jit(solution)/shard_map/all_to_all | solution.py:453
  141.2 5.5 %collective-permute-start.12 = (f32[4,8,128]{2,1,0:T(8,128)S(1)}, f32[4,8,128]{2,1,0:T(8,128)S(1)}, u32[]{:S(2)}, u32[]{:S(2)}) collective-permute-start(f32[4,8,128]{2,1,0:T(8,128)S(1)} %get-tuple-element.60.cols), channel_id=1, source_target_pairs={{0,16},{16,32},{32,48},{48,64},{64,80},{80,96},{96,112},{1,17},{17... | collective-permute-start | bytes 49160 | tf_op jit(solution)/shard_map/ppermute | solution.py:460
  144.7 5.4 %collective-permute-start.13 = (f32[4,8,128]{2,1,0:T(8,128)S(1)}, f32[4,8,128]{2,1,0:T(8,128)S(1)}, u32[]{:S(2)}, u32[]{:S(2)}) collective-permute-start(f32[4,8,128]{2,1,0:T(8,128)S(1)} %get-tuple-element.60.cols), channel_id=1, source_target_pairs={{16,0},{32,16},{48,32},{64,48},{80,64},{96,80},{112,96},{17,1},{33... | collective-permute-start | bytes 49160 | tf_op jit(solution)/shard_map/ppermute | solution.py:460
  156.9 23.0 %collective-permute-start.18 = (f32[16,16,128]{2,1,0:T(8,128)S(1)}, f32[16,16,128]{2,1,0:T(8,128)S(1)}, u32[]{:S(2)}, u32[]{:S(2)}) collective-permute-start(f32[16,16,128]{2,1,0:T(8,128)S(1)} %get-tuple-element.67.hi), channel_id=1, source_target_pairs={{0,1},{1,2},{2,3},{3,4},{4,5},{5,6},{6,7},{7,8},{8,9},{9,10},{10,1... | collective-permute-start | bytes 393224 | tf_op jit(solution)/shard_map/ppermute | solution.py:460
  159.6 20.3 %collective-permute-start.19 = (f32[16,16,128]{2,1,0:T(8,128)S(1)}, f32[16,16,128]{2,1,0:T(8,128)S(1)}, u32[]{:S(2)}, u32[]{:S(2)}) collective-permute-start(f32[16,16,128]{2,1,0:T(8,128)S(1)} %get-tuple-element.66.lo), channel_id=1, source_target_pairs={{1,0},{2,1},{3,2},{4,3},{5,4},{6,5},{7,6},{8,7},{9,8},{10,9},{11,1... | collective-permute-start | bytes 393224 | tf_op jit(solution)/shard_map/ppermute | solution.py:460
  160.9 19.0 %all-to-all-start.4 = ((f32[128,1,128]{2,1,0:T(1,128)}), f32[128,1,128]{2,1,0:T(1,128)S(1)}, u32[]{:S(2)}, u32[]{:S(2)}) async-start(f32[128,1,128]{2,1,0:T(1,128)} %get-tuple-element.68), calls=%async_computation.4 | async-start | bytes 131072 | tf_op jit(solution)/shard_map/all_to_all | solution.py:453
  170.4 5.5 %collective-permute-start.16 = (f32[4,8,128]{2,1,0:T(8,128)S(1)}, f32[4,8,128]{2,1,0:T(8,128)S(1)}, u32[]{:S(2)}, u32[]{:S(2)}) collective-permute-start(f32[4,8,128]{2,1,0:T(8,128)S(1)} %get-tuple-element.65.cols), channel_id=1, source_target_pairs={{0,16},{16,32},{32,48},{48,64},{64,80},{80,96},{96,112},{1,17},{17... | collective-permute-start | bytes 49160 | tf_op jit(solution)/shard_map/ppermute | solution.py:460
  173.9 5.4 %collective-permute-start.17 = (f32[4,8,128]{2,1,0:T(8,128)S(1)}, f32[4,8,128]{2,1,0:T(8,128)S(1)}, u32[]{:S(2)}, u32[]{:S(2)}) collective-permute-start(f32[4,8,128]{2,1,0:T(8,128)S(1)} %get-tuple-element.65.cols), channel_id=1, source_target_pairs={{16,0},{32,16},{48,32},{64,48},{80,64},{96,80},{112,96},{17,1},{33... | collective-permute-start | bytes 49160 | tf_op jit(solution)/shard_map/ppermute | solution.py:460
  186.1 48.3 %copy-start.8 = (f32[16,512]{1,0:T(8,128)S(1)}, f32[16,512]{1,0:T(8,128)}, u32[]{:S(2)}) copy-start(f32[16,512]{1,0:T(8,128)} %noise.1) | copy-start | bytes 98308
  186.1 48.3 %copy-start.11 = (s32[512]{0:T(512)S(1)}, s32[512]{0:T(512)}, u32[]{:S(2)}) copy-start(s32[512]{0:T(512)} %param.14) | copy-start | bytes 6148
  186.1 48.3 %copy-start.12 = (f32[512]{0:T(512)S(1)}, f32[512]{0:T(512)}, u32[]{:S(2)}) copy-start(f32[512]{0:T(512)} %param.15) | copy-start | bytes 6148
  186.1 48.3 %copy-start.13 = (f32[512]{0:T(512)S(1)}, f32[512]{0:T(512)}, u32[]{:S(2)}) copy-start(f32[512]{0:T(512)} %param.16) | copy-start | bytes 6148
  186.1 23.1 %collective-permute-start.22 = (f32[16,16,128]{2,1,0:T(8,128)S(1)}, f32[16,16,128]{2,1,0:T(8,128)S(1)}, u32[]{:S(2)}, u32[]{:S(2)}) collective-permute-start(f32[16,16,128]{2,1,0:T(8,128)S(1)} %get-tuple-element.72.hi), channel_id=1, source_target_pairs={{0,1},{1,2},{2,3},{3,4},{4,5},{5,6},{6,7},{7,8},{8,9},{9,10},{10,1... | collective-permute-start | bytes 393224 | tf_op jit(solution)/shard_map/ppermute | solution.py:460
  188.9 20.3 %collective-permute-start.23 = (f32[16,16,128]{2,1,0:T(8,128)S(1)}, f32[16,16,128]{2,1,0:T(8,128)S(1)}, u32[]{:S(2)}, u32[]{:S(2)}) collective-permute-start(f32[16,16,128]{2,1,0:T(8,128)S(1)} %get-tuple-element.71.lo), channel_id=1, source_target_pairs={{1,0},{2,1},{3,2},{4,3},{5,4},{6,5},{7,6},{8,7},{9,8},{10,9},{11,1... | collective-permute-start | bytes 393224 | tf_op jit(solution)/shard_map/ppermute | solution.py:460
  190.2 19.0 %all-to-all-start.5 = ((f32[128,1,128]{2,1,0:T(1,128)}), f32[128,1,128]{2,1,0:T(1,128)S(1)}, u32[]{:S(2)}, u32[]{:S(2)}) async-start(f32[128,1,128]{2,1,0:T(1,128)} %get-tuple-element.73), calls=%async_computation.5 | async-start | bytes 131072 | tf_op jit(solution)/shard_map/all_to_all | solution.py:453
  199.7 5.5 %collective-permute-start.20 = (f32[4,8,128]{2,1,0:T(8,128)S(1)}, f32[4,8,128]{2,1,0:T(8,128)S(1)}, u32[]{:S(2)}, u32[]{:S(2)}) collective-permute-start(f32[4,8,128]{2,1,0:T(8,128)S(1)} %get-tuple-element.70.cols), channel_id=1, source_target_pairs={{0,16},{16,32},{32,48},{48,64},{64,80},{80,96},{96,112},{1,17},{17... | collective-permute-start | bytes 49160 | tf_op jit(solution)/shard_map/ppermute | solution.py:460
  203.3 5.4 %collective-permute-start.21 = (f32[4,8,128]{2,1,0:T(8,128)S(1)}, f32[4,8,128]{2,1,0:T(8,128)S(1)}, u32[]{:S(2)}, u32[]{:S(2)}) collective-permute-start(f32[4,8,128]{2,1,0:T(8,128)S(1)} %get-tuple-element.70.cols), channel_id=1, source_target_pairs={{16,0},{32,16},{48,32},{64,48},{80,64},{96,80},{112,96},{17,1},{33... | collective-permute-start | bytes 49160 | tf_op jit(solution)/shard_map/ppermute | solution.py:460
  215.4 23.0 %collective-permute-start.26 = (f32[16,16,128]{2,1,0:T(8,128)S(1)}, f32[16,16,128]{2,1,0:T(8,128)S(1)}, u32[]{:S(2)}, u32[]{:S(2)}) collective-permute-start(f32[16,16,128]{2,1,0:T(8,128)S(1)} %get-tuple-element.77.hi), channel_id=1, source_target_pairs={{0,1},{1,2},{2,3},{3,4},{4,5},{5,6},{6,7},{7,8},{8,9},{9,10},{10,1... | collective-permute-start | bytes 393224 | tf_op jit(solution)/shard_map/ppermute | solution.py:460
  218.1 20.3 %collective-permute-start.27 = (f32[16,16,128]{2,1,0:T(8,128)S(1)}, f32[16,16,128]{2,1,0:T(8,128)S(1)}, u32[]{:S(2)}, u32[]{:S(2)}) collective-permute-start(f32[16,16,128]{2,1,0:T(8,128)S(1)} %get-tuple-element.76.lo), channel_id=1, source_target_pairs={{1,0},{2,1},{3,2},{4,3},{5,4},{6,5},{7,6},{8,7},{9,8},{10,9},{11,1... | collective-permute-start | bytes 393224 | tf_op jit(solution)/shard_map/ppermute | solution.py:460
  219.4 19.0 %all-to-all-start.6 = ((f32[128,1,128]{2,1,0:T(1,128)}), f32[128,1,128]{2,1,0:T(1,128)S(1)}, u32[]{:S(2)}, u32[]{:S(2)}) async-start(f32[128,1,128]{2,1,0:T(1,128)} %get-tuple-element.78), calls=%async_computation.6 | async-start | bytes 131072 | tf_op jit(solution)/shard_map/all_to_all | solution.py:453
  228.9 7.3 %collective-permute-start.24 = (f32[4,8,128]{2,1,0:T(8,128)S(1)}, f32[4,8,128]{2,1,0:T(8,128)S(1)}, u32[]{:S(2)}, u32[]{:S(2)}) collective-permute-start(f32[4,8,128]{2,1,0:T(8,128)S(1)} %get-tuple-element.75.cols), channel_id=1, source_target_pairs={{0,16},{16,32},{32,48},{48,64},{64,80},{80,96},{96,112},{1,17},{17... | collective-permute-start | bytes 49160 | tf_op jit(solution)/shard_map/ppermute | solution.py:460
  232.4 5.4 %collective-permute-start.25 = (f32[4,8,128]{2,1,0:T(8,128)S(1)}, f32[4,8,128]{2,1,0:T(8,128)S(1)}, u32[]{:S(2)}, u32[]{:S(2)}) collective-permute-start(f32[4,8,128]{2,1,0:T(8,128)S(1)} %get-tuple-element.75.cols), channel_id=1, source_target_pairs={{16,0},{32,16},{48,32},{64,48},{80,64},{96,80},{112,96},{17,1},{33... | collective-permute-start | bytes 49160 | tf_op jit(solution)/shard_map/ppermute | solution.py:460
  (2 other events, 1.3 us)

commit v2 on v1

v2 whole, which is shorter than its diff:
```python
import functools

import jax
import jax.numpy as jnp
from jax import lax
from jax.experimental import pallas as pl
from jax.experimental.pallas import tpu as pltpu
from jax.sharding import PartitionSpec as P

SUBSTEPS = 6
CAP = 2
COOL = 0.1
SHARE = 0.9
F32 = jnp.float32
BF16 = jnp.bfloat16
VM = pltpu.VMEM
LIMIT = 48 * 1024 * 1024
NT = (((1,), (1,)), ((), ()))
BOTH = ("gx", "gy")

M, NZ, CY, CX = 16, 16, 8, 128
ROWS = 40


def vspec():
    return pl.BlockSpec(memory_space=pltpu.VMEM)


def params():
    return pltpu.CompilerParams(vmem_limit_bytes=LIMIT)


def lanes():
    return lax.broadcasted_iota(jnp.int32, (CY, CX), 1)


def rows():
    return lax.broadcasted_iota(jnp.int32, (CY, CX), 0)


def pack_kernel(owner, heat, voxel, out, wide, high, low, inverse):
    blocks = owner.shape[0]
    devices = out.shape[0]

    def clear(i, carry):
        inverse[i] = blocks
        return carry

    lax.fori_loop(0, devices * CAP, clear, 0, unroll=16)

    def place(b, carry):
        base = owner[b] * CAP
        base = base + jnp.where(inverse[base] != blocks, 1, 0)
        inverse[base] = b
        return carry

    lax.fori_loop(0, blocks, place, 0, unroll=8)

    def widen(m, carry):
        wide[m, 0:blocks, :] = heat[m].astype(F32)
        wide[m, blocks:, :] = jnp.zeros((8, CX), F32)
        return carry

    lax.fori_loop(0, M, widen, 0)
    cells = voxel[...]
    high[0:blocks, :] = (cells >> 7).astype(F32)
    high[blocks:, :] = jnp.zeros((8, CX), F32)
    low[0:blocks, :] = (cells & 127).astype(F32)
    low[blocks:, :] = jnp.zeros((8, CX), F32)
    row = rows()

    def emit(d, carry):
        first = inverse[d * CAP]
        second = inverse[d * CAP + 1]
        index = jnp.where(
            row == 0,
            high[pl.ds(first, 1), :],
            jnp.where(
                row == 1,
                high[pl.ds(second, 1), :],
                jnp.where(
                    row == 2,
                    low[pl.ds(first, 1), :],
                    jnp.where(row == 3, low[pl.ds(second, 1), :], 0.0),
                ),
            ),
        )
        chunk = jnp.concatenate(
            [
                wide[:, pl.ds(first, 1), :].reshape(M, CX),
                wide[:, pl.ds(second, 1), :].reshape(M, CX),
                index,
            ],
            axis=0,
        )
        out[d] = chunk.astype(BF16)
        return carry

    lax.fori_loop(0, devices, emit, 0, unroll=4)


def pack(owner, heat, voxel, devices):
    blocks = owner.shape[0]
    return pl.pallas_call(
        pack_kernel,
        out_shape=jax.ShapeDtypeStruct((devices, ROWS, CX), BF16),
        in_specs=[pl.BlockSpec(memory_space=pltpu.SMEM), vspec(), vspec()],
        out_specs=vspec(),
        scratch_shapes=[
            VM((M, blocks + 8, CX), F32),
            VM((blocks + 8, CX), F32),
            VM((blocks + 8, CX), F32),
            pltpu.SMEM((devices * CAP,), jnp.int32),
        ],
        compiler_params=params(),
        name="pack",
    )(owner, heat, voxel)


HALO = 6
YS = CY + 2 * HALO
XT = CX // 8 + 2
ZG = NZ // 2
OWN = jax.ShapeDtypeStruct((2, CY, XT - 2, 8, CX), F32)
ROWHALO = jax.ShapeDtypeStruct((2, HALO, XT - 2, 8, CX), F32)
WIDE = jax.ShapeDtypeStruct((2, YS, XT, 8, CX), F32)


def relayout_kernel(state, own, to_high, to_low):
    for zi in range(2):
        for y in range(CY):
            parts = [
                state[m0 : m0 + 8, 2 * group + zi, y, :] for group in range(ZG) for m0 in (0, 8)
            ]
            turned = (0.5 * jnp.concatenate(parts, axis=0)).T.reshape(XT - 2, 8, CX)
            own[zi, y] = turned
            if y >= CY - HALO:
                to_high[zi, y - (CY - HALO)] = turned
            if y < HALO:
                to_low[zi, y] = turned


def relayout(state):
    return pl.pallas_call(
        relayout_kernel,
        out_shape=[OWN, ROWHALO, ROWHALO],
        in_specs=[vspec()],
        out_specs=[vspec()] * 3,
        compiler_params=params(),
        name="relayout",
    )(state)


def side_kernel(own, low, high, to_left, to_right):
    for out, t in ((to_left, 0), (to_right, XT - 3)):
        for zi in range(2):
            for y in range(YS):
                if y < HALO:
                    out[zi, y] = low[zi, y, t]
                elif y < HALO + CY:
                    out[zi, y] = own[zi, y - HALO, t]
                else:
                    out[zi, y] = high[zi, y - HALO - CY, t]


def sides(own, low, high):
    shape = jax.ShapeDtypeStruct((2, YS, 8, CX), F32)
    return pl.pallas_call(
        side_kernel,
        out_shape=[shape, shape],
        in_specs=[vspec()] * 3,
        out_specs=[vspec()] * 2,
        compiler_params=params(),
        name="sides",
    )(own, low, high)


def coef_kernel(own, low, high, out, turned):
    for g, tiles in enumerate((low, own, high)):
        for t in range(3):
            turned[g, t] = (0.5 * tiles[t].reshape(CX, CX)).T
    source = lax.broadcasted_iota(jnp.int32, (CX, CX), 0)
    target = lax.broadcasted_iota(jnp.int32, (CX, CX), 1)

    def put(g, y0, yy):
        strip = jnp.concatenate([turned[g, 0, CX - 8 :, :], turned[g, 1], turned[g, 2, 0:8, :]], axis=0)
        for zi in range(2):
            wanted = (2 * (target >> 4) + zi) * CY + y0
            hot = jnp.where(source == wanted, 1.0, 0.0).astype(F32)
            part = jnp.dot(
                strip, hot, precision=lax.Precision.HIGHEST, preferred_element_type=F32
            )
            out[zi, yy] = part.reshape(XT, 8, CX)

    for y in range(HALO):
        put(0, y + CY - HALO, y)
    for y in range(CY):
        put(1, y, y + HALO)
    for y in range(HALO):
        put(2, y, y + HALO + CY)


def coefs(own, low, high):
    return pl.pallas_call(
        coef_kernel,
        out_shape=WIDE,
        in_specs=[vspec()] * 3,
        out_specs=vspec(),
        scratch_shapes=[VM((3, 3, CX, CX), F32)],
        compiler_params=params(),
        name="coefs",
    )(own, low, high)


def deposit_kernel(incoming, out, total):
    sources = incoming.shape[0]
    group = 4
    place = lax.broadcasted_iota(jnp.int32, (CX, CX), 0).astype(F32).astype(BF16)
    zero = jnp.zeros((M, CX), BF16)
    total[...] = jnp.zeros_like(total)

    def one(g, carry):
        left = []
        right = []
        for s in range(group):
            source = g * group + s
            index = incoming[source, 32:40, :].astype(F32)
            for slot in range(CAP):
                heat = incoming[source, slot * M : (slot + 1) * M, :]
                layer = jnp.broadcast_to(index[slot : slot + 1, :], (M, CX)).astype(BF16)
                cell = jnp.broadcast_to(index[2 + slot : 3 + slot, :], (CX, CX)).astype(BF16)
                left.append(
                    jnp.concatenate(
                        [jnp.where(layer == h, heat, zero) for h in range(2 * CY)], axis=0
                    )
                )
                right.append(jnp.where(place == cell, 1.0, 0.0).astype(BF16))
        total[...] += lax.dot_general(
            jnp.concatenate(left, axis=1),
            jnp.concatenate(right, axis=1),
            NT,
            preferred_element_type=F32,
        )
        return carry

    lax.fori_loop(0, sources // group, one, 0)
    for zi in range(2):
        out[zi] = (0.5 * total[zi * CX : (zi + 1) * CX, :]).T


def deposit(incoming):
    return pl.pallas_call(
        deposit_kernel,
        out_shape=jax.ShapeDtypeStruct((2, CX, CX), F32),
        in_specs=[vspec()],
        out_specs=vspec(),
        scratch_shapes=[VM((2 * CY * M, CX), F32)],
        compiler_params=params(),
        name="deposit",
    )(incoming)


def heat_side_kernel(low, own, high, to_left, to_right):
    for g, part in enumerate((low, own, high)):
        to_left[g] = part[:, 0:8, :]
        to_right[g] = part[:, CX - 8 :, :]


def heat_sides(low, own, high):
    shape = jax.ShapeDtypeStruct((3, 2, 8, CX), F32)
    return pl.pallas_call(
        heat_side_kernel,
        out_shape=[shape, shape],
        in_specs=[vspec()] * 3,
        out_specs=[vspec()] * 2,
        compiler_params=params(),
        name="heat_sides",
    )(low, own, high)


def heated_kernel(
    own, low, high, left, right, heat_low, heat_own, heat_high, heat_left, heat_right, coef, out, peaks
):
    top = lanes() < M
    peak = jnp.zeros((8, CX), F32)

    def row(g, heat, tile_of, y0, yy, peak, inner):
        shift = (CX - 16 * y0) % CX
        for zi in range(2):
            for t in range(XT):
                if t == 0:
                    prior, add = left[zi, yy], heat_left[g, zi]
                elif t == XT - 1:
                    prior, add = right[zi, yy], heat_right[g, zi]
                else:
                    prior, add = tile_of(zi, t - 1), heat[zi, 8 * t - 8 : 8 * t, :]
                if shift:
                    add = pltpu.roll(add, shift, axis=1)
                value = prior + jnp.where(top, add, 0.0)
                out[zi, yy, t] = value
                if inner and 0 < t < XT - 1:
                    c = coef[zi, yy, t]
                    peak = jnp.maximum(peak, c + c * (value * value))
        return peak

    for y in range(HALO):
        y0 = y + CY - HALO
        row(0, heat_low, lambda zi, t: low[zi, y, t], y0, y, peak, False)
    for y in range(CY):
        peak = row(1, heat_own, lambda zi, t: own[zi, y, t], y, y + HALO, peak, True)
    for y in range(HALO):
        row(2, heat_high, lambda zi, t: high[zi, y, t], y, y + HALO + CY, peak, False)
    spread_peak(peak, peaks)


def spread_peak(peak, out):
    row = jnp.max(peak, axis=0, keepdims=True)
    for d in range(out.shape[0]):
        out[d] = row


def heated(prior, halos, heat, coef, devices):
    operands = [*prior, *halos, *heat, coef]
    return pl.pallas_call(
        heated_kernel,
        out_shape=[WIDE, jax.ShapeDtypeStruct((devices, 1, CX), F32)],
        in_specs=[vspec()] * len(operands),
        out_specs=[vspec()] * 2,
        compiler_params=params(),
        name="heated",
    )(*operands)


def substep_kernel(number, inside, field, coef, peaks, *rest):
    last = number == SUBSTEPS - 1
    if last:
        weight, data, out, sums, above, below_h, flat = rest
    else:
        out, out_peaks, above, below_h = rest
    first, end = number + 1, YS - 1 - number
    lane = lanes()
    row = rows()
    last_row = row == 7
    first_row = row == 0
    inner_lane = lane < CX - M
    cooling = jnp.where(lane < M, COOL, 0.0)

    peak = peaks[0]
    for d in range(1, peaks.shape[0]):
        peak = jnp.maximum(peak, peaks[d])
    peak = 2.0 * jnp.max(peak, axis=(0, 1), keepdims=True)
    step = jnp.broadcast_to(SHARE / (6.0 * peak + COOL), (8, CX))

    def conduct(zi, y, t):
        u = field[zi, y, t]
        c = coef[zi, y, t]
        return u, c + c * (u * u)

    for zi in range(2):
        for t in range(XT):
            u, h = conduct(zi, first - 1, t)
            v, g = conduct(zi, first, t)
            above[zi, t] = (h + g) * (v - u)
            below_h[zi, t] = g

    def line(y, peak):
        kept = jnp.where(y < HALO, inside[2], jnp.where(y >= HALO + CY, inside[3], 1.0))
        mid = step * kept
        steps = [mid * inside[0]] + [mid] * (XT - 2) + [mid * inside[1]]
        top = jnp.zeros((8, CX), F32)

        def load(t):
            us = [field[zi, y, t] for zi in range(2)]
            hs = [below_h[zi, t] for zi in range(2)]
            return us, hs, [pltpu.roll(a, 7, axis=0) for a in us], [pltpu.roll(a, 7, axis=0) for a in hs]

        us, hs, ru, rh = load(0)
        carried = [jnp.zeros((8, CX), F32)] * 2
        for t in range(XT):
            if t < XT - 1:
                after = load(t + 1)
                next_u = [jnp.where(last_row, after[2][z], ru[z]) for z in range(2)]
                next_h = [jnp.where(last_row, after[3][z], rh[z]) for z in range(2)]
            else:
                next_u = [jnp.where(last_row, us[z], ru[z]) for z in range(2)]
                next_h = rh
            change = []
            for zi in range(2):
                u, h = us[zi], hs[zi]
                along = (h + next_h[zi]) * (next_u[zi] - u)
                turned = pltpu.roll(along, 1, axis=0)
                total = along - jnp.where(first_row, carried[zi], turned)
                carried[zi] = turned
                v, g = conduct(zi, y + 1, t)
                across = (h + g) * (v - u)
                total = total + (across - above[zi, t])
                above[zi, t] = across
                below_h[zi, t] = g
                change.append(total)
            within = (hs[0] + hs[1]) * (us[1] - us[0])
            between = (hs[1] + pltpu.roll(hs[0], CX - M, axis=1)) * (
                pltpu.roll(us[0], CX - M, axis=1) - us[1]
            )
            between = jnp.where(inner_lane, between, 0.0)
            change[0] = change[0] + (within - pltpu.roll(between, M, axis=1)) - cooling * us[0]
            change[1] = change[1] + (between - within)
            for zi in range(2):
                value = us[zi] + steps[t] * change[zi]
                if last:
                    if 0 < t < XT - 1:
                        out[zi, y - HALO, t - 1] = value
                else:
                    out[zi, y, t] = value
                    if 0 < t < XT - 1:
                        c = coef[zi, y, t]
                        top = jnp.maximum(top, c + c * (value * value))
            if t < XT - 1:
                us, hs, ru, rh = after
        own = jnp.where((y >= HALO) & (y < HALO + CY), 1.0, 0.0)
        return jnp.maximum(peak, top * own)

    peak = lax.fori_loop(first, end, line, jnp.zeros((8, CX), F32))
    if not last:
        spread_peak(peak, out_peaks)
        return

    grams = jnp.zeros((M, 2 * M), F32)
    for y in range(CY):
        seen = 2.0 * out[0, y].reshape(CX, CX).T[0:M, :]
        for m in range(M):
            flat[m : m + 1, :] = data[m, y : y + 1, :]
        w = weight[y : y + 1, :]
        spread = seen - jnp.mean(seen, axis=0, keepdims=True)
        both = jnp.concatenate([spread * w, flat[...] - seen * w], axis=0)
        grams = grams + lax.dot_general(
            spread, both, NT, precision=lax.Precision.HIGHEST, preferred_element_type=F32
        )
    grams = jnp.concatenate([grams, jnp.zeros((M, CX - 2 * M), F32)], axis=1)
    pair = grams[0:8] + pltpu.roll(grams[8:16], 32, axis=1)
    quad = pair + pltpu.roll(pltpu.roll(pair, 64, axis=1), 4, axis=0)
    quad = quad[0:4]
    for d in range(sums.shape[0]):
        sums[d] = quad


def substep(number, inside, field, coef, peaks, pixels):
    devices = peaks.shape[0]
    operands = [inside, field, coef, peaks]
    scratch = [VM((2, XT, 8, CX), F32), VM((2, XT, 8, CX), F32)]
    if number == SUBSTEPS - 1:
        operands += list(pixels)
        out_shape = [OWN, jax.ShapeDtypeStruct((devices, 4, CX), F32)]
        scratch += [VM((M, CX), F32)]
    else:
        out_shape = [WIDE, jax.ShapeDtypeStruct((devices, 1, CX), F32)]
    return pl.pallas_call(
        functools.partial(substep_kernel, number),
        out_shape=out_shape,
        in_specs=[pl.BlockSpec(memory_space=pltpu.SMEM)] + [vspec()] * (len(operands) - 1),
        out_specs=[vspec()] * 2,
        scratch_shapes=scratch,
        compiler_params=params(),
        name=f"substep_{number}",
    )(*operands)

def pixel_kernel(cell, observed, variance, noise, weight, data):
    pixels = cell.shape[1]
    place = cell[...]
    var = variance[...]
    inverse = 1.0 / var
    values = (observed[...] + noise[...] * jnp.sqrt(var)) * inverse
    stack = jnp.concatenate([values, jnp.broadcast_to(inverse, (8, pixels))], axis=0)
    width = place >> 7
    hot = jnp.where(
        lax.broadcasted_iota(jnp.int32, (CX, pixels), 0) == (place & 127), 1.0, 0.0
    ).astype(F32)
    for y in range(CY):
        part = lax.dot_general(
            jnp.where(width == y, stack, 0.0),
            hot,
            NT,
            precision=lax.Precision.HIGHEST,
            preferred_element_type=F32,
        )
        weight[y : y + 1, :] = part[M : M + 1, :]
        for m in range(M):
            data[m, y : y + 1, :] = part[m : m + 1, :]


def pixel_sums(cell, observed, variance, noise):
    return pl.pallas_call(
        pixel_kernel,
        out_shape=[
            jax.ShapeDtypeStruct((CY, CX), F32),
            jax.ShapeDtypeStruct((M, CY, CX), F32),
        ],
        in_specs=[vspec()] * 4,
        out_specs=[vspec()] * 2,
        compiler_params=params(),
        name="pixels",
    )(cell, observed, variance, noise)


def update_kernel(sums, field, out):
    quad = sums[0]
    for d in range(1, sums.shape[0]):
        quad = quad + sums[d]
    row = rows()
    quad = jnp.concatenate([quad, jnp.zeros_like(quad)], axis=0)
    pair = jnp.where(row < 4, quad, pltpu.roll(pltpu.roll(quad, 64, axis=1), 4, axis=0))
    system = jnp.concatenate([pair, pltpu.roll(pair, CX - 32, axis=1)], axis=0)
    tall = lax.broadcasted_iota(jnp.int32, (M, CX), 0)
    wide = lax.broadcasted_iota(jnp.int32, (M, CX), 1)
    system = jnp.where(tall == wide, system + (M - 1.0), system)
    for i in range(M):
        pivot = system[i : i + 1, :]
        pivot = pivot / pivot[:, i : i + 1]
        factor = jnp.where(tall == i, 0.0, jnp.broadcast_to(system[:, i : i + 1], (M, CX)))
        system = jnp.where(tall == i, pivot, system - factor * pivot)
    mixing = system - jnp.mean(system, axis=0, keepdims=True)
    mixing = pltpu.roll(mixing, CX - M, axis=1)
    mixing = jnp.where(wide < M, mixing + jnp.where(tall == wide, 1.0, 0.0), 0.0)
    for shift in (16, 32, 64):
        mixing = mixing + pltpu.roll(mixing, shift, axis=1)
    mixing = jnp.concatenate([mixing] * ZG, axis=0)
    tall = lax.broadcasted_iota(jnp.int32, (CX, CX), 0)
    wide = lax.broadcasted_iota(jnp.int32, (CX, CX), 1)
    mixing = jnp.where((tall >> 4) == (wide >> 4), 2.0 * mixing, 0.0).T
    for zi in range(2):
        for y in range(CY):
            part = lax.dot_general(
                mixing,
                field[zi, y].reshape(CX, CX),
                NT,
                precision=lax.Precision.HIGHEST,
                preferred_element_type=F32,
            )
            for group in range(ZG):
                for m0 in (0, 8):
                    at = group * M + m0
                    out[m0 : m0 + 8, 2 * group + zi, y, :] = part[at : at + 8, :]


def update(sums, field):
    return pl.pallas_call(
        update_kernel,
        out_shape=jax.ShapeDtypeStruct((M, NZ, CY, CX), F32),
        in_specs=[vspec()] * 2,
        out_specs=vspec(),
        compiler_params=params(),
        name="update",
    )(sums, field)


def exchange(parts):
    return lax.all_to_all(parts, BOTH, split_axis=0, concat_axis=0, tiled=True)


def move(part, axis, ahead):
    count = lax.axis_size(axis)
    pairs = [(i, i + 1) if ahead else (i + 1, i) for i in range(count - 1)]
    return lax.ppermute(part, axis, pairs)


def on_device(
    state_prior,
    conductivity,
    heat_input,
    owner_tile,
    voxel_list,
    pixel_cell,
    observed,
    pixel_variance,
    pixel_noise,
):
    devices = lax.axis_size("gx") * lax.axis_size("gy")
    pixels = pixel_cell.shape[0]
    outgoing = pack(owner_tile.reshape(-1), heat_input, voxel_list, devices)
    incoming = exchange(outgoing)

    gx, gy = lax.axis_index("gx"), lax.axis_index("gy")
    inside = jnp.stack(
        [gx > 0, gx < lax.axis_size("gx") - 1, gy > 0, gy < lax.axis_size("gy") - 1]
    ).astype(F32)
    own, to_high, to_low = relayout(state_prior)
    low, high = move(to_high, "gy", True), move(to_low, "gy", False)
    to_left, to_right = sides(own, low, high)
    left, right = move(to_right, "gx", True), move(to_left, "gx", False)

    tiles = jnp.stack(
        [move(conductivity, "gx", True), conductivity, move(conductivity, "gx", False)]
    )
    coef = coefs(tiles, move(tiles, "gy", True), move(tiles, "gy", False))
    seen = pixel_sums(
        pixel_cell.reshape(1, pixels),
        observed.reshape(1, pixels),
        pixel_variance.reshape(1, pixels),
        pixel_noise,
    )

    heat = deposit(incoming)
    heat_low, heat_high = move(heat, "gy", True), move(heat, "gy", False)
    to_left, to_right = heat_sides(heat_low, heat, heat_high)
    heat_left, heat_right = move(to_right, "gx", True), move(to_left, "gx", False)
    field, peaks = heated(
        (own, low, high),
        (left, right),
        (heat_low, heat, heat_high, heat_left, heat_right),
        coef,
        devices,
    )
    for number in range(SUBSTEPS):
        field, peaks = substep(number, inside, field, coef, exchange(peaks), seen)
    return update(exchange(peaks), field)


def solution(mesh):
    in_specs = (
        P(None, None, "gy", "gx"),
        P(None, "gy", "gx"),
        P(None, BOTH, None),
        P(BOTH, None),
        P(BOTH, None),
        P(BOTH),
        P(BOTH),
        P(BOTH),
        P(None, BOTH),
    )
    out_specs = P(None, None, "gy", "gx")
    return jax.shard_map(
        on_device, mesh=mesh, in_specs=in_specs, out_specs=out_specs, check_vma=False
    )
```

time: 267 us -> 232 us (0.87)
  starting transfers between devices: 138 us -> 56.4 us
  blocking collectives: 19.2 us -> 71 us
  waiting for transfers between devices: 42.6 us -> 32 us
  Pallas kernels: 60.3 us -> 64.6 us
    all_to_all x1 -> x5, blocking collectives: 19.2 us -> 71 us  [exchange(): return lax.all_to_all(parts, BOTH, split_axis=0, concat_axis=0, tiled=True)]
    all_to_all x7 -> x3, starting transfers between devices: 71 us -> 26.8 us  [exchange(): return lax.all_to_all(parts, BOTH, split_axis=0, concat_axis=0, tiled=True)]
    ppermute x28 -> x12, starting transfers between devices: 67.3 us -> 29.7 us  [move(): return lax.ppermute(part, axis, pairs)]
    ppermute x28 -> x12, waiting for transfers between devices: 18.4 us -> 5.47 us  [move(): return lax.ppermute(part, axis, pairs)]
    pallas_call x8 -> x12, Pallas kernels: 50.1 us -> 53.2 us  [the longest x6 31.7 us: substep(): pl.pallas_call(functools.partial(substep_kernel, number), out_shape=out_s...]
    all_to_all x7 -> x3, waiting for transfers between devices: 24.2 us -> 26.5 us  [exchange(): return lax.all_to_all(parts, BOTH, split_axis=0, concat_axis=0, tiled=True)]
    unnamed x30 -> x22, local copies, waits for them, and re-layouts: 4.56 us -> 6.04 us
  transfers between devices with their start and end apart: 35 -> 15, of which waited for: 12 -> 4; matrix products, arithmetic and copies ran while one was open for 0% -> 0% of each run, Pallas kernels for 1% -> 8%
where the time goes in v2:
time: 232 us; the launch traced here: 231 us
  blocking collectives  71 us (31%)
  Pallas kernels  64.6 us (28%)
  starting transfers between devices  56.4 us (24%)
  waiting for transfers between devices  32 us (14%)
  local copies, waits for them, and re-layouts  6.04 us (3%)
    all_to_all x5, blocking collectives, exchange(): return lax.all_to_all(parts, BOTH, split_axis=0, concat_axis=0, tiled=True)  71 us
    pallas_call x6, Pallas kernels, substep(): pl.pallas_call(functools.partial(substep_kernel, number), out_shape=out_s...  31.7 us
    ppermute x12, starting transfers between devices, move(): return lax.ppermute(part, axis, pairs)  29.7 us
    all_to_all x3, starting transfers between devices, exchange(): return lax.all_to_all(parts, BOTH, split_axis=0, concat_axis=0, tiled=True)  26.8 us
    all_to_all x3, waiting for transfers between devices, exchange(): return lax.all_to_all(parts, BOTH, split_axis=0, concat_axis=0, tiled=True)  26.5 us
    pallas_call x1, Pallas kernels, deposit(): pl.pallas_call(deposit_kernel, out_shape=jax.ShapeDtypeStruct((2, CX, CX)...  10.9 us
    unnamed x22, local copies, waits for them, and re-layouts  6.04 us
    ppermute x12, waiting for transfers between devices, move(): return lax.ppermute(part, axis, pairs)  5.47 us
  transfers between devices with their start and end apart: 15, of which 4 were waited for; matrix products, arithmetic and copies ran while one was open for 0% of the time, Pallas kernels for 8%

profile of v2, /device:TPU:1, one launch (start us, length us, event | category | flops | bytes accessed | tf_op | source)
XLA Modules:
  0.0 230.6 jit_solution(12098397320389696539)
XLA Ops:
  0.0 1.1 copy-done.3
  1.1 0.8 copy-done.4
  2.0 0.7 copy-done.9
  2.6 4.4 %pack.1 = bf16[128,40,128]{2,1,0:T(8,128)(2,1)} custom-call(s32[128]{0:T(128)S(1)} %bitcast.14, bf16[16,128,128]{2,1,0:T(8,128)(2,1)S(1)} %copy-done.3, s32[128,128]{1,0:T(8,128)S(1)} %copy-done.4), custom_call_target="tpu_custom_call" | custom-call | tf_op jit(solution)/shard_map/pack/pallas_call | solution.py:104
  7.0 11.5 %all-to-all-start = ((bf16[128,40,128]{2,1,0:T(8,128)(2,1)}), bf16[128,40,128]{2,1,0:T(8,128)(2,1)S(1)}, u32[]{:S(2)}, u32[]{:S(2)}) async-start(bf16[128,40,128]{2,1,0:T(8,128)(2,1)} %pack.1), calls=%async_computation | async-start | bytes 2621440 | tf_op jit(solution)/shard_map/all_to_all | solution.py:556
  18.6 1.7 relayout.1
  20.3 3.4 %collective-permute-start = (f32[2,6,16,8,128]{4,3,2,1,0:T(8,128)}, f32[2,6,16,8,128]{4,3,2,1,0:T(8,128)S(1)}, u32[]{:S(2)}, u32[]{:S(2)}) collective-permute-start(f32[2,6,16,8,128]{4,3,2,1,0:T(8,128)} %get-tuple-element.29), channel_id=1, source_target_pairs={{0,1},{1,2},{2,3},{3,4},{4,5},{5,6},{6,7},{7,8},{8,9},{9,10},{10,1... | collective-permute-start | bytes 2359304 | tf_op jit(solution)/shard_map/ppermute | solution.py:562
  23.7 1.3 collective-permute-start.1
  25.1 3.6 %collective-permute-start.8 = (f32[16,8,128]{2,1,0:T(8,128)S(1)}, f32[16,8,128]{2,1,0:T(8,128)S(1)}, u32[]{:S(2)}, u32[]{:S(2)}) collective-permute-start(f32[16,8,128]{2,1,0:T(8,128)S(1)} %copy-done.10), channel_id=1, source_target_pairs={{0,16},{16,32},{32,48},{48,64},{64,80},{80,96},{96,112},{1,17},{17... | collective-permute-start | bytes 196616 | tf_op jit(solution)/shard_map/ppermute | solution.py:562
  28.7 1.9 collective-permute-start.9
  30.6 9.3 %all-to-all-done.incoming = bf16[128,40,128]{2,1,0:T(8,128)(2,1)S(1)} async-done(((bf16[128,40,128]{2,1,0:T(8,128)(2,1)}), bf16[128,40,128]{2,1,0:T(8,128)(2,1)S(1)}, u32[]{:S(2)}, u32[]{:S(2)}) %all-to-all-start) | async-done | bytes 1310752 | tf_op jit(solution)/shard_map/all_to_all | solution.py:556
  39.9 10.9 %deposit.1.own.heat_own = f32[2,128,128]{2,1,0:T(8,128)S(1)} custom-call(bf16[128,40,128]{2,1,0:T(8,128)(2,1)S(1)} %all-to-all-done.incoming), custom_call_target="tpu_custom_call" | custom-call | tf_op jit(solution)/shard_map/deposit/pallas_call | solution.py:252
  50.8 2.7 %collective-permute-start.4 = (f32[2,128,128]{2,1,0:T(8,128)S(1)}, f32[2,128,128]{2,1,0:T(8,128)S(1)}, u32[]{:S(2)}, u32[]{:S(2)}) collective-permute-start(f32[2,128,128]{2,1,0:T(8,128)S(1)} %deposit.1.own.heat_own), channel_id=1, source_target_pairs={{0,1},{1,2},{2,3},{3,4},{4,5},{5,6},{6,7},{7,8},{8,9},{9,10},{10,1... | collective-permute-start | bytes 393224 | tf_op jit(solution)/shard_map/ppermute | solution.py:562
  53.5 0.0 collective-permute-done.8
  53.5 0.0 collective-permute-done.9
  53.6 2.9 %collective-permute-start.10 = (f32[3,16,8,128]{3,2,1,0:T(8,128)S(1)}, f32[3,16,8,128]{3,2,1,0:T(8,128)S(1)}, u32[]{:S(2)}, u32[]{:S(2)}) collective-permute-start(f32[3,16,8,128]{3,2,1,0:T(8,128)S(1)} %pad_maximum_fusion.own), channel_id=1, source_target_pairs={{0,1},{1,2},{2,3},{3,4},{4,5},{5,6},{6,7},{7,8},{8,9},{9,10},{10,1... | collective-permute-start | bytes 589832 | tf_op jit(solution)/shard_map/ppermute | solution.py:562
  56.4 1.3 collective-permute-start.11
  57.8 1.8 sides.1
  59.6 3.0 %collective-permute-start.2 = (f32[2,20,8,128]{3,2,1,0:T(8,128)}, f32[2,20,8,128]{3,2,1,0:T(8,128)S(1)}, u32[]{:S(2)}, u32[]{:S(2)}) collective-permute-start(f32[2,20,8,128]{3,2,1,0:T(8,128)} %get-tuple-element.31), channel_id=1, source_target_pairs={{0,16},{16,32},{32,48},{48,64},{64,80},{80,96},{96,112},{1,17},{17... | collective-permute-start | bytes 491528 | tf_op jit(solution)/shard_map/ppermute | solution.py:562
  62.6 1.9 collective-permute-start.3
  64.5 0.0 collective-permute-done.4.low.heat_low
  64.5 1.3 collective-permute-start.5
  65.8 5.4 %collective-permute-done.5.high.heat_high = f32[2,128,128]{2,1,0:T(8,128)S(1)} collective-permute-done((f32[2,128,128]{2,1,0:T(8,128)S(1)}, f32[2,128,128]{2,1,0:T(8,128)S(1)}, u32[]{:S(2)}, u32[]{:S(2)}) %collective-permute-start.5) | collective-permute-done | bytes 131104 | tf_op jit(solution)/shard_map/ppermute | solution.py:562
  71.2 4.4 %collective-permute-start.6 = (f32[3,2,8,128]{3,2,1,0:T(8,128)S(1)}, f32[3,2,8,128]{3,2,1,0:T(8,128)S(1)}, u32[]{:S(2)}, u32[]{:S(2)}) collective-permute-start(f32[3,2,8,128]{3,2,1,0:T(8,128)S(1)} %get-tuple-element.33), channel_id=1, source_target_pairs={{0,16},{16,32},{32,48},{48,64},{64,80},{80,96},{96,112},{1,17},{17... | collective-permute-start | bytes 73736 | tf_op jit(solution)/shard_map/ppermute | solution.py:562
  75.6 1.9 collective-permute-start.7
  77.6 0.0 collective-permute-done.11.high
  77.6 2.6 %coefs.1.coef = f32[2,20,18,8,128]{4,3,2,1,0:T(8,128)S(1)} custom-call(f32[3,16,8,128]{3,2,1,0:T(8,128)S(1)} %pad_maximum_fusion.own, f32[3,16,8,128]{3,2,1,0:T(8,128)S(1)} %collective-permute-done.10.low, f32[3,16,8,128]{3,2,1,0:T(8,128)S(1)} %collective-permute-done.11.high), custom_call_target="tpu_custom_call" | custom-call | tf_op jit(solution)/shard_map/coefs/pallas_call | solution.py:204
  80.2 1.6 copy-done
  81.8 4.5 %heated.1 = (f32[2,20,18,8,128]{4,3,2,1,0:T(8,128)}, f32[128,1,128]{2,1,0:T(1,128)}) custom-call(f32[2,8,16,8,128]{4,3,2,1,0:T(8,128)S(1)} %get-tuple-element.28.own, f32[2,6,16,8,128]{4,3,2,1,0:T(8,128)S(1)} %collective-permute-done.low, f32[2,6,16,8,128]{4,3,2,1,0:T(8,128)} %collective-permute-done.1.high, ...), custom_call_target="tpu_custom_call" | custom-call | tf_op jit(solution)/shard_map/heated/pallas_call | solution.py:324
  86.2 10.7 %all-to-all-start.1 = ((f32[128,1,128]{2,1,0:T(1,128)}), f32[128,1,128]{2,1,0:T(1,128)S(1)}, u32[]{:S(2)}, u32[]{:S(2)}) async-start(f32[128,1,128]{2,1,0:T(1,128)} %get-tuple-element.36), calls=%async_computation.1 | async-start | bytes 131072 | tf_op jit(solution)/shard_map/all_to_all | solution.py:556
  97.0 0.1 add_convert_fusion.inside
  97.1 9.4 %all-to-all-done.1.peaks = f32[128,1,128]{2,1,0:T(1,128)S(1)} async-done(((f32[128,1,128]{2,1,0:T(1,128)}), f32[128,1,128]{2,1,0:T(1,128)S(1)}, u32[]{:S(2)}, u32[]{:S(2)}) %all-to-all-start.1) | async-done | bytes 65568 | tf_op jit(solution)/shard_map/all_to_all | solution.py:556
  106.5 1.8 copy-done.1
  108.3 6.2 %substep_0.1 = (f32[2,20,18,8,128]{4,3,2,1,0:T(8,128)S(1)}, f32[128,1,128]{2,1,0:T(1,128)S(1)}) custom-call(f32[4]{0:T(128)S(1)} %add_convert_fusion.inside, f32[2,20,18,8,128]{4,3,2,1,0:T(8,128)S(1)} %copy-done.1, f32[2,20,18,8,128]{4,3,2,1,0:T(8,128)} %copy-done, f32[128,1,128]{2,1,0:T(1,128)S(1)} %all-to-all-done.1.peaks), custom_call_target="tpu_custom_call" | custom-call | tf_op jit(solution)/shard_map/substep_0/pallas_call | solution.py:456
  114.6 13.9 %all_to_all.40.peaks = f32[128,1,128]{2,1,0:T(1,128)S(1)} all-to-all(f32[128,1,128]{2,1,0:T(1,128)S(1)} %get-tuple-element.38), channel_id=1, replica_groups=mesh['gx'=8,'gy'=16] {'gx','gy'}, dimensions={0} | all-to-all | bytes 131072 | tf_op jit(solution)/shard_map/all_to_all | solution.py:556
  128.5 5.9 %substep_1.1 = (f32[2,20,18,8,128]{4,3,2,1,0:T(8,128)S(1)}, f32[128,1,128]{2,1,0:T(1,128)S(1)}) custom-call(f32[4]{0:T(128)S(1)} %add_convert_fusion.inside, f32[2,20,18,8,128]{4,3,2,1,0:T(8,128)S(1)} %get-tuple-element.37.field, f32[2,20,18,8,128]{4,3,2,1,0:T(8,128)} %copy-done, f32[128,1,128]{2,1,0:T(1,128)S(1)} %all_to_all.40.peaks), custom_call_target="tpu_custom_call" | custom-call | tf_op jit(solution)/shard_map/substep_1/pallas_call | solution.py:456
  134.3 13.9 %all_to_all.41.peaks = f32[128,1,128]{2,1,0:T(1,128)S(1)} all-to-all(f32[128,1,128]{2,1,0:T(1,128)S(1)} %get-tuple-element.40), channel_id=1, replica_groups=mesh['gx'=8,'gy'=16] {'gx','gy'}, dimensions={0} | all-to-all | bytes 131072 | tf_op jit(solution)/shard_map/all_to_all | solution.py:556
  148.2 5.4 %substep_2.1 = (f32[2,20,18,8,128]{4,3,2,1,0:T(8,128)S(1)}, f32[128,1,128]{2,1,0:T(1,128)S(1)}) custom-call(f32[4]{0:T(128)S(1)} %add_convert_fusion.inside, f32[2,20,18,8,128]{4,3,2,1,0:T(8,128)S(1)} %get-tuple-element.39.field, f32[2,20,18,8,128]{4,3,2,1,0:T(8,128)} %copy-done, f32[128,1,128]{2,1,0:T(1,128)S(1)} %all_to_all.41.peaks), custom_call_target="tpu_custom_call" | custom-call | tf_op jit(solution)/shard_map/substep_2/pallas_call | solution.py:456
  153.6 13.9 %all_to_all.42.peaks = f32[128,1,128]{2,1,0:T(1,128)S(1)} all-to-all(f32[128,1,128]{2,1,0:T(1,128)S(1)} %get-tuple-element.42), channel_id=1, replica_groups=mesh['gx'=8,'gy'=16] {'gx','gy'}, dimensions={0} | all-to-all | bytes 131072 | tf_op jit(solution)/shard_map/all_to_all | solution.py:556
  167.5 4.9 %substep_3.1 = (f32[2,20,18,8,128]{4,3,2,1,0:T(8,128)S(1)}, f32[128,1,128]{2,1,0:T(1,128)S(1)}) custom-call(f32[4]{0:T(128)S(1)} %add_convert_fusion.inside, f32[2,20,18,8,128]{4,3,2,1,0:T(8,128)S(1)} %get-tuple-element.41.field, f32[2,20,18,8,128]{4,3,2,1,0:T(8,128)} %copy-done, f32[128,1,128]{2,1,0:T(1,128)S(1)} %all_to_all.42.peaks), custom_call_target="tpu_custom_call" | custom-call | tf_op jit(solution)/shard_map/substep_3/pallas_call | solution.py:456
  172.4 13.9 %all_to_all.43.peaks = f32[128,1,128]{2,1,0:T(1,128)S(1)} all-to-all(f32[128,1,128]{2,1,0:T(1,128)S(1)} %get-tuple-element.44), channel_id=1, replica_groups=mesh['gx'=8,'gy'=16] {'gx','gy'}, dimensions={0} | all-to-all | bytes 131072 | tf_op jit(solution)/shard_map/all_to_all | solution.py:556
  186.3 5.2 %substep_4.1 = (f32[2,20,18,8,128]{4,3,2,1,0:T(8,128)S(1)}, f32[128,1,128]{2,1,0:T(1,128)}) custom-call(f32[4]{0:T(128)S(1)} %add_convert_fusion.inside, f32[2,20,18,8,128]{4,3,2,1,0:T(8,128)S(1)} %get-tuple-element.43.field, f32[2,20,18,8,128]{4,3,2,1,0:T(8,128)} %copy-done, f32[128,1,128]{2,1,0:T(1,128)S(1)} %all_to_all.43.peaks), custom_call_target="tpu_custom_call" | custom-call | tf_op jit(solution)/shard_map/substep_4/pallas_call | solution.py:456
  191.5 4.5 %all-to-all-start.6 = ((f32[128,1,128]{2,1,0:T(1,128)}), f32[128,1,128]{2,1,0:T(1,128)S(1)}, u32[]{:S(2)}, u32[]{:S(2)}) async-start(f32[128,1,128]{2,1,0:T(1,128)} %get-tuple-element.46), calls=%async_computation.6 | async-start | bytes 131072 | tf_op jit(solution)/shard_map/all_to_all | solution.py:556
  196.1 1.7 pixels.1
  197.8 7.9 %all-to-all-done.6.peaks = f32[128,1,128]{2,1,0:T(1,128)S(1)} async-done(((f32[128,1,128]{2,1,0:T(1,128)}), f32[128,1,128]{2,1,0:T(1,128)S(1)}, u32[]{:S(2)}, u32[]{:S(2)}) %all-to-all-start.6) | async-done | bytes 65568 | tf_op jit(solution)/shard_map/all_to_all | solution.py:556
  205.7 4.1 %substep_5.1 = (f32[2,8,16,8,128]{4,3,2,1,0:T(8,128)S(1)}, f32[128,4,128]{2,1,0:T(4,128)S(1)}) custom-call(f32[4]{0:T(128)S(1)} %add_convert_fusion.inside, f32[2,20,18,8,128]{4,3,2,1,0:T(8,128)S(1)} %get-tuple-element.45.field, f32[2,20,18,8,128]{4,3,2,1,0:T(8,128)} %copy-done, f32[128,1,128]{2,1,0:T(1,128)S(1)} %all-to-all-done.6.peaks, ...), custom_call_target="tpu_custom_call" | custom-call | tf_op jit(solution)/shard_map/substep_5/pallas_call | solution.py:456
  209.8 15.5 %all_to_all.44.sums = f32[128,4,128]{2,1,0:T(4,128)S(1)} all-to-all(f32[128,4,128]{2,1,0:T(4,128)S(1)} %get-tuple-element.49), channel_id=1, replica_groups=mesh['gx'=8,'gy'=16] {'gx','gy'}, dimensions={0} | all-to-all | bytes 524288 | tf_op jit(solution)/shard_map/all_to_all | solution.py:556
  225.3 5.3 %update.1 = f32[16,16,8,128]{3,2,1,0:T(8,128)} custom-call(f32[128,4,128]{2,1,0:T(4,128)S(1)} %all_to_all.44.sums, f32[2,8,16,8,128]{4,3,2,1,0:T(8,128)S(1)} %get-tuple-element.50.field), custom_call_target="tpu_custom_call" | custom-call | tf_op jit(solution)/shard_map/update/pallas_call | solution.py:545
  (26 shorter events, 0.1 us)
Async XLA Ops:
  0.0 18.5 %copy-start.2 = (f32[16,16,8,128]{3,2,1,0:T(8,128)S(1)}, f32[16,16,8,128]{3,2,1,0:T(8,128)}, u32[]{:S(2)}) copy-start(f32[16,16,8,128]{3,2,1,0:T(8,128)} %state.1) | copy-start | bytes 3145732
  0.0 1.1 copy-start.3
  1.1 0.8 copy-start.4
  2.0 0.7 copy-start.9
  2.6 22.4 %copy-start.10 = (f32[16,8,128]{2,1,0:T(8,128)S(1)}, f32[16,8,128]{2,1,0:T(8,128)}, u32[]{:S(2)}) copy-start(f32[16,8,128]{2,1,0:T(8,128)} %param.10) | copy-start | bytes 196612
  7.0 32.9 %all-to-all-start = ((bf16[128,40,128]{2,1,0:T(8,128)(2,1)}), bf16[128,40,128]{2,1,0:T(8,128)(2,1)S(1)}, u32[]{:S(2)}, u32[]{:S(2)}) async-start(bf16[128,40,128]{2,1,0:T(8,128)(2,1)} %pack.1), calls=%async_computation | async-start | bytes 2621440 | tf_op jit(solution)/shard_map/all_to_all | solution.py:556
  20.3 37.4 %collective-permute-start = (f32[2,6,16,8,128]{4,3,2,1,0:T(8,128)}, f32[2,6,16,8,128]{4,3,2,1,0:T(8,128)S(1)}, u32[]{:S(2)}, u32[]{:S(2)}) collective-permute-start(f32[2,6,16,8,128]{4,3,2,1,0:T(8,128)} %get-tuple-element.29), channel_id=1, source_target_pairs={{0,1},{1,2},{2,3},{3,4},{4,5},{5,6},{6,7},{7,8},{8,9},{9,10},{10,1... | collective-permute-start | bytes 2359304 | tf_op jit(solution)/shard_map/ppermute | solution.py:562
  23.7 34.0 %collective-permute-start.1 = (f32[2,6,16,8,128]{4,3,2,1,0:T(8,128)}, f32[2,6,16,8,128]{4,3,2,1,0:T(8,128)}, u32[]{:S(2)}, u32[]{:S(2)}) collective-permute-start(f32[2,6,16,8,128]{4,3,2,1,0:T(8,128)} %get-tuple-element.30), channel_id=1, source_target_pairs={{1,0},{2,1},{3,2},{4,3},{5,4},{6,5},{7,6},{8,7},{9,8},{10,9},{11,1... | collective-permute-start | bytes 2359304 | tf_op jit(solution)/shard_map/ppermute | solution.py:562
  25.1 28.5 %collective-permute-start.8 = (f32[16,8,128]{2,1,0:T(8,128)S(1)}, f32[16,8,128]{2,1,0:T(8,128)S(1)}, u32[]{:S(2)}, u32[]{:S(2)}) collective-permute-start(f32[16,8,128]{2,1,0:T(8,128)S(1)} %copy-done.10), channel_id=1, source_target_pairs={{0,16},{16,32},{32,48},{48,64},{64,80},{80,96},{96,112},{1,17},{17... | collective-permute-start | bytes 196616 | tf_op jit(solution)/shard_map/ppermute | solution.py:562
  28.7 24.8 %collective-permute-start.9 = (f32[16,8,128]{2,1,0:T(8,128)S(1)}, f32[16,8,128]{2,1,0:T(8,128)S(1)}, u32[]{:S(2)}, u32[]{:S(2)}) collective-permute-start(f32[16,8,128]{2,1,0:T(8,128)S(1)} %copy-done.10), channel_id=1, source_target_pairs={{16,0},{32,16},{48,32},{64,48},{80,64},{96,80},{112,96},{17,1},{33... | collective-permute-start | bytes 196616 | tf_op jit(solution)/shard_map/ppermute | solution.py:562
  50.8 13.7 %collective-permute-start.4 = (f32[2,128,128]{2,1,0:T(8,128)S(1)}, f32[2,128,128]{2,1,0:T(8,128)S(1)}, u32[]{:S(2)}, u32[]{:S(2)}) collective-permute-start(f32[2,128,128]{2,1,0:T(8,128)S(1)} %deposit.1.own.heat_own), channel_id=1, source_target_pairs={{0,1},{1,2},{2,3},{3,4},{4,5},{5,6},{6,7},{7,8},{8,9},{9,10},{10,1... | collective-permute-start | bytes 393224 | tf_op jit(solution)/shard_map/ppermute | solution.py:562
  53.6 22.1 %collective-permute-start.10 = (f32[3,16,8,128]{3,2,1,0:T(8,128)S(1)}, f32[3,16,8,128]{3,2,1,0:T(8,128)S(1)}, u32[]{:S(2)}, u32[]{:S(2)}) collective-permute-start(f32[3,16,8,128]{3,2,1,0:T(8,128)S(1)} %pad_maximum_fusion.own), channel_id=1, source_target_pairs={{0,1},{1,2},{2,3},{3,4},{4,5},{5,6},{6,7},{7,8},{8,9},{9,10},{10,1... | collective-permute-start | bytes 589832 | tf_op jit(solution)/shard_map/ppermute | solution.py:562
  56.4 21.1 %collective-permute-start.11 = (f32[3,16,8,128]{3,2,1,0:T(8,128)S(1)}, f32[3,16,8,128]{3,2,1,0:T(8,128)S(1)}, u32[]{:S(2)}, u32[]{:S(2)}) collective-permute-start(f32[3,16,8,128]{3,2,1,0:T(8,128)S(1)} %pad_maximum_fusion.own), channel_id=1, source_target_pairs={{1,0},{2,1},{3,2},{4,3},{5,4},{6,5},{7,6},{8,7},{9,8},{10,9},{11,1... | collective-permute-start | bytes 589832 | tf_op jit(solution)/shard_map/ppermute | solution.py:562
  59.6 22.2 %collective-permute-start.2 = (f32[2,20,8,128]{3,2,1,0:T(8,128)}, f32[2,20,8,128]{3,2,1,0:T(8,128)S(1)}, u32[]{:S(2)}, u32[]{:S(2)}) collective-permute-start(f32[2,20,8,128]{3,2,1,0:T(8,128)} %get-tuple-element.31), channel_id=1, source_target_pairs={{0,16},{16,32},{32,48},{48,64},{64,80},{80,96},{96,112},{1,17},{17... | collective-permute-start | bytes 491528 | tf_op jit(solution)/shard_map/ppermute | solution.py:562
  62.6 19.2 %collective-permute-start.3 = (f32[2,20,8,128]{3,2,1,0:T(8,128)S(1)}, f32[2,20,8,128]{3,2,1,0:T(8,128)S(1)}, u32[]{:S(2)}, u32[]{:S(2)}) collective-permute-start(f32[2,20,8,128]{3,2,1,0:T(8,128)S(1)} %get-tuple-element.32), channel_id=1, source_target_pairs={{16,0},{32,16},{48,32},{64,48},{80,64},{96,80},{112,96},{17,1},{33... | collective-permute-start | bytes 491528 | tf_op jit(solution)/shard_map/ppermute | solution.py:562
  64.5 6.7 %collective-permute-start.5 = (f32[2,128,128]{2,1,0:T(8,128)S(1)}, f32[2,128,128]{2,1,0:T(8,128)S(1)}, u32[]{:S(2)}, u32[]{:S(2)}) collective-permute-start(f32[2,128,128]{2,1,0:T(8,128)S(1)} %deposit.1.own.heat_own), channel_id=1, source_target_pairs={{1,0},{2,1},{3,2},{4,3},{5,4},{6,5},{7,6},{8,7},{9,8},{10,9},{11,1... | collective-permute-start | bytes 393224 | tf_op jit(solution)/shard_map/ppermute | solution.py:562
  71.2 10.5 %collective-permute-start.6 = (f32[3,2,8,128]{3,2,1,0:T(8,128)S(1)}, f32[3,2,8,128]{3,2,1,0:T(8,128)S(1)}, u32[]{:S(2)}, u32[]{:S(2)}) collective-permute-start(f32[3,2,8,128]{3,2,1,0:T(8,128)S(1)} %get-tuple-element.33), channel_id=1, source_target_pairs={{0,16},{16,32},{32,48},{48,64},{64,80},{80,96},{96,112},{1,17},{17... | collective-permute-start | bytes 73736 | tf_op jit(solution)/shard_map/ppermute | solution.py:562
  75.6 6.1 %collective-permute-start.7 = (f32[3,2,8,128]{3,2,1,0:T(8,128)S(1)}, f32[3,2,8,128]{3,2,1,0:T(8,128)S(1)}, u32[]{:S(2)}, u32[]{:S(2)}) collective-permute-start(f32[3,2,8,128]{3,2,1,0:T(8,128)S(1)} %get-tuple-element.34), channel_id=1, source_target_pairs={{16,0},{32,16},{48,32},{64,48},{80,64},{96,80},{112,96},{17,1},{33... | collective-permute-start | bytes 73736 | tf_op jit(solution)/shard_map/ppermute | solution.py:562
  80.2 1.6 copy-start
  86.2 20.3 %all-to-all-start.1 = ((f32[128,1,128]{2,1,0:T(1,128)}), f32[128,1,128]{2,1,0:T(1,128)S(1)}, u32[]{:S(2)}, u32[]{:S(2)}) async-start(f32[128,1,128]{2,1,0:T(1,128)} %get-tuple-element.36), calls=%async_computation.1 | async-start | bytes 131072 | tf_op jit(solution)/shard_map/all_to_all | solution.py:556
  106.5 1.8 copy-start.1
  186.3 9.7 %copy-start.5 = (f32[16,512]{1,0:T(8,128)S(1)}, f32[16,512]{1,0:T(8,128)}, u32[]{:S(2)}) copy-start(f32[16,512]{1,0:T(8,128)} %noise.1) | copy-start | bytes 98308
  186.3 9.7 %copy-start.6 = (s32[512]{0:T(512)S(1)}, s32[512]{0:T(512)}, u32[]{:S(2)}) copy-start(s32[512]{0:T(512)} %param.14) | copy-start | bytes 6148
  186.3 9.7 %copy-start.7 = (f32[512]{0:T(512)S(1)}, f32[512]{0:T(512)}, u32[]{:S(2)}) copy-start(f32[512]{0:T(512)} %param.15) | copy-start | bytes 6148
  186.3 9.7 %copy-start.8 = (f32[512]{0:T(512)S(1)}, f32[512]{0:T(512)}, u32[]{:S(2)}) copy-start(f32[512]{0:T(512)} %param.16) | copy-start | bytes 6148
  191.5 14.2 %all-to-all-start.6 = ((f32[128,1,128]{2,1,0:T(1,128)}), f32[128,1,128]{2,1,0:T(1,128)S(1)}, u32[]{:S(2)}, u32[]{:S(2)}) async-start(f32[128,1,128]{2,1,0:T(1,128)} %get-tuple-element.46), calls=%async_computation.6 | async-start | bytes 131072 | tf_op jit(solution)/shard_map/all_to_all | solution.py:556

commit v3 on v2

--- a/solution.py
+++ b/solution.py
@@ -14,7 +14,7 @@
 F32 = jnp.float32
 BF16 = jnp.bfloat16
 VM = pltpu.VMEM
-LIMIT = 48 * 1024 * 1024
+LIMIT = 24 * 1024 * 1024
 NT = (((1,), (1,)), ((), ()))
 BOTH = ("gx", "gy")
 
@@ -121,12 +121,18 @@
 YS = CY + 2 * HALO
 XT = CX // 8 + 2
 ZG = NZ // 2
+TOLERANCE = 1e-6
 OWN = jax.ShapeDtypeStruct((2, CY, XT - 2, 8, CX), F32)
-ROWHALO = jax.ShapeDtypeStruct((2, HALO, XT - 2, 8, CX), F32)
 WIDE = jax.ShapeDtypeStruct((2, YS, XT, 8, CX), F32)
-
-
-def relayout_kernel(state, own, to_high, to_low):
+EDGE = 2 * HALO * (XT - 2)
+SIDE = 2 * YS
+
+
+def relayout_kernel(state, conduct, own, turned_c, to_high, to_low):
+    turned = (0.5 * conduct[...].reshape(CX, CX)).T.reshape(XT - 2, 8, CX)
+    turned_c[...] = turned
+    to_high[EDGE:] = turned
+    to_low[EDGE:] = turned
     for zi in range(2):
         for y in range(CY):
             parts = [
@@ -135,60 +141,67 @@
             turned = (0.5 * jnp.concatenate(parts, axis=0)).T.reshape(XT - 2, 8, CX)
             own[zi, y] = turned
             if y >= CY - HALO:
-                to_high[zi, y - (CY - HALO)] = turned
+                at = (zi * HALO + y - (CY - HALO)) * (XT - 2)
+                to_high[at : at + XT - 2] = turned
             if y < HALO:
-                to_low[zi, y] = turned
-
-
-def relayout(state):
+                at = (zi * HALO + y) * (XT - 2)
+                to_low[at : at + XT - 2] = turned
+
+
+def relayout(state, conduct):
+    edge = jax.ShapeDtypeStruct((EDGE + XT - 2, 8, CX), F32)
     return pl.pallas_call(
         relayout_kernel,
-        out_shape=[OWN, ROWHALO, ROWHALO],
-        in_specs=[vspec()],
-        out_specs=[vspec()] * 3,
+        out_shape=[OWN, jax.ShapeDtypeStruct((XT - 2, 8, CX), F32), edge, edge],
+        in_specs=[vspec()] * 2,
+        out_specs=[vspec()] * 4,
         compiler_params=params(),
         name="relayout",
-    )(state)
-
-
-def side_kernel(own, low, high, to_left, to_right):
+    )(state, conduct)
+
+
+def side_kernel(own, turned_c, low, high, to_left, to_right):
     for out, t in ((to_left, 0), (to_right, XT - 3)):
         for zi in range(2):
             for y in range(YS):
                 if y < HALO:
-                    out[zi, y] = low[zi, y, t]
+                    part = low[(zi * HALO + y) * (XT - 2) + t]
                 elif y < HALO + CY:
-                    out[zi, y] = own[zi, y - HALO, t]
+                    part = own[zi, y - HALO, t]
                 else:
-                    out[zi, y] = high[zi, y - HALO - CY, t]
-
-
-def sides(own, low, high):
-    shape = jax.ShapeDtypeStruct((2, YS, 8, CX), F32)
+                    part = high[(zi * HALO + y - HALO - CY) * (XT - 2) + t]
+                out[zi * YS + y] = part
+        out[SIDE] = low[EDGE + t]
+        out[SIDE + 1] = turned_c[t]
+        out[SIDE + 2] = high[EDGE + t]
+
+
+def sides(own, turned_c, low, high):
+    shape = jax.ShapeDtypeStruct((SIDE + 3, 8, CX), F32)
     return pl.pallas_call(
         side_kernel,
         out_shape=[shape, shape],
-        in_specs=[vspec()] * 3,
+        in_specs=[vspec()] * 4,
         out_specs=[vspec()] * 2,
         compiler_params=params(),
         name="sides",
-    )(own, low, high)
-
-
-def coef_kernel(own, low, high, out, turned):
-    for g, tiles in enumerate((low, own, high)):
-        for t in range(3):
-            turned[g, t] = (0.5 * tiles[t].reshape(CX, CX)).T
+    )(own, turned_c, low, high)
+
+
+def coef_kernel(turned_c, low, high, left, right, out):
     source = lax.broadcasted_iota(jnp.int32, (CX, CX), 0)
     target = lax.broadcasted_iota(jnp.int32, (CX, CX), 1)
+    strips = []
+    for g in range(3):
+        mid = (low[EDGE:], turned_c[...], high[EDGE:])[g].reshape(CX, CX)
+        strips.append(jnp.concatenate([left[SIDE + g], mid, right[SIDE + g]], axis=0))
 
     def put(g, y0, yy):
-        strip = jnp.concatenate([turned[g, 0, CX - 8 :, :], turned[g, 1], turned[g, 2, 0:8, :]], axis=0)
         for zi in range(2):
             wanted = (2 * (target >> 4) + zi) * CY + y0
             hot = jnp.where(source == wanted, 1.0, 0.0).astype(F32)
             part = jnp.dot(
-                strip, hot, precision=lax.Precision.HIGHEST, preferred_element_type=F32
+                strips[g], hot, precision=lax.Precision.HIGHEST, preferred_element_type=F32
             )
             out[zi, yy] = part.reshape(XT, 8, CX)
 
@@ -200,16 +213,15 @@
         put(2, y, y + HALO + CY)
 
 
-def coefs(own, low, high):
+def coefs(turned_c, low, high, left, right):
     return pl.pallas_call(
         coef_kernel,
         out_shape=WIDE,
-        in_specs=[vspec()] * 3,
+        in_specs=[vspec()] * 5,
         out_specs=vspec(),
-        scratch_shapes=[VM((3, 3, CX, CX), F32)],
         compiler_params=params(),
         name="coefs",
-    )(own, low, high)
+    )(turned_c, low, high, left, right)
 
 
 def deposit_kernel(incoming, out, total):
@@ -278,66 +290,36 @@
     )(low, own, high)
 
 
-def heated_kernel(
-    own, low, high, left, right, heat_low, heat_own, heat_high, heat_left, heat_right, coef, out, peaks
-):
-    top = lanes() < M
-    peak = jnp.zeros((8, CX), F32)
-
-    def row(g, heat, tile_of, y0, yy, peak, inner):
-        shift = (CX - 16 * y0) % CX
-        for zi in range(2):
-            for t in range(XT):
-                if t == 0:
-                    prior, add = left[zi, yy], heat_left[g, zi]
-                elif t == XT - 1:
-                    prior, add = right[zi, yy], heat_right[g, zi]
-                else:
-                    prior, add = tile_of(zi, t - 1), heat[zi, 8 * t - 8 : 8 * t, :]
-                if shift:
-                    add = pltpu.roll(add, shift, axis=1)
-                value = prior + jnp.where(top, add, 0.0)
-                out[zi, yy, t] = value
-                if inner and 0 < t < XT - 1:
-                    c = coef[zi, yy, t]
-                    peak = jnp.maximum(peak, c + c * (value * value))
-        return peak
-
-    for y in range(HALO):
-        y0 = y + CY - HALO
-        row(0, heat_low, lambda zi, t: low[zi, y, t], y0, y, peak, False)
-    for y in range(CY):
-        peak = row(1, heat_own, lambda zi, t: own[zi, y, t], y, y + HALO, peak, True)
-    for y in range(HALO):
-        row(2, heat_high, lambda zi, t: high[zi, y, t], y, y + HALO + CY, peak, False)
-    spread_peak(peak, peaks)
-
-
-def spread_peak(peak, out):
-    row = jnp.max(peak, axis=0, keepdims=True)
-    for d in range(out.shape[0]):
-        out[d] = row
-
-
-def heated(prior, halos, heat, coef, devices):
-    operands = [*prior, *halos, *heat, coef]
-    return pl.pallas_call(
-        heated_kernel,
-        out_shape=[WIDE, jax.ShapeDtypeStruct((devices, 1, CX), F32)],
-        in_specs=[vspec()] * len(operands),
-        out_specs=[vspec()] * 2,
-        compiler_params=params(),
-        name="heated",
-    )(*operands)
-
-
-def substep_kernel(number, inside, field, coef, peaks, *rest):
-    last = number == SUBSTEPS - 1
-    if last:
-        weight, data, out, sums, above, below_h, flat = rest
-    else:
-        out, out_peaks, above, below_h = rest
-    first, end = number + 1, YS - 1 - number
+def columns_peak(value):
+    for shift in (4, 2, 1):
+        value = jnp.maximum(value, pltpu.roll(value, shift, axis=0))
+    return value
+
+
+def whole_peak(value):
+    return jnp.broadcast_to(jnp.max(value, axis=(0, 1), keepdims=True), (8, CX))
+
+
+def step_of(peak):
+    return SHARE / (12.0 * peak + COOL)
+
+
+def conductance(field, coef, zi, y, t):
+    u = field[zi, y, t]
+    c = coef[zi, y, t]
+    return u, c + c * (u * u)
+
+
+def own_row(y):
+    return jnp.where((y >= HALO) & (y < HALO + CY), 1.0, 0.0)
+
+
+def masks(inside, y):
+    kept = jnp.where(y < HALO, inside[2], jnp.where(y >= HALO + CY, inside[3], 1.0))
+    return [kept * inside[0]] + [kept] * (XT - 2) + [kept * inside[1]]
+
+
+def sweep(field, coef, above, below_h, first, end, emit, carry):
     lane = lanes()
     row = rows()
     last_row = row == 7
@@ -345,34 +327,23 @@
     inner_lane = lane < CX - M
     cooling = jnp.where(lane < M, COOL, 0.0)
 
-    peak = peaks[0]
-    for d in range(1, peaks.shape[0]):
-        peak = jnp.maximum(peak, peaks[d])
-    peak = 2.0 * jnp.max(peak, axis=(0, 1), keepdims=True)
-    step = jnp.broadcast_to(SHARE / (6.0 * peak + COOL), (8, CX))
-
-    def conduct(zi, y, t):
-        u = field[zi, y, t]
-        c = coef[zi, y, t]
-        return u, c + c * (u * u)
-
     for zi in range(2):
         for t in range(XT):
-            u, h = conduct(zi, first - 1, t)
-            v, g = conduct(zi, first, t)
+            u, h = conductance(field, coef, zi, first - 1, t)
+            v, g = conductance(field, coef, zi, first, t)
             above[zi, t] = (h + g) * (v - u)
             below_h[zi, t] = g
 
-    def line(y, peak):
-        kept = jnp.where(y < HALO, inside[2], jnp.where(y >= HALO + CY, inside[3], 1.0))
-        mid = step * kept
-        steps = [mid * inside[0]] + [mid] * (XT - 2) + [mid * inside[1]]
-        top = jnp.zeros((8, CX), F32)
-
+    def line(y, state):
         def load(t):
             us = [field[zi, y, t] for zi in range(2)]
             hs = [below_h[zi, t] for zi in range(2)]
-            return us, hs, [pltpu.roll(a, 7, axis=0) for a in us], [pltpu.roll(a, 7, axis=0) for a in hs]
+            return (
+                us,
+                hs,
+                [pltpu.roll(a, 7, axis=0) for a in us],
+                [pltpu.roll(a, 7, axis=0) for a in hs],
+            )
 
         us, hs, ru, rh = load(0)
         carried = [jnp.zeros((8, CX), F32)] * 2
@@ -391,7 +362,7 @@
                 turned = pltpu.roll(along, 1, axis=0)
                 total = along - jnp.where(first_row, carried[zi], turned)
                 carried[zi] = turned
-                v, g = conduct(zi, y + 1, t)
+                v, g = conductance(field, coef, zi, y + 1, t)
                 across = (h + g) * (v - u)
                 total = total + (across - above[zi, t])
                 above[zi, t] = across
@@ -404,29 +375,205 @@
             between = jnp.where(inner_lane, between, 0.0)
             change[0] = change[0] + (within - pltpu.roll(between, M, axis=1)) - cooling * us[0]
             change[1] = change[1] + (between - within)
-            for zi in range(2):
-                value = us[zi] + steps[t] * change[zi]
-                if last:
-                    if 0 < t < XT - 1:
-                        out[zi, y - HALO, t - 1] = value
-                else:
-                    out[zi, y, t] = value
-                    if 0 < t < XT - 1:
-                        c = coef[zi, y, t]
-                        top = jnp.maximum(top, c + c * (value * value))
+            state = emit(y, t, us, change, state)
             if t < XT - 1:
                 us, hs, ru, rh = after
-        own = jnp.where((y >= HALO) & (y < HALO + CY), 1.0, 0.0)
-        return jnp.maximum(peak, top * own)
-
-    peak = lax.fori_loop(first, end, line, jnp.zeros((8, CX), F32))
-    if not last:
-        spread_peak(peak, out_peaks)
-        return
-
+        return state
+
+    return lax.fori_loop(first, end, line, carry)
+
+
+def advance(field, coef, above, below_h, inside, step, first, end, put):
+    def emit(y, t, us, change, peak):
+        part = masks(inside, y)[t] * step
+        own = own_row(y)
+        for zi in range(2):
+            value = us[zi] + part * change[zi]
+            put(zi, y, t, value)
+            if 0 < t < XT - 1:
+                c = coef[zi, y, t]
+                peak = jnp.maximum(peak, own * (c + c * (value * value)))
+        return peak
+
+    return sweep(field, coef, above, below_h, first, end, emit, jnp.zeros((8, CX), F32))
+
+
+def propose(field, coef, above, below_h, inside, guess, first, end, changes, peak, late, out):
+    def emit(y, t, us, change, best):
+        part = masks(inside, y)[t]
+        own = own_row(y)
+        for zi in range(2):
+            moved = change[zi] * part
+            changes[zi, y, t] = moved
+            if 0 < t < XT - 1:
+                c = coef[zi, y, t]
+                value = us[zi] + guess * moved
+                rank = own * (c + c * (value * value))
+                better = rank > best[0]
+                best = tuple(
+                    jnp.where(better, new, old)
+                    for new, old in zip((rank, us[zi], moved, c), best)
+                )
+        return best
+
+    best = sweep(
+        field, coef, above, below_h, first, end, emit, (jnp.zeros((8, CX), F32),) * 4
+    )
+    for shift in (4, 2, 1):
+        other = tuple(pltpu.roll(part, shift, axis=0) for part in best)
+        better = other[0] > best[0]
+        best = tuple(jnp.where(better, new, old) for new, old in zip(other, best))
+    row = rows()
+    head = jnp.where(lanes() < CX // 2, whole_peak(peak), whole_peak(late))
+    chunk = jnp.where(
+        row == 0, head, jnp.where(row == 1, best[1], jnp.where(row == 2, best[2], best[3]))
+    )[0:4]
+    for d in range(out.shape[0]):
+        out[d] = chunk
+
+
+def agree(parts):
+    lane = lanes()
+    now = jnp.zeros((8, CX), F32)
+    for d in range(0, parts.shape[0], 8):
+        now = jnp.maximum(now, parts[d : d + 8, 0, :])
+    late = whole_peak(jnp.where(lane < CX // 2, 0.0, now))
+    now = whole_peak(jnp.where(lane < CX // 2, now, 0.0))
+    step = step_of(now)
+    then = jnp.zeros((8, CX), F32)
+    for d in range(0, parts.shape[0], 8):
+        value = parts[d : d + 8, 1, :] + step * parts[d : d + 8, 2, :]
+        c = parts[d : d + 8, 3, :]
+        then = jnp.maximum(then, c + c * (value * value))
+    return now, whole_peak(then), late
+
+
+def differs(late, used):
+    return jnp.where(late > used * (1.0 + TOLERANCE), 1.0, 0.0)
+
+
+def heated_kernel(
+    inside, own, low, high, left, right,
+    heat_low, heat_own, heat_high, heat_left, heat_right,
+    coef, out, changes, parts, above, below_h,
+):
+    top = lanes() < M
+    peak = jnp.zeros((8, CX), F32)
+
+    def row(g, heat, tile_of, y0, yy, peak):
+        shift = (CX - 16 * y0) % CX
+        for zi in range(2):
+            for t in range(XT):
+                if t == 0:
+                    prior, add = left[zi * YS + yy], heat_left[g, zi]
+                elif t == XT - 1:
+                    prior, add = right[zi * YS + yy], heat_right[g, zi]
+                else:
+                    prior, add = tile_of(zi, t - 1), heat[zi, 8 * t - 8 : 8 * t, :]
+                if shift:
+                    add = pltpu.roll(add, shift, axis=1)
+                value = prior + jnp.where(top, add, 0.0)
+                out[zi, yy, t] = value
+                if g == 1 and 0 < t < XT - 1:
+                    c = coef[zi, yy, t]
+                    peak = jnp.maximum(peak, c + c * (value * value))
+        return peak
+
+    def edge(ref, y):
+        return lambda zi, t: ref[(zi * HALO + y) * (XT - 2) + t]
+
+    for y in range(HALO):
+        row(0, heat_low, edge(low, y), y + CY - HALO, y, peak)
+    for y in range(CY):
+        peak = row(1, heat_own, lambda zi, t: own[zi, y, t], y, y + HALO, peak)
+    for y in range(HALO):
+        row(2, heat_high, edge(high, y), y, y + HALO + CY, peak)
+    guess = step_of(whole_peak(peak))
+    zero = jnp.zeros((8, CX), F32)
+    propose(out, coef, above, below_h, inside, guess, 1, YS - 1, changes, peak, zero, parts)
+
+
+ROW = (2, XT, 8, CX)
+
+
+def smem():
+    return pl.BlockSpec(memory_space=pltpu.SMEM)
+
+
+def heated(inside, prior, halos, heat, coef, devices):
+    operands = [inside, *prior, *halos, *heat, coef]
+    return pl.pallas_call(
+        heated_kernel,
+        out_shape=[WIDE, WIDE, jax.ShapeDtypeStruct((devices, 4, CX), F32)],
+        in_specs=[smem()] + [vspec()] * (len(operands) - 1),
+        out_specs=[vspec()] * 3,
+        scratch_shapes=[VM(ROW, F32), VM(ROW, F32)],
+        compiler_params=params(),
+        name="heated",
+    )(*operands)
+
+
+def first_of_pair(field, changes, coef, step, first, end, out):
+    def line(y, peak):
+        own = own_row(y)
+        top = jnp.zeros((8, CX), F32)
+        for zi in range(2):
+            for t in range(XT):
+                value = field[zi, y, t] + step * changes[zi, y, t]
+                out[zi, y, t] = value
+                if 0 < t < XT - 1:
+                    c = coef[zi, y, t]
+                    top = jnp.maximum(top, c + c * (value * value))
+        return jnp.maximum(peak, own * top)
+
+    return lax.fori_loop(first, end, line, jnp.zeros((8, CX), F32))
+
+
+def pair_kernel(
+    number, inside, field, changes, coef, parts, status,
+    out, out_changes, out_parts, out_status, middle, above, below_h,
+):
+    now, then, late = agree(parts)
+    bad = status[1:2, :]
+    if number:
+        bad = jnp.maximum(bad, differs(late[0:1], status[0:1, :]))
+    out_status[...] = jnp.where(rows() == 0, then, bad)
+    seen = first_of_pair(field, changes, coef, step_of(now), number + 1, YS - 1 - number, middle)
+
+    def put(zi, y, t, value):
+        out[zi, y, t] = value
+
+    step = step_of(then)
+    peak = advance(
+        middle, coef, above, below_h, inside, step, number + 2, YS - 2 - number, put
+    )
+    guess = jnp.minimum(step_of(whole_peak(peak)), 1.2 * step)
+    propose(
+        out, coef, above, below_h, inside, guess, number + 3, YS - 3 - number,
+        out_changes, peak, seen, out_parts,
+    )
+
+
+STATUS = jax.ShapeDtypeStruct((8, CX), F32)
+
+
+def pair(number, inside, field, changes, coef, parts, status):
+    operands = [inside, field, changes, coef, parts, status]
+    return pl.pallas_call(
+        functools.partial(pair_kernel, number),
+        out_shape=[WIDE, WIDE, jax.ShapeDtypeStruct(parts.shape, F32), STATUS],
+        in_specs=[smem()] + [vspec()] * 5,
+        out_specs=[vspec()] * 4,
+        scratch_shapes=[VM(WIDE.shape, F32), VM(ROW, F32), VM(ROW, F32)],
+        compiler_params=params(),
+        name=f"pair_{number}",
+    )(*operands)
+
+
+def pixel_grams(field, weight, data, flat, late, sums):
     grams = jnp.zeros((M, 2 * M), F32)
     for y in range(CY):
-        seen = 2.0 * out[0, y].reshape(CX, CX).T[0:M, :]
+        seen = 2.0 * field[0, y].reshape(CX, CX).T[0:M, :]
         for m in range(M):
             flat[m : m + 1, :] = data[m, y : y + 1, :]
         w = weight[y : y + 1, :]
@@ -436,17 +583,72 @@
             spread, both, NT, precision=lax.Precision.HIGHEST, preferred_element_type=F32
         )
     grams = jnp.concatenate([grams, jnp.zeros((M, CX - 2 * M), F32)], axis=1)
-    pair = grams[0:8] + pltpu.roll(grams[8:16], 32, axis=1)
-    quad = pair + pltpu.roll(pltpu.roll(pair, 64, axis=1), 4, axis=0)
-    quad = quad[0:4]
+    two = grams[0:8] + pltpu.roll(grams[8:16], 32, axis=1)
+    quad = two + pltpu.roll(pltpu.roll(two, 64, axis=1), 4, axis=0)
+    quad = jnp.where((rows() == 0) & (lanes() == 1), whole_peak(late), quad)[0:4]
     for d in range(sums.shape[0]):
         sums[d] = quad
 
 
-def substep(number, inside, field, coef, peaks, pixels):
+def last_kernel(
+    inside, field, changes, coef, parts, status, weight, data,
+    out, sums, out_status, middle, above, below_h, flat,
+):
+    number = SUBSTEPS - 2
+    now, then, late = agree(parts)
+    bad = jnp.maximum(status[1:2, :], differs(late[0:1], status[0:1, :]))
+    out_status[...] = jnp.where(rows() == 0, then, bad)
+    seen = first_of_pair(field, changes, coef, step_of(now), number + 1, YS - 1 - number, middle)
+
+    def put(zi, y, t, value):
+        if 0 < t < XT - 1:
+            out[zi, y - HALO, t - 1] = value
+
+    advance(middle, coef, above, below_h, inside, step_of(then), HALO, HALO + CY, put)
+    pixel_grams(out, weight, data, flat, seen, sums)
+
+
+def last(inside, field, changes, coef, parts, status, pixels):
+    operands = [inside, field, changes, coef, parts, status, *pixels]
+    return pl.pallas_call(
+        last_kernel,
+        out_shape=[OWN, jax.ShapeDtypeStruct(parts.shape, F32), STATUS],
+        in_specs=[smem()] + [vspec()] * (len(operands) - 1),
+        out_specs=[vspec()] * 3,
+        scratch_shapes=[VM(WIDE.shape, F32), VM(ROW, F32), VM(ROW, F32), VM((M, CX), F32)],
+        compiler_params=params(),
+        name="last_pair",
+    )(*operands)
+
+
+def single_kernel(number, inside, field, coef, peaks, *rest):
+    final = number == SUBSTEPS - 1
+    if final:
+        weight, data, out, sums, above, below_h, flat = rest
+    else:
+        out, out_peaks, above, below_h = rest
+    peak = peaks[0]
+    for d in range(1, peaks.shape[0]):
+        peak = jnp.maximum(peak, peaks[d])
+    step = step_of(whole_peak(peak))
+
+    def put(zi, y, t, value):
+        if not final:
+            out[zi, y, t] = value
+        elif 0 < t < XT - 1:
+            out[zi, y - HALO, t - 1] = value
+
+    peak = advance(field, coef, above, below_h, inside, step, number + 1, YS - 1 - number, put)
+    if final:
+        pixel_grams(out, weight, data, flat, jnp.zeros((8, CX), F32), sums)
+    else:
+        out_peaks[...] = jnp.broadcast_to(columns_peak(peak)[0:1].reshape(1, 1, CX), out_peaks.shape)
+
+
+def single(number, inside, field, coef, peaks, pixels):
     devices = peaks.shape[0]
     operands = [inside, field, coef, peaks]
-    scratch = [VM((2, XT, 8, CX), F32), VM((2, XT, 8, CX), F32)]
+    scratch = [VM(ROW, F32), VM(ROW, F32)]
     if number == SUBSTEPS - 1:
         operands += list(pixels)
         out_shape = [OWN, jax.ShapeDtypeStruct((devices, 4, CX), F32)]
@@ -454,14 +656,15 @@
     else:
         out_shape = [WIDE, jax.ShapeDtypeStruct((devices, 1, CX), F32)]
     return pl.pallas_call(
-        functools.partial(substep_kernel, number),
+        functools.partial(single_kernel, number),
         out_shape=out_shape,
-        in_specs=[pl.BlockSpec(memory_space=pltpu.SMEM)] + [vspec()] * (len(operands) - 1),
+        in_specs=[smem()] + [vspec()] * (len(operands) - 1),
         out_specs=[vspec()] * 2,
         scratch_shapes=scratch,
         compiler_params=params(),
-        name=f"substep_{number}",
+        name=f"single_{number}",
     )(*operands)
+
 
 def pixel_kernel(cell, observed, variance, noise, weight, data):
     pixels = cell.shape[1]
@@ -501,10 +704,15 @@
     )(cell, observed, variance, noise)
 
 
-def update_kernel(sums, field, out):
+def update_kernel(sums, field, status, out, flag):
     quad = sums[0]
+    late = quad
     for d in range(1, sums.shape[0]):
         quad = quad + sums[d]
+        late = jnp.maximum(late, sums[d])
+    late = jnp.broadcast_to(late[0:1, 1:2], (1, CX))
+    bad = jnp.maximum(status[1:2, :], differs(late, status[0:1, :]))
+    flag[0] = jnp.where(jnp.max(bad) > 0.0, 1, 0)
     row = rows()
     quad = jnp.concatenate([quad, jnp.zeros_like(quad)], axis=0)
     pair = jnp.where(row < 4, quad, pltpu.roll(pltpu.roll(quad, 64, axis=1), 4, axis=0))
@@ -512,6 +720,8 @@
     tall = lax.broadcasted_iota(jnp.int32, (M, CX), 0)
     wide = lax.broadcasted_iota(jnp.int32, (M, CX), 1)
     system = jnp.where(tall == wide, system + (M - 1.0), system)
+    mirror = jnp.broadcast_to(system[1:2, 0:1], (M, CX))
+    system = jnp.where((tall == 0) & (wide == 1), mirror, system)
     for i in range(M):
         pivot = system[i : i + 1, :]
         pivot = pivot / pivot[:, i : i + 1]
@@ -541,15 +751,18 @@
                     out[m0 : m0 + 8, 2 * group + zi, y, :] = part[at : at + 8, :]
 
 
-def update(sums, field):
+def update(sums, field, status):
     return pl.pallas_call(
         update_kernel,
-        out_shape=jax.ShapeDtypeStruct((M, NZ, CY, CX), F32),
-        in_specs=[vspec()] * 2,
-        out_specs=vspec(),
+        out_shape=[
+            jax.ShapeDtypeStruct((M, NZ, CY, CX), F32),
+            jax.ShapeDtypeStruct((1,), jnp.int32),
+        ],
+        in_specs=[vspec()] * 3,
+        out_specs=[vspec(), smem()],
         compiler_params=params(),
         name="update",
-    )(sums, field)
+    )(sums, field, status)
 
 
 def exchange(parts):
@@ -582,36 +795,51 @@
     inside = jnp.stack(
         [gx > 0, gx < lax.axis_size("gx") - 1, gy > 0, gy < lax.axis_size("gy") - 1]
     ).astype(F32)
-    own, to_high, to_low = relayout(state_prior)
+    own, turned_c, to_high, to_low = relayout(state_prior, conductivity)
     low, high = move(to_high, "gy", True), move(to_low, "gy", False)
-    to_left, to_right = sides(own, low, high)
-    left, right = move(to_right, "gx", True), move(to_left, "gx", False)
-
-    tiles = jnp.stack(
-        [move(conductivity, "gx", True), conductivity, move(conductivity, "gx", False)]
-    )
-    coef = coefs(tiles, move(tiles, "gy", True), move(tiles, "gy", False))
+    to_left, to_right = sides(own, turned_c, low, high)
     seen = pixel_sums(
         pixel_cell.reshape(1, pixels),
         observed.reshape(1, pixels),
         pixel_variance.reshape(1, pixels),
         pixel_noise,
     )
+    incoming, to_left, to_right, inside, *seen = lax.optimization_barrier(
+        (incoming, to_left, to_right, inside, *seen)
+    )
+    left, right = move(to_right, "gx", True), move(to_left, "gx", False)
 
     heat = deposit(incoming)
     heat_low, heat_high = move(heat, "gy", True), move(heat, "gy", False)
     to_left, to_right = heat_sides(heat_low, heat, heat_high)
     heat_left, heat_right = move(to_right, "gx", True), move(to_left, "gx", False)
-    field, peaks = heated(
+    coef = coefs(turned_c, low, high, left, right)
+    start, changes, parts = heated(
+        inside,
         (own, low, high),
         (left, right),
         (heat_low, heat, heat_high, heat_left, heat_right),
         coef,
         devices,
     )
-    for number in range(SUBSTEPS):
-        field, peaks = substep(number, inside, field, coef, exchange(peaks), seen)
-    return update(exchange(peaks), field)
+    field, status = start, jnp.zeros((8, CX), F32)
+    for number in range(0, SUBSTEPS - 2, 2):
+        field, changes, parts, status = pair(
+            number, inside, field, changes, coef, exchange(parts), status
+        )
+    field, sums, status = last(inside, field, changes, coef, exchange(parts), status, seen)
+    result, flag = update(exchange(sums), field, status)
+
+    def again():
+        peak = coef * (1.0 + start * start)
+        peak = jnp.max(peak[:, HALO : HALO + CY, 1 : XT - 1])
+        peaks = jnp.full((devices, 1, CX), peak)
+        field = start
+        for number in range(SUBSTEPS):
+            field, peaks = single(number, inside, field, coef, exchange(peaks), seen)
+        return update(exchange(peaks), field, jnp.ones((8, CX), F32))[0]
+
+    return lax.cond(flag[0] > 0, again, lambda: result)
 
 
 def solution(mesh):

time: 232 us -> 189 us (0.81)
  blocking collectives: 71 us -> 51.5 us
  starting transfers between devices: 56.4 us -> 38 us
  Pallas kernels: 64.6 us -> 52.3 us
  waiting for transfers between devices: 32 us -> 40.5 us
    ppermute x12 -> x8, waiting for transfers between devices: 5.47 us -> 29.1 us  [move(): return lax.ppermute(part, axis, pairs)]
    all_to_all x5 -> x3, blocking collectives: 71 us -> 51.5 us  [exchange(): return lax.all_to_all(parts, BOTH, split_axis=0, concat_axis=0, tiled=True)]
    all_to_all x3 -> x2, waiting for transfers between devices: 26.5 us -> 11.4 us  [exchange(): return lax.all_to_all(parts, BOTH, split_axis=0, concat_axis=0, tiled=True)]
    all_to_all x3 -> x2, starting transfers between devices: 26.8 us -> 15.8 us  [exchange(): return lax.all_to_all(parts, BOTH, split_axis=0, concat_axis=0, tiled=True)]
    pallas_call x10 -> x7, Pallas kernels: 45.8 us -> 35.3 us  [the longest x2 15.8 us: pair(): pl.pallas_call(functools.partial(pair_kernel, number), out_shape=[WIDE, W...]
    ppermute x12 -> x8, starting transfers between devices: 29.7 us -> 22.2 us  [move(): return lax.ppermute(part, axis, pairs)]
    unnamed x22 -> x28, local copies, waits for them, and re-layouts: 6.04 us -> 4.86 us
  transfers between devices with their start and end apart: 15 -> 10, of which waited for: 4 -> 6; matrix products, arithmetic and copies ran while one was open for 0% -> 0% of each run, Pallas kernels for 8% -> 9%
where the time goes in v3:
time: 189 us; the launch traced here: 188 us
  Pallas kernels  52.3 us (28%)
  blocking collectives  51.5 us (27%)
  waiting for transfers between devices  40.5 us (21%)
  starting transfers between devices  38 us (20%)
  local copies, waits for them, and re-layouts  4.86 us (3%)
    all_to_all x3, blocking collectives, exchange(): return lax.all_to_all(parts, BOTH, split_axis=0, concat_axis=0, tiled=True)  51.5 us
    ppermute x8, waiting for transfers between devices, move(): return lax.ppermute(part, axis, pairs)  29.1 us
    ppermute x8, starting transfers between devices, move(): return lax.ppermute(part, axis, pairs)  22.2 us
    all_to_all x2, starting transfers between devices, exchange(): return lax.all_to_all(parts, BOTH, split_axis=0, concat_axis=0, tiled=True)  15.8 us
    pallas_call x2, Pallas kernels, pair(): pl.pallas_call(functools.partial(pair_kernel, number), out_shape=[WIDE, W...  15.8 us
    all_to_all x2, waiting for transfers between devices, exchange(): return lax.all_to_all(parts, BOTH, split_axis=0, concat_axis=0, tiled=True)  11.4 us
    pallas_call x1, Pallas kernels, deposit(): pl.pallas_call(deposit_kernel, out_shape=jax.ShapeDtypeStruct((2, CX, CX)...  10.9 us
    pallas_call x1, Pallas kernels, heated(): pl.pallas_call(heated_kernel, out_shape=[WIDE, WIDE, jax.ShapeDtypeStruct...  5.55 us
  transfers between devices with their start and end apart: 10, of which 6 were waited for; matrix products, arithmetic and copies ran while one was open for 0% of the time, Pallas kernels for 9%

profile of v3, /device:TPU:1, one launch (start us, length us, event | category | flops | bytes accessed | tf_op | source)
XLA Modules:
  0.0 188.4 jit_solution(4980373042318207793)
XLA Ops:
  0.0 1.1 copy-done.4
  1.1 0.8 copy-done.5
  2.0 0.7 copy-done.11
  2.6 0.0 copy-start.10
  2.7 4.4 %pack.1 = bf16[128,40,128]{2,1,0:T(8,128)(2,1)} custom-call(s32[128]{0:T(128)S(1)} %bitcast.12, bf16[16,128,128]{2,1,0:T(8,128)(2,1)S(1)} %copy-done.4, s32[128,128]{1,0:T(8,128)S(1)} %copy-done.5), custom_call_target="tpu_custom_call" | custom-call | tf_op jit(solution)/shard_map/pack/pallas_call | solution.py:104
  7.1 11.5 %all-to-all-start.7 = ((bf16[128,40,128]{2,1,0:T(8,128)(2,1)}), bf16[128,40,128]{2,1,0:T(8,128)(2,1)S(1)}, u32[]{:S(2)}, u32[]{:S(2)}) async-start(bf16[128,40,128]{2,1,0:T(8,128)(2,1)} %pack.1), calls=%async_computation.7 | async-start | bytes 2621440 | tf_op jit(solution)/shard_map/all_to_all | solution.py:769
  18.6 0.0 copy-done.3
  18.6 0.0 copy-done.6
  18.6 1.8 relayout.1
  20.4 1.0 copy-done
  21.4 3.5 %collective-permute-start = (f32[208,8,128]{2,1,0:T(8,128)}, f32[208,8,128]{2,1,0:T(8,128)S(1)}, u32[]{:S(2)}, u32[]{:S(2)}) collective-permute-start(f32[208,8,128]{2,1,0:T(8,128)} %get-tuple-element.71), channel_id=1, source_target_pairs={{0,1},{1,2},{2,3},{3,4},{4,5},{5,6},{6,7},{7,8},{8,9},{9,10},{10,1... | collective-permute-start | bytes 2555912 | tf_op jit(solution)/shard_map/ppermute | solution.py:775
  24.8 1.3 collective-permute-start.1
  26.2 0.0 copy-done.7
  26.2 0.0 copy-done.8
  26.2 0.0 copy-done.9
  26.2 1.7 pixels.1
  27.9 0.1 add_convert_fusion.inside
  28.0 24.5 %collective-permute-done.low = f32[208,8,128]{2,1,0:T(8,128)S(1)} collective-permute-done((f32[208,8,128]{2,1,0:T(8,128)}, f32[208,8,128]{2,1,0:T(8,128)S(1)}, u32[]{:S(2)}, u32[]{:S(2)}) %collective-permute-start) | collective-permute-done | bytes 852000 | tf_op jit(solution)/shard_map/ppermute | solution.py:775
  52.6 1.8 collective-permute-done.1.high
  54.3 1.2 copy-done.1
  55.6 0.0 all-to-all-done.7.incoming
  55.6 3.4 %collective-permute-start.2 = (f32[43,8,128]{2,1,0:T(8,128)S(1)}, f32[43,8,128]{2,1,0:T(8,128)S(1)}, u32[]{:S(2)}, u32[]{:S(2)}) collective-permute-start(f32[43,8,128]{2,1,0:T(8,128)S(1)} %get-tuple-element.78), channel_id=1, source_target_pairs={{0,16},{16,32},{32,48},{48,64},{64,80},{80,96},{96,112},{1,17},{17... | collective-permute-start | bytes 528392 | tf_op jit(solution)/shard_map/ppermute | solution.py:775
  58.9 1.9 %collective-permute-start.3 = (f32[43,8,128]{2,1,0:T(8,128)S(1)}, f32[43,8,128]{2,1,0:T(8,128)S(1)}, u32[]{:S(2)}, u32[]{:S(2)}) collective-permute-start(f32[43,8,128]{2,1,0:T(8,128)S(1)} %get-tuple-element.79), channel_id=1, source_target_pairs={{16,0},{32,16},{48,32},{64,48},{80,64},{96,80},{112,96},{17,1},{33... | collective-permute-start | bytes 528392 | tf_op jit(solution)/shard_map/ppermute | solution.py:775
  60.9 10.9 %deposit.1.own.heat_own = f32[2,128,128]{2,1,0:T(8,128)S(1)} custom-call(bf16[128,40,128]{2,1,0:T(8,128)(2,1)S(1)} %all-to-all-done.7.incoming), custom_call_target="tpu_custom_call" | custom-call | tf_op jit(solution)/shard_map/deposit/pallas_call | solution.py:264
  71.8 0.0 copy-start.2
  71.8 1.4 collective-permute-start.5
  73.2 4.3 %collective-permute-start.4 = (f32[2,128,128]{2,1,0:T(8,128)S(1)}, f32[2,128,128]{2,1,0:T(8,128)S(1)}, u32[]{:S(2)}, u32[]{:S(2)}) collective-permute-start(f32[2,128,128]{2,1,0:T(8,128)S(1)} %deposit.1.own.heat_own), channel_id=1, source_target_pairs={{0,1},{1,2},{2,3},{3,4},{4,5},{5,6},{6,7},{7,8},{8,9},{9,10},{10,1... | collective-permute-start | bytes 393224 | tf_op jit(solution)/shard_map/ppermute | solution.py:775
  77.5 0.4 collective-permute-done.5.high.heat_high
  77.9 1.7 collective-permute-done.4.low.heat_low
  79.7 4.6 %collective-permute-start.6 = (f32[3,2,8,128]{3,2,1,0:T(8,128)S(1)}, f32[3,2,8,128]{3,2,1,0:T(8,128)S(1)}, u32[]{:S(2)}, u32[]{:S(2)}) collective-permute-start(f32[3,2,8,128]{3,2,1,0:T(8,128)S(1)} %get-tuple-element.81), channel_id=1, source_target_pairs={{0,16},{16,32},{32,48},{48,64},{64,80},{80,96},{96,112},{1,17},{17... | collective-permute-start | bytes 73736 | tf_op jit(solution)/shard_map/ppermute | solution.py:775
  84.2 1.9 %collective-permute-start.7 = (f32[3,2,8,128]{3,2,1,0:T(8,128)S(1)}, f32[3,2,8,128]{3,2,1,0:T(8,128)S(1)}, u32[]{:S(2)}, u32[]{:S(2)}) collective-permute-start(f32[3,2,8,128]{3,2,1,0:T(8,128)S(1)} %get-tuple-element.82), channel_id=1, source_target_pairs={{16,0},{32,16},{48,32},{64,48},{80,64},{96,80},{112,96},{17,1},{33... | collective-permute-start | bytes 73736 | tf_op jit(solution)/shard_map/ppermute | solution.py:775
  86.2 0.0 collective-permute-done.2.left
  86.2 0.0 collective-permute-done.3.right
  86.2 2.5 %coefs.1.coef = f32[2,20,18,8,128]{4,3,2,1,0:T(8,128)S(1)} custom-call(f32[16,8,128]{2,1,0:T(8,128)S(1)} %get-tuple-element.70.turned_c, f32[208,8,128]{2,1,0:T(8,128)S(1)} %collective-permute-done.low, f32[208,8,128]{2,1,0:T(8,128)S(1)} %collective-permute-done.1.high, f32[43,8,128]{2,1,0:T(8,128)S(1)} %collective-permute-done.2.left, ...), custom_call_target="tpu_custom_call" | custom-call | tf_op jit(solution)/shard_map/coefs/pallas_call | solution.py:217
  88.7 0.0 collective-permute-done.6.heat_left
  88.7 0.7 collective-permute-done.7.heat_right
  89.4 0.0 copy-done.2
  89.4 5.6 %heated.1 = (f32[2,20,18,8,128]{4,3,2,1,0:T(8,128)S(1)}, f32[2,20,18,8,128]{4,3,2,1,0:T(8,128)S(1)}, f32[128,4,128]{2,1,0:T(4,128)S(1)}) custom-call(f32[4]{0:T(128)S(1)} %add_convert_fusion.inside, f32[2,8,16,8,128]{4,3,2,1,0:T(8,128)S(1)} %copy-done.2, f32[208,8,128]{2,1,0:T(8,128)S(1)} %collective-permute-done.low, ...), custom_call_target="tpu_custom_call" | custom-call | tf_op jit(solution)/shard_map/heated/pallas_call | solution.py:505
  95.0 21.0 %all_to_all.60.parts = f32[128,4,128]{2,1,0:T(4,128)S(1)} all-to-all(f32[128,4,128]{2,1,0:T(4,128)S(1)} %get-tuple-element.85), channel_id=1, replica_groups=mesh['gx'=8,'gy'=16] {'gx','gy'}, dimensions={0} | all-to-all | bytes 524288 | tf_op jit(solution)/shard_map/all_to_all | solution.py:769
  116.0 8.8 %pair_0.1 = (f32[2,20,18,8,128]{4,3,2,1,0:T(8,128)S(1)}, f32[2,20,18,8,128]{4,3,2,1,0:T(8,128)S(1)}, f32[128,4,128]{2,1,0:T(4,128)S(1)}, f32[8,128]{1,0:T(8,128)S(1)}) custom-call(f32[4]{0:T(128)S(1)} %add_convert_fusion.inside, f32[2,20,18,8,128]{4,3,2,1,0:T(8,128)S(1)} %get-tuple-element.83.field, f32[2,20,18,8,128]{4,3,2,1,0:T(8,128)S(1)} %get-tuple-element.84.changes, ...), custom_call_target="tpu_custom_call" | custom-call | tf_op jit(solution)/shard_map/pair_0/pallas_call | solution.py:562
  124.8 15.2 %all_to_all.61.parts = f32[128,4,128]{2,1,0:T(4,128)S(1)} all-to-all(f32[128,4,128]{2,1,0:T(4,128)S(1)} %get-tuple-element.88), channel_id=1, replica_groups=mesh['gx'=8,'gy'=16] {'gx','gy'}, dimensions={0} | all-to-all | bytes 524288 | tf_op jit(solution)/shard_map/all_to_all | solution.py:769
  140.1 0.0 copy-done.14
  140.1 6.9 %pair_2.1 = (f32[2,20,18,8,128]{4,3,2,1,0:T(8,128)S(1)}, f32[2,20,18,8,128]{4,3,2,1,0:T(8,128)S(1)}, f32[128,4,128]{2,1,0:T(4,128)S(1)}, f32[8,128]{1,0:T(8,128)S(1)}) custom-call(f32[4]{0:T(128)S(1)} %add_convert_fusion.inside, f32[2,20,18,8,128]{4,3,2,1,0:T(8,128)S(1)} %get-tuple-element.86.field, f32[2,20,18,8,128]{4,3,2,1,0:T(8,128)S(1)} %get-tuple-element.87.changes, ...), custom_call_target="tpu_custom_call" | custom-call | tf_op jit(solution)/shard_map/pair_2/pallas_call | solution.py:562
  147.0 15.2 %all_to_all.62.parts = f32[128,4,128]{2,1,0:T(4,128)S(1)} all-to-all(f32[128,4,128]{2,1,0:T(4,128)S(1)} %get-tuple-element.92), channel_id=1, replica_groups=mesh['gx'=8,'gy'=16] {'gx','gy'}, dimensions={0} | all-to-all | bytes 524288 | tf_op jit(solution)/shard_map/all_to_all | solution.py:769
  162.3 4.2 %last_pair.1 = (f32[2,8,16,8,128]{4,3,2,1,0:T(8,128)S(1)}, f32[128,4,128]{2,1,0:T(4,128)}, f32[8,128]{1,0:T(8,128)S(1)}) custom-call(f32[4]{0:T(128)S(1)} %add_convert_fusion.inside, f32[2,20,18,8,128]{4,3,2,1,0:T(8,128)S(1)} %get-tuple-element.90.field, f32[2,20,18,8,128]{4,3,2,1,0:T(8,128)S(1)} %get-tuple-element.91.changes, ...), custom_call_target="tpu_custom_call" | custom-call | tf_op jit(solution)/shard_map/last_pair/pallas_call | solution.py:613
  166.5 4.3 %all-to-all-start.11 = ((f32[128,4,128]{2,1,0:T(4,128)}), f32[128,4,128]{2,1,0:T(4,128)S(1)}, u32[]{:S(2)}, u32[]{:S(2)}) async-start(f32[128,4,128]{2,1,0:T(4,128)} %get-tuple-element.96), calls=%async_computation.11 | async-start | bytes 524288 | tf_op jit(solution)/shard_map/all_to_all | solution.py:769
  170.8 11.4 %all-to-all-done.11.sums = f32[128,4,128]{2,1,0:T(4,128)S(1)} async-done(((f32[128,4,128]{2,1,0:T(4,128)}), f32[128,4,128]{2,1,0:T(4,128)S(1)}, u32[]{:S(2)}, u32[]{:S(2)}) %all-to-all-start.11) | async-done | bytes 262176 | tf_op jit(solution)/shard_map/all_to_all | solution.py:769
  182.2 5.4 %update.3 = (f32[16,16,8,128]{3,2,1,0:T(8,128)}, s32[1]{0:T(128)}) custom-call(f32[128,4,128]{2,1,0:T(4,128)S(1)} %all-to-all-done.11.sums, f32[2,8,16,8,128]{4,3,2,1,0:T(8,128)S(1)} %get-tuple-element.97.field, f32[8,128]{1,0:T(8,128)S(1)} %get-tuple-element.98.status), custom_call_target="tpu_custom_call" | custom-call | tf_op jit(solution)/shard_map/update/pallas_call | solution.py:755
  (18 shorter events, 0.1 us)
Async XLA Ops:
  0.0 18.6 %copy-start.3 = (f32[16,16,8,128]{3,2,1,0:T(8,128)S(1)}, f32[16,16,8,128]{3,2,1,0:T(8,128)}, u32[]{:S(2)}) copy-start(f32[16,16,8,128]{3,2,1,0:T(8,128)} %state.1) | copy-start | bytes 3145732
  0.0 1.1 copy-start.4
  1.1 0.8 copy-start.5
  2.0 0.7 copy-start.11
  2.6 16.0 %copy-start.6 = (f32[16,8,128]{2,1,0:T(8,128)S(1)}, f32[16,8,128]{2,1,0:T(8,128)}, u32[]{:S(2)}) copy-start(f32[16,8,128]{2,1,0:T(8,128)} %conduct.1) | copy-start | bytes 196612
  2.6 23.5 %copy-start.7 = (f32[16,512]{1,0:T(8,128)S(1)}, f32[16,512]{1,0:T(8,128)}, u32[]{:S(2)}) copy-start(f32[16,512]{1,0:T(8,128)} %noise.1) | copy-start | bytes 98308
  2.6 23.5 %copy-start.8 = (s32[512]{0:T(512)S(1)}, s32[512]{0:T(512)}, u32[]{:S(2)}) copy-start(s32[512]{0:T(512)} %param.16) | copy-start | bytes 6148
  2.6 23.5 %copy-start.9 = (f32[512]{0:T(512)S(1)}, f32[512]{0:T(512)}, u32[]{:S(2)}) copy-start(f32[512]{0:T(512)} %param.17) | copy-start | bytes 6148
  2.6 23.5 %copy-start.10 = (f32[512]{0:T(512)S(1)}, f32[512]{0:T(512)}, u32[]{:S(2)}) copy-start(f32[512]{0:T(512)} %param.18) | copy-start | bytes 6148
  7.1 48.5 %all-to-all-start.7 = ((bf16[128,40,128]{2,1,0:T(8,128)(2,1)}), bf16[128,40,128]{2,1,0:T(8,128)(2,1)S(1)}, u32[]{:S(2)}, u32[]{:S(2)}) async-start(bf16[128,40,128]{2,1,0:T(8,128)(2,1)} %pack.1), calls=%async_computation.7 | async-start | bytes 2621440 | tf_op jit(solution)/shard_map/all_to_all | solution.py:769
  20.4 1.0 copy-start
  21.4 31.2 %collective-permute-start = (f32[208,8,128]{2,1,0:T(8,128)}, f32[208,8,128]{2,1,0:T(8,128)S(1)}, u32[]{:S(2)}, u32[]{:S(2)}) collective-permute-start(f32[208,8,128]{2,1,0:T(8,128)} %get-tuple-element.71), channel_id=1, source_target_pairs={{0,1},{1,2},{2,3},{3,4},{4,5},{5,6},{6,7},{7,8},{8,9},{9,10},{10,1... | collective-permute-start | bytes 2555912 | tf_op jit(solution)/shard_map/ppermute | solution.py:775
  24.8 29.5 %collective-permute-start.1 = (f32[208,8,128]{2,1,0:T(8,128)}, f32[208,8,128]{2,1,0:T(8,128)S(1)}, u32[]{:S(2)}, u32[]{:S(2)}) collective-permute-start(f32[208,8,128]{2,1,0:T(8,128)} %get-tuple-element.72), channel_id=1, source_target_pairs={{1,0},{2,1},{3,2},{4,3},{5,4},{6,5},{7,6},{8,7},{9,8},{10,9},{11,1... | collective-permute-start | bytes 2555912 | tf_op jit(solution)/shard_map/ppermute | solution.py:775
  54.3 1.2 copy-start.1
  55.6 30.6 %collective-permute-start.2 = (f32[43,8,128]{2,1,0:T(8,128)S(1)}, f32[43,8,128]{2,1,0:T(8,128)S(1)}, u32[]{:S(2)}, u32[]{:S(2)}) collective-permute-start(f32[43,8,128]{2,1,0:T(8,128)S(1)} %get-tuple-element.78), channel_id=1, source_target_pairs={{0,16},{16,32},{32,48},{48,64},{64,80},{80,96},{96,112},{1,17},{17... | collective-permute-start | bytes 528392 | tf_op jit(solution)/shard_map/ppermute | solution.py:775
  58.9 27.2 %collective-permute-start.3 = (f32[43,8,128]{2,1,0:T(8,128)S(1)}, f32[43,8,128]{2,1,0:T(8,128)S(1)}, u32[]{:S(2)}, u32[]{:S(2)}) collective-permute-start(f32[43,8,128]{2,1,0:T(8,128)S(1)} %get-tuple-element.79), channel_id=1, source_target_pairs={{16,0},{32,16},{48,32},{64,48},{80,64},{96,80},{112,96},{17,1},{33... | collective-permute-start | bytes 528392 | tf_op jit(solution)/shard_map/ppermute | solution.py:775
  71.8 17.6 %copy-start.2 = (f32[2,8,16,8,128]{4,3,2,1,0:T(8,128)S(1)}, f32[2,8,16,8,128]{4,3,2,1,0:T(8,128)}, u32[]{:S(2)}) copy-start(f32[2,8,16,8,128]{4,3,2,1,0:T(8,128)} %copy-done) | copy-start | bytes 3145732
  71.8 6.2 %collective-permute-start.5 = (f32[2,128,128]{2,1,0:T(8,128)S(1)}, f32[2,128,128]{2,1,0:T(8,128)S(1)}, u32[]{:S(2)}, u32[]{:S(2)}) collective-permute-start(f32[2,128,128]{2,1,0:T(8,128)S(1)} %deposit.1.own.heat_own), channel_id=1, source_target_pairs={{1,0},{2,1},{3,2},{4,3},{5,4},{6,5},{7,6},{8,7},{9,8},{10,9},{11,1... | collective-permute-start | bytes 393224 | tf_op jit(solution)/shard_map/ppermute | solution.py:775
  73.2 6.5 %collective-permute-start.4 = (f32[2,128,128]{2,1,0:T(8,128)S(1)}, f32[2,128,128]{2,1,0:T(8,128)S(1)}, u32[]{:S(2)}, u32[]{:S(2)}) collective-permute-start(f32[2,128,128]{2,1,0:T(8,128)S(1)} %deposit.1.own.heat_own), channel_id=1, source_target_pairs={{0,1},{1,2},{2,3},{3,4},{4,5},{5,6},{6,7},{7,8},{8,9},{9,10},{10,1... | collective-permute-start | bytes 393224 | tf_op jit(solution)/shard_map/ppermute | solution.py:775
  79.7 9.0 %collective-permute-start.6 = (f32[3,2,8,128]{3,2,1,0:T(8,128)S(1)}, f32[3,2,8,128]{3,2,1,0:T(8,128)S(1)}, u32[]{:S(2)}, u32[]{:S(2)}) collective-permute-start(f32[3,2,8,128]{3,2,1,0:T(8,128)S(1)} %get-tuple-element.81), channel_id=1, source_target_pairs={{0,16},{16,32},{32,48},{48,64},{64,80},{80,96},{96,112},{1,17},{17... | collective-permute-start | bytes 73736 | tf_op jit(solution)/shard_map/ppermute | solution.py:775
  84.2 5.1 %collective-permute-start.7 = (f32[3,2,8,128]{3,2,1,0:T(8,128)S(1)}, f32[3,2,8,128]{3,2,1,0:T(8,128)S(1)}, u32[]{:S(2)}, u32[]{:S(2)}) collective-permute-start(f32[3,2,8,128]{3,2,1,0:T(8,128)S(1)} %get-tuple-element.82), channel_id=1, source_target_pairs={{16,0},{32,16},{48,32},{64,48},{80,64},{96,80},{112,96},{17,1},{33... | collective-permute-start | bytes 73736 | tf_op jit(solution)/shard_map/ppermute | solution.py:775
  88.7 73.6 %copy-start.12 = (f32[2,20,18,8,128]{4,3,2,1,0:T(8,128)}, f32[2,20,18,8,128]{4,3,2,1,0:T(8,128)S(1)}, u32[]{:S(2)}) copy-start(f32[2,20,18,8,128]{4,3,2,1,0:T(8,128)S(1)} %coefs.1.coef) | copy-start | bytes 8847364
  95.0 45.1 %copy-start.14 = (f32[2,20,18,8,128]{4,3,2,1,0:T(8,128)}, f32[2,20,18,8,128]{4,3,2,1,0:T(8,128)S(1)}, u32[]{:S(2)}) copy-start(f32[2,20,18,8,128]{4,3,2,1,0:T(8,128)S(1)} %get-tuple-element.83.field) | copy-start | bytes 8847364
  166.5 15.7 %all-to-all-start.11 = ((f32[128,4,128]{2,1,0:T(4,128)}), f32[128,4,128]{2,1,0:T(4,128)S(1)}, u32[]{:S(2)}, u32[]{:S(2)}) async-start(f32[128,4,128]{2,1,0:T(4,128)} %get-tuple-element.96), calls=%async_computation.11 | async-start | bytes 524288 | tf_op jit(solution)/shard_map/all_to_all | solution.py:769

commit v4 on v3

--- a/solution.py
+++ b/solution.py
@@ -38,7 +38,15 @@
     return lax.broadcasted_iota(jnp.int32, (CY, CX), 0)
 
 
-def pack_kernel(owner, heat, voxel, out, wide, high, low, inverse):
+def pack_kernel(owner_far, heat_far, voxel_far, out, owner, heat, voxel, wide, high, low, inverse, sems):
+    copies = [
+        pltpu.make_async_copy(far, near, sems.at[i])
+        for i, (far, near) in enumerate(
+            ((owner_far, owner), (heat_far, heat), (voxel_far, voxel))
+        )
+    ]
+    for copy in copies:
+        copy.start()
     blocks = owner.shape[0]
     devices = out.shape[0]
 
@@ -47,6 +55,7 @@
         return carry
 
     lax.fori_loop(0, devices * CAP, clear, 0, unroll=16)
+    copies[0].wait()
 
     def place(b, carry):
         base = owner[b] * CAP
@@ -55,6 +64,8 @@
         return carry
 
     lax.fori_loop(0, blocks, place, 0, unroll=8)
+    copies[1].wait()
+    copies[2].wait()
 
     def widen(m, carry):
         wide[m, 0:blocks, :] = heat[m].astype(F32)
@@ -104,13 +115,17 @@
     return pl.pallas_call(
         pack_kernel,
         out_shape=jax.ShapeDtypeStruct((devices, ROWS, CX), BF16),
-        in_specs=[pl.BlockSpec(memory_space=pltpu.SMEM), vspec(), vspec()],
+        in_specs=[pl.BlockSpec(memory_space=pl.ANY)] * 3,
         out_specs=vspec(),
         scratch_shapes=[
+            pltpu.SMEM((blocks,), jnp.int32),
+            VM((M, blocks, CX), BF16),
+            VM((blocks, CX), jnp.int32),
             VM((M, blocks + 8, CX), F32),
             VM((blocks + 8, CX), F32),
             VM((blocks + 8, CX), F32),
             pltpu.SMEM((devices * CAP,), jnp.int32),
+            pltpu.SemaphoreType.DMA((3,)),
         ],
         compiler_params=params(),
         name="pack",
@@ -128,11 +143,7 @@
 SIDE = 2 * YS
 
 
-def relayout_kernel(state, conduct, own, turned_c, to_high, to_low):
-    turned = (0.5 * conduct[...].reshape(CX, CX)).T.reshape(XT - 2, 8, CX)
-    turned_c[...] = turned
-    to_high[EDGE:] = turned
-    to_low[EDGE:] = turned
+def relayout_kernel(state, own, to_high, to_low):
     for zi in range(2):
         for y in range(CY):
             parts = [
@@ -148,19 +159,19 @@
                 to_low[at : at + XT - 2] = turned
 
 
-def relayout(state, conduct):
-    edge = jax.ShapeDtypeStruct((EDGE + XT - 2, 8, CX), F32)
+def relayout(state):
+    edge = jax.ShapeDtypeStruct((EDGE, 8, CX), F32)
     return pl.pallas_call(
         relayout_kernel,
-        out_shape=[OWN, jax.ShapeDtypeStruct((XT - 2, 8, CX), F32), edge, edge],
-        in_specs=[vspec()] * 2,
-        out_specs=[vspec()] * 4,
+        out_shape=[OWN, edge, edge],
+        in_specs=[vspec()],
+        out_specs=[vspec()] * 3,
         compiler_params=params(),
         name="relayout",
-    )(state, conduct)
-
-
-def side_kernel(own, turned_c, low, high, to_left, to_right):
+    )(state)
+
+
+def side_kernel(own, low, high, heat_low, heat_own, heat_high, to_left, to_right):
     for out, t in ((to_left, 0), (to_right, XT - 3)):
         for zi in range(2):
             for y in range(YS):
@@ -171,30 +182,47 @@
                 else:
                     part = high[(zi * HALO + y - HALO - CY) * (XT - 2) + t]
                 out[zi * YS + y] = part
-        out[SIDE] = low[EDGE + t]
-        out[SIDE + 1] = turned_c[t]
-        out[SIDE + 2] = high[EDGE + t]
-
-
-def sides(own, turned_c, low, high):
-    shape = jax.ShapeDtypeStruct((SIDE + 3, 8, CX), F32)
+        for g, heat in enumerate((heat_low, heat_own, heat_high)):
+            for zi in range(2):
+                out[SIDE + 2 * g + zi] = heat[zi, 8 * t : 8 * t + 8, :]
+
+
+def sides(own, low, high, heat_low, heat_own, heat_high):
+    shape = jax.ShapeDtypeStruct((SIDE + 6, 8, CX), F32)
     return pl.pallas_call(
         side_kernel,
         out_shape=[shape, shape],
-        in_specs=[vspec()] * 4,
+        in_specs=[vspec()] * 6,
         out_specs=[vspec()] * 2,
         compiler_params=params(),
         name="sides",
-    )(own, turned_c, low, high)
-
-
-def coef_kernel(turned_c, low, high, left, right, out):
+    )(own, low, high, heat_low, heat_own, heat_high)
+
+
+def strip_kernel(own, left, right, out):
+    def turn(tile):
+        return (0.5 * tile[...].reshape(CX, CX)).T
+
+    out[0] = turn(left)[CX - 8 :, :]
+    out[1 : XT - 1] = turn(own).reshape(XT - 2, 8, CX)
+    out[XT - 1] = turn(right)[0:8, :]
+
+
+def strip(own, left, right):
+    return pl.pallas_call(
+        strip_kernel,
+        out_shape=jax.ShapeDtypeStruct((XT, 8, CX), F32),
+        in_specs=[vspec()] * 3,
+        out_specs=vspec(),
+        compiler_params=params(),
+        name="strip",
+    )(own, left, right)
+
+
+def coef_kernel(own, low, high, out):
     source = lax.broadcasted_iota(jnp.int32, (CX, CX), 0)
     target = lax.broadcasted_iota(jnp.int32, (CX, CX), 1)
-    strips = []
-    for g in range(3):
-        mid = (low[EDGE:], turned_c[...], high[EDGE:])[g].reshape(CX, CX)
-        strips.append(jnp.concatenate([left[SIDE + g], mid, right[SIDE + g]], axis=0))
+    strips = [part[...].reshape(XT * 8, CX) for part in (low, own, high)]
 
     def put(g, y0, yy):
         for zi in range(2):
@@ -213,15 +241,15 @@
         put(2, y, y + HALO + CY)
 
 
-def coefs(turned_c, low, high, left, right):
+def coefs(own, low, high):
     return pl.pallas_call(
         coef_kernel,
         out_shape=WIDE,
-        in_specs=[vspec()] * 5,
+        in_specs=[vspec()] * 3,
         out_specs=vspec(),
         compiler_params=params(),
         name="coefs",
-    )(turned_c, low, high, left, right)
+    )(own, low, high)
 
 
 def deposit_kernel(incoming, out, total):
@@ -270,24 +298,6 @@
         compiler_params=params(),
         name="deposit",
     )(incoming)
-
-
-def heat_side_kernel(low, own, high, to_left, to_right):
-    for g, part in enumerate((low, own, high)):
-        to_left[g] = part[:, 0:8, :]
-        to_right[g] = part[:, CX - 8 :, :]
-
-
-def heat_sides(low, own, high):
-    shape = jax.ShapeDtypeStruct((3, 2, 8, CX), F32)
-    return pl.pallas_call(
-        heat_side_kernel,
-        out_shape=[shape, shape],
-        in_specs=[vspec()] * 3,
-        out_specs=[vspec()] * 2,
-        compiler_params=params(),
-        name="heat_sides",
-    )(low, own, high)
 
 
 def columns_peak(value):
@@ -454,7 +464,7 @@
 
 def heated_kernel(
     inside, own, low, high, left, right,
-    heat_low, heat_own, heat_high, heat_left, heat_right,
+    heat_low, heat_own, heat_high,
     coef, out, changes, parts, above, below_h,
 ):
     top = lanes() < M
@@ -465,9 +475,9 @@
         for zi in range(2):
             for t in range(XT):
                 if t == 0:
-                    prior, add = left[zi * YS + yy], heat_left[g, zi]
+                    prior, add = left[zi * YS + yy], left[SIDE + 2 * g + zi]
                 elif t == XT - 1:
-                    prior, add = right[zi * YS + yy], heat_right[g, zi]
+                    prior, add = right[zi * YS + yy], right[SIDE + 2 * g + zi]
                 else:
                     prior, add = tile_of(zi, t - 1), heat[zi, 8 * t - 8 : 8 * t, :]
                 if shift:
@@ -795,32 +805,26 @@
     inside = jnp.stack(
         [gx > 0, gx < lax.axis_size("gx") - 1, gy > 0, gy < lax.axis_size("gy") - 1]
     ).astype(F32)
-    own, turned_c, to_high, to_low = relayout(state_prior, conductivity)
+    left_c, right_c = move(conductivity, "gx", True), move(conductivity, "gx", False)
+    strips = strip(conductivity, left_c, right_c)
+    coef = coefs(strips, move(strips, "gy", True), move(strips, "gy", False))
+    own, to_high, to_low = relayout(state_prior)
     low, high = move(to_high, "gy", True), move(to_low, "gy", False)
-    to_left, to_right = sides(own, turned_c, low, high)
     seen = pixel_sums(
         pixel_cell.reshape(1, pixels),
         observed.reshape(1, pixels),
         pixel_variance.reshape(1, pixels),
         pixel_noise,
     )
-    incoming, to_left, to_right, inside, *seen = lax.optimization_barrier(
-        (incoming, to_left, to_right, inside, *seen)
+    incoming, coef, own, inside, *seen = lax.optimization_barrier(
+        (incoming, coef, own, inside, *seen)
     )
-    left, right = move(to_right, "gx", True), move(to_left, "gx", False)
-
     heat = deposit(incoming)
     heat_low, heat_high = move(heat, "gy", True), move(heat, "gy", False)
-    to_left, to_right = heat_sides(heat_low, heat, heat_high)
-    heat_left, heat_right = move(to_right, "gx", True), move(to_left, "gx", False)
-    coef = coefs(turned_c, low, high, left, right)
+    to_left, to_right = sides(own, low, high, heat_low, heat, heat_high)
+    left, right = move(to_right, "gx", True), move(to_left, "gx", False)
     start, changes, parts = heated(
-        inside,
-        (own, low, high),
-        (left, right),
-        (heat_low, heat, heat_high, heat_left, heat_right),
-        coef,
-        devices,
+        inside, (own, low, high), (left, right), (heat_low, heat, heat_high), coef, devices
     )
     field, status = start, jnp.zeros((8, CX), F32)
     for number in range(0, SUBSTEPS - 2, 2):

time: 189 us -> 190 us (level)
  waiting for transfers between devices: 40.5 us -> 34.9 us
  starting transfers between devices: 38 us -> 43.5 us
  Pallas kernels: 52.3 us -> 55.5 us
  local copies, waits for them, and re-layouts: 4.86 us -> 2.66 us
    ppermute x8 -> x10, waiting for transfers between devices: 29.1 us -> 23.5 us  [move(): return lax.ppermute(part, axis, pairs)]
    ppermute x8 -> x10, starting transfers between devices: 22.2 us -> 27.7 us  [move(): return lax.ppermute(part, axis, pairs)]
    unnamed x28 -> x22, local copies, waits for them, and re-layouts: 4.86 us -> 2.65 us
  transfers between devices with their start and end apart: 10 -> 12, of which waited for: 6 -> 8; matrix products, arithmetic and copies ran while one was open for 0% -> 0% of each run, Pallas kernels for 9% -> 10%
where the time goes in v4:
time: 190 us; the launch traced here: 189 us
  Pallas kernels  55.5 us (29%)
  blocking collectives  51.3 us (27%)
  starting transfers between devices  43.5 us (23%)
  waiting for transfers between devices  34.9 us (18%)
  local copies, waits for them, and re-layouts  2.66 us (1%)
    all_to_all x3, blocking collectives, exchange(): return lax.all_to_all(parts, BOTH, split_axis=0, concat_axis=0, tiled=True)  51.3 us
    ppermute x10, starting transfers between devices, move(): return lax.ppermute(part, axis, pairs)  27.7 us
    ppermute x10, waiting for transfers between devices, move(): return lax.ppermute(part, axis, pairs)  23.5 us
    all_to_all x2, starting transfers between devices, exchange(): return lax.all_to_all(parts, BOTH, split_axis=0, concat_axis=0, tiled=True)  15.8 us
    pallas_call x2, Pallas kernels, pair(): pl.pallas_call(functools.partial(pair_kernel, number), out_shape=[WIDE, W...  15.8 us
    all_to_all x2, waiting for transfers between devices, exchange(): return lax.all_to_all(parts, BOTH, split_axis=0, concat_axis=0, tiled=True)  11.4 us
    pallas_call x1, Pallas kernels, deposit(): pl.pallas_call(deposit_kernel, out_shape=jax.ShapeDtypeStruct((2, CX, CX)...  10.9 us
    pallas_call x1, Pallas kernels, heated(): pl.pallas_call(heated_kernel, out_shape=[WIDE, WIDE, jax.ShapeDtypeStruct...  6.14 us
  transfers between devices with their start and end apart: 12, of which 8 were waited for; matrix products, arithmetic and copies ran while one was open for 0% of the time, Pallas kernels for 10%

profile of v4, /device:TPU:1, one launch (start us, length us, event | category | flops | bytes accessed | tf_op | source)
XLA Modules:
  0.0 189.0 jit_solution(6417489099539337047)
XLA Ops:
  0.0 1.1 copy-done.1
  1.1 0.8 copy-done.2
  2.0 0.7 copy-done.8
  2.7 4.2 %pack.1 = bf16[128,40,128]{2,1,0:T(8,128)(2,1)} custom-call(s32[128]{0:T(128)S(1)} %bitcast.12, bf16[16,128,128]{2,1,0:T(8,128)(2,1)S(1)} %copy-done.1, s32[128,128]{1,0:T(8,128)S(1)} %copy-done.2), custom_call_target="tpu_custom_call" | custom-call | tf_op jit(solution)/shard_map/pack/pallas_call | solution.py:115
  6.9 11.5 %all-to-all-start.7 = ((bf16[128,40,128]{2,1,0:T(8,128)(2,1)}), bf16[128,40,128]{2,1,0:T(8,128)(2,1)S(1)}, u32[]{:S(2)}, u32[]{:S(2)}) async-start(bf16[128,40,128]{2,1,0:T(8,128)(2,1)} %pack.1), calls=%async_computation.7 | async-start | bytes 2621440 | tf_op jit(solution)/shard_map/all_to_all | solution.py:779
  18.4 1.7 relayout.1
  20.1 3.4 %collective-permute-start.4 = (f32[192,8,128]{2,1,0:T(8,128)}, f32[192,8,128]{2,1,0:T(8,128)S(1)}, u32[]{:S(2)}, u32[]{:S(2)}) collective-permute-start(f32[192,8,128]{2,1,0:T(8,128)} %get-tuple-element.71), channel_id=1, source_target_pairs={{0,1},{1,2},{2,3},{3,4},{4,5},{5,6},{6,7},{7,8},{8,9},{9,10},{10,1... | collective-permute-start | bytes 2359304 | tf_op jit(solution)/shard_map/ppermute | solution.py:785
  23.6 1.3 collective-permute-start.5
  24.9 3.6 %collective-permute-start = (f32[16,8,128]{2,1,0:T(8,128)S(1)}, f32[16,8,128]{2,1,0:T(8,128)S(1)}, u32[]{:S(2)}, u32[]{:S(2)}) collective-permute-start(f32[16,8,128]{2,1,0:T(8,128)S(1)} %copy-done.3), channel_id=1, source_target_pairs={{0,16},{16,32},{32,48},{48,64},{64,80},{80,96},{96,112},{1,17},{17... | collective-permute-start | bytes 196616 | tf_op jit(solution)/shard_map/ppermute | solution.py:785
  28.5 1.9 %collective-permute-start.1 = (f32[16,8,128]{2,1,0:T(8,128)S(1)}, f32[16,8,128]{2,1,0:T(8,128)S(1)}, u32[]{:S(2)}, u32[]{:S(2)}) collective-permute-start(f32[16,8,128]{2,1,0:T(8,128)S(1)} %copy-done.3), channel_id=1, source_target_pairs={{16,0},{32,16},{48,32},{64,48},{80,64},{96,80},{112,96},{17,1},{33... | collective-permute-start | bytes 196616 | tf_op jit(solution)/shard_map/ppermute | solution.py:785
  30.5 0.0 copy-done.4
  30.5 0.0 copy-done.5
  30.5 0.0 copy-done.6
  30.5 0.0 copy-done.7
  30.5 1.7 pixels.1
  32.3 0.3 collective-permute-done.left
  32.6 2.7 %collective-permute-done.1.right = f32[16,8,128]{2,1,0:T(8,128)S(1)} collective-permute-done((f32[16,8,128]{2,1,0:T(8,128)S(1)}, f32[16,8,128]{2,1,0:T(8,128)S(1)}, u32[]{:S(2)}, u32[]{:S(2)}) %collective-permute-start.1) | collective-permute-done | bytes 65568 | tf_op jit(solution)/shard_map/ppermute | solution.py:785
  35.2 0.1 strip.1.own
  35.3 1.3 collective-permute-start.3
  36.6 4.2 %collective-permute-start.2 = (f32[18,8,128]{2,1,0:T(8,128)S(1)}, f32[18,8,128]{2,1,0:T(8,128)S(1)}, u32[]{:S(2)}, u32[]{:S(2)}) collective-permute-start(f32[18,8,128]{2,1,0:T(8,128)S(1)} %strip.1.own), channel_id=1, source_target_pairs={{0,1},{1,2},{2,3},{3,4},{4,5},{5,6},{6,7},{7,8},{8,9},{9,10},{10,1... | collective-permute-start | bytes 221192 | tf_op jit(solution)/shard_map/ppermute | solution.py:785
  40.8 0.1 add_convert_fusion.inside
  40.9 13.5 %collective-permute-done.3.high = f32[18,8,128]{2,1,0:T(8,128)S(1)} collective-permute-done((f32[18,8,128]{2,1,0:T(8,128)S(1)}, f32[18,8,128]{2,1,0:T(8,128)S(1)}, u32[]{:S(2)}, u32[]{:S(2)}) %collective-permute-start.3) | collective-permute-done | bytes 73760 | tf_op jit(solution)/shard_map/ppermute | solution.py:785
  54.4 0.0 collective-permute-done.2.low
  54.4 4.1 %coefs.1.coef = f32[2,20,18,8,128]{4,3,2,1,0:T(8,128)} custom-call(f32[18,8,128]{2,1,0:T(8,128)S(1)} %strip.1.own, f32[18,8,128]{2,1,0:T(8,128)S(1)} %collective-permute-done.2.low, f32[18,8,128]{2,1,0:T(8,128)S(1)} %collective-permute-done.3.high), custom_call_target="tpu_custom_call" | custom-call | tf_op jit(solution)/shard_map/coefs/pallas_call | solution.py:245
  58.5 0.0 all-to-all-done.7.incoming
  58.5 10.9 %deposit.1.heat_own = f32[2,128,128]{2,1,0:T(8,128)S(1)} custom-call(bf16[128,40,128]{2,1,0:T(8,128)(2,1)S(1)} %all-to-all-done.7.incoming), custom_call_target="tpu_custom_call" | custom-call | tf_op jit(solution)/shard_map/deposit/pallas_call | solution.py:292
  69.4 1.3 collective-permute-start.7
  70.7 4.1 %collective-permute-start.6 = (f32[2,128,128]{2,1,0:T(8,128)S(1)}, f32[2,128,128]{2,1,0:T(8,128)S(1)}, u32[]{:S(2)}, u32[]{:S(2)}) collective-permute-start(f32[2,128,128]{2,1,0:T(8,128)S(1)} %deposit.1.heat_own), channel_id=1, source_target_pairs={{0,1},{1,2},{2,3},{3,4},{4,5},{5,6},{6,7},{7,8},{8,9},{9,10},{10,1... | collective-permute-start | bytes 393224 | tf_op jit(solution)/shard_map/ppermute | solution.py:785
  74.8 0.0 collective-permute-done.4.low
  74.8 0.0 collective-permute-done.5.high
  74.8 1.3 collective-permute-done.7.heat_high
  76.1 0.9 collective-permute-done.6.heat_low
  77.0 1.2 sides.1
  78.2 4.5 %collective-permute-start.8 = (f32[46,8,128]{2,1,0:T(8,128)S(1)}, f32[46,8,128]{2,1,0:T(8,128)S(1)}, u32[]{:S(2)}, u32[]{:S(2)}) collective-permute-start(f32[46,8,128]{2,1,0:T(8,128)S(1)} %get-tuple-element.74), channel_id=1, source_target_pairs={{0,16},{16,32},{32,48},{48,64},{64,80},{80,96},{96,112},{1,17},{17... | collective-permute-start | bytes 565256 | tf_op jit(solution)/shard_map/ppermute | solution.py:785
  82.7 1.9 %collective-permute-start.9 = (f32[46,8,128]{2,1,0:T(8,128)S(1)}, f32[46,8,128]{2,1,0:T(8,128)S(1)}, u32[]{:S(2)}, u32[]{:S(2)}) collective-permute-start(f32[46,8,128]{2,1,0:T(8,128)S(1)} %get-tuple-element.75), channel_id=1, source_target_pairs={{16,0},{32,16},{48,32},{64,48},{80,64},{96,80},{112,96},{17,1},{33... | collective-permute-start | bytes 565256 | tf_op jit(solution)/shard_map/ppermute | solution.py:785
  84.6 0.6 collective-permute-done.8.left
  85.2 4.4 %collective-permute-done.9.right = f32[46,8,128]{2,1,0:T(8,128)S(1)} collective-permute-done((f32[46,8,128]{2,1,0:T(8,128)S(1)}, f32[46,8,128]{2,1,0:T(8,128)S(1)}, u32[]{:S(2)}, u32[]{:S(2)}) %collective-permute-start.9) | collective-permute-done | bytes 188448 | tf_op jit(solution)/shard_map/ppermute | solution.py:785
  89.6 6.1 %heated.1 = (f32[2,20,18,8,128]{4,3,2,1,0:T(8,128)S(1)}, f32[2,20,18,8,128]{4,3,2,1,0:T(8,128)S(1)}, f32[128,4,128]{2,1,0:T(4,128)S(1)}) custom-call(f32[4]{0:T(128)S(1)} %add_convert_fusion.inside, f32[2,8,16,8,128]{4,3,2,1,0:T(8,128)S(1)} %get-tuple-element.70.own, f32[192,8,128]{2,1,0:T(8,128)S(1)} %collective-permute-done.4.low, ...), custom_call_target="tpu_custom_call" | custom-call | tf_op jit(solution)/shard_map/heated/pallas_call | solution.py:515
  95.7 0.0 copy-start.11
  95.7 20.8 %all_to_all.60.parts = f32[128,4,128]{2,1,0:T(4,128)S(1)} all-to-all(f32[128,4,128]{2,1,0:T(4,128)S(1)} %get-tuple-element.79), channel_id=1, replica_groups=mesh['gx'=8,'gy'=16] {'gx','gy'}, dimensions={0} | all-to-all | bytes 524288 | tf_op jit(solution)/shard_map/all_to_all | solution.py:779
  116.5 8.8 %pair_0.1 = (f32[2,20,18,8,128]{4,3,2,1,0:T(8,128)S(1)}, f32[2,20,18,8,128]{4,3,2,1,0:T(8,128)S(1)}, f32[128,4,128]{2,1,0:T(4,128)S(1)}, f32[8,128]{1,0:T(8,128)S(1)}) custom-call(f32[4]{0:T(128)S(1)} %add_convert_fusion.inside, f32[2,20,18,8,128]{4,3,2,1,0:T(8,128)S(1)} %get-tuple-element.77.field, f32[2,20,18,8,128]{4,3,2,1,0:T(8,128)S(1)} %get-tuple-element.78.changes, ...), custom_call_target="tpu_custom_call" | custom-call | tf_op jit(solution)/shard_map/pair_0/pallas_call | solution.py:572
  125.4 15.2 %all_to_all.61.parts = f32[128,4,128]{2,1,0:T(4,128)S(1)} all-to-all(f32[128,4,128]{2,1,0:T(4,128)S(1)} %get-tuple-element.82), channel_id=1, replica_groups=mesh['gx'=8,'gy'=16] {'gx','gy'}, dimensions={0} | all-to-all | bytes 524288 | tf_op jit(solution)/shard_map/all_to_all | solution.py:779
  140.6 6.9 %pair_2.1 = (f32[2,20,18,8,128]{4,3,2,1,0:T(8,128)S(1)}, f32[2,20,18,8,128]{4,3,2,1,0:T(8,128)S(1)}, f32[128,4,128]{2,1,0:T(4,128)S(1)}, f32[8,128]{1,0:T(8,128)S(1)}) custom-call(f32[4]{0:T(128)S(1)} %add_convert_fusion.inside, f32[2,20,18,8,128]{4,3,2,1,0:T(8,128)S(1)} %get-tuple-element.80.field, f32[2,20,18,8,128]{4,3,2,1,0:T(8,128)S(1)} %get-tuple-element.81.changes, ...), custom_call_target="tpu_custom_call" | custom-call | tf_op jit(solution)/shard_map/pair_2/pallas_call | solution.py:572
  147.6 15.2 %all_to_all.62.parts = f32[128,4,128]{2,1,0:T(4,128)S(1)} all-to-all(f32[128,4,128]{2,1,0:T(4,128)S(1)} %get-tuple-element.86), channel_id=1, replica_groups=mesh['gx'=8,'gy'=16] {'gx','gy'}, dimensions={0} | all-to-all | bytes 524288 | tf_op jit(solution)/shard_map/all_to_all | solution.py:779
  162.8 4.2 %last_pair.1 = (f32[2,8,16,8,128]{4,3,2,1,0:T(8,128)S(1)}, f32[128,4,128]{2,1,0:T(4,128)}, f32[8,128]{1,0:T(8,128)S(1)}) custom-call(f32[4]{0:T(128)S(1)} %add_convert_fusion.inside, f32[2,20,18,8,128]{4,3,2,1,0:T(8,128)S(1)} %get-tuple-element.84.field, f32[2,20,18,8,128]{4,3,2,1,0:T(8,128)S(1)} %get-tuple-element.85.changes, ...), custom_call_target="tpu_custom_call" | custom-call | tf_op jit(solution)/shard_map/last_pair/pallas_call | solution.py:623
  167.1 4.3 %all-to-all-start.11 = ((f32[128,4,128]{2,1,0:T(4,128)}), f32[128,4,128]{2,1,0:T(4,128)S(1)}, u32[]{:S(2)}, u32[]{:S(2)}) async-start(f32[128,4,128]{2,1,0:T(4,128)} %get-tuple-element.90), calls=%async_computation.11 | async-start | bytes 524288 | tf_op jit(solution)/shard_map/all_to_all | solution.py:779
  171.4 11.4 %all-to-all-done.11.sums = f32[128,4,128]{2,1,0:T(4,128)S(1)} async-done(((f32[128,4,128]{2,1,0:T(4,128)}), f32[128,4,128]{2,1,0:T(4,128)S(1)}, u32[]{:S(2)}, u32[]{:S(2)}) %all-to-all-start.11) | async-done | bytes 262176 | tf_op jit(solution)/shard_map/all_to_all | solution.py:779
  182.8 5.4 %update.3 = (f32[16,16,8,128]{3,2,1,0:T(8,128)}, s32[1]{0:T(128)}) custom-call(f32[128,4,128]{2,1,0:T(4,128)S(1)} %all-to-all-done.11.sums, f32[2,8,16,8,128]{4,3,2,1,0:T(8,128)S(1)} %get-tuple-element.91.field, f32[8,128]{1,0:T(8,128)S(1)} %get-tuple-element.92.status), custom_call_target="tpu_custom_call" | custom-call | tf_op jit(solution)/shard_map/update/pallas_call | solution.py:765
  (16 shorter events, 0.0 us)
Async XLA Ops:
  0.0 18.4 %copy-start = (f32[16,16,8,128]{3,2,1,0:T(8,128)S(1)}, f32[16,16,8,128]{3,2,1,0:T(8,128)}, u32[]{:S(2)}) copy-start(f32[16,16,8,128]{3,2,1,0:T(8,128)} %state.1) | copy-start | bytes 3145732
  0.0 1.1 copy-start.1
  1.1 0.8 copy-start.2
  2.0 0.7 copy-start.8
  2.6 22.3 %copy-start.3 = (f32[16,8,128]{2,1,0:T(8,128)S(1)}, f32[16,8,128]{2,1,0:T(8,128)}, u32[]{:S(2)}) copy-start(f32[16,8,128]{2,1,0:T(8,128)} %own.1) | copy-start | bytes 196612
  2.6 27.9 %copy-start.4 = (f32[16,512]{1,0:T(8,128)S(1)}, f32[16,512]{1,0:T(8,128)}, u32[]{:S(2)}) copy-start(f32[16,512]{1,0:T(8,128)} %noise.1) | copy-start | bytes 98308
  2.6 27.9 %copy-start.5 = (s32[512]{0:T(512)S(1)}, s32[512]{0:T(512)}, u32[]{:S(2)}) copy-start(s32[512]{0:T(512)} %param.16) | copy-start | bytes 6148
  2.6 27.9 %copy-start.6 = (f32[512]{0:T(512)S(1)}, f32[512]{0:T(512)}, u32[]{:S(2)}) copy-start(f32[512]{0:T(512)} %param.17) | copy-start | bytes 6148
  2.6 27.9 %copy-start.7 = (f32[512]{0:T(512)S(1)}, f32[512]{0:T(512)}, u32[]{:S(2)}) copy-start(f32[512]{0:T(512)} %param.18) | copy-start | bytes 6148
  6.9 51.6 %all-to-all-start.7 = ((bf16[128,40,128]{2,1,0:T(8,128)(2,1)}), bf16[128,40,128]{2,1,0:T(8,128)(2,1)S(1)}, u32[]{:S(2)}, u32[]{:S(2)}) async-start(bf16[128,40,128]{2,1,0:T(8,128)(2,1)} %pack.1), calls=%async_computation.7 | async-start | bytes 2621440 | tf_op jit(solution)/shard_map/all_to_all | solution.py:779
  20.1 54.7 %collective-permute-start.4 = (f32[192,8,128]{2,1,0:T(8,128)}, f32[192,8,128]{2,1,0:T(8,128)S(1)}, u32[]{:S(2)}, u32[]{:S(2)}) collective-permute-start(f32[192,8,128]{2,1,0:T(8,128)} %get-tuple-element.71), channel_id=1, source_target_pairs={{0,1},{1,2},{2,3},{3,4},{4,5},{5,6},{6,7},{7,8},{8,9},{9,10},{10,1... | collective-permute-start | bytes 2359304 | tf_op jit(solution)/shard_map/ppermute | solution.py:785
  23.6 51.2 %collective-permute-start.5 = (f32[192,8,128]{2,1,0:T(8,128)}, f32[192,8,128]{2,1,0:T(8,128)}, u32[]{:S(2)}, u32[]{:S(2)}) collective-permute-start(f32[192,8,128]{2,1,0:T(8,128)} %get-tuple-element.72), channel_id=1, source_target_pairs={{1,0},{2,1},{3,2},{4,3},{5,4},{6,5},{7,6},{8,7},{9,8},{10,9},{11,1... | collective-permute-start | bytes 2359304 | tf_op jit(solution)/shard_map/ppermute | solution.py:785
  24.9 7.6 %collective-permute-start = (f32[16,8,128]{2,1,0:T(8,128)S(1)}, f32[16,8,128]{2,1,0:T(8,128)S(1)}, u32[]{:S(2)}, u32[]{:S(2)}) collective-permute-start(f32[16,8,128]{2,1,0:T(8,128)S(1)} %copy-done.3), channel_id=1, source_target_pairs={{0,16},{16,32},{32,48},{48,64},{64,80},{80,96},{96,112},{1,17},{17... | collective-permute-start | bytes 196616 | tf_op jit(solution)/shard_map/ppermute | solution.py:785
  28.5 6.7 %collective-permute-start.1 = (f32[16,8,128]{2,1,0:T(8,128)S(1)}, f32[16,8,128]{2,1,0:T(8,128)S(1)}, u32[]{:S(2)}, u32[]{:S(2)}) collective-permute-start(f32[16,8,128]{2,1,0:T(8,128)S(1)} %copy-done.3), channel_id=1, source_target_pairs={{16,0},{32,16},{48,32},{64,48},{80,64},{96,80},{112,96},{17,1},{33... | collective-permute-start | bytes 196616 | tf_op jit(solution)/shard_map/ppermute | solution.py:785
  35.3 19.1 %collective-permute-start.3 = (f32[18,8,128]{2,1,0:T(8,128)S(1)}, f32[18,8,128]{2,1,0:T(8,128)S(1)}, u32[]{:S(2)}, u32[]{:S(2)}) collective-permute-start(f32[18,8,128]{2,1,0:T(8,128)S(1)} %strip.1.own), channel_id=1, source_target_pairs={{1,0},{2,1},{3,2},{4,3},{5,4},{6,5},{7,6},{8,7},{9,8},{10,9},{11,1... | collective-permute-start | bytes 221192 | tf_op jit(solution)/shard_map/ppermute | solution.py:785
  36.6 17.8 %collective-permute-start.2 = (f32[18,8,128]{2,1,0:T(8,128)S(1)}, f32[18,8,128]{2,1,0:T(8,128)S(1)}, u32[]{:S(2)}, u32[]{:S(2)}) collective-permute-start(f32[18,8,128]{2,1,0:T(8,128)S(1)} %strip.1.own), channel_id=1, source_target_pairs={{0,1},{1,2},{2,3},{3,4},{4,5},{5,6},{6,7},{7,8},{8,9},{9,10},{10,1... | collective-permute-start | bytes 221192 | tf_op jit(solution)/shard_map/ppermute | solution.py:785
  58.5 31.1 %copy-start.9 = (f32[2,20,18,8,128]{4,3,2,1,0:T(8,128)S(1)}, f32[2,20,18,8,128]{4,3,2,1,0:T(8,128)}, u32[]{:S(2)}) copy-start(f32[2,20,18,8,128]{4,3,2,1,0:T(8,128)} %coefs.1.coef) | copy-start | bytes 8847364
  69.4 6.8 %collective-permute-start.7 = (f32[2,128,128]{2,1,0:T(8,128)S(1)}, f32[2,128,128]{2,1,0:T(8,128)S(1)}, u32[]{:S(2)}, u32[]{:S(2)}) collective-permute-start(f32[2,128,128]{2,1,0:T(8,128)S(1)} %deposit.1.heat_own), channel_id=1, source_target_pairs={{1,0},{2,1},{3,2},{4,3},{5,4},{6,5},{7,6},{8,7},{9,8},{10,9},{11,1... | collective-permute-start | bytes 393224 | tf_op jit(solution)/shard_map/ppermute | solution.py:785
  70.7 6.3 %collective-permute-start.6 = (f32[2,128,128]{2,1,0:T(8,128)S(1)}, f32[2,128,128]{2,1,0:T(8,128)S(1)}, u32[]{:S(2)}, u32[]{:S(2)}) collective-permute-start(f32[2,128,128]{2,1,0:T(8,128)S(1)} %deposit.1.heat_own), channel_id=1, source_target_pairs={{0,1},{1,2},{2,3},{3,4},{4,5},{5,6},{6,7},{7,8},{8,9},{9,10},{10,1... | collective-permute-start | bytes 393224 | tf_op jit(solution)/shard_map/ppermute | solution.py:785
  78.2 7.0 %collective-permute-start.8 = (f32[46,8,128]{2,1,0:T(8,128)S(1)}, f32[46,8,128]{2,1,0:T(8,128)S(1)}, u32[]{:S(2)}, u32[]{:S(2)}) collective-permute-start(f32[46,8,128]{2,1,0:T(8,128)S(1)} %get-tuple-element.74), channel_id=1, source_target_pairs={{0,16},{16,32},{32,48},{48,64},{64,80},{80,96},{96,112},{1,17},{17... | collective-permute-start | bytes 565256 | tf_op jit(solution)/shard_map/ppermute | solution.py:785
  82.7 6.9 %collective-permute-start.9 = (f32[46,8,128]{2,1,0:T(8,128)S(1)}, f32[46,8,128]{2,1,0:T(8,128)S(1)}, u32[]{:S(2)}, u32[]{:S(2)}) collective-permute-start(f32[46,8,128]{2,1,0:T(8,128)S(1)} %get-tuple-element.75), channel_id=1, source_target_pairs={{16,0},{32,16},{48,32},{64,48},{80,64},{96,80},{112,96},{17,1},{33... | collective-permute-start | bytes 565256 | tf_op jit(solution)/shard_map/ppermute | solution.py:785
  95.7 44.9 %copy-start.11 = (f32[2,20,18,8,128]{4,3,2,1,0:T(8,128)}, f32[2,20,18,8,128]{4,3,2,1,0:T(8,128)S(1)}, u32[]{:S(2)}) copy-start(f32[2,20,18,8,128]{4,3,2,1,0:T(8,128)S(1)} %get-tuple-element.77.field) | copy-start | bytes 8847364
  167.1 15.7 %all-to-all-start.11 = ((f32[128,4,128]{2,1,0:T(4,128)}), f32[128,4,128]{2,1,0:T(4,128)S(1)}, u32[]{:S(2)}, u32[]{:S(2)}) async-start(f32[128,4,128]{2,1,0:T(4,128)} %get-tuple-element.90), calls=%async_computation.11 | async-start | bytes 524288 | tf_op jit(solution)/shard_map/all_to_all | solution.py:779

commit v5 on v4

--- a/solution.py
+++ b/solution.py
@@ -143,7 +143,7 @@
 SIDE = 2 * YS
 
 
-def relayout_kernel(state, own, to_high, to_low):
+def relayout_kernel(state, own, to_high, to_low, to_left, to_right):
     for zi in range(2):
         for y in range(CY):
             parts = [
@@ -151,6 +151,8 @@
             ]
             turned = (0.5 * jnp.concatenate(parts, axis=0)).T.reshape(XT - 2, 8, CX)
             own[zi, y] = turned
+            to_left[zi * CY + y] = turned[0]
+            to_right[zi * CY + y] = turned[XT - 3]
             if y >= CY - HALO:
                 at = (zi * HALO + y - (CY - HALO)) * (XT - 2)
                 to_high[at : at + XT - 2] = turned
@@ -161,42 +163,15 @@
 
 def relayout(state):
     edge = jax.ShapeDtypeStruct((EDGE, 8, CX), F32)
+    side = jax.ShapeDtypeStruct((2 * CY, 8, CX), F32)
     return pl.pallas_call(
         relayout_kernel,
-        out_shape=[OWN, edge, edge],
+        out_shape=[OWN, edge, edge, side, side],
         in_specs=[vspec()],
-        out_specs=[vspec()] * 3,
+        out_specs=[vspec()] * 5,
         compiler_params=params(),
         name="relayout",
     )(state)
-
-
-def side_kernel(own, low, high, heat_low, heat_own, heat_high, to_left, to_right):
-    for out, t in ((to_left, 0), (to_right, XT - 3)):
-        for zi in range(2):
-            for y in range(YS):
-                if y < HALO:
-                    part = low[(zi * HALO + y) * (XT - 2) + t]
-                elif y < HALO + CY:
-                    part = own[zi, y - HALO, t]
-                else:
-                    part = high[(zi * HALO + y - HALO - CY) * (XT - 2) + t]
-                out[zi * YS + y] = part
-        for g, heat in enumerate((heat_low, heat_own, heat_high)):
-            for zi in range(2):
-                out[SIDE + 2 * g + zi] = heat[zi, 8 * t : 8 * t + 8, :]
-
-
-def sides(own, low, high, heat_low, heat_own, heat_high):
-    shape = jax.ShapeDtypeStruct((SIDE + 6, 8, CX), F32)
-    return pl.pallas_call(
-        side_kernel,
-        out_shape=[shape, shape],
-        in_specs=[vspec()] * 6,
-        out_specs=[vspec()] * 2,
-        compiler_params=params(),
-        name="sides",
-    )(own, low, high, heat_low, heat_own, heat_high)
 
 
 def strip_kernel(own, left, right, out):
@@ -252,7 +227,7 @@
     )(own, low, high)
 
 
-def deposit_kernel(incoming, out, total):
+def deposit_kernel(incoming, out, to_left, to_right, total):
     sources = incoming.shape[0]
     group = 4
     place = lax.broadcasted_iota(jnp.int32, (CX, CX), 0).astype(F32).astype(BF16)
@@ -285,15 +260,18 @@
 
     lax.fori_loop(0, sources // group, one, 0)
     for zi in range(2):
-        out[zi] = (0.5 * total[zi * CX : (zi + 1) * CX, :]).T
+        turned = (0.5 * total[zi * CX : (zi + 1) * CX, :]).T
+        out[zi] = turned
+        to_left[zi] = turned[0:8]
+        to_right[zi] = turned[CX - 8 :]
 
 
 def deposit(incoming):
     return pl.pallas_call(
         deposit_kernel,
-        out_shape=jax.ShapeDtypeStruct((2, CX, CX), F32),
+        out_shape=[jax.ShapeDtypeStruct((2, rows_, CX), F32) for rows_ in (CX, 8, 8)],
         in_specs=[vspec()],
-        out_specs=vspec(),
+        out_specs=[vspec()] * 3,
         scratch_shapes=[VM((2 * CY * M, CX), F32)],
         compiler_params=params(),
         name="deposit",
@@ -414,7 +392,8 @@
         own = own_row(y)
         for zi in range(2):
             moved = change[zi] * part
-            changes[zi, y, t] = moved
+            if changes is not None:
+                changes[zi, y, t] = moved
             if 0 < t < XT - 1:
                 c = coef[zi, y, t]
                 value = us[zi] + guess * moved
@@ -464,29 +443,35 @@
 
 def heated_kernel(
     inside, own, low, high, left, right,
-    heat_low, heat_own, heat_high,
-    coef, out, changes, parts, above, below_h,
+    heat_low, heat_own, heat_high, heat_left, heat_right,
+    coef, out, parts, to_left, to_right, above, below_h,
 ):
     top = lanes() < M
     peak = jnp.zeros((8, CX), F32)
 
+    def warm(prior, heat, y0):
+        shift = (CX - 16 * y0) % CX
+        if shift:
+            heat = pltpu.roll(heat, shift, axis=1)
+        return prior + jnp.where(top, heat, 0.0)
+
     def row(g, heat, tile_of, y0, yy, peak):
-        shift = (CX - 16 * y0) % CX
         for zi in range(2):
-            for t in range(XT):
-                if t == 0:
-                    prior, add = left[zi * YS + yy], left[SIDE + 2 * g + zi]
-                elif t == XT - 1:
-                    prior, add = right[zi * YS + yy], right[SIDE + 2 * g + zi]
-                else:
-                    prior, add = tile_of(zi, t - 1), heat[zi, 8 * t - 8 : 8 * t, :]
-                if shift:
-                    add = pltpu.roll(add, shift, axis=1)
-                value = prior + jnp.where(top, add, 0.0)
+            for t in range(1, XT - 1):
+                value = warm(tile_of(zi, t - 1), heat[zi, 8 * t - 8 : 8 * t, :], y0)
                 out[zi, yy, t] = value
-                if g == 1 and 0 < t < XT - 1:
+                if t == 1:
+                    to_left[zi * YS + yy] = value
+                if t == XT - 2:
+                    to_right[zi * YS + yy] = value
+                if g == 1:
                     c = coef[zi, yy, t]
                     peak = jnp.maximum(peak, c + c * (value * value))
+            for t, ref, edge_heat in ((0, left, heat_left), (XT - 1, right, heat_right)):
+                if g == 1:
+                    out[zi, yy, t] = warm(ref[zi * CY + y0], edge_heat[zi], y0)
+                else:
+                    out[zi, yy, t] = jnp.zeros((8, CX), F32)
         return peak
 
     def edge(ref, y):
@@ -500,7 +485,22 @@
         row(2, heat_high, edge(high, y), y, y + HALO + CY, peak)
     guess = step_of(whole_peak(peak))
     zero = jnp.zeros((8, CX), F32)
-    propose(out, coef, above, below_h, inside, guess, 1, YS - 1, changes, peak, zero, parts)
+    propose(
+        out, coef, above, below_h, inside, guess, HALO, HALO + CY, None, peak, zero, parts
+    )
+
+
+class Joined:
+    def __init__(self, field, left, right):
+        self.field, self.left, self.right = field, left, right
+
+    def __getitem__(self, at):
+        zi, y, t = at
+        if t == 0:
+            return self.left[zi * YS + y]
+        if t == XT - 1:
+            return self.right[zi * YS + y]
+        return self.field[zi, y, t]
 
 
 ROW = (2, XT, 8, CX)
@@ -512,11 +512,12 @@
 
 def heated(inside, prior, halos, heat, coef, devices):
     operands = [inside, *prior, *halos, *heat, coef]
+    side = jax.ShapeDtypeStruct((SIDE, 8, CX), F32)
     return pl.pallas_call(
         heated_kernel,
-        out_shape=[WIDE, WIDE, jax.ShapeDtypeStruct((devices, 4, CX), F32)],
+        out_shape=[WIDE, jax.ShapeDtypeStruct((devices, 4, CX), F32), side, side],
         in_specs=[smem()] + [vspec()] * (len(operands) - 1),
-        out_specs=[vspec()] * 3,
+        out_specs=[vspec()] * 4,
         scratch_shapes=[VM(ROW, F32), VM(ROW, F32)],
         compiler_params=params(),
         name="heated",
@@ -539,21 +540,44 @@
     return lax.fori_loop(first, end, line, jnp.zeros((8, CX), F32))
 
 
+def first_pair_kernel(
+    inside, field, left, right, coef, parts,
+    out, out_changes, out_parts, out_status, middle, above, below_h,
+):
+    now, then, _ = agree(parts)
+    out_status[...] = jnp.where(rows() == 0, then, 0.0)
+
+    def put_middle(zi, y, t, value):
+        middle[zi, y, t] = value
+
+    seen = advance(
+        Joined(field, left, right), coef, above, below_h, inside, step_of(now), 1, YS - 1, put_middle
+    )
+    second_of_pair(
+        0, inside, middle, coef, step_of(then), seen, out, out_changes, out_parts, above, below_h
+    )
+
+
 def pair_kernel(
     number, inside, field, changes, coef, parts, status,
     out, out_changes, out_parts, out_status, middle, above, below_h,
 ):
     now, then, late = agree(parts)
-    bad = status[1:2, :]
-    if number:
-        bad = jnp.maximum(bad, differs(late[0:1], status[0:1, :]))
+    bad = jnp.maximum(status[1:2, :], differs(late[0:1], status[0:1, :]))
     out_status[...] = jnp.where(rows() == 0, then, bad)
     seen = first_of_pair(field, changes, coef, step_of(now), number + 1, YS - 1 - number, middle)
-
+    second_of_pair(
+        number, inside, middle, coef, step_of(then), seen,
+        out, out_changes, out_parts, above, below_h,
+    )
+
+
+def second_of_pair(
+    number, inside, middle, coef, step, seen, out, out_changes, out_parts, above, below_h
+):
     def put(zi, y, t, value):
         out[zi, y, t] = value
 
-    step = step_of(then)
     peak = advance(
         middle, coef, above, below_h, inside, step, number + 2, YS - 2 - number, put
     )
@@ -567,17 +591,25 @@
 STATUS = jax.ShapeDtypeStruct((8, CX), F32)
 
 
-def pair(number, inside, field, changes, coef, parts, status):
-    operands = [inside, field, changes, coef, parts, status]
-    return pl.pallas_call(
-        functools.partial(pair_kernel, number),
+def pair(number, kernel, operands, parts):
+    return pl.pallas_call(
+        kernel,
         out_shape=[WIDE, WIDE, jax.ShapeDtypeStruct(parts.shape, F32), STATUS],
-        in_specs=[smem()] + [vspec()] * 5,
+        in_specs=[smem()] + [vspec()] * (len(operands) - 1),
         out_specs=[vspec()] * 4,
         scratch_shapes=[VM(WIDE.shape, F32), VM(ROW, F32), VM(ROW, F32)],
         compiler_params=params(),
         name=f"pair_{number}",
     )(*operands)
+
+
+def first_pair(inside, start, coef, parts):
+    return pair(0, first_pair_kernel, [inside, *start, coef, parts], parts)
+
+
+def later_pair(number, inside, field, changes, coef, parts, status):
+    operands = [inside, field, changes, coef, parts, status]
+    return pair(number, functools.partial(pair_kernel, number), operands, parts)
 
 
 def pixel_grams(field, weight, data, flat, late, sums):
@@ -631,8 +663,11 @@
     )(*operands)
 
 
-def single_kernel(number, inside, field, coef, peaks, *rest):
+def single_kernel(number, inside, coef, peaks, field, *rest):
     final = number == SUBSTEPS - 1
+    if number == 0:
+        field = Joined(field, *rest[:2])
+        rest = rest[2:]
     if final:
         weight, data, out, sums, above, below_h, flat = rest
     else:
@@ -657,7 +692,7 @@
 
 def single(number, inside, field, coef, peaks, pixels):
     devices = peaks.shape[0]
-    operands = [inside, field, coef, peaks]
+    operands = [inside, coef, peaks, *field]
     scratch = [VM(ROW, F32), VM(ROW, F32)]
     if number == SUBSTEPS - 1:
         operands += list(pixels)
@@ -808,40 +843,48 @@
     left_c, right_c = move(conductivity, "gx", True), move(conductivity, "gx", False)
     strips = strip(conductivity, left_c, right_c)
     coef = coefs(strips, move(strips, "gy", True), move(strips, "gy", False))
-    own, to_high, to_low = relayout(state_prior)
+    state_prior, strips = lax.optimization_barrier((state_prior, strips))
+    own, to_high, to_low, to_left, to_right = relayout(state_prior)
     low, high = move(to_high, "gy", True), move(to_low, "gy", False)
+    left, right = move(to_right, "gx", True), move(to_left, "gx", False)
     seen = pixel_sums(
         pixel_cell.reshape(1, pixels),
         observed.reshape(1, pixels),
         pixel_variance.reshape(1, pixels),
         pixel_noise,
     )
-    incoming, coef, own, inside, *seen = lax.optimization_barrier(
-        (incoming, coef, own, inside, *seen)
-    )
-    heat = deposit(incoming)
+    incoming, coef, own, left, right, inside, *seen = lax.optimization_barrier(
+        (incoming, coef, own, left, right, inside, *seen)
+    )
+    heat, to_left, to_right = deposit(incoming)
     heat_low, heat_high = move(heat, "gy", True), move(heat, "gy", False)
-    to_left, to_right = sides(own, low, high, heat_low, heat, heat_high)
-    left, right = move(to_right, "gx", True), move(to_left, "gx", False)
-    start, changes, parts = heated(
-        inside, (own, low, high), (left, right), (heat_low, heat, heat_high), coef, devices
-    )
-    field, status = start, jnp.zeros((8, CX), F32)
-    for number in range(0, SUBSTEPS - 2, 2):
-        field, changes, parts, status = pair(
+    heat_left, heat_right = move(to_right, "gx", True), move(to_left, "gx", False)
+    start, parts, to_left, to_right = heated(
+        inside,
+        (own, low, high),
+        (left, right),
+        (heat_low, heat, heat_high, heat_left, heat_right),
+        coef,
+        devices,
+    )
+    start = (start, move(to_right, "gx", True), move(to_left, "gx", False))
+    field, changes, parts, status = first_pair(inside, start, coef, exchange(parts))
+    for number in range(2, SUBSTEPS - 2, 2):
+        field, changes, parts, status = later_pair(
             number, inside, field, changes, coef, exchange(parts), status
         )
     field, sums, status = last(inside, field, changes, coef, exchange(parts), status, seen)
     result, flag = update(exchange(sums), field, status)
 
     def again():
-        peak = coef * (1.0 + start * start)
+        peak = coef * (1.0 + start[0] * start[0])
         peak = jnp.max(peak[:, HALO : HALO + CY, 1 : XT - 1])
         peaks = jnp.full((devices, 1, CX), peak)
         field = start
         for number in range(SUBSTEPS):
             field, peaks = single(number, inside, field, coef, exchange(peaks), seen)
-        return update(exchange(peaks), field, jnp.ones((8, CX), F32))[0]
+            field = (field,)
+        return update(exchange(peaks), field[0], jnp.ones((8, CX), F32))[0]
 
     return lax.cond(flag[0] > 0, again, lambda: result)
 

time: 190 us -> 207 us (1.089)
  starting transfers between devices: 43.5 us -> 65.9 us
  blocking collectives: 51.3 us -> 34.3 us
  waiting for transfers between devices: 34.9 us -> 41.2 us
  Pallas kernels: 55.5 us -> 60.4 us
    all_to_all x3 -> x2, blocking collectives: 51.3 us -> 34.3 us  [exchange(): return lax.all_to_all(parts, BOTH, split_axis=0, concat_axis=0, tiled=True)]
    all_to_all x2 -> x3, starting transfers between devices: 15.8 us -> 27.6 us  [exchange(): return lax.all_to_all(parts, BOTH, split_axis=0, concat_axis=0, tiled=True)]
    ppermute x10 -> x14, starting transfers between devices: 27.7 us -> 38.3 us  [move(): return lax.ppermute(part, axis, pairs)]
    ppermute x10 -> x14, waiting for transfers between devices: 23.5 us -> 29 us  [move(): return lax.ppermute(part, axis, pairs)]
    pallas_call x6 -> x5, Pallas kernels: 35.7 us -> 40 us  [the longest x2 21.4 us: pair(): pl.pallas_call(kernel, out_shape=[WIDE, WIDE, jax.ShapeDtypeStruct(parts....]
    all_to_all x2 -> x3, waiting for transfers between devices: 11.4 us -> 12.1 us  [exchange(): return lax.all_to_all(parts, BOTH, split_axis=0, concat_axis=0, tiled=True)]
  transfers between devices with their start and end apart: 12 -> 17, of which waited for: 8 -> 9; matrix products, arithmetic and copies ran while one was open for 0% -> 0% of each run, Pallas kernels for 10% -> 9%
where the time goes in v5:
time: 207 us; the launch traced here: 206 us
  starting transfers between devices  65.9 us (32%)
  Pallas kernels  60.4 us (29%)
  waiting for transfers between devices  41.2 us (20%)
  blocking collectives  34.3 us (17%)
  local copies, waits for them, and re-layouts  3.29 us (2%)
    ppermute x14, starting transfers between devices, move(): return lax.ppermute(part, axis, pairs)  38.3 us
    all_to_all x2, blocking collectives, exchange(): return lax.all_to_all(parts, BOTH, split_axis=0, concat_axis=0, tiled=True)  34.3 us
    ppermute x14, waiting for transfers between devices, move(): return lax.ppermute(part, axis, pairs)  29 us
    all_to_all x3, starting transfers between devices, exchange(): return lax.all_to_all(parts, BOTH, split_axis=0, concat_axis=0, tiled=True)  27.6 us
    pallas_call x2, Pallas kernels, pair(): pl.pallas_call(kernel, out_shape=[WIDE, WIDE, jax.ShapeDtypeStruct(parts....  21.4 us
    all_to_all x3, waiting for transfers between devices, exchange(): return lax.all_to_all(parts, BOTH, split_axis=0, concat_axis=0, tiled=True)  12.1 us
    pallas_call x1, Pallas kernels, deposit(): pl.pallas_call(deposit_kernel, out_shape=[jax.ShapeDtypeStruct((2, rows_,...  10.9 us
    pallas_call x1, Pallas kernels, heated(): pl.pallas_call(heated_kernel, out_shape=[WIDE, jax.ShapeDtypeStruct((devi...  5.97 us
  transfers between devices with their start and end apart: 17, of which 9 were waited for; matrix products, arithmetic and copies ran while one was open for 0% of the time, Pallas kernels for 9%

profile of v5, /device:TPU:1, one launch (start us, length us, event | category | flops | bytes accessed | tf_op | source)
XLA Modules:
  0.0 206.2 jit_solution(13547912709134005468)
XLA Ops:
  0.0 1.1 copy-done.1
  1.1 0.8 copy-done.2
  2.0 0.7 copy-done.8
  2.7 4.2 %pack.1 = bf16[128,40,128]{2,1,0:T(8,128)(2,1)} custom-call(s32[128]{0:T(128)S(1)} %bitcast.12, bf16[16,128,128]{2,1,0:T(8,128)(2,1)S(1)} %copy-done.1, s32[128,128]{1,0:T(8,128)S(1)} %copy-done.2), custom_call_target="tpu_custom_call" | custom-call | tf_op jit(solution)/shard_map/pack/pallas_call | solution.py:115
  6.9 11.5 %all-to-all-start.7 = ((bf16[128,40,128]{2,1,0:T(8,128)(2,1)}), bf16[128,40,128]{2,1,0:T(8,128)(2,1)S(1)}, u32[]{:S(2)}, u32[]{:S(2)}) async-start(bf16[128,40,128]{2,1,0:T(8,128)(2,1)} %pack.1), calls=%async_computation.7 | async-start | bytes 2621440 | tf_op jit(solution)/shard_map/all_to_all | solution.py:814
  18.4 3.5 %collective-permute-start = (f32[16,8,128]{2,1,0:T(8,128)S(1)}, f32[16,8,128]{2,1,0:T(8,128)S(1)}, u32[]{:S(2)}, u32[]{:S(2)}) collective-permute-start(f32[16,8,128]{2,1,0:T(8,128)S(1)} %copy-done.3), channel_id=1, source_target_pairs={{0,16},{16,32},{32,48},{48,64},{64,80},{80,96},{96,112},{1,17},{17... | collective-permute-start | bytes 196616 | tf_op jit(solution)/shard_map/ppermute | solution.py:820
  21.9 1.9 collective-permute-start.1
  23.9 8.7 %collective-permute-done.left = f32[16,8,128]{2,1,0:T(8,128)S(1)} collective-permute-done((f32[16,8,128]{2,1,0:T(8,128)S(1)}, f32[16,8,128]{2,1,0:T(8,128)S(1)}, u32[]{:S(2)}, u32[]{:S(2)}) %collective-permute-start) | collective-permute-done | bytes 65568 | tf_op jit(solution)/shard_map/ppermute | solution.py:820
  32.5 2.6 %collective-permute-done.1.right = f32[16,8,128]{2,1,0:T(8,128)S(1)} collective-permute-done((f32[16,8,128]{2,1,0:T(8,128)S(1)}, f32[16,8,128]{2,1,0:T(8,128)S(1)}, u32[]{:S(2)}, u32[]{:S(2)}) %collective-permute-start.1) | collective-permute-done | bytes 65568 | tf_op jit(solution)/shard_map/ppermute | solution.py:820
  35.1 0.1 strip.1.own
  35.2 1.7 relayout.1
  37.0 0.6 copy-done.10
  37.6 3.3 %collective-permute-start.6 = (f32[192,8,128]{2,1,0:T(8,128)}, f32[192,8,128]{2,1,0:T(8,128)S(1)}, u32[]{:S(2)}, u32[]{:S(2)}) collective-permute-start(f32[192,8,128]{2,1,0:T(8,128)} %get-tuple-element.87), channel_id=1, source_target_pairs={{0,1},{1,2},{2,3},{3,4},{4,5},{5,6},{6,7},{7,8},{8,9},{9,10},{10,1... | collective-permute-start | bytes 2359304 | tf_op jit(solution)/shard_map/ppermute | solution.py:820
  40.9 1.3 collective-permute-start.7
  42.2 1.3 collective-permute-start.3
  43.5 2.4 %pixels.1 = (f32[8,128]{1,0:T(8,128)S(1)}, f32[16,8,128]{2,1,0:T(8,128)}) custom-call(s32[1,512]{1,0:T(1,128)S(1)} %bitcast.9, f32[1,512]{1,0:T(1,128)S(1)} %bitcast.10, f32[1,512]{1,0:T(1,128)S(1)} %bitcast.11, f32[16,512]{1,0:T(8,128)S(1)} %copy-done.4), custom_call_target="tpu_custom_call" | custom-call | tf_op jit(solution)/shard_map/pixels/pallas_call | solution.py:739
  45.9 4.6 %collective-permute-start.2 = (f32[18,8,128]{2,1,0:T(8,128)S(1)}, f32[18,8,128]{2,1,0:T(8,128)S(1)}, u32[]{:S(2)}, u32[]{:S(2)}) collective-permute-start(f32[18,8,128]{2,1,0:T(8,128)S(1)} %strip.1.own), channel_id=1, source_target_pairs={{0,1},{1,2},{2,3},{3,4},{4,5},{5,6},{6,7},{7,8},{8,9},{9,10},{10,1... | collective-permute-start | bytes 221192 | tf_op jit(solution)/shard_map/ppermute | solution.py:820
  50.5 3.3 %collective-permute-start.4 = (f32[16,8,128]{2,1,0:T(8,128)}, f32[16,8,128]{2,1,0:T(8,128)S(1)}, u32[]{:S(2)}, u32[]{:S(2)}) collective-permute-start(f32[16,8,128]{2,1,0:T(8,128)} %copy-done.10), channel_id=1, source_target_pairs={{0,16},{16,32},{32,48},{48,64},{64,80},{80,96},{96,112},{1,17},{17... | collective-permute-start | bytes 196616 | tf_op jit(solution)/shard_map/ppermute | solution.py:820
  53.8 1.5 collective-permute-done.3.high
  55.3 1.9 collective-permute-start.5
  57.3 0.1 add_convert_fusion.inside
  57.3 0.0 collective-permute-done.2.low
  57.4 4.1 %coefs.1.coef = f32[2,20,18,8,128]{4,3,2,1,0:T(8,128)} custom-call(f32[18,8,128]{2,1,0:T(8,128)S(1)} %strip.1.own, f32[18,8,128]{2,1,0:T(8,128)S(1)} %collective-permute-done.2.low, f32[18,8,128]{2,1,0:T(8,128)S(1)} %collective-permute-done.3.high), custom_call_target="tpu_custom_call" | custom-call | tf_op jit(solution)/shard_map/coefs/pallas_call | solution.py:220
  61.4 0.0 collective-permute-done.4.left
  61.4 8.2 %collective-permute-done.5.right = f32[16,8,128]{2,1,0:T(8,128)S(1)} collective-permute-done((f32[16,8,128]{2,1,0:T(8,128)}, f32[16,8,128]{2,1,0:T(8,128)S(1)}, u32[]{:S(2)}, u32[]{:S(2)}) %collective-permute-start.5) | collective-permute-done | bytes 65568 | tf_op jit(solution)/shard_map/ppermute | solution.py:820
  69.7 0.0 all-to-all-done.7.incoming
  69.7 10.9 %deposit.1 = (f32[2,128,128]{2,1,0:T(8,128)S(1)}, f32[2,8,128]{2,1,0:T(8,128)S(1)}, f32[2,8,128]{2,1,0:T(8,128)S(1)}) custom-call(bf16[128,40,128]{2,1,0:T(8,128)(2,1)S(1)} %all-to-all-done.7.incoming), custom_call_target="tpu_custom_call" | custom-call | tf_op jit(solution)/shard_map/deposit/pallas_call | solution.py:270
  80.5 1.3 collective-permute-start.9
  81.8 4.0 %collective-permute-start.8 = (f32[2,128,128]{2,1,0:T(8,128)S(1)}, f32[2,128,128]{2,1,0:T(8,128)S(1)}, u32[]{:S(2)}, u32[]{:S(2)}) collective-permute-start(f32[2,128,128]{2,1,0:T(8,128)S(1)} %get-tuple-element.92.heat_own), channel_id=1, source_target_pairs={{0,1},{1,2},{2,3},{3,4},{4,5},{5,6},{6,7},{7,8},{8,9},{9,10},{10,1... | collective-permute-start | bytes 393224 | tf_op jit(solution)/shard_map/ppermute | solution.py:820
  85.8 4.5 %collective-permute-start.10 = (f32[2,8,128]{2,1,0:T(8,128)S(1)}, f32[2,8,128]{2,1,0:T(8,128)S(1)}, u32[]{:S(2)}, u32[]{:S(2)}) collective-permute-start(f32[2,8,128]{2,1,0:T(8,128)S(1)} %get-tuple-element.93), channel_id=1, source_target_pairs={{0,16},{16,32},{32,48},{48,64},{64,80},{80,96},{96,112},{1,17},{17... | collective-permute-start | bytes 24584 | tf_op jit(solution)/shard_map/ppermute | solution.py:820
  90.4 0.0 collective-permute-done.6.low
  90.4 1.9 collective-permute-start.11
  92.3 3.0 %collective-permute-done.11.heat_right = f32[2,8,128]{2,1,0:T(8,128)S(1)} collective-permute-done((f32[2,8,128]{2,1,0:T(8,128)S(1)}, f32[2,8,128]{2,1,0:T(8,128)S(1)}, u32[]{:S(2)}, u32[]{:S(2)}) %collective-permute-start.11) | collective-permute-done | bytes 8224 | tf_op jit(solution)/shard_map/ppermute | solution.py:820
  95.3 6.0 %heated.1 = (f32[2,20,18,8,128]{4,3,2,1,0:T(8,128)}, f32[128,4,128]{2,1,0:T(4,128)}, f32[40,8,128]{2,1,0:T(8,128)S(1)}, f32[40,8,128]{2,1,0:T(8,128)S(1)}) custom-call(f32[4]{0:T(128)S(1)} %add_convert_fusion.inside, f32[2,8,16,8,128]{4,3,2,1,0:T(8,128)S(1)} %get-tuple-element.86.own, f32[192,8,128]{2,1,0:T(8,128)S(1)} %collective-permute-done.6.low, ...), custom_call_target="tpu_custom_call" | custom-call | tf_op jit(solution)/shard_map/heated/pallas_call | solution.py:516
  101.3 11.8 %all-to-all-start.8 = ((f32[128,4,128]{2,1,0:T(4,128)}), f32[128,4,128]{2,1,0:T(4,128)S(1)}, u32[]{:S(2)}, u32[]{:S(2)}) async-start(f32[128,4,128]{2,1,0:T(4,128)} %get-tuple-element.99), calls=%async_computation.8 | async-start | bytes 524288 | tf_op jit(solution)/shard_map/all_to_all | solution.py:814
  113.2 3.5 %collective-permute-start.12 = (f32[40,8,128]{2,1,0:T(8,128)S(1)}, f32[40,8,128]{2,1,0:T(8,128)S(1)}, u32[]{:S(2)}, u32[]{:S(2)}) collective-permute-start(f32[40,8,128]{2,1,0:T(8,128)S(1)} %get-tuple-element.97), channel_id=1, source_target_pairs={{0,16},{16,32},{32,48},{48,64},{64,80},{80,96},{96,112},{1,17},{17... | collective-permute-start | bytes 491528 | tf_op jit(solution)/shard_map/ppermute | solution.py:820
  116.7 1.9 collective-permute-start.13
  118.7 0.3 collective-permute-done.12.left
  119.0 4.7 %collective-permute-done.13.right = f32[40,8,128]{2,1,0:T(8,128)S(1)} collective-permute-done((f32[40,8,128]{2,1,0:T(8,128)S(1)}, f32[40,8,128]{2,1,0:T(8,128)S(1)}, u32[]{:S(2)}, u32[]{:S(2)}) %collective-permute-start.13) | collective-permute-done | bytes 163872 | tf_op jit(solution)/shard_map/ppermute | solution.py:820
  123.7 0.8 all-to-all-done.8.parts
  124.4 14.5 %pair_0.1 = (f32[2,20,18,8,128]{4,3,2,1,0:T(8,128)S(1)}, f32[2,20,18,8,128]{4,3,2,1,0:T(8,128)S(1)}, f32[128,4,128]{2,1,0:T(4,128)S(1)}, f32[8,128]{1,0:T(8,128)S(1)}) custom-call(f32[4]{0:T(128)S(1)} %add_convert_fusion.inside, f32[2,20,18,8,128]{4,3,2,1,0:T(8,128)} %get-tuple-element.96.field, f32[40,8,128]{2,1,0:T(8,128)S(1)} %collective-permute-done.12.left, ...), custom_call_target="tpu_custom_call" | custom-call | tf_op jit(solution)/shard_map/pair_0/pallas_call | solution.py:595
  138.9 19.0 %all_to_all.60.parts = f32[128,4,128]{2,1,0:T(4,128)S(1)} all-to-all(f32[128,4,128]{2,1,0:T(4,128)S(1)} %get-tuple-element.102), channel_id=1, replica_groups=mesh['gx'=8,'gy'=16] {'gx','gy'}, dimensions={0} | all-to-all | bytes 524288 | tf_op jit(solution)/shard_map/all_to_all | solution.py:814
  158.0 6.9 %pair_2.1 = (f32[2,20,18,8,128]{4,3,2,1,0:T(8,128)S(1)}, f32[2,20,18,8,128]{4,3,2,1,0:T(8,128)S(1)}, f32[128,4,128]{2,1,0:T(4,128)S(1)}, f32[8,128]{1,0:T(8,128)S(1)}) custom-call(f32[4]{0:T(128)S(1)} %add_convert_fusion.inside, f32[2,20,18,8,128]{4,3,2,1,0:T(8,128)S(1)} %get-tuple-element.100.field, f32[2,20,18,8,128]{4,3,2,1,0:T(8,128)S(1)} %get-tuple-element.101.changes, ...), custom_call_target="tpu_custom_call" | custom-call | tf_op jit(solution)/shard_map/pair_2/pallas_call | solution.py:595
  164.9 15.2 %all_to_all.61.parts = f32[128,4,128]{2,1,0:T(4,128)S(1)} all-to-all(f32[128,4,128]{2,1,0:T(4,128)S(1)} %get-tuple-element.106), channel_id=1, replica_groups=mesh['gx'=8,'gy'=16] {'gx','gy'}, dimensions={0} | all-to-all | bytes 524288 | tf_op jit(solution)/shard_map/all_to_all | solution.py:814
  180.2 4.2 %last_pair.1 = (f32[2,8,16,8,128]{4,3,2,1,0:T(8,128)S(1)}, f32[128,4,128]{2,1,0:T(4,128)}, f32[8,128]{1,0:T(8,128)S(1)}) custom-call(f32[4]{0:T(128)S(1)} %add_convert_fusion.inside, f32[2,20,18,8,128]{4,3,2,1,0:T(8,128)S(1)} %get-tuple-element.104.field, f32[2,20,18,8,128]{4,3,2,1,0:T(8,128)S(1)} %get-tuple-element.105.changes, ...), custom_call_target="tpu_custom_call" | custom-call | tf_op jit(solution)/shard_map/last_pair/pallas_call | solution.py:655
  184.3 4.3 %all-to-all-start.11 = ((f32[128,4,128]{2,1,0:T(4,128)}), f32[128,4,128]{2,1,0:T(4,128)S(1)}, u32[]{:S(2)}, u32[]{:S(2)}) async-start(f32[128,4,128]{2,1,0:T(4,128)} %get-tuple-element.110), calls=%async_computation.11 | async-start | bytes 524288 | tf_op jit(solution)/shard_map/all_to_all | solution.py:814
  188.6 11.4 %all-to-all-done.11.sums = f32[128,4,128]{2,1,0:T(4,128)S(1)} async-done(((f32[128,4,128]{2,1,0:T(4,128)}), f32[128,4,128]{2,1,0:T(4,128)S(1)}, u32[]{:S(2)}, u32[]{:S(2)}) %all-to-all-start.11) | async-done | bytes 262176 | tf_op jit(solution)/shard_map/all_to_all | solution.py:814
  200.0 5.4 %update.3 = (f32[16,16,8,128]{3,2,1,0:T(8,128)}, s32[1]{0:T(128)}) custom-call(f32[128,4,128]{2,1,0:T(4,128)S(1)} %all-to-all-done.11.sums, f32[2,8,16,8,128]{4,3,2,1,0:T(8,128)S(1)} %get-tuple-element.111.field, f32[8,128]{1,0:T(8,128)S(1)} %get-tuple-element.112.status), custom_call_target="tpu_custom_call" | custom-call | tf_op jit(solution)/shard_map/update/pallas_call | solution.py:800
  (27 shorter events, 0.1 us)
Async XLA Ops:
  0.0 35.2 %copy-start = (f32[16,16,8,128]{3,2,1,0:T(8,128)S(1)}, f32[16,16,8,128]{3,2,1,0:T(8,128)}, u32[]{:S(2)}) copy-start(f32[16,16,8,128]{3,2,1,0:T(8,128)} %state) | copy-start | bytes 3145732
  0.0 1.1 copy-start.1
  1.1 0.8 copy-start.2
  2.0 0.7 copy-start.8
  2.6 15.8 %copy-start.3 = (f32[16,8,128]{2,1,0:T(8,128)S(1)}, f32[16,8,128]{2,1,0:T(8,128)}, u32[]{:S(2)}) copy-start(f32[16,8,128]{2,1,0:T(8,128)} %own.1) | copy-start | bytes 196612
  2.6 40.9 %copy-start.4 = (f32[16,512]{1,0:T(8,128)S(1)}, f32[16,512]{1,0:T(8,128)}, u32[]{:S(2)}) copy-start(f32[16,512]{1,0:T(8,128)} %noise.1) | copy-start | bytes 98308
  2.6 40.9 %copy-start.5 = (s32[512]{0:T(512)S(1)}, s32[512]{0:T(512)}, u32[]{:S(2)}) copy-start(s32[512]{0:T(512)} %param.16) | copy-start | bytes 6148
  2.6 40.9 %copy-start.6 = (f32[512]{0:T(512)S(1)}, f32[512]{0:T(512)}, u32[]{:S(2)}) copy-start(f32[512]{0:T(512)} %param.17) | copy-start | bytes 6148
  2.6 40.9 %copy-start.7 = (f32[512]{0:T(512)S(1)}, f32[512]{0:T(512)}, u32[]{:S(2)}) copy-start(f32[512]{0:T(512)} %param.18) | copy-start | bytes 6148
  6.9 62.8 %all-to-all-start.7 = ((bf16[128,40,128]{2,1,0:T(8,128)(2,1)}), bf16[128,40,128]{2,1,0:T(8,128)(2,1)S(1)}, u32[]{:S(2)}, u32[]{:S(2)}) async-start(bf16[128,40,128]{2,1,0:T(8,128)(2,1)} %pack.1), calls=%async_computation.7 | async-start | bytes 2621440 | tf_op jit(solution)/shard_map/all_to_all | solution.py:814
  18.4 14.2 %collective-permute-start = (f32[16,8,128]{2,1,0:T(8,128)S(1)}, f32[16,8,128]{2,1,0:T(8,128)S(1)}, u32[]{:S(2)}, u32[]{:S(2)}) collective-permute-start(f32[16,8,128]{2,1,0:T(8,128)S(1)} %copy-done.3), channel_id=1, source_target_pairs={{0,16},{16,32},{32,48},{48,64},{64,80},{80,96},{96,112},{1,17},{17... | collective-permute-start | bytes 196616 | tf_op jit(solution)/shard_map/ppermute | solution.py:820
  21.9 13.2 %collective-permute-start.1 = (f32[16,8,128]{2,1,0:T(8,128)S(1)}, f32[16,8,128]{2,1,0:T(8,128)S(1)}, u32[]{:S(2)}, u32[]{:S(2)}) collective-permute-start(f32[16,8,128]{2,1,0:T(8,128)S(1)} %copy-done.3), channel_id=1, source_target_pairs={{16,0},{32,16},{48,32},{64,48},{80,64},{96,80},{112,96},{17,1},{33... | collective-permute-start | bytes 196616 | tf_op jit(solution)/shard_map/ppermute | solution.py:820
  37.0 0.6 copy-start.10
  37.6 3.3 %copy-start.9 = (f32[16,8,128]{2,1,0:T(8,128)}, f32[16,8,128]{2,1,0:T(8,128)S(1)}, u32[]{:S(2)}) copy-start(f32[16,8,128]{2,1,0:T(8,128)S(1)} %get-tuple-element.82) | copy-start | bytes 196612
  37.6 52.8 %collective-permute-start.6 = (f32[192,8,128]{2,1,0:T(8,128)}, f32[192,8,128]{2,1,0:T(8,128)S(1)}, u32[]{:S(2)}, u32[]{:S(2)}) collective-permute-start(f32[192,8,128]{2,1,0:T(8,128)} %get-tuple-element.87), channel_id=1, source_target_pairs={{0,1},{1,2},{2,3},{3,4},{4,5},{5,6},{6,7},{7,8},{8,9},{9,10},{10,1... | collective-permute-start | bytes 2359304 | tf_op jit(solution)/shard_map/ppermute | solution.py:820
  40.9 51.4 %collective-permute-start.7 = (f32[192,8,128]{2,1,0:T(8,128)}, f32[192,8,128]{2,1,0:T(8,128)}, u32[]{:S(2)}, u32[]{:S(2)}) collective-permute-start(f32[192,8,128]{2,1,0:T(8,128)} %get-tuple-element.88), channel_id=1, source_target_pairs={{1,0},{2,1},{3,2},{4,3},{5,4},{6,5},{7,6},{8,7},{9,8},{10,9},{11,1... | collective-permute-start | bytes 2359304 | tf_op jit(solution)/shard_map/ppermute | solution.py:820
  42.2 13.2 %collective-permute-start.3 = (f32[18,8,128]{2,1,0:T(8,128)S(1)}, f32[18,8,128]{2,1,0:T(8,128)S(1)}, u32[]{:S(2)}, u32[]{:S(2)}) collective-permute-start(f32[18,8,128]{2,1,0:T(8,128)S(1)} %strip.1.own), channel_id=1, source_target_pairs={{1,0},{2,1},{3,2},{4,3},{5,4},{6,5},{7,6},{8,7},{9,8},{10,9},{11,1... | collective-permute-start | bytes 221192 | tf_op jit(solution)/shard_map/ppermute | solution.py:820
  45.9 11.5 %collective-permute-start.2 = (f32[18,8,128]{2,1,0:T(8,128)S(1)}, f32[18,8,128]{2,1,0:T(8,128)S(1)}, u32[]{:S(2)}, u32[]{:S(2)}) collective-permute-start(f32[18,8,128]{2,1,0:T(8,128)S(1)} %strip.1.own), channel_id=1, source_target_pairs={{0,1},{1,2},{2,3},{3,4},{4,5},{5,6},{6,7},{7,8},{8,9},{9,10},{10,1... | collective-permute-start | bytes 221192 | tf_op jit(solution)/shard_map/ppermute | solution.py:820
  50.5 10.9 %collective-permute-start.4 = (f32[16,8,128]{2,1,0:T(8,128)}, f32[16,8,128]{2,1,0:T(8,128)S(1)}, u32[]{:S(2)}, u32[]{:S(2)}) collective-permute-start(f32[16,8,128]{2,1,0:T(8,128)} %copy-done.10), channel_id=1, source_target_pairs={{0,16},{16,32},{32,48},{48,64},{64,80},{80,96},{96,112},{1,17},{17... | collective-permute-start | bytes 196616 | tf_op jit(solution)/shard_map/ppermute | solution.py:820
  55.3 14.3 %collective-permute-start.5 = (f32[16,8,128]{2,1,0:T(8,128)}, f32[16,8,128]{2,1,0:T(8,128)S(1)}, u32[]{:S(2)}, u32[]{:S(2)}) collective-permute-start(f32[16,8,128]{2,1,0:T(8,128)} %copy-done.9), channel_id=1, source_target_pairs={{16,0},{32,16},{48,32},{64,48},{80,64},{96,80},{112,96},{17,1},{33... | collective-permute-start | bytes 196616 | tf_op jit(solution)/shard_map/ppermute | solution.py:820
  80.5 14.8 %collective-permute-start.9 = (f32[2,128,128]{2,1,0:T(8,128)S(1)}, f32[2,128,128]{2,1,0:T(8,128)S(1)}, u32[]{:S(2)}, u32[]{:S(2)}) collective-permute-start(f32[2,128,128]{2,1,0:T(8,128)S(1)} %get-tuple-element.92.heat_own), channel_id=1, source_target_pairs={{1,0},{2,1},{3,2},{4,3},{5,4},{6,5},{7,6},{8,7},{9,8},{10,9},{11,1... | collective-permute-start | bytes 393224 | tf_op jit(solution)/shard_map/ppermute | solution.py:820
  81.8 13.5 %collective-permute-start.8 = (f32[2,128,128]{2,1,0:T(8,128)S(1)}, f32[2,128,128]{2,1,0:T(8,128)S(1)}, u32[]{:S(2)}, u32[]{:S(2)}) collective-permute-start(f32[2,128,128]{2,1,0:T(8,128)S(1)} %get-tuple-element.92.heat_own), channel_id=1, source_target_pairs={{0,1},{1,2},{2,3},{3,4},{4,5},{5,6},{6,7},{7,8},{8,9},{9,10},{10,1... | collective-permute-start | bytes 393224 | tf_op jit(solution)/shard_map/ppermute | solution.py:820
  85.8 6.5 %collective-permute-start.10 = (f32[2,8,128]{2,1,0:T(8,128)S(1)}, f32[2,8,128]{2,1,0:T(8,128)S(1)}, u32[]{:S(2)}, u32[]{:S(2)}) collective-permute-start(f32[2,8,128]{2,1,0:T(8,128)S(1)} %get-tuple-element.93), channel_id=1, source_target_pairs={{0,16},{16,32},{32,48},{48,64},{64,80},{80,96},{96,112},{1,17},{17... | collective-permute-start | bytes 24584 | tf_op jit(solution)/shard_map/ppermute | solution.py:820
  90.4 5.0 %collective-permute-start.11 = (f32[2,8,128]{2,1,0:T(8,128)S(1)}, f32[2,8,128]{2,1,0:T(8,128)S(1)}, u32[]{:S(2)}, u32[]{:S(2)}) collective-permute-start(f32[2,8,128]{2,1,0:T(8,128)S(1)} %get-tuple-element.94), channel_id=1, source_target_pairs={{16,0},{32,16},{48,32},{64,48},{80,64},{96,80},{112,96},{17,1},{33... | collective-permute-start | bytes 24584 | tf_op jit(solution)/shard_map/ppermute | solution.py:820
  101.3 23.1 %all-to-all-start.8 = ((f32[128,4,128]{2,1,0:T(4,128)}), f32[128,4,128]{2,1,0:T(4,128)S(1)}, u32[]{:S(2)}, u32[]{:S(2)}) async-start(f32[128,4,128]{2,1,0:T(4,128)} %get-tuple-element.99), calls=%async_computation.8 | async-start | bytes 524288 | tf_op jit(solution)/shard_map/all_to_all | solution.py:814
  113.2 5.8 %collective-permute-start.12 = (f32[40,8,128]{2,1,0:T(8,128)S(1)}, f32[40,8,128]{2,1,0:T(8,128)S(1)}, u32[]{:S(2)}, u32[]{:S(2)}) collective-permute-start(f32[40,8,128]{2,1,0:T(8,128)S(1)} %get-tuple-element.97), channel_id=1, source_target_pairs={{0,16},{16,32},{32,48},{48,64},{64,80},{80,96},{96,112},{1,17},{17... | collective-permute-start | bytes 491528 | tf_op jit(solution)/shard_map/ppermute | solution.py:820
  116.7 6.9 %collective-permute-start.13 = (f32[40,8,128]{2,1,0:T(8,128)S(1)}, f32[40,8,128]{2,1,0:T(8,128)S(1)}, u32[]{:S(2)}, u32[]{:S(2)}) collective-permute-start(f32[40,8,128]{2,1,0:T(8,128)S(1)} %get-tuple-element.98), channel_id=1, source_target_pairs={{16,0},{32,16},{48,32},{64,48},{80,64},{96,80},{112,96},{17,1},{33... | collective-permute-start | bytes 491528 | tf_op jit(solution)/shard_map/ppermute | solution.py:820
  124.4 33.6 %copy-start.11 = (f32[2,20,18,8,128]{4,3,2,1,0:T(8,128)S(1)}, f32[2,20,18,8,128]{4,3,2,1,0:T(8,128)}, u32[]{:S(2)}) copy-start(f32[2,20,18,8,128]{4,3,2,1,0:T(8,128)} %coefs.1.coef) | copy-start | bytes 8847364
  158.0 22.2 %copy-start.13 = (f32[16,8,128]{2,1,0:T(8,128)S(1)}, f32[16,8,128]{2,1,0:T(8,128)}, u32[]{:S(2)}) copy-start(f32[16,8,128]{2,1,0:T(8,128)} %get-tuple-element.109.data) | copy-start | bytes 196612
  184.3 15.7 %all-to-all-start.11 = ((f32[128,4,128]{2,1,0:T(4,128)}), f32[128,4,128]{2,1,0:T(4,128)S(1)}, u32[]{:S(2)}, u32[]{:S(2)}) async-start(f32[128,4,128]{2,1,0:T(4,128)} %get-tuple-element.110), calls=%async_computation.11 | async-start | bytes 524288 | tf_op jit(solution)/shard_map/all_to_all | solution.py:814

commit v6 on v3

--- a/solution.py
+++ b/solution.py
@@ -38,7 +38,15 @@
     return lax.broadcasted_iota(jnp.int32, (CY, CX), 0)
 
 
-def pack_kernel(owner, heat, voxel, out, wide, high, low, inverse):
+def pack_kernel(owner_far, heat_far, voxel_far, out, owner, heat, voxel, wide, high, low, inverse, sems):
+    copies = [
+        pltpu.make_async_copy(far, near, sems.at[i])
+        for i, (far, near) in enumerate(
+            ((owner_far, owner), (heat_far, heat), (voxel_far, voxel))
+        )
+    ]
+    for copy in copies:
+        copy.start()
     blocks = owner.shape[0]
     devices = out.shape[0]
 
@@ -47,6 +55,7 @@
         return carry
 
     lax.fori_loop(0, devices * CAP, clear, 0, unroll=16)
+    copies[0].wait()
 
     def place(b, carry):
         base = owner[b] * CAP
@@ -55,6 +64,8 @@
         return carry
 
     lax.fori_loop(0, blocks, place, 0, unroll=8)
+    copies[1].wait()
+    copies[2].wait()
 
     def widen(m, carry):
         wide[m, 0:blocks, :] = heat[m].astype(F32)
@@ -104,13 +115,17 @@
     return pl.pallas_call(
         pack_kernel,
         out_shape=jax.ShapeDtypeStruct((devices, ROWS, CX), BF16),
-        in_specs=[pl.BlockSpec(memory_space=pltpu.SMEM), vspec(), vspec()],
+        in_specs=[pl.BlockSpec(memory_space=pl.ANY)] * 3,
         out_specs=vspec(),
         scratch_shapes=[
+            pltpu.SMEM((blocks,), jnp.int32),
+            VM((M, blocks, CX), BF16),
+            VM((blocks, CX), jnp.int32),
             VM((M, blocks + 8, CX), F32),
             VM((blocks + 8, CX), F32),
             VM((blocks + 8, CX), F32),
             pltpu.SMEM((devices * CAP,), jnp.int32),
+            pltpu.SemaphoreType.DMA((3,)),
         ],
         compiler_params=params(),
         name="pack",
@@ -122,8 +137,9 @@
 XT = CX // 8 + 2
 ZG = NZ // 2
 TOLERANCE = 1e-6
-OWN = jax.ShapeDtypeStruct((2, CY, XT - 2, 8, CX), F32)
-WIDE = jax.ShapeDtypeStruct((2, YS, XT, 8, CX), F32)
+OWN = jax.ShapeDtypeStruct((2, CY, CX, CX), F32)
+XS = 8 * XT
+WIDE = jax.ShapeDtypeStruct((2, YS, XS, CX), F32)
 EDGE = 2 * HALO * (XT - 2)
 SIDE = 2 * YS
 
@@ -138,8 +154,9 @@
             parts = [
                 state[m0 : m0 + 8, 2 * group + zi, y, :] for group in range(ZG) for m0 in (0, 8)
             ]
-            turned = (0.5 * jnp.concatenate(parts, axis=0)).T.reshape(XT - 2, 8, CX)
+            turned = (0.5 * jnp.concatenate(parts, axis=0)).T
             own[zi, y] = turned
+            turned = turned.reshape(XT - 2, 8, CX)
             if y >= CY - HALO:
                 at = (zi * HALO + y - (CY - HALO)) * (XT - 2)
                 to_high[at : at + XT - 2] = turned
@@ -167,7 +184,7 @@
                 if y < HALO:
                     part = low[(zi * HALO + y) * (XT - 2) + t]
                 elif y < HALO + CY:
-                    part = own[zi, y - HALO, t]
+                    part = own[zi, y - HALO, 8 * t : 8 * t + 8, :]
                 else:
                     part = high[(zi * HALO + y - HALO - CY) * (XT - 2) + t]
                 out[zi * YS + y] = part
@@ -203,7 +220,7 @@
             part = jnp.dot(
                 strips[g], hot, precision=lax.Precision.HIGHEST, preferred_element_type=F32
             )
-            out[zi, yy] = part.reshape(XT, 8, CX)
+            out[zi, yy] = part
 
     for y in range(HALO):
         put(0, y + CY - HALO, y)
@@ -226,7 +243,7 @@
 
 def deposit_kernel(incoming, out, total):
     sources = incoming.shape[0]
-    group = 4
+    group = 32
     place = lax.broadcasted_iota(jnp.int32, (CX, CX), 0).astype(F32).astype(BF16)
     zero = jnp.zeros((M, CX), BF16)
     total[...] = jnp.zeros_like(total)
@@ -290,12 +307,6 @@
     )(low, own, high)
 
 
-def columns_peak(value):
-    for shift in (4, 2, 1):
-        value = jnp.maximum(value, pltpu.roll(value, shift, axis=0))
-    return value
-
-
 def whole_peak(value):
     return jnp.broadcast_to(jnp.max(value, axis=(0, 1), keepdims=True), (8, CX))
 
@@ -304,22 +315,33 @@
     return SHARE / (12.0 * peak + COOL)
 
 
-def conductance(field, coef, zi, y, t):
-    u = field[zi, y, t]
-    c = coef[zi, y, t]
-    return u, c + c * (u * u)
-
-
-def own_row(y):
-    return jnp.where((y >= HALO) & (y < HALO + CY), 1.0, 0.0)
-
-
-def masks(inside, y):
-    kept = jnp.where(y < HALO, inside[2], jnp.where(y >= HALO + CY, inside[3], 1.0))
-    return [kept * inside[0]] + [kept] * (XT - 2) + [kept * inside[1]]
-
-
-def sweep(field, coef, above, below_h, first, end, emit, carry):
+def tile(t):
+    return slice(8 * t, 8 * t + 8)
+
+
+def half_conductance(c, u):
+    return c + c * (u * u)
+
+
+def segments(inside, first, end):
+    parts = []
+    if first < HALO:
+        parts.append((first, HALO, False, inside[2]))
+    parts.append((max(first, HALO), min(end, HALO + CY), True, None))
+    if end > HALO + CY:
+        parts.append((HALO + CY, end, False, inside[3]))
+    return parts
+
+
+def mask_of(inside, row_mask, t):
+    if t == 0:
+        return inside[0] if row_mask is None else inside[0] * row_mask
+    if t == XT - 1:
+        return inside[1] if row_mask is None else inside[1] * row_mask
+    return row_mask
+
+
+def sweep(field, half, above, inside, first, end, emit, carry):
     lane = lanes()
     row = rows()
     last_row = row == 7
@@ -329,44 +351,33 @@
 
     for zi in range(2):
         for t in range(XT):
-            u, h = conductance(field, coef, zi, first - 1, t)
-            v, g = conductance(field, coef, zi, first, t)
-            above[zi, t] = (h + g) * (v - u)
-            below_h[zi, t] = g
-
-    def line(y, state):
-        def load(t):
-            us = [field[zi, y, t] for zi in range(2)]
-            hs = [below_h[zi, t] for zi in range(2)]
-            return (
-                us,
-                hs,
-                [pltpu.roll(a, 7, axis=0) for a in us],
-                [pltpu.roll(a, 7, axis=0) for a in hs],
+            s = tile(t)
+            above[zi, t] = (half[zi, first - 1, s, :] + half[zi, first, s, :]) * (
+                field[zi, first, s, :] - field[zi, first - 1, s, :]
             )
 
-        us, hs, ru, rh = load(0)
+    def line(own, row_mask, y, state):
         carried = [jnp.zeros((8, CX), F32)] * 2
         for t in range(XT):
-            if t < XT - 1:
-                after = load(t + 1)
-                next_u = [jnp.where(last_row, after[2][z], ru[z]) for z in range(2)]
-                next_h = [jnp.where(last_row, after[3][z], rh[z]) for z in range(2)]
-            else:
-                next_u = [jnp.where(last_row, us[z], ru[z]) for z in range(2)]
-                next_h = rh
+            s = tile(t)
+            us = [field[zi, y, s, :] for zi in range(2)]
+            hs = [half[zi, y, s, :] for zi in range(2)]
             change = []
             for zi in range(2):
                 u, h = us[zi], hs[zi]
-                along = (h + next_h[zi]) * (next_u[zi] - u)
+                if t < XT - 1:
+                    after = slice(8 * t + 1, 8 * t + 9)
+                    u_after, h_after = field[zi, y, after, :], half[zi, y, after, :]
+                else:
+                    u_after = jnp.where(last_row, u, pltpu.roll(u, 7, axis=0))
+                    h_after = pltpu.roll(h, 7, axis=0)
+                along = (h + h_after) * (u_after - u)
                 turned = pltpu.roll(along, 1, axis=0)
                 total = along - jnp.where(first_row, carried[zi], turned)
                 carried[zi] = turned
-                v, g = conductance(field, coef, zi, y + 1, t)
-                across = (h + g) * (v - u)
+                across = (h + half[zi, y + 1, s, :]) * (field[zi, y + 1, s, :] - u)
                 total = total + (across - above[zi, t])
                 above[zi, t] = across
-                below_h[zi, t] = g
                 change.append(total)
             within = (hs[0] + hs[1]) * (us[1] - us[0])
             between = (hs[1] + pltpu.roll(hs[0], CX - M, axis=1)) * (
@@ -375,40 +386,36 @@
             between = jnp.where(inner_lane, between, 0.0)
             change[0] = change[0] + (within - pltpu.roll(between, M, axis=1)) - cooling * us[0]
             change[1] = change[1] + (between - within)
-            state = emit(y, t, us, change, state)
-            if t < XT - 1:
-                us, hs, ru, rh = after
+            state = emit(y, t, us, change, own, mask_of(inside, row_mask, t), state)
         return state
 
-    return lax.fori_loop(first, end, line, carry)
-
-
-def advance(field, coef, above, below_h, inside, step, first, end, put):
-    def emit(y, t, us, change, peak):
-        part = masks(inside, y)[t] * step
-        own = own_row(y)
+    for start, stop, own, row_mask in segments(inside, first, end):
+        carry = lax.fori_loop(start, stop, functools.partial(line, own, row_mask), carry)
+    return carry
+
+
+def advance(field, half, coef, above, inside, step, first, end, put):
+    def emit(y, t, us, change, own, mask, peak):
+        part = step if mask is None else step * mask
         for zi in range(2):
             value = us[zi] + part * change[zi]
-            put(zi, y, t, value)
-            if 0 < t < XT - 1:
-                c = coef[zi, y, t]
-                peak = jnp.maximum(peak, own * (c + c * (value * value)))
+            after = half_conductance(coef[zi, y, tile(t), :], value)
+            put(zi, y, t, value, after)
+            if own and 0 < t < XT - 1:
+                peak = jnp.maximum(peak, after)
         return peak
 
-    return sweep(field, coef, above, below_h, first, end, emit, jnp.zeros((8, CX), F32))
-
-
-def propose(field, coef, above, below_h, inside, guess, first, end, changes, peak, late, out):
-    def emit(y, t, us, change, best):
-        part = masks(inside, y)[t]
-        own = own_row(y)
+    return sweep(field, half, above, inside, first, end, emit, jnp.zeros((8, CX), F32))
+
+
+def propose(field, half, coef, above, inside, guess, first, end, changes, peak, late, out):
+    def emit(y, t, us, change, own, mask, best):
         for zi in range(2):
-            moved = change[zi] * part
-            changes[zi, y, t] = moved
-            if 0 < t < XT - 1:
-                c = coef[zi, y, t]
-                value = us[zi] + guess * moved
-                rank = own * (c + c * (value * value))
+            moved = change[zi] if mask is None else change[zi] * mask
+            changes[zi, y, tile(t), :] = moved
+            if own and 0 < t < XT - 1:
+                c = coef[zi, y, tile(t), :]
+                rank = half_conductance(c, us[zi] + guess * moved)
                 better = rank > best[0]
                 best = tuple(
                     jnp.where(better, new, old)
@@ -417,35 +424,35 @@
         return best
 
     best = sweep(
-        field, coef, above, below_h, first, end, emit, (jnp.zeros((8, CX), F32),) * 4
-    )
-    for shift in (4, 2, 1):
-        other = tuple(pltpu.roll(part, shift, axis=0) for part in best)
+        field, half, above, inside, first, end, emit, (jnp.zeros((8, CX), F32),) * 4
+    )
+    for shift, axis in ((4, 0), (2, 0), (1, 0), (64, 1), (32, 1)):
+        other = tuple(pltpu.roll(part, shift, axis=axis) for part in best)
         better = other[0] > best[0]
         best = tuple(jnp.where(better, new, old) for new, old in zip(other, best))
-    row = rows()
-    head = jnp.where(lanes() < CX // 2, whole_peak(peak), whole_peak(late))
-    chunk = jnp.where(
-        row == 0, head, jnp.where(row == 1, best[1], jnp.where(row == 2, best[2], best[3]))
-    )[0:4]
-    for d in range(out.shape[0]):
-        out[d] = chunk
+    part = lanes() >> 4
+    chunk = jnp.where(part == 6, whole_peak(peak), whole_peak(late))
+    for place, value in ((2, best[3]), (1, best[2]), (0, best[1])):
+        chunk = jnp.where((part >> 1) == place, value, chunk)
+    for d in range(0, out.shape[0], 8):
+        out[d : d + 8, 0, :] = chunk
 
 
 def agree(parts):
-    lane = lanes()
-    now = jnp.zeros((8, CX), F32)
-    for d in range(0, parts.shape[0], 8):
-        now = jnp.maximum(now, parts[d : d + 8, 0, :])
-    late = whole_peak(jnp.where(lane < CX // 2, 0.0, now))
-    now = whole_peak(jnp.where(lane < CX // 2, now, 0.0))
+    part = lanes() >> 4
+    rows_of = [parts[d : d + 8, 0, :] for d in range(0, parts.shape[0], 8)]
+    most = rows_of[0]
+    for value in rows_of[1:]:
+        most = jnp.maximum(most, value)
+    now = whole_peak(jnp.where(part == 6, most, 0.0))
+    late = whole_peak(jnp.where(part == 7, most, 0.0))
     step = step_of(now)
     then = jnp.zeros((8, CX), F32)
-    for d in range(0, parts.shape[0], 8):
-        value = parts[d : d + 8, 1, :] + step * parts[d : d + 8, 2, :]
-        c = parts[d : d + 8, 3, :]
-        then = jnp.maximum(then, c + c * (value * value))
-    return now, whole_peak(then), late
+    for value in rows_of:
+        moved = pltpu.roll(value, CX - 32, axis=1)
+        c = pltpu.roll(value, CX - 64, axis=1)
+        then = jnp.maximum(then, half_conductance(c, value + step * moved))
+    return now, whole_peak(jnp.where(part < 2, then, 0.0)), late
 
 
 def differs(late, used):
@@ -455,7 +462,7 @@
 def heated_kernel(
     inside, own, low, high, left, right,
     heat_low, heat_own, heat_high, heat_left, heat_right,
-    coef, out, changes, parts, above, below_h,
+    coef, out, changes, parts, half, above,
 ):
     top = lanes() < M
     peak = jnp.zeros((8, CX), F32)
@@ -469,14 +476,15 @@
                 elif t == XT - 1:
                     prior, add = right[zi * YS + yy], heat_right[g, zi]
                 else:
-                    prior, add = tile_of(zi, t - 1), heat[zi, 8 * t - 8 : 8 * t, :]
+                    prior, add = tile_of(zi, t - 1), heat[zi, tile(t - 1), :]
                 if shift:
                     add = pltpu.roll(add, shift, axis=1)
                 value = prior + jnp.where(top, add, 0.0)
-                out[zi, yy, t] = value
+                after = half_conductance(coef[zi, yy, tile(t), :], value)
+                out[zi, yy, tile(t), :] = value
+                half[zi, yy, tile(t), :] = after
                 if g == 1 and 0 < t < XT - 1:
-                    c = coef[zi, yy, t]
-                    peak = jnp.maximum(peak, c + c * (value * value))
+                    peak = jnp.maximum(peak, after)
         return peak
 
     def edge(ref, y):
@@ -485,12 +493,12 @@
     for y in range(HALO):
         row(0, heat_low, edge(low, y), y + CY - HALO, y, peak)
     for y in range(CY):
-        peak = row(1, heat_own, lambda zi, t: own[zi, y, t], y, y + HALO, peak)
+        peak = row(1, heat_own, lambda zi, t: own[zi, y, tile(t), :], y, y + HALO, peak)
     for y in range(HALO):
         row(2, heat_high, edge(high, y), y, y + HALO + CY, peak)
     guess = step_of(whole_peak(peak))
     zero = jnp.zeros((8, CX), F32)
-    propose(out, coef, above, below_h, inside, guess, 1, YS - 1, changes, peak, zero, parts)
+    propose(out, half, coef, above, inside, guess, 1, YS - 1, changes, peak, zero, parts)
 
 
 ROW = (2, XT, 8, CX)
@@ -504,26 +512,27 @@
     operands = [inside, *prior, *halos, *heat, coef]
     return pl.pallas_call(
         heated_kernel,
-        out_shape=[WIDE, WIDE, jax.ShapeDtypeStruct((devices, 4, CX), F32)],
+        out_shape=[WIDE, WIDE, jax.ShapeDtypeStruct((devices, 1, CX), F32)],
         in_specs=[smem()] + [vspec()] * (len(operands) - 1),
         out_specs=[vspec()] * 3,
-        scratch_shapes=[VM(ROW, F32), VM(ROW, F32)],
+        scratch_shapes=[VM(WIDE.shape, F32), VM(ROW, F32)],
         compiler_params=params(),
         name="heated",
     )(*operands)
 
 
-def first_of_pair(field, changes, coef, step, first, end, out):
+def first_of_pair(field, changes, coef, step, first, end, out, half):
     def line(y, peak):
-        own = own_row(y)
         top = jnp.zeros((8, CX), F32)
         for zi in range(2):
             for t in range(XT):
-                value = field[zi, y, t] + step * changes[zi, y, t]
-                out[zi, y, t] = value
+                value = field[zi, y, tile(t), :] + step * changes[zi, y, tile(t), :]
+                after = half_conductance(coef[zi, y, tile(t), :], value)
+                out[zi, y, tile(t), :] = value
+                half[zi, y, tile(t), :] = after
                 if 0 < t < XT - 1:
-                    c = coef[zi, y, t]
-                    top = jnp.maximum(top, c + c * (value * value))
+                    top = jnp.maximum(top, after)
+        own = jnp.where((y >= HALO) & (y < HALO + CY), 1.0, 0.0)
         return jnp.maximum(peak, own * top)
 
     return lax.fori_loop(first, end, line, jnp.zeros((8, CX), F32))
@@ -531,25 +540,28 @@
 
 def pair_kernel(
     number, inside, field, changes, coef, parts, status,
-    out, out_changes, out_parts, out_status, middle, above, below_h,
+    out, out_changes, out_parts, out_status, middle, half, next_half, above,
 ):
     now, then, late = agree(parts)
     bad = status[1:2, :]
     if number:
         bad = jnp.maximum(bad, differs(late[0:1], status[0:1, :]))
     out_status[...] = jnp.where(rows() == 0, then, bad)
-    seen = first_of_pair(field, changes, coef, step_of(now), number + 1, YS - 1 - number, middle)
-
-    def put(zi, y, t, value):
-        out[zi, y, t] = value
+    seen = first_of_pair(
+        field, changes, coef, step_of(now), number + 1, YS - 1 - number, middle, half
+    )
+
+    def put(zi, y, t, value, after):
+        out[zi, y, tile(t), :] = value
+        next_half[zi, y, tile(t), :] = after
 
     step = step_of(then)
     peak = advance(
-        middle, coef, above, below_h, inside, step, number + 2, YS - 2 - number, put
+        middle, half, coef, above, inside, step, number + 2, YS - 2 - number, put
     )
     guess = jnp.minimum(step_of(whole_peak(peak)), 1.2 * step)
     propose(
-        out, coef, above, below_h, inside, guess, number + 3, YS - 3 - number,
+        out, next_half, coef, above, inside, guess, number + 3, YS - 3 - number,
         out_changes, peak, seen, out_parts,
     )
 
@@ -564,7 +576,7 @@
         out_shape=[WIDE, WIDE, jax.ShapeDtypeStruct(parts.shape, F32), STATUS],
         in_specs=[smem()] + [vspec()] * 5,
         out_specs=[vspec()] * 4,
-        scratch_shapes=[VM(WIDE.shape, F32), VM(ROW, F32), VM(ROW, F32)],
+        scratch_shapes=[VM(WIDE.shape, F32)] * 3 + [VM(ROW, F32)],
         compiler_params=params(),
         name=f"pair_{number}",
     )(*operands)
@@ -573,7 +585,7 @@
 def pixel_grams(field, weight, data, flat, late, sums):
     grams = jnp.zeros((M, 2 * M), F32)
     for y in range(CY):
-        seen = 2.0 * field[0, y].reshape(CX, CX).T[0:M, :]
+        seen = 2.0 * field[0, y].T[0:M, :]
         for m in range(M):
             flat[m : m + 1, :] = data[m, y : y + 1, :]
         w = weight[y : y + 1, :]
@@ -592,19 +604,21 @@
 
 def last_kernel(
     inside, field, changes, coef, parts, status, weight, data,
-    out, sums, out_status, middle, above, below_h, flat,
+    out, sums, out_status, middle, half, above, flat,
 ):
     number = SUBSTEPS - 2
     now, then, late = agree(parts)
     bad = jnp.maximum(status[1:2, :], differs(late[0:1], status[0:1, :]))
     out_status[...] = jnp.where(rows() == 0, then, bad)
-    seen = first_of_pair(field, changes, coef, step_of(now), number + 1, YS - 1 - number, middle)
-
-    def put(zi, y, t, value):
+    seen = first_of_pair(
+        field, changes, coef, step_of(now), number + 1, YS - 1 - number, middle, half
+    )
+
+    def put(zi, y, t, value, after):
         if 0 < t < XT - 1:
-            out[zi, y - HALO, t - 1] = value
-
-    advance(middle, coef, above, below_h, inside, step_of(then), HALO, HALO + CY, put)
+            out[zi, y - HALO, tile(t - 1), :] = value
+
+    advance(middle, half, coef, above, inside, step_of(then), HALO, HALO + CY, put)
     pixel_grams(out, weight, data, flat, seen, sums)
 
 
@@ -612,10 +626,10 @@
     operands = [inside, field, changes, coef, parts, status, *pixels]
     return pl.pallas_call(
         last_kernel,
-        out_shape=[OWN, jax.ShapeDtypeStruct(parts.shape, F32), STATUS],
+        out_shape=[OWN, jax.ShapeDtypeStruct((parts.shape[0], 4, CX), F32), STATUS],
         in_specs=[smem()] + [vspec()] * (len(operands) - 1),
         out_specs=[vspec()] * 3,
-        scratch_shapes=[VM(WIDE.shape, F32), VM(ROW, F32), VM(ROW, F32), VM((M, CX), F32)],
+        scratch_shapes=[VM(WIDE.shape, F32)] * 2 + [VM(ROW, F32), VM((M, CX), F32)],
         compiler_params=params(),
         name="last_pair",
     )(*operands)
@@ -624,31 +638,40 @@
 def single_kernel(number, inside, field, coef, peaks, *rest):
     final = number == SUBSTEPS - 1
     if final:
-        weight, data, out, sums, above, below_h, flat = rest
+        weight, data, out, sums, half, above, flat = rest
     else:
-        out, out_peaks, above, below_h = rest
+        out, out_peaks, half, above = rest
     peak = peaks[0]
     for d in range(1, peaks.shape[0]):
         peak = jnp.maximum(peak, peaks[d])
     step = step_of(whole_peak(peak))
 
-    def put(zi, y, t, value):
+    def fill(y, carry):
+        for zi in range(2):
+            half[zi, y] = half_conductance(coef[zi, y], field[zi, y])
+        return carry
+
+    lax.fori_loop(number, YS - number, fill, 0)
+
+    def put(zi, y, t, value, after):
         if not final:
-            out[zi, y, t] = value
+            out[zi, y, tile(t), :] = value
         elif 0 < t < XT - 1:
-            out[zi, y - HALO, t - 1] = value
-
-    peak = advance(field, coef, above, below_h, inside, step, number + 1, YS - 1 - number, put)
+            out[zi, y - HALO, tile(t - 1), :] = value
+
+    peak = advance(field, half, coef, above, inside, step, number + 1, YS - 1 - number, put)
     if final:
         pixel_grams(out, weight, data, flat, jnp.zeros((8, CX), F32), sums)
     else:
-        out_peaks[...] = jnp.broadcast_to(columns_peak(peak)[0:1].reshape(1, 1, CX), out_peaks.shape)
+        peak = whole_peak(peak)
+        for d in range(0, out_peaks.shape[0], 8):
+            out_peaks[d : d + 8, 0, :] = peak
 
 
 def single(number, inside, field, coef, peaks, pixels):
     devices = peaks.shape[0]
     operands = [inside, field, coef, peaks]
-    scratch = [VM(ROW, F32), VM(ROW, F32)]
+    scratch = [VM(WIDE.shape, F32), VM(ROW, F32)]
     if number == SUBSTEPS - 1:
         operands += list(pixels)
         out_shape = [OWN, jax.ShapeDtypeStruct((devices, 4, CX), F32)]
@@ -740,7 +763,7 @@
         for y in range(CY):
             part = lax.dot_general(
                 mixing,
-                field[zi, y].reshape(CX, CX),
+                field[zi, y],
                 NT,
                 precision=lax.Precision.HIGHEST,
                 preferred_element_type=F32,
@@ -788,15 +811,14 @@
 ):
     devices = lax.axis_size("gx") * lax.axis_size("gy")
     pixels = pixel_cell.shape[0]
-    outgoing = pack(owner_tile.reshape(-1), heat_input, voxel_list, devices)
-    incoming = exchange(outgoing)
-
     gx, gy = lax.axis_index("gx"), lax.axis_index("gy")
     inside = jnp.stack(
         [gx > 0, gx < lax.axis_size("gx") - 1, gy > 0, gy < lax.axis_size("gy") - 1]
     ).astype(F32)
     own, turned_c, to_high, to_low = relayout(state_prior, conductivity)
+    own, owner_tile, to_high, to_low = lax.optimization_barrier((own, owner_tile, to_high, to_low))
     low, high = move(to_high, "gy", True), move(to_low, "gy", False)
+    incoming = exchange(pack(owner_tile.reshape(-1), heat_input, voxel_list, devices))
     to_left, to_right = sides(own, turned_c, low, high)
     seen = pixel_sums(
         pixel_cell.reshape(1, pixels),
@@ -832,7 +854,7 @@
 
     def again():
         peak = coef * (1.0 + start * start)
-        peak = jnp.max(peak[:, HALO : HALO + CY, 1 : XT - 1])
+        peak = jnp.max(peak[:, HALO : HALO + CY, 8 : XS - 8])
         peaks = jnp.full((devices, 1, CX), peak)
         field = start
         for number in range(SUBSTEPS):

time: 189 us -> 183 us (0.968)
  Pallas kernels: 52.3 us -> 44.6 us
  blocking collectives: 51.5 us -> 47.3 us
  local copies, waits for them, and re-layouts: 4.86 us -> 8.07 us
  waiting for transfers between devices: 40.5 us -> 43.4 us
    pallas_call x1, Pallas kernels: 10.9 us -> 5.9 us  [deposit(): pl.pallas_call(deposit_kernel, out_shape=jax.ShapeDtypeStruct((2, CX, CX)...]
    all_to_all x3, blocking collectives: 51.5 us -> 47.3 us  [exchange(): return lax.all_to_all(parts, BOTH, split_axis=0, concat_axis=0, tiled=True)]
    unnamed x28 -> x32, local copies, waits for them, and re-layouts: 4.86 us -> 8.07 us
    ppermute x8, waiting for transfers between devices: 29.1 us -> 32.1 us  [move(): return lax.ppermute(part, axis, pairs)]
  transfers between devices with their start and end apart: 10 -> 10, of which waited for: 6 -> 6; matrix products, arithmetic and copies ran while one was open for 0% -> 0% of each run, Pallas kernels for 9% -> 6%
where the time goes in v6:
time: 183 us; the launch traced here: 182 us
  blocking collectives  47.3 us (26%)
  Pallas kernels  44.6 us (24%)
  waiting for transfers between devices  43.4 us (24%)
  starting transfers between devices  37.7 us (21%)
  local copies, waits for them, and re-layouts  8.07 us (4%)
    all_to_all x3, blocking collectives, exchange(): return lax.all_to_all(parts, BOTH, split_axis=0, concat_axis=0, tiled=True)  47.3 us
    ppermute x8, waiting for transfers between devices, move(): return lax.ppermute(part, axis, pairs)  32.1 us
    ppermute x8, starting transfers between devices, move(): return lax.ppermute(part, axis, pairs)  21.7 us
    all_to_all x2, starting transfers between devices, exchange(): return lax.all_to_all(parts, BOTH, split_axis=0, concat_axis=0, tiled=True)  16 us
    pallas_call x2, Pallas kernels, pair(): pl.pallas_call(functools.partial(pair_kernel, number), out_shape=[WIDE, W...  14.5 us
    all_to_all x2, waiting for transfers between devices, exchange(): return lax.all_to_all(parts, BOTH, split_axis=0, concat_axis=0, tiled=True)  11.3 us
    unnamed x32, local copies, waits for them, and re-layouts  8.07 us
    pallas_call x1, Pallas kernels, deposit(): pl.pallas_call(deposit_kernel, out_shape=jax.ShapeDtypeStruct((2, CX, CX)...  5.9 us
  transfers between devices with their start and end apart: 10, of which 6 were waited for; matrix products, arithmetic and copies ran while one was open for 0% of the time, Pallas kernels for 6%

profile of v6, /device:TPU:1, one launch (start us, length us, event | category | flops | bytes accessed | tf_op | source)
XLA Modules:
  0.0 182.3 jit_solution(18175467234160778714)
XLA Ops:
  0.0 1.2 copy-done.3
  1.2 0.8 copy-done.5
  2.1 0.7 relayout.1
  2.8 0.0 copy-start
  2.8 1.0 copy-done
  3.8 0.9 copy-done.12
  4.7 1.3 copy-done.4
  6.0 0.8 copy-done.6
  6.9 0.7 copy-done.11
  7.5 4.2 %pack.1 = bf16[128,40,128]{2,1,0:T(8,128)(2,1)} custom-call(s32[128]{0:T(128)S(1)} %bitcast.12, bf16[16,128,128]{2,1,0:T(8,128)(2,1)S(1)} %copy-done.4, s32[128,128]{1,0:T(8,128)S(1)} %copy-done.6), custom_call_target="tpu_custom_call" | custom-call | tf_op jit(solution)/shard_map/pack/pallas_call | solution.py:115
  11.8 0.0 copy-done.13
  11.8 11.5 %all-to-all-start.7 = ((bf16[128,40,128]{2,1,0:T(8,128)(2,1)}), bf16[128,40,128]{2,1,0:T(8,128)(2,1)S(1)}, u32[]{:S(2)}, u32[]{:S(2)}) async-start(bf16[128,40,128]{2,1,0:T(8,128)(2,1)} %pack.1), calls=%async_computation.7 | async-start | bytes 2621440 | tf_op jit(solution)/shard_map/all_to_all | solution.py:792
  23.3 3.5 %collective-permute-start = (f32[208,8,128]{2,1,0:T(8,128)}, f32[208,8,128]{2,1,0:T(8,128)S(1)}, u32[]{:S(2)}, u32[]{:S(2)}) collective-permute-start(f32[208,8,128]{2,1,0:T(8,128)} %copy-done.13), channel_id=1, source_target_pairs={{0,1},{1,2},{2,3},{3,4},{4,5},{5,6},{6,7},{7,8},{8,9},{9,10},{10,1... | collective-permute-start | bytes 2555912 | tf_op jit(solution)/shard_map/ppermute | solution.py:798
  26.8 1.3 collective-permute-start.1
  28.1 0.0 copy-done.7
  28.1 0.0 copy-done.8
  28.1 0.0 copy-done.9
  28.1 1.7 pixels.1
  29.9 0.1 add_convert_fusion.inside
  30.0 26.9 %collective-permute-done.low = f32[208,8,128]{2,1,0:T(8,128)S(1)} collective-permute-done((f32[208,8,128]{2,1,0:T(8,128)}, f32[208,8,128]{2,1,0:T(8,128)S(1)}, u32[]{:S(2)}, u32[]{:S(2)}) %collective-permute-start) | collective-permute-done | bytes 852000 | tf_op jit(solution)/shard_map/ppermute | solution.py:798
  56.8 2.1 %collective-permute-done.1.high = f32[208,8,128]{2,1,0:T(8,128)S(1)} collective-permute-done((f32[208,8,128]{2,1,0:T(8,128)}, f32[208,8,128]{2,1,0:T(8,128)S(1)}, u32[]{:S(2)}, u32[]{:S(2)}) %collective-permute-start.1) | collective-permute-done | bytes 852000 | tf_op jit(solution)/shard_map/ppermute | solution.py:798
  58.9 1.2 copy-done.1
  60.2 0.0 all-to-all-done.7.incoming
  60.2 3.2 %collective-permute-start.2 = (f32[43,8,128]{2,1,0:T(8,128)S(1)}, f32[43,8,128]{2,1,0:T(8,128)S(1)}, u32[]{:S(2)}, u32[]{:S(2)}) collective-permute-start(f32[43,8,128]{2,1,0:T(8,128)S(1)} %get-tuple-element.86), channel_id=1, source_target_pairs={{0,16},{16,32},{32,48},{48,64},{64,80},{80,96},{96,112},{1,17},{17... | collective-permute-start | bytes 528392 | tf_op jit(solution)/shard_map/ppermute | solution.py:798
  63.3 1.9 %collective-permute-start.3 = (f32[43,8,128]{2,1,0:T(8,128)S(1)}, f32[43,8,128]{2,1,0:T(8,128)S(1)}, u32[]{:S(2)}, u32[]{:S(2)}) collective-permute-start(f32[43,8,128]{2,1,0:T(8,128)S(1)} %get-tuple-element.87), channel_id=1, source_target_pairs={{16,0},{32,16},{48,32},{64,48},{80,64},{96,80},{112,96},{17,1},{33... | collective-permute-start | bytes 528392 | tf_op jit(solution)/shard_map/ppermute | solution.py:798
  65.3 5.9 %deposit.1.own.heat_own = f32[2,128,128]{2,1,0:T(8,128)S(1)} custom-call(bf16[128,40,128]{2,1,0:T(8,128)(2,1)S(1)} %all-to-all-done.7.incoming), custom_call_target="tpu_custom_call" | custom-call | tf_op jit(solution)/shard_map/deposit/pallas_call | solution.py:281
  71.2 0.0 copy-start.2
  71.2 1.4 collective-permute-start.5
  72.6 4.2 %collective-permute-start.4 = (f32[2,128,128]{2,1,0:T(8,128)S(1)}, f32[2,128,128]{2,1,0:T(8,128)S(1)}, u32[]{:S(2)}, u32[]{:S(2)}) collective-permute-start(f32[2,128,128]{2,1,0:T(8,128)S(1)} %deposit.1.own.heat_own), channel_id=1, source_target_pairs={{0,1},{1,2},{2,3},{3,4},{4,5},{5,6},{6,7},{7,8},{8,9},{9,10},{10,1... | collective-permute-start | bytes 393224 | tf_op jit(solution)/shard_map/ppermute | solution.py:798
  76.8 0.7 collective-permute-done.5.high.heat_high
  77.5 1.8 collective-permute-done.4.low.heat_low
  79.3 4.4 %collective-permute-start.6 = (f32[3,2,8,128]{3,2,1,0:T(8,128)S(1)}, f32[3,2,8,128]{3,2,1,0:T(8,128)S(1)}, u32[]{:S(2)}, u32[]{:S(2)}) collective-permute-start(f32[3,2,8,128]{3,2,1,0:T(8,128)S(1)} %get-tuple-element.89), channel_id=1, source_target_pairs={{0,16},{16,32},{32,48},{48,64},{64,80},{80,96},{96,112},{1,17},{17... | collective-permute-start | bytes 73736 | tf_op jit(solution)/shard_map/ppermute | solution.py:798
  83.7 1.9 %collective-permute-start.7 = (f32[3,2,8,128]{3,2,1,0:T(8,128)S(1)}, f32[3,2,8,128]{3,2,1,0:T(8,128)S(1)}, u32[]{:S(2)}, u32[]{:S(2)}) collective-permute-start(f32[3,2,8,128]{3,2,1,0:T(8,128)S(1)} %get-tuple-element.90), channel_id=1, source_target_pairs={{16,0},{32,16},{48,32},{64,48},{80,64},{96,80},{112,96},{17,1},{33... | collective-permute-start | bytes 73736 | tf_op jit(solution)/shard_map/ppermute | solution.py:798
  85.6 0.0 collective-permute-done.2.left
  85.6 0.0 collective-permute-done.3.right
  85.6 2.5 %coefs.1.coef = f32[2,20,144,128]{3,2,1,0:T(8,128)S(1)} custom-call(f32[16,8,128]{2,1,0:T(8,128)S(1)} %get-tuple-element.78.turned_c, f32[208,8,128]{2,1,0:T(8,128)S(1)} %collective-permute-done.low, f32[208,8,128]{2,1,0:T(8,128)S(1)} %collective-permute-done.1.high, f32[43,8,128]{2,1,0:T(8,128)S(1)} %collective-permute-done.2.left, ...), custom_call_target="tpu_custom_call" | custom-call | tf_op jit(solution)/shard_map/coefs/pallas_call | solution.py:234
  88.1 0.0 collective-permute-done.6.heat_left
  88.1 0.7 collective-permute-done.7.heat_right
  88.8 5.4 %heated.1 = (f32[2,20,144,128]{3,2,1,0:T(8,128)S(1)}, f32[2,20,144,128]{3,2,1,0:T(8,128)S(1)}, f32[128,1,128]{2,1,0:T(1,128)S(1)}) custom-call(f32[4]{0:T(128)S(1)} %add_convert_fusion.inside, f32[2,8,128,128]{3,2,1,0:T(8,128)S(1)} %copy-done.2, f32[208,8,128]{2,1,0:T(8,128)S(1)} %collective-permute-done.low, ...), custom_call_target="tpu_custom_call" | custom-call | tf_op jit(solution)/shard_map/heated/pallas_call | solution.py:513
  94.2 19.6 %all_to_all.60.parts = f32[128,1,128]{2,1,0:T(1,128)S(1)} all-to-all(f32[128,1,128]{2,1,0:T(1,128)S(1)} %get-tuple-element.93), channel_id=1, replica_groups=mesh['gx'=8,'gy'=16] {'gx','gy'}, dimensions={0} | all-to-all | bytes 131072 | tf_op jit(solution)/shard_map/all_to_all | solution.py:792
  113.8 8.4 %pair_0.1 = (f32[2,20,144,128]{3,2,1,0:T(8,128)S(1)}, f32[2,20,144,128]{3,2,1,0:T(8,128)S(1)}, f32[128,1,128]{2,1,0:T(1,128)S(1)}, f32[8,128]{1,0:T(8,128)S(1)}) custom-call(f32[4]{0:T(128)S(1)} %add_convert_fusion.inside, f32[2,20,144,128]{3,2,1,0:T(8,128)S(1)} %get-tuple-element.91.field, f32[2,20,144,128]{3,2,1,0:T(8,128)S(1)} %get-tuple-element.92.changes, ...), custom_call_target="tpu_custom_call" | custom-call | tf_op jit(solution)/shard_map/pair_0/pallas_call | solution.py:574
  122.2 13.9 %all_to_all.61.parts = f32[128,1,128]{2,1,0:T(1,128)S(1)} all-to-all(f32[128,1,128]{2,1,0:T(1,128)S(1)} %get-tuple-element.96), channel_id=1, replica_groups=mesh['gx'=8,'gy'=16] {'gx','gy'}, dimensions={0} | all-to-all | bytes 131072 | tf_op jit(solution)/shard_map/all_to_all | solution.py:792
  136.1 6.2 %pair_2.1 = (f32[2,20,144,128]{3,2,1,0:T(8,128)S(1)}, f32[2,20,144,128]{3,2,1,0:T(8,128)S(1)}, f32[128,1,128]{2,1,0:T(1,128)S(1)}, f32[8,128]{1,0:T(8,128)S(1)}) custom-call(f32[4]{0:T(128)S(1)} %add_convert_fusion.inside, f32[2,20,144,128]{3,2,1,0:T(8,128)S(1)} %get-tuple-element.94.field, f32[2,20,144,128]{3,2,1,0:T(8,128)S(1)} %get-tuple-element.95.changes, ...), custom_call_target="tpu_custom_call" | custom-call | tf_op jit(solution)/shard_map/pair_2/pallas_call | solution.py:574
  142.3 13.9 %all_to_all.62.parts = f32[128,1,128]{2,1,0:T(1,128)S(1)} all-to-all(f32[128,1,128]{2,1,0:T(1,128)S(1)} %get-tuple-element.100), channel_id=1, replica_groups=mesh['gx'=8,'gy'=16] {'gx','gy'}, dimensions={0} | all-to-all | bytes 131072 | tf_op jit(solution)/shard_map/all_to_all | solution.py:792
  156.2 4.1 %last_pair.1 = (f32[2,8,128,128]{3,2,1,0:T(8,128)S(1)}, f32[128,4,128]{2,1,0:T(4,128)}, f32[8,128]{1,0:T(8,128)S(1)}) custom-call(f32[4]{0:T(128)S(1)} %add_convert_fusion.inside, f32[2,20,144,128]{3,2,1,0:T(8,128)S(1)} %get-tuple-element.98.field, f32[2,20,144,128]{3,2,1,0:T(8,128)S(1)} %get-tuple-element.99.changes, f32[2,20,144,128]{3,2,1,0:T(8,128)S(1)} %coefs.1.coef, ...), custom_call_target="tpu_custom_call" | custom-call | tf_op jit(solution)/shard_map/last_pair/pallas_call | solution.py:627
  160.3 4.5 %all-to-all-start.11 = ((f32[128,4,128]{2,1,0:T(4,128)}), f32[128,4,128]{2,1,0:T(4,128)S(1)}, u32[]{:S(2)}, u32[]{:S(2)}) async-start(f32[128,4,128]{2,1,0:T(4,128)} %get-tuple-element.104), calls=%async_computation.11 | async-start | bytes 524288 | tf_op jit(solution)/shard_map/all_to_all | solution.py:792
  164.8 11.3 %all-to-all-done.11.sums = f32[128,4,128]{2,1,0:T(4,128)S(1)} async-done(((f32[128,4,128]{2,1,0:T(4,128)}), f32[128,4,128]{2,1,0:T(4,128)S(1)}, u32[]{:S(2)}, u32[]{:S(2)}) %all-to-all-start.11) | async-done | bytes 262176 | tf_op jit(solution)/shard_map/all_to_all | solution.py:792
  176.1 5.4 %update.3 = (f32[16,16,8,128]{3,2,1,0:T(8,128)}, s32[1]{0:T(128)}) custom-call(f32[128,4,128]{2,1,0:T(4,128)S(1)} %all-to-all-done.11.sums, f32[2,8,128,128]{3,2,1,0:T(8,128)S(1)} %get-tuple-element.105.field, f32[8,128]{1,0:T(8,128)S(1)} %get-tuple-element.106.status), custom_call_target="tpu_custom_call" | custom-call | tf_op jit(solution)/shard_map/update/pallas_call | solution.py:778
  (22 shorter events, 0.1 us)
Async XLA Ops:
  0.0 1.2 copy-start.3
  1.2 0.8 copy-start.5
  2.1 26.0 %copy-start.7 = (f32[16,512]{1,0:T(8,128)S(1)}, f32[16,512]{1,0:T(8,128)}, u32[]{:S(2)}) copy-start(f32[16,512]{1,0:T(8,128)} %noise.1) | copy-start | bytes 98308
  2.1 26.0 %copy-start.8 = (s32[512]{0:T(512)S(1)}, s32[512]{0:T(512)}, u32[]{:S(2)}) copy-start(s32[512]{0:T(512)} %param.16) | copy-start | bytes 6148
  2.1 26.1 %copy-start.9 = (f32[512]{0:T(512)S(1)}, f32[512]{0:T(512)}, u32[]{:S(2)}) copy-start(f32[512]{0:T(512)} %param.17) | copy-start | bytes 6148
  2.1 26.1 %copy-start.10 = (f32[512]{0:T(512)S(1)}, f32[512]{0:T(512)}, u32[]{:S(2)}) copy-start(f32[512]{0:T(512)} %param.18) | copy-start | bytes 6148
  2.8 1.0 copy-start
  3.7 0.9 copy-start.12
  4.7 7.1 %copy-start.13 = (f32[208,8,128]{2,1,0:T(8,128)}, f32[208,8,128]{2,1,0:T(8,128)S(1)}, u32[]{:S(2)}) copy-start(f32[208,8,128]{2,1,0:T(8,128)S(1)} %get-tuple-element.79) | copy-start | bytes 2555908
  4.7 1.3 copy-start.4
  6.0 0.8 copy-start.6
  6.9 0.7 copy-start.11
  11.8 48.4 %all-to-all-start.7 = ((bf16[128,40,128]{2,1,0:T(8,128)(2,1)}), bf16[128,40,128]{2,1,0:T(8,128)(2,1)S(1)}, u32[]{:S(2)}, u32[]{:S(2)}) async-start(bf16[128,40,128]{2,1,0:T(8,128)(2,1)} %pack.1), calls=%async_computation.7 | async-start | bytes 2621440 | tf_op jit(solution)/shard_map/all_to_all | solution.py:792
  23.3 33.5 %collective-permute-start = (f32[208,8,128]{2,1,0:T(8,128)}, f32[208,8,128]{2,1,0:T(8,128)S(1)}, u32[]{:S(2)}, u32[]{:S(2)}) collective-permute-start(f32[208,8,128]{2,1,0:T(8,128)} %copy-done.13), channel_id=1, source_target_pairs={{0,1},{1,2},{2,3},{3,4},{4,5},{5,6},{6,7},{7,8},{8,9},{9,10},{10,1... | collective-permute-start | bytes 2555912 | tf_op jit(solution)/shard_map/ppermute | solution.py:798
  26.8 32.1 %collective-permute-start.1 = (f32[208,8,128]{2,1,0:T(8,128)}, f32[208,8,128]{2,1,0:T(8,128)S(1)}, u32[]{:S(2)}, u32[]{:S(2)}) collective-permute-start(f32[208,8,128]{2,1,0:T(8,128)} %copy-done.12), channel_id=1, source_target_pairs={{1,0},{2,1},{3,2},{4,3},{5,4},{6,5},{7,6},{8,7},{9,8},{10,9},{11,1... | collective-permute-start | bytes 2555912 | tf_op jit(solution)/shard_map/ppermute | solution.py:798
  58.9 1.2 copy-start.1
  60.2 25.4 %collective-permute-start.2 = (f32[43,8,128]{2,1,0:T(8,128)S(1)}, f32[43,8,128]{2,1,0:T(8,128)S(1)}, u32[]{:S(2)}, u32[]{:S(2)}) collective-permute-start(f32[43,8,128]{2,1,0:T(8,128)S(1)} %get-tuple-element.86), channel_id=1, source_target_pairs={{0,16},{16,32},{32,48},{48,64},{64,80},{80,96},{96,112},{1,17},{17... | collective-permute-start | bytes 528392 | tf_op jit(solution)/shard_map/ppermute | solution.py:798
  63.3 22.3 %collective-permute-start.3 = (f32[43,8,128]{2,1,0:T(8,128)S(1)}, f32[43,8,128]{2,1,0:T(8,128)S(1)}, u32[]{:S(2)}, u32[]{:S(2)}) collective-permute-start(f32[43,8,128]{2,1,0:T(8,128)S(1)} %get-tuple-element.87), channel_id=1, source_target_pairs={{16,0},{32,16},{48,32},{64,48},{80,64},{96,80},{112,96},{17,1},{33... | collective-permute-start | bytes 528392 | tf_op jit(solution)/shard_map/ppermute | solution.py:798
  71.2 17.6 %copy-start.2 = (f32[2,8,128,128]{3,2,1,0:T(8,128)S(1)}, f32[2,8,128,128]{3,2,1,0:T(8,128)}, u32[]{:S(2)}) copy-start(f32[2,8,128,128]{3,2,1,0:T(8,128)} %copy-done) | copy-start | bytes 3145732
  71.2 6.3 %collective-permute-start.5 = (f32[2,128,128]{2,1,0:T(8,128)S(1)}, f32[2,128,128]{2,1,0:T(8,128)S(1)}, u32[]{:S(2)}, u32[]{:S(2)}) collective-permute-start(f32[2,128,128]{2,1,0:T(8,128)S(1)} %deposit.1.own.heat_own), channel_id=1, source_target_pairs={{1,0},{2,1},{3,2},{4,3},{5,4},{6,5},{7,6},{8,7},{9,8},{10,9},{11,1... | collective-permute-start | bytes 393224 | tf_op jit(solution)/shard_map/ppermute | solution.py:798
  72.6 6.7 %collective-permute-start.4 = (f32[2,128,128]{2,1,0:T(8,128)S(1)}, f32[2,128,128]{2,1,0:T(8,128)S(1)}, u32[]{:S(2)}, u32[]{:S(2)}) collective-permute-start(f32[2,128,128]{2,1,0:T(8,128)S(1)} %deposit.1.own.heat_own), channel_id=1, source_target_pairs={{0,1},{1,2},{2,3},{3,4},{4,5},{5,6},{6,7},{7,8},{8,9},{9,10},{10,1... | collective-permute-start | bytes 393224 | tf_op jit(solution)/shard_map/ppermute | solution.py:798
  79.3 8.8 %collective-permute-start.6 = (f32[3,2,8,128]{3,2,1,0:T(8,128)S(1)}, f32[3,2,8,128]{3,2,1,0:T(8,128)S(1)}, u32[]{:S(2)}, u32[]{:S(2)}) collective-permute-start(f32[3,2,8,128]{3,2,1,0:T(8,128)S(1)} %get-tuple-element.89), channel_id=1, source_target_pairs={{0,16},{16,32},{32,48},{48,64},{64,80},{80,96},{96,112},{1,17},{17... | collective-permute-start | bytes 73736 | tf_op jit(solution)/shard_map/ppermute | solution.py:798
  83.7 5.1 %collective-permute-start.7 = (f32[3,2,8,128]{3,2,1,0:T(8,128)S(1)}, f32[3,2,8,128]{3,2,1,0:T(8,128)S(1)}, u32[]{:S(2)}, u32[]{:S(2)}) collective-permute-start(f32[3,2,8,128]{3,2,1,0:T(8,128)S(1)} %get-tuple-element.90), channel_id=1, source_target_pairs={{16,0},{32,16},{48,32},{64,48},{80,64},{96,80},{112,96},{17,1},{33... | collective-permute-start | bytes 73736 | tf_op jit(solution)/shard_map/ppermute | solution.py:798
  88.1 68.0 %copy-start.14 = (f32[2,20,144,128]{3,2,1,0:T(8,128)}, f32[2,20,144,128]{3,2,1,0:T(8,128)S(1)}, u32[]{:S(2)}) copy-start(f32[2,20,144,128]{3,2,1,0:T(8,128)S(1)} %coefs.1.coef) | copy-start | bytes 8847364
  94.2 28.0 %copy-start.16 = (f32[2,20,144,128]{3,2,1,0:T(8,128)}, f32[2,20,144,128]{3,2,1,0:T(8,128)S(1)}, u32[]{:S(2)}) copy-start(f32[2,20,144,128]{3,2,1,0:T(8,128)S(1)} %get-tuple-element.91.field) | copy-start | bytes 8847364
  160.3 15.8 %all-to-all-start.11 = ((f32[128,4,128]{2,1,0:T(4,128)}), f32[128,4,128]{2,1,0:T(4,128)S(1)}, u32[]{:S(2)}, u32[]{:S(2)}) async-start(f32[128,4,128]{2,1,0:T(4,128)} %get-tuple-element.104), calls=%async_computation.11 | async-start | bytes 524288 | tf_op jit(solution)/shard_map/all_to_all | solution.py:792

commit v7 on v6

--- a/solution.py
+++ b/solution.py
@@ -177,7 +177,7 @@
     )(state, conduct)
 
 
-def side_kernel(own, turned_c, low, high, to_left, to_right):
+def side_kernel(own, turned_c, low, high, heat_low, heat_own, heat_high, to_left, to_right):
     for out, t in ((to_left, 0), (to_right, XT - 3)):
         for zi in range(2):
             for y in range(YS):
@@ -191,54 +191,57 @@
         out[SIDE] = low[EDGE + t]
         out[SIDE + 1] = turned_c[t]
         out[SIDE + 2] = high[EDGE + t]
-
-
-def sides(own, turned_c, low, high):
-    shape = jax.ShapeDtypeStruct((SIDE + 3, 8, CX), F32)
+        for g, heat in enumerate((heat_low, heat_own, heat_high)):
+            for zi in range(2):
+                out[SIDE + 3 + 2 * g + zi] = heat[zi, 8 * t : 8 * t + 8, :]
+
+
+def sides(own, turned_c, low, high, heat_low, heat_own, heat_high):
+    shape = jax.ShapeDtypeStruct((SIDE + 9, 8, CX), F32)
     return pl.pallas_call(
         side_kernel,
         out_shape=[shape, shape],
-        in_specs=[vspec()] * 4,
+        in_specs=[vspec()] * 7,
         out_specs=[vspec()] * 2,
         compiler_params=params(),
         name="sides",
-    )(own, turned_c, low, high)
-
-
-def coef_kernel(turned_c, low, high, left, right, out):
+    )(own, turned_c, low, high, heat_low, heat_own, heat_high)
+
+
+def placed(strip, zi, y0):
     source = lax.broadcasted_iota(jnp.int32, (CX, CX), 0)
     target = lax.broadcasted_iota(jnp.int32, (CX, CX), 1)
-    strips = []
-    for g in range(3):
-        mid = (low[EDGE:], turned_c[...], high[EDGE:])[g].reshape(CX, CX)
-        strips.append(jnp.concatenate([left[SIDE + g], mid, right[SIDE + g]], axis=0))
-
-    def put(g, y0, yy):
-        for zi in range(2):
-            wanted = (2 * (target >> 4) + zi) * CY + y0
-            hot = jnp.where(source == wanted, 1.0, 0.0).astype(F32)
-            part = jnp.dot(
-                strips[g], hot, precision=lax.Precision.HIGHEST, preferred_element_type=F32
-            )
-            out[zi, yy] = part
-
-    for y in range(HALO):
-        put(0, y + CY - HALO, y)
-    for y in range(CY):
-        put(1, y, y + HALO)
-    for y in range(HALO):
-        put(2, y, y + HALO + CY)
-
-
-def coefs(turned_c, low, high, left, right):
+    hot = jnp.where(source == (2 * (target >> 4) + zi) * CY + y0, 1.0, 0.0).astype(F32)
+    return jnp.dot(strip, hot, precision=lax.Precision.HIGHEST, preferred_element_type=F32)
+
+
+def halo_row(g, y0):
+    row = y0 + HALO + (g - 1) * CY
+    return row if 0 <= row < YS else None
+
+
+def coef_kernel(own, low, high, out):
+    strip = jnp.concatenate(
+        [low[EDGE:].reshape(CX, CX), own[...].reshape(CX, CX), high[EDGE:].reshape(CX, CX)], axis=0
+    )
+    for zi in range(2):
+        for y0 in range(CY):
+            part = placed(strip, zi, y0)
+            for g in range(3):
+                row = halo_row(g, y0)
+                if row is not None:
+                    out[zi, row] = part[g * CX : (g + 1) * CX, :]
+
+
+def coefs(own, low, high):
     return pl.pallas_call(
         coef_kernel,
-        out_shape=WIDE,
-        in_specs=[vspec()] * 5,
+        out_shape=jax.ShapeDtypeStruct((2, YS, CX, CX), F32),
+        in_specs=[vspec()] * 3,
         out_specs=vspec(),
         compiler_params=params(),
         name="coefs",
-    )(turned_c, low, high, left, right)
+    )(own, low, high)
 
 
 def deposit_kernel(incoming, out, total):
@@ -287,24 +290,6 @@
         compiler_params=params(),
         name="deposit",
     )(incoming)
-
-
-def heat_side_kernel(low, own, high, to_left, to_right):
-    for g, part in enumerate((low, own, high)):
-        to_left[g] = part[:, 0:8, :]
-        to_right[g] = part[:, CX - 8 :, :]
-
-
-def heat_sides(low, own, high):
-    shape = jax.ShapeDtypeStruct((3, 2, 8, CX), F32)
-    return pl.pallas_call(
-        heat_side_kernel,
-        out_shape=[shape, shape],
-        in_specs=[vspec()] * 3,
-        out_specs=[vspec()] * 2,
-        compiler_params=params(),
-        name="heat_sides",
-    )(low, own, high)
 
 
 def whole_peak(value):
@@ -461,26 +446,43 @@
 
 def heated_kernel(
     inside, own, low, high, left, right,
-    heat_low, heat_own, heat_high, heat_left, heat_right,
-    coef, out, changes, parts, half, above,
+    heat_low, heat_own, heat_high,
+    coef_main, out, coef, changes, parts, half, above,
 ):
     top = lanes() < M
     peak = jnp.zeros((8, CX), F32)
+
+    strip = jnp.concatenate(
+        [side[SIDE + g] for g in range(3) for side in (left, right)], axis=0
+    )
+    for zi in range(2):
+        for y0 in range(CY):
+            part = placed(strip, zi, y0)
+            for g in range(3):
+                at = halo_row(g, y0)
+                if at is not None:
+                    coef[zi, at, tile(0), :] = part[16 * g : 16 * g + 8, :]
+                    coef[zi, at, tile(XT - 1), :] = part[16 * g + 8 : 16 * g + 16, :]
 
     def row(g, heat, tile_of, y0, yy, peak):
         shift = (CX - 16 * y0) % CX
         for zi in range(2):
             for t in range(XT):
                 if t == 0:
-                    prior, add = left[zi * YS + yy], heat_left[g, zi]
+                    prior, add = left[zi * YS + yy], left[SIDE + 3 + 2 * g + zi]
                 elif t == XT - 1:
-                    prior, add = right[zi * YS + yy], heat_right[g, zi]
+                    prior, add = right[zi * YS + yy], right[SIDE + 3 + 2 * g + zi]
                 else:
                     prior, add = tile_of(zi, t - 1), heat[zi, tile(t - 1), :]
                 if shift:
                     add = pltpu.roll(add, shift, axis=1)
                 value = prior + jnp.where(top, add, 0.0)
-                after = half_conductance(coef[zi, yy, tile(t), :], value)
+                if 0 < t < XT - 1:
+                    c = coef_main[zi, yy, tile(t - 1), :]
+                    coef[zi, yy, tile(t), :] = c
+                else:
+                    c = coef[zi, yy, tile(t), :]
+                after = half_conductance(c, value)
                 out[zi, yy, tile(t), :] = value
                 half[zi, yy, tile(t), :] = after
                 if g == 1 and 0 < t < XT - 1:
@@ -512,9 +514,9 @@
     operands = [inside, *prior, *halos, *heat, coef]
     return pl.pallas_call(
         heated_kernel,
-        out_shape=[WIDE, WIDE, jax.ShapeDtypeStruct((devices, 1, CX), F32)],
+        out_shape=[WIDE, WIDE, WIDE, jax.ShapeDtypeStruct((devices, 1, CX), F32)],
         in_specs=[smem()] + [vspec()] * (len(operands) - 1),
-        out_specs=[vspec()] * 3,
+        out_specs=[vspec()] * 4,
         scratch_shapes=[VM(WIDE.shape, F32), VM(ROW, F32)],
         compiler_params=params(),
         name="heated",
@@ -815,33 +817,26 @@
     inside = jnp.stack(
         [gx > 0, gx < lax.axis_size("gx") - 1, gy > 0, gy < lax.axis_size("gy") - 1]
     ).astype(F32)
+    incoming = exchange(pack(owner_tile.reshape(-1), heat_input, voxel_list, devices))
     own, turned_c, to_high, to_low = relayout(state_prior, conductivity)
-    own, owner_tile, to_high, to_low = lax.optimization_barrier((own, owner_tile, to_high, to_low))
     low, high = move(to_high, "gy", True), move(to_low, "gy", False)
-    incoming = exchange(pack(owner_tile.reshape(-1), heat_input, voxel_list, devices))
-    to_left, to_right = sides(own, turned_c, low, high)
     seen = pixel_sums(
         pixel_cell.reshape(1, pixels),
         observed.reshape(1, pixels),
         pixel_variance.reshape(1, pixels),
         pixel_noise,
     )
-    incoming, to_left, to_right, inside, *seen = lax.optimization_barrier(
-        (incoming, to_left, to_right, inside, *seen)
-    )
-    left, right = move(to_right, "gx", True), move(to_left, "gx", False)
-
+    incoming, own, inside, *seen = lax.optimization_barrier((incoming, own, inside, *seen))
     heat = deposit(incoming)
     heat_low, heat_high = move(heat, "gy", True), move(heat, "gy", False)
-    to_left, to_right = heat_sides(heat_low, heat, heat_high)
-    heat_left, heat_right = move(to_right, "gx", True), move(to_left, "gx", False)
-    coef = coefs(turned_c, low, high, left, right)
-    start, changes, parts = heated(
+    to_left, to_right = sides(own, turned_c, low, high, heat_low, heat, heat_high)
+    left, right = move(to_right, "gx", True), move(to_left, "gx", False)
+    start, coef, changes, parts = heated(
         inside,
         (own, low, high),
         (left, right),
-        (heat_low, heat, heat_high, heat_left, heat_right),
-        coef,
+        (heat_low, heat, heat_high),
+        coefs(turned_c, low, high),
         devices,
     )
     field, status = start, jnp.zeros((8, CX), F32)

time: 183 us -> 161 us (0.88)
  waiting for transfers between devices: 43.4 us -> 31.6 us
  starting transfers between devices: 37.7 us -> 31.4 us
  local copies, waits for them, and re-layouts: 8.07 us -> 4.86 us
  blocking collectives: 47.3 us -> 44.9 us
    ppermute x8 -> x6, waiting for transfers between devices: 32.1 us -> 8.46 us  [move(): return lax.ppermute(part, axis, pairs)]
    all_to_all x2, waiting for transfers between devices: 11.3 us -> 23.2 us  [exchange(): return lax.all_to_all(parts, BOTH, split_axis=0, concat_axis=0, tiled=True)]
    ppermute x8 -> x6, starting transfers between devices: 21.7 us -> 15.5 us  [move(): return lax.ppermute(part, axis, pairs)]
    unnamed x32 -> x28, local copies, waits for them, and re-layouts: 8.07 us -> 4.86 us
    all_to_all x3, blocking collectives: 47.3 us -> 44.9 us  [exchange(): return lax.all_to_all(parts, BOTH, split_axis=0, concat_axis=0, tiled=True)]
    pallas_call x3 -> x2, Pallas kernels: 7.91 us -> 8.51 us  [the longest x1 5.91 us: heated(): pl.pallas_call(heated_kernel, out_shape=[WIDE, WIDE, WIDE, jax.ShapeDtype...]
  transfers between devices with their start and end apart: 10 -> 8, of which waited for: 6 -> 6; matrix products, arithmetic and copies ran while one was open for 0% -> 0% of each run, Pallas kernels for 6% -> 8%
where the time goes in v7:
time: 161 us; the launch traced here: 160 us
  Pallas kernels  46.2 us (29%)
  blocking collectives  44.9 us (28%)
  waiting for transfers between devices  31.6 us (20%)
  starting transfers between devices  31.4 us (20%)
  local copies, waits for them, and re-layouts  4.86 us (3%)
    all_to_all x3, blocking collectives, exchange(): return lax.all_to_all(parts, BOTH, split_axis=0, concat_axis=0, tiled=True)  44.9 us
    all_to_all x2, waiting for transfers between devices, exchange(): return lax.all_to_all(parts, BOTH, split_axis=0, concat_axis=0, tiled=True)  23.2 us
    all_to_all x2, starting transfers between devices, exchange(): return lax.all_to_all(parts, BOTH, split_axis=0, concat_axis=0, tiled=True)  16 us
    ppermute x6, starting transfers between devices, move(): return lax.ppermute(part, axis, pairs)  15.5 us
    pallas_call x2, Pallas kernels, pair(): pl.pallas_call(functools.partial(pair_kernel, number), out_shape=[WIDE, W...  14.5 us
    ppermute x6, waiting for transfers between devices, move(): return lax.ppermute(part, axis, pairs)  8.46 us
    pallas_call x1, Pallas kernels, heated(): pl.pallas_call(heated_kernel, out_shape=[WIDE, WIDE, WIDE, jax.ShapeDtype...  5.91 us
    pallas_call x1, Pallas kernels, deposit(): pl.pallas_call(deposit_kernel, out_shape=jax.ShapeDtypeStruct((2, CX, CX)...  5.89 us
  transfers between devices with their start and end apart: 8, of which 6 were waited for; matrix products, arithmetic and copies ran while one was open for 0% of the time, Pallas kernels for 8%

profile of v7, /device:TPU:1, one launch (start us, length us, event | category | flops | bytes accessed | tf_op | source)
XLA Modules:
  0.0 160.2 jit_solution(16587687540761803417)
XLA Ops:
  0.0 1.1 copy-done.4
  1.1 0.8 copy-done.5
  2.0 0.7 copy-done.11
  2.6 0.0 copy-start.10
  2.7 4.2 %pack.1 = bf16[128,40,128]{2,1,0:T(8,128)(2,1)} custom-call(s32[128]{0:T(128)S(1)} %bitcast.12, bf16[16,128,128]{2,1,0:T(8,128)(2,1)S(1)} %copy-done.4, s32[128,128]{1,0:T(8,128)S(1)} %copy-done.5), custom_call_target="tpu_custom_call" | custom-call | tf_op jit(solution)/shard_map/pack/pallas_call | solution.py:115
  6.9 11.5 %all-to-all-start.7 = ((bf16[128,40,128]{2,1,0:T(8,128)(2,1)}), bf16[128,40,128]{2,1,0:T(8,128)(2,1)S(1)}, u32[]{:S(2)}, u32[]{:S(2)}) async-start(bf16[128,40,128]{2,1,0:T(8,128)(2,1)} %pack.1), calls=%async_computation.7 | async-start | bytes 2621440 | tf_op jit(solution)/shard_map/all_to_all | solution.py:794
  18.4 0.0 copy-done.3
  18.4 0.0 copy-done.6
  18.4 1.8 %relayout.1 = (f32[2,8,128,128]{3,2,1,0:T(8,128)S(1)}, f32[16,8,128]{2,1,0:T(8,128)S(1)}, f32[208,8,128]{2,1,0:T(8,128)}, f32[208,8,128]{2,1,0:T(8,128)}) custom-call(f32[16,16,8,128]{3,2,1,0:T(8,128)S(1)} %copy-done.3, f32[16,8,128]{2,1,0:T(8,128)S(1)} %copy-done.6), custom_call_target="tpu_custom_call" | custom-call | tf_op jit(solution)/shard_map/relayout/pallas_call | solution.py:170
  20.2 1.0 copy-done
  21.2 3.5 %collective-permute-start = (f32[208,8,128]{2,1,0:T(8,128)}, f32[208,8,128]{2,1,0:T(8,128)S(1)}, u32[]{:S(2)}, u32[]{:S(2)}) collective-permute-start(f32[208,8,128]{2,1,0:T(8,128)} %get-tuple-element.72), channel_id=1, source_target_pairs={{0,1},{1,2},{2,3},{3,4},{4,5},{5,6},{6,7},{7,8},{8,9},{9,10},{10,1... | collective-permute-start | bytes 2555912 | tf_op jit(solution)/shard_map/ppermute | solution.py:800
  24.7 1.3 collective-permute-start.1
  26.0 0.0 copy-done.7
  26.0 0.0 copy-done.8
  26.0 0.0 copy-done.9
  26.0 0.0 copy-done.10
  26.0 1.7 %pixels.1 = (f32[8,128]{1,0:T(8,128)S(1)}, f32[16,8,128]{2,1,0:T(8,128)S(1)}) custom-call(s32[1,512]{1,0:T(1,128)S(1)} %bitcast.9, f32[1,512]{1,0:T(1,128)S(1)} %bitcast.10, f32[1,512]{1,0:T(1,128)S(1)} %bitcast.11, f32[16,512]{1,0:T(8,128)S(1)} %copy-done.7), custom_call_target="tpu_custom_call" | custom-call | tf_op jit(solution)/shard_map/pixels/pallas_call | solution.py:719
  27.8 0.1 add_convert_fusion.inside
  27.9 11.9 %all-to-all-done.7.incoming = bf16[128,40,128]{2,1,0:T(8,128)(2,1)S(1)} async-done(((bf16[128,40,128]{2,1,0:T(8,128)(2,1)}), bf16[128,40,128]{2,1,0:T(8,128)(2,1)S(1)}, u32[]{:S(2)}, u32[]{:S(2)}) %all-to-all-start.7) | async-done | bytes 1310752 | tf_op jit(solution)/shard_map/all_to_all | solution.py:794
  39.8 5.9 %deposit.1.heat_own = f32[2,128,128]{2,1,0:T(8,128)S(1)} custom-call(bf16[128,40,128]{2,1,0:T(8,128)(2,1)S(1)} %all-to-all-done.7.incoming), custom_call_target="tpu_custom_call" | custom-call | tf_op jit(solution)/shard_map/deposit/pallas_call | solution.py:284
  45.7 1.3 collective-permute-start.3
  47.0 4.0 %collective-permute-start.2 = (f32[2,128,128]{2,1,0:T(8,128)S(1)}, f32[2,128,128]{2,1,0:T(8,128)S(1)}, u32[]{:S(2)}, u32[]{:S(2)}) collective-permute-start(f32[2,128,128]{2,1,0:T(8,128)S(1)} %deposit.1.heat_own), channel_id=1, source_target_pairs={{0,1},{1,2},{2,3},{3,4},{4,5},{5,6},{6,7},{7,8},{8,9},{9,10},{10,1... | collective-permute-start | bytes 393224 | tf_op jit(solution)/shard_map/ppermute | solution.py:800
  51.0 1.4 collective-permute-done.low
  52.4 1.8 %collective-permute-done.1.high = f32[208,8,128]{2,1,0:T(8,128)S(1)} collective-permute-done((f32[208,8,128]{2,1,0:T(8,128)}, f32[208,8,128]{2,1,0:T(8,128)S(1)}, u32[]{:S(2)}, u32[]{:S(2)}) %collective-permute-start.1) | collective-permute-done | bytes 852000 | tf_op jit(solution)/shard_map/ppermute | solution.py:800
  54.1 2.8 %collective-permute-done.3.heat_high = f32[2,128,128]{2,1,0:T(8,128)S(1)} collective-permute-done((f32[2,128,128]{2,1,0:T(8,128)S(1)}, f32[2,128,128]{2,1,0:T(8,128)S(1)}, u32[]{:S(2)}, u32[]{:S(2)}) %collective-permute-start.3) | collective-permute-done | bytes 131104 | tf_op jit(solution)/shard_map/ppermute | solution.py:800
  56.9 0.0 collective-permute-done.2.heat_low
  56.9 1.2 copy-done.1
  58.2 0.0 copy-start.2
  58.2 3.5 %collective-permute-start.4 = (f32[49,8,128]{2,1,0:T(8,128)S(1)}, f32[49,8,128]{2,1,0:T(8,128)S(1)}, u32[]{:S(2)}, u32[]{:S(2)}) collective-permute-start(f32[49,8,128]{2,1,0:T(8,128)S(1)} %get-tuple-element.76), channel_id=1, source_target_pairs={{0,16},{16,32},{32,48},{48,64},{64,80},{80,96},{96,112},{1,17},{17... | collective-permute-start | bytes 602120 | tf_op jit(solution)/shard_map/ppermute | solution.py:800
  61.7 1.9 %collective-permute-start.5 = (f32[49,8,128]{2,1,0:T(8,128)S(1)}, f32[49,8,128]{2,1,0:T(8,128)S(1)}, u32[]{:S(2)}, u32[]{:S(2)}) collective-permute-start(f32[49,8,128]{2,1,0:T(8,128)S(1)} %get-tuple-element.77), channel_id=1, source_target_pairs={{16,0},{32,16},{48,32},{64,48},{80,64},{96,80},{112,96},{17,1},{33... | collective-permute-start | bytes 602120 | tf_op jit(solution)/shard_map/ppermute | solution.py:800
  63.6 2.6 %coefs.1.coef_main = f32[2,20,128,128]{3,2,1,0:T(8,128)S(1)} custom-call(f32[16,8,128]{2,1,0:T(8,128)S(1)} %get-tuple-element.74.turned_c.own, f32[208,8,128]{2,1,0:T(8,128)S(1)} %collective-permute-done.low, f32[208,8,128]{2,1,0:T(8,128)S(1)} %collective-permute-done.1.high), custom_call_target="tpu_custom_call" | custom-call | tf_op jit(solution)/shard_map/coefs/pallas_call | solution.py:237
  66.3 0.0 collective-permute-done.4.left
  66.3 2.5 %collective-permute-done.5.right = f32[49,8,128]{2,1,0:T(8,128)S(1)} collective-permute-done((f32[49,8,128]{2,1,0:T(8,128)S(1)}, f32[49,8,128]{2,1,0:T(8,128)S(1)}, u32[]{:S(2)}, u32[]{:S(2)}) %collective-permute-start.5) | collective-permute-done | bytes 200736 | tf_op jit(solution)/shard_map/ppermute | solution.py:800
  68.7 0.0 copy-done.2
  68.8 5.9 %heated.1 = (f32[2,20,144,128]{3,2,1,0:T(8,128)S(1)}, f32[2,20,144,128]{3,2,1,0:T(8,128)S(1)}, f32[2,20,144,128]{3,2,1,0:T(8,128)S(1)}, f32[128,1,128]{2,1,0:T(1,128)S(1)}) custom-call(f32[4]{0:T(128)S(1)} %add_convert_fusion.inside, f32[2,8,128,128]{3,2,1,0:T(8,128)S(1)} %copy-done.2, f32[208,8,128]{2,1,0:T(8,128)S(1)} %collective-permute-done.low, ...), custom_call_target="tpu_custom_call" | custom-call | tf_op jit(solution)/shard_map/heated/pallas_call | solution.py:515
  74.7 0.0 copy-start.14
  74.7 0.0 copy-start.12
  74.7 17.1 %all_to_all.60.parts = f32[128,1,128]{2,1,0:T(1,128)S(1)} all-to-all(f32[128,1,128]{2,1,0:T(1,128)S(1)} %get-tuple-element.81), channel_id=1, replica_groups=mesh['gx'=8,'gy'=16] {'gx','gy'}, dimensions={0} | all-to-all | bytes 131072 | tf_op jit(solution)/shard_map/all_to_all | solution.py:794
  91.8 8.2 %pair_0.1 = (f32[2,20,144,128]{3,2,1,0:T(8,128)S(1)}, f32[2,20,144,128]{3,2,1,0:T(8,128)S(1)}, f32[128,1,128]{2,1,0:T(1,128)S(1)}, f32[8,128]{1,0:T(8,128)S(1)}) custom-call(f32[4]{0:T(128)S(1)} %add_convert_fusion.inside, f32[2,20,144,128]{3,2,1,0:T(8,128)S(1)} %get-tuple-element.78.field, f32[2,20,144,128]{3,2,1,0:T(8,128)S(1)} %get-tuple-element.79.changes, ...), custom_call_target="tpu_custom_call" | custom-call | tf_op jit(solution)/shard_map/pair_0/pallas_call | solution.py:576
  100.0 13.9 %all_to_all.61.parts = f32[128,1,128]{2,1,0:T(1,128)S(1)} all-to-all(f32[128,1,128]{2,1,0:T(1,128)S(1)} %get-tuple-element.84), channel_id=1, replica_groups=mesh['gx'=8,'gy'=16] {'gx','gy'}, dimensions={0} | all-to-all | bytes 131072 | tf_op jit(solution)/shard_map/all_to_all | solution.py:794
  113.9 0.0 copy-done.14
  113.9 6.3 %pair_2.1 = (f32[2,20,144,128]{3,2,1,0:T(8,128)S(1)}, f32[2,20,144,128]{3,2,1,0:T(8,128)S(1)}, f32[128,1,128]{2,1,0:T(1,128)S(1)}, f32[8,128]{1,0:T(8,128)S(1)}) custom-call(f32[4]{0:T(128)S(1)} %add_convert_fusion.inside, f32[2,20,144,128]{3,2,1,0:T(8,128)S(1)} %get-tuple-element.82.field, f32[2,20,144,128]{3,2,1,0:T(8,128)S(1)} %get-tuple-element.83.changes, ...), custom_call_target="tpu_custom_call" | custom-call | tf_op jit(solution)/shard_map/pair_2/pallas_call | solution.py:576
  120.2 13.9 %all_to_all.62.parts = f32[128,1,128]{2,1,0:T(1,128)S(1)} all-to-all(f32[128,1,128]{2,1,0:T(1,128)S(1)} %get-tuple-element.88), channel_id=1, replica_groups=mesh['gx'=8,'gy'=16] {'gx','gy'}, dimensions={0} | all-to-all | bytes 131072 | tf_op jit(solution)/shard_map/all_to_all | solution.py:794
  134.1 0.0 copy-done.12
  134.1 4.1 %last_pair.1 = (f32[2,8,128,128]{3,2,1,0:T(8,128)S(1)}, f32[128,4,128]{2,1,0:T(4,128)}, f32[8,128]{1,0:T(8,128)S(1)}) custom-call(f32[4]{0:T(128)S(1)} %add_convert_fusion.inside, f32[2,20,144,128]{3,2,1,0:T(8,128)S(1)} %get-tuple-element.86.field, f32[2,20,144,128]{3,2,1,0:T(8,128)S(1)} %get-tuple-element.87.changes, ...), custom_call_target="tpu_custom_call" | custom-call | tf_op jit(solution)/shard_map/last_pair/pallas_call | solution.py:629
  138.2 4.5 %all-to-all-start.11 = ((f32[128,4,128]{2,1,0:T(4,128)}), f32[128,4,128]{2,1,0:T(4,128)S(1)}, u32[]{:S(2)}, u32[]{:S(2)}) async-start(f32[128,4,128]{2,1,0:T(4,128)} %get-tuple-element.92), calls=%async_computation.11 | async-start | bytes 524288 | tf_op jit(solution)/shard_map/all_to_all | solution.py:794
  142.7 11.3 %all-to-all-done.11.sums = f32[128,4,128]{2,1,0:T(4,128)S(1)} async-done(((f32[128,4,128]{2,1,0:T(4,128)}), f32[128,4,128]{2,1,0:T(4,128)S(1)}, u32[]{:S(2)}, u32[]{:S(2)}) %all-to-all-start.11) | async-done | bytes 262176 | tf_op jit(solution)/shard_map/all_to_all | solution.py:794
  154.0 5.4 %update.3 = (f32[16,16,8,128]{3,2,1,0:T(8,128)}, s32[1]{0:T(128)}) custom-call(f32[128,4,128]{2,1,0:T(4,128)S(1)} %all-to-all-done.11.sums, f32[2,8,128,128]{3,2,1,0:T(8,128)S(1)} %get-tuple-element.93.field, f32[8,128]{1,0:T(8,128)S(1)} %get-tuple-element.94.status), custom_call_target="tpu_custom_call" | custom-call | tf_op jit(solution)/shard_map/update/pallas_call | solution.py:780
  (13 shorter events, 0.1 us)
Async XLA Ops:
  0.0 18.4 %copy-start.3 = (f32[16,16,8,128]{3,2,1,0:T(8,128)S(1)}, f32[16,16,8,128]{3,2,1,0:T(8,128)}, u32[]{:S(2)}) copy-start(f32[16,16,8,128]{3,2,1,0:T(8,128)} %state.1) | copy-start | bytes 3145732
  0.0 1.1 copy-start.4
  1.1 0.8 copy-start.5
  2.0 0.7 copy-start.11
  2.6 15.8 %copy-start.6 = (f32[16,8,128]{2,1,0:T(8,128)S(1)}, f32[16,8,128]{2,1,0:T(8,128)}, u32[]{:S(2)}) copy-start(f32[16,8,128]{2,1,0:T(8,128)} %conduct.1) | copy-start | bytes 196612
  2.6 23.4 %copy-start.7 = (f32[16,512]{1,0:T(8,128)S(1)}, f32[16,512]{1,0:T(8,128)}, u32[]{:S(2)}) copy-start(f32[16,512]{1,0:T(8,128)} %noise.1) | copy-start | bytes 98308
  2.6 23.4 %copy-start.8 = (s32[512]{0:T(512)S(1)}, s32[512]{0:T(512)}, u32[]{:S(2)}) copy-start(s32[512]{0:T(512)} %param.16) | copy-start | bytes 6148
  2.6 23.4 %copy-start.9 = (f32[512]{0:T(512)S(1)}, f32[512]{0:T(512)}, u32[]{:S(2)}) copy-start(f32[512]{0:T(512)} %param.17) | copy-start | bytes 6148
  2.6 23.4 %copy-start.10 = (f32[512]{0:T(512)S(1)}, f32[512]{0:T(512)}, u32[]{:S(2)}) copy-start(f32[512]{0:T(512)} %param.18) | copy-start | bytes 6148
  6.9 32.9 %all-to-all-start.7 = ((bf16[128,40,128]{2,1,0:T(8,128)(2,1)}), bf16[128,40,128]{2,1,0:T(8,128)(2,1)S(1)}, u32[]{:S(2)}, u32[]{:S(2)}) async-start(bf16[128,40,128]{2,1,0:T(8,128)(2,1)} %pack.1), calls=%async_computation.7 | async-start | bytes 2621440 | tf_op jit(solution)/shard_map/all_to_all | solution.py:794
  20.2 1.0 copy-start
  21.2 31.2 %collective-permute-start = (f32[208,8,128]{2,1,0:T(8,128)}, f32[208,8,128]{2,1,0:T(8,128)S(1)}, u32[]{:S(2)}, u32[]{:S(2)}) collective-permute-start(f32[208,8,128]{2,1,0:T(8,128)} %get-tuple-element.72), channel_id=1, source_target_pairs={{0,1},{1,2},{2,3},{3,4},{4,5},{5,6},{6,7},{7,8},{8,9},{9,10},{10,1... | collective-permute-start | bytes 2555912 | tf_op jit(solution)/shard_map/ppermute | solution.py:800
  24.7 29.5 %collective-permute-start.1 = (f32[208,8,128]{2,1,0:T(8,128)}, f32[208,8,128]{2,1,0:T(8,128)S(1)}, u32[]{:S(2)}, u32[]{:S(2)}) collective-permute-start(f32[208,8,128]{2,1,0:T(8,128)} %get-tuple-element.73), channel_id=1, source_target_pairs={{1,0},{2,1},{3,2},{4,3},{5,4},{6,5},{7,6},{8,7},{9,8},{10,9},{11,1... | collective-permute-start | bytes 2555912 | tf_op jit(solution)/shard_map/ppermute | solution.py:800
  45.7 11.3 %collective-permute-start.3 = (f32[2,128,128]{2,1,0:T(8,128)S(1)}, f32[2,128,128]{2,1,0:T(8,128)S(1)}, u32[]{:S(2)}, u32[]{:S(2)}) collective-permute-start(f32[2,128,128]{2,1,0:T(8,128)S(1)} %deposit.1.heat_own), channel_id=1, source_target_pairs={{1,0},{2,1},{3,2},{4,3},{5,4},{6,5},{7,6},{8,7},{9,8},{10,9},{11,1... | collective-permute-start | bytes 393224 | tf_op jit(solution)/shard_map/ppermute | solution.py:800
  47.0 10.0 %collective-permute-start.2 = (f32[2,128,128]{2,1,0:T(8,128)S(1)}, f32[2,128,128]{2,1,0:T(8,128)S(1)}, u32[]{:S(2)}, u32[]{:S(2)}) collective-permute-start(f32[2,128,128]{2,1,0:T(8,128)S(1)} %deposit.1.heat_own), channel_id=1, source_target_pairs={{0,1},{1,2},{2,3},{3,4},{4,5},{5,6},{6,7},{7,8},{8,9},{9,10},{10,1... | collective-permute-start | bytes 393224 | tf_op jit(solution)/shard_map/ppermute | solution.py:800
  56.9 1.2 copy-start.1
  58.2 10.6 %copy-start.2 = (f32[2,8,128,128]{3,2,1,0:T(8,128)S(1)}, f32[2,8,128,128]{3,2,1,0:T(8,128)}, u32[]{:S(2)}) copy-start(f32[2,8,128,128]{3,2,1,0:T(8,128)} %copy-done) | copy-start | bytes 3145732
  58.2 8.1 %collective-permute-start.4 = (f32[49,8,128]{2,1,0:T(8,128)S(1)}, f32[49,8,128]{2,1,0:T(8,128)S(1)}, u32[]{:S(2)}, u32[]{:S(2)}) collective-permute-start(f32[49,8,128]{2,1,0:T(8,128)S(1)} %get-tuple-element.76), channel_id=1, source_target_pairs={{0,16},{16,32},{32,48},{48,64},{64,80},{80,96},{96,112},{1,17},{17... | collective-permute-start | bytes 602120 | tf_op jit(solution)/shard_map/ppermute | solution.py:800
  61.7 7.0 %collective-permute-start.5 = (f32[49,8,128]{2,1,0:T(8,128)S(1)}, f32[49,8,128]{2,1,0:T(8,128)S(1)}, u32[]{:S(2)}, u32[]{:S(2)}) collective-permute-start(f32[49,8,128]{2,1,0:T(8,128)S(1)} %get-tuple-element.77), channel_id=1, source_target_pairs={{16,0},{32,16},{48,32},{64,48},{80,64},{96,80},{112,96},{17,1},{33... | collective-permute-start | bytes 602120 | tf_op jit(solution)/shard_map/ppermute | solution.py:800
  74.7 39.2 %copy-start.14 = (f32[2,20,144,128]{3,2,1,0:T(8,128)}, f32[2,20,144,128]{3,2,1,0:T(8,128)S(1)}, u32[]{:S(2)}) copy-start(f32[2,20,144,128]{3,2,1,0:T(8,128)S(1)} %get-tuple-element.78.field) | copy-start | bytes 8847364
  74.7 59.4 %copy-start.12 = (f32[2,20,144,128]{3,2,1,0:T(8,128)}, f32[2,20,144,128]{3,2,1,0:T(8,128)S(1)}, u32[]{:S(2)}) copy-start(f32[2,20,144,128]{3,2,1,0:T(8,128)S(1)} %get-tuple-element.80.coef) | copy-start | bytes 8847364
  138.2 15.8 %all-to-all-start.11 = ((f32[128,4,128]{2,1,0:T(4,128)}), f32[128,4,128]{2,1,0:T(4,128)S(1)}, u32[]{:S(2)}, u32[]{:S(2)}) async-start(f32[128,4,128]{2,1,0:T(4,128)} %get-tuple-element.92), calls=%async_computation.11 | async-start | bytes 524288 | tf_op jit(solution)/shard_map/all_to_all | solution.py:794

commit v8 on v7

--- a/solution.py
+++ b/solution.py
@@ -14,7 +14,7 @@
 F32 = jnp.float32
 BF16 = jnp.bfloat16
 VM = pltpu.VMEM
-LIMIT = 24 * 1024 * 1024
+LIMIT = 32 * 1024 * 1024
 NT = (((1,), (1,)), ((), ()))
 BOTH = ("gx", "gy")
 
@@ -115,7 +115,7 @@
     return pl.pallas_call(
         pack_kernel,
         out_shape=jax.ShapeDtypeStruct((devices, ROWS, CX), BF16),
-        in_specs=[pl.BlockSpec(memory_space=pl.ANY)] * 3,
+        in_specs=[pl.BlockSpec(memory_space=pltpu.HBM)] * 3,
         out_specs=vspec(),
         scratch_shapes=[
             pltpu.SMEM((blocks,), jnp.int32),
@@ -144,47 +144,74 @@
 SIDE = 2 * YS
 
 
-def relayout_kernel(state, conduct, own, turned_c, to_high, to_low):
+def relayout_kernel(
+    state, conduct, own, turned_c, to_high, to_low, edge_left, edge_right, top, quiet
+):
     turned = (0.5 * conduct[...].reshape(CX, CX)).T.reshape(XT - 2, 8, CX)
     turned_c[...] = turned
     to_high[EDGE:] = turned
     to_low[EDGE:] = turned
+    peak = jnp.zeros((8, CX), F32)
     for zi in range(2):
         for y in range(CY):
-            parts = [
-                state[m0 : m0 + 8, 2 * group + zi, y, :] for group in range(ZG) for m0 in (0, 8)
-            ]
-            turned = (0.5 * jnp.concatenate(parts, axis=0)).T
+            parts = []
+            for group in range(ZG):
+                layer = 2 * group + zi
+                c = 0.5 * conduct[layer, y : y + 1, :]
+                for m0 in (0, 8):
+                    part = 0.5 * state[m0 : m0 + 8, layer, y, :]
+                    parts.append(part)
+                    if group:
+                        peak = jnp.maximum(peak, c + c * (part * part))
+            turned = jnp.concatenate(parts, axis=0).T
             own[zi, y] = turned
             turned = turned.reshape(XT - 2, 8, CX)
+            edge_left[zi * CY + y] = turned[0]
+            edge_right[zi * CY + y] = turned[XT - 3]
             if y >= CY - HALO:
                 at = (zi * HALO + y - (CY - HALO)) * (XT - 2)
                 to_high[at : at + XT - 2] = turned
             if y < HALO:
                 at = (zi * HALO + y) * (XT - 2)
                 to_low[at : at + XT - 2] = turned
+    quiet[...] = peak
+    for m in range(M):
+        for zi in range(2):
+            top[m, zi] = 0.5 * state[m, zi]
 
 
 def relayout(state, conduct):
     edge = jax.ShapeDtypeStruct((EDGE + XT - 2, 8, CX), F32)
+    side = jax.ShapeDtypeStruct((2 * CY, 8, CX), F32)
     return pl.pallas_call(
         relayout_kernel,
-        out_shape=[OWN, jax.ShapeDtypeStruct((XT - 2, 8, CX), F32), edge, edge],
+        out_shape=[
+            OWN,
+            jax.ShapeDtypeStruct((XT - 2, 8, CX), F32),
+            edge,
+            edge,
+            side,
+            side,
+            jax.ShapeDtypeStruct((M, 2, CY, CX), F32),
+            jax.ShapeDtypeStruct((8, CX), F32),
+        ],
         in_specs=[vspec()] * 2,
-        out_specs=[vspec()] * 4,
+        out_specs=[vspec()] * 8,
         compiler_params=params(),
         name="relayout",
     )(state, conduct)
 
 
-def side_kernel(own, turned_c, low, high, heat_low, heat_own, heat_high, to_left, to_right):
-    for out, t in ((to_left, 0), (to_right, XT - 3)):
+def side_kernel(
+    edge_left, edge_right, turned_c, low, high, heat_low, heat_own, heat_high, to_left, to_right
+):
+    for out, edge, t in ((to_left, edge_left, 0), (to_right, edge_right, XT - 3)):
         for zi in range(2):
             for y in range(YS):
                 if y < HALO:
                     part = low[(zi * HALO + y) * (XT - 2) + t]
                 elif y < HALO + CY:
-                    part = own[zi, y - HALO, 8 * t : 8 * t + 8, :]
+                    part = edge[zi * CY + y - HALO]
                 else:
                     part = high[(zi * HALO + y - HALO - CY) * (XT - 2) + t]
                 out[zi * YS + y] = part
@@ -196,16 +223,16 @@
                 out[SIDE + 3 + 2 * g + zi] = heat[zi, 8 * t : 8 * t + 8, :]
 
 
-def sides(own, turned_c, low, high, heat_low, heat_own, heat_high):
+def sides(*operands):
     shape = jax.ShapeDtypeStruct((SIDE + 9, 8, CX), F32)
     return pl.pallas_call(
         side_kernel,
         out_shape=[shape, shape],
-        in_specs=[vspec()] * 7,
+        in_specs=[vspec()] * len(operands),
         out_specs=[vspec()] * 2,
         compiler_params=params(),
         name="sides",
-    )(own, turned_c, low, high, heat_low, heat_own, heat_high)
+    )(*operands)
 
 
 def placed(strip, zi, y0):
@@ -244,7 +271,7 @@
     )(own, low, high)
 
 
-def deposit_kernel(incoming, out, total):
+def deposit_kernel(incoming, top, conduct, quiet, out, peaks, total):
     sources = incoming.shape[0]
     group = 32
     place = lax.broadcasted_iota(jnp.int32, (CX, CX), 0).astype(F32).astype(BF16)
@@ -278,18 +305,34 @@
     lax.fori_loop(0, sources // group, one, 0)
     for zi in range(2):
         out[zi] = (0.5 * total[zi * CX : (zi + 1) * CX, :]).T
-
-
-def deposit(incoming):
+    peak = quiet[...]
+    for zi in range(2):
+        c = 0.5 * conduct[zi]
+        for m in range(M):
+            value = top[m, zi] + 0.5 * total[pl.ds(zi * CX + m, CY, stride=M), :]
+            peak = jnp.maximum(peak, c + c * (value * value))
+    send_row(whole_peak(peak), peaks)
+
+
+def send_row(row, out):
+    for d in range(0, out.shape[0], 8):
+        out[d : d + 8, 0, :] = row
+
+
+def deposit(incoming, top, conduct, quiet):
+    devices = incoming.shape[0]
     return pl.pallas_call(
         deposit_kernel,
-        out_shape=jax.ShapeDtypeStruct((2, CX, CX), F32),
-        in_specs=[vspec()],
-        out_specs=vspec(),
+        out_shape=[
+            jax.ShapeDtypeStruct((2, CX, CX), F32),
+            jax.ShapeDtypeStruct((devices, 1, CX), F32),
+        ],
+        in_specs=[vspec()] * 4,
+        out_specs=[vspec()] * 2,
         scratch_shapes=[VM((2 * CY * M, CX), F32)],
         compiler_params=params(),
         name="deposit",
-    )(incoming)
+    )(incoming, top, conduct, quiet)
 
 
 def whole_peak(value):
@@ -419,16 +462,24 @@
     chunk = jnp.where(part == 6, whole_peak(peak), whole_peak(late))
     for place, value in ((2, best[3]), (1, best[2]), (0, best[1])):
         chunk = jnp.where((part >> 1) == place, value, chunk)
-    for d in range(0, out.shape[0], 8):
-        out[d : d + 8, 0, :] = chunk
+    send_row(chunk, out)
+
+
+def gather_rows(parts):
+    return [parts[d : d + 8, 0, :] for d in range(0, parts.shape[0], 8)]
+
+
+def largest(values):
+    most = values[0]
+    for value in values[1:]:
+        most = jnp.maximum(most, value)
+    return most
 
 
 def agree(parts):
     part = lanes() >> 4
-    rows_of = [parts[d : d + 8, 0, :] for d in range(0, parts.shape[0], 8)]
-    most = rows_of[0]
-    for value in rows_of[1:]:
-        most = jnp.maximum(most, value)
+    rows_of = gather_rows(parts)
+    most = largest(rows_of)
     now = whole_peak(jnp.where(part == 6, most, 0.0))
     late = whole_peak(jnp.where(part == 7, most, 0.0))
     step = step_of(now)
@@ -447,10 +498,9 @@
 def heated_kernel(
     inside, own, low, high, left, right,
     heat_low, heat_own, heat_high,
-    coef_main, out, coef, changes, parts, half, above,
+    coef_main, peaks, out, coef, changes, parts, start, half, next_half, above,
 ):
     top = lanes() < M
-    peak = jnp.zeros((8, CX), F32)
 
     strip = jnp.concatenate(
         [side[SIDE + g] for g in range(3) for side in (left, right)], axis=0
@@ -464,7 +514,7 @@
                     coef[zi, at, tile(0), :] = part[16 * g : 16 * g + 8, :]
                     coef[zi, at, tile(XT - 1), :] = part[16 * g + 8 : 16 * g + 16, :]
 
-    def row(g, heat, tile_of, y0, yy, peak):
+    def row(g, heat, tile_of, y0, yy):
         shift = (CX - 16 * y0) % CX
         for zi in range(2):
             for t in range(XT):
@@ -483,24 +533,30 @@
                 else:
                     c = coef[zi, yy, tile(t), :]
                 after = half_conductance(c, value)
-                out[zi, yy, tile(t), :] = value
+                start[zi, yy, tile(t), :] = value
                 half[zi, yy, tile(t), :] = after
-                if g == 1 and 0 < t < XT - 1:
-                    peak = jnp.maximum(peak, after)
-        return peak
 
     def edge(ref, y):
         return lambda zi, t: ref[(zi * HALO + y) * (XT - 2) + t]
 
     for y in range(HALO):
-        row(0, heat_low, edge(low, y), y + CY - HALO, y, peak)
+        row(0, heat_low, edge(low, y), y + CY - HALO, y)
     for y in range(CY):
-        peak = row(1, heat_own, lambda zi, t: own[zi, y, tile(t), :], y, y + HALO, peak)
+        row(1, heat_own, lambda zi, t: own[zi, y, tile(t), :], y, y + HALO)
     for y in range(HALO):
-        row(2, heat_high, edge(high, y), y, y + HALO + CY, peak)
-    guess = step_of(whole_peak(peak))
+        row(2, heat_high, edge(high, y), y, y + HALO + CY)
+
+    def put(zi, y, t, value, after):
+        out[zi, y, tile(t), :] = value
+        next_half[zi, y, tile(t), :] = after
+
+    step = step_of(whole_peak(largest(gather_rows(peaks))))
+    peak = advance(start, half, coef, above, inside, step, 1, YS - 1, put)
+    guess = jnp.minimum(step_of(whole_peak(peak)), 2.0 * step)
     zero = jnp.zeros((8, CX), F32)
-    propose(out, half, coef, above, inside, guess, 1, YS - 1, changes, peak, zero, parts)
+    propose(
+        out, next_half, coef, above, inside, guess, 2, YS - 2, changes, peak, zero, parts
+    )
 
 
 ROW = (2, XT, 8, CX)
@@ -510,14 +566,14 @@
     return pl.BlockSpec(memory_space=pltpu.SMEM)
 
 
-def heated(inside, prior, halos, heat, coef, devices):
-    operands = [inside, *prior, *halos, *heat, coef]
+def heated(inside, prior, halos, heat, coef, peaks):
+    operands = [inside, *prior, *halos, *heat, coef, peaks]
     return pl.pallas_call(
         heated_kernel,
-        out_shape=[WIDE, WIDE, WIDE, jax.ShapeDtypeStruct((devices, 1, CX), F32)],
+        out_shape=[WIDE, WIDE, WIDE, jax.ShapeDtypeStruct(peaks.shape, F32)],
         in_specs=[smem()] + [vspec()] * (len(operands) - 1),
         out_specs=[vspec()] * 4,
-        scratch_shapes=[VM(WIDE.shape, F32), VM(ROW, F32)],
+        scratch_shapes=[VM(WIDE.shape, F32)] * 3 + [VM(ROW, F32)],
         compiler_params=params(),
         name="heated",
     )(*operands)
@@ -541,14 +597,11 @@
 
 
 def pair_kernel(
-    number, inside, field, changes, coef, parts, status,
-    out, out_changes, out_parts, out_status, middle, half, next_half, above,
+    number, inside, field, changes, coef, parts,
+    out, out_changes, out_parts, status, middle, half, next_half, above,
 ):
-    now, then, late = agree(parts)
-    bad = status[1:2, :]
-    if number:
-        bad = jnp.maximum(bad, differs(late[0:1], status[0:1, :]))
-    out_status[...] = jnp.where(rows() == 0, then, bad)
+    now, then, _ = agree(parts)
+    status[...] = jnp.where(rows() == 0, then, 0.0)
     seen = first_of_pair(
         field, changes, coef, step_of(now), number + 1, YS - 1 - number, middle, half
     )
@@ -571,12 +624,12 @@
 STATUS = jax.ShapeDtypeStruct((8, CX), F32)
 
 
-def pair(number, inside, field, changes, coef, parts, status):
-    operands = [inside, field, changes, coef, parts, status]
+def pair(number, inside, field, changes, coef, parts):
+    operands = [inside, field, changes, coef, parts]
     return pl.pallas_call(
         functools.partial(pair_kernel, number),
         out_shape=[WIDE, WIDE, jax.ShapeDtypeStruct(parts.shape, F32), STATUS],
-        in_specs=[smem()] + [vspec()] * 5,
+        in_specs=[smem()] + [vspec()] * 4,
         out_specs=[vspec()] * 4,
         scratch_shapes=[VM(WIDE.shape, F32)] * 3 + [VM(ROW, F32)],
         compiler_params=params(),
@@ -584,110 +637,163 @@
     )(*operands)
 
 
-def pixel_grams(field, weight, data, flat, late, sums):
-    grams = jnp.zeros((M, 2 * M), F32)
+def closing(
+    field, half, above, inside, weight, data, peak, late, out, out_changes, sums, flat
+):
+    def emit(y, t, us, change, own, mask, state):
+        if 0 < t < XT - 1:
+            for zi in range(2):
+                out[zi, y - HALO, tile(t - 1), :] = us[zi]
+                out_changes[zi, y - HALO, tile(t - 1), :] = change[zi]
+        return state
+
+    sweep(field, half, above, inside, HALO, HALO + CY, emit, 0)
+    grams = jnp.zeros((5 * CY, 3 * M), F32)
     for y in range(CY):
-        seen = 2.0 * field[0, y].T[0:M, :]
+        w = weight[y : y + 1, :]
         for m in range(M):
             flat[m : m + 1, :] = data[m, y : y + 1, :]
-        w = weight[y : y + 1, :]
-        spread = seen - jnp.mean(seen, axis=0, keepdims=True)
-        both = jnp.concatenate([spread * w, flat[...] - seen * w], axis=0)
+        means = []
+        spreads = []
+        for part in (out, out_changes):
+            seen = 2.0 * part[0, y].T[0:M, :]
+            mean = jnp.mean(seen, axis=0, keepdims=True)
+            means.append(mean)
+            spreads.append(seen - mean)
+        left = jnp.concatenate(spreads + means + [jnp.zeros((6, CX), F32)], axis=0)
+        right = jnp.concatenate([part * w for part in spreads] + [flat[...]], axis=0)
         grams = grams + lax.dot_general(
-            spread, both, NT, precision=lax.Precision.HIGHEST, preferred_element_type=F32
+            left, right, NT, precision=lax.Precision.HIGHEST, preferred_element_type=F32
         )
-    grams = jnp.concatenate([grams, jnp.zeros((M, CX - 2 * M), F32)], axis=1)
-    two = grams[0:8] + pltpu.roll(grams[8:16], 32, axis=1)
-    quad = two + pltpu.roll(pltpu.roll(two, 64, axis=1), 4, axis=0)
-    quad = jnp.where((rows() == 0) & (lanes() == 1), whole_peak(late), quad)[0:4]
+    grams = jnp.concatenate([grams, jnp.zeros((5 * CY, CX - 3 * M), F32)], axis=1)
+    tall = lax.broadcasted_iota(jnp.int32, (M, CX), 0)
+    wide = lax.broadcasted_iota(jnp.int32, (M, CX), 1)
+    first, second, means = grams[0:M], grams[M : 2 * M], grams[2 * M : 2 * M + 8]
+
+    def block(part, at):
+        return jnp.where(wide < M, pltpu.roll(part, (CX - M * at) % CX, axis=1), 0.0)
+
+    def lone(part, row, at):
+        moved = pltpu.roll(part, (CX - M * at) % CX, axis=1) if at else part
+        return jnp.broadcast_to(moved[row : row + 1, :], (M, CX))
+
+    tops = [
+        lone(means, 0, 1) + lone(means, 1, 0),
+        lone(means, 0, 0),
+        lone(means, 1, 1),
+    ]
+    blocks = [
+        jnp.where(tall < wide, block(first, 0), block(second, 1)),
+        block(first, 1) + block(second, 0),
+        block(first, 2),
+        block(second, 2),
+    ]
+    scalar = jnp.where(wide == 0, whole_peak(peak)[0:1], whole_peak(late)[0:1])
+    blocks[0] = jnp.where(tall == wide, scalar, blocks[0])
+    for i, top in enumerate(tops):
+        blocks[i + 1] = jnp.where(tall == 0, jnp.where(wide < M, top, 0.0), blocks[i + 1])
+    packed = blocks[0]
+    for i in range(1, 4):
+        packed = packed + pltpu.roll(blocks[i], M * i, axis=1)
+    packed = packed[0:8] + pltpu.roll(packed[8:16], CX // 2, axis=1)
     for d in range(sums.shape[0]):
-        sums[d] = quad
+        sums[d] = packed
 
 
 def last_kernel(
     inside, field, changes, coef, parts, status, weight, data,
-    out, sums, out_status, middle, half, above, flat,
+    out, out_changes, sums, out_status, middle, half, near, near_half, above, flat,
 ):
-    number = SUBSTEPS - 2
+    number = SUBSTEPS - 3
     now, then, late = agree(parts)
-    bad = jnp.maximum(status[1:2, :], differs(late[0:1], status[0:1, :]))
+    bad = differs(late[0:1], status[0:1, :])
     out_status[...] = jnp.where(rows() == 0, then, bad)
     seen = first_of_pair(
         field, changes, coef, step_of(now), number + 1, YS - 1 - number, middle, half
     )
 
     def put(zi, y, t, value, after):
-        if 0 < t < XT - 1:
-            out[zi, y - HALO, tile(t - 1), :] = value
-
-    advance(middle, half, coef, above, inside, step_of(then), HALO, HALO + CY, put)
-    pixel_grams(out, weight, data, flat, seen, sums)
+        near[zi, y, tile(t), :] = value
+        near_half[zi, y, tile(t), :] = after
+
+    peak = advance(
+        middle, half, coef, above, inside, step_of(then), number + 2, YS - 2 - number, put
+    )
+    closing(
+        near, near_half, above, inside, weight, data, peak, seen, out, out_changes, sums, flat
+    )
+
+
+def sums_shape(devices):
+    return jax.ShapeDtypeStruct((devices, 8, CX), F32)
 
 
 def last(inside, field, changes, coef, parts, status, pixels):
     operands = [inside, field, changes, coef, parts, status, *pixels]
     return pl.pallas_call(
         last_kernel,
-        out_shape=[OWN, jax.ShapeDtypeStruct((parts.shape[0], 4, CX), F32), STATUS],
+        out_shape=[OWN, OWN, sums_shape(parts.shape[0]), STATUS],
         in_specs=[smem()] + [vspec()] * (len(operands) - 1),
-        out_specs=[vspec()] * 3,
-        scratch_shapes=[VM(WIDE.shape, F32)] * 2 + [VM(ROW, F32), VM((M, CX), F32)],
+        out_specs=[vspec()] * 4,
+        scratch_shapes=[VM(WIDE.shape, F32)] * 4 + [VM(ROW, F32), VM((M, CX), F32)],
         compiler_params=params(),
         name="last_pair",
     )(*operands)
 
 
-def single_kernel(number, inside, field, coef, peaks, *rest):
-    final = number == SUBSTEPS - 1
-    if final:
-        weight, data, out, sums, half, above, flat = rest
-    else:
-        out, out_peaks, half, above = rest
-    peak = peaks[0]
-    for d in range(1, peaks.shape[0]):
-        peak = jnp.maximum(peak, peaks[d])
-    step = step_of(whole_peak(peak))
-
+def fill_half(field, coef, half, first, end):
     def fill(y, carry):
         for zi in range(2):
             half[zi, y] = half_conductance(coef[zi, y], field[zi, y])
         return carry
 
-    lax.fori_loop(number, YS - number, fill, 0)
+    lax.fori_loop(first, end, fill, 0)
+
+
+def single_kernel(number, inside, field, coef, peaks, out, out_peaks, half, above):
+    step = step_of(whole_peak(largest(gather_rows(peaks))))
+    fill_half(field, coef, half, number, YS - number)
 
     def put(zi, y, t, value, after):
-        if not final:
-            out[zi, y, tile(t), :] = value
-        elif 0 < t < XT - 1:
-            out[zi, y - HALO, tile(t - 1), :] = value
+        out[zi, y, tile(t), :] = value
 
     peak = advance(field, half, coef, above, inside, step, number + 1, YS - 1 - number, put)
-    if final:
-        pixel_grams(out, weight, data, flat, jnp.zeros((8, CX), F32), sums)
-    else:
-        peak = whole_peak(peak)
-        for d in range(0, out_peaks.shape[0], 8):
-            out_peaks[d : d + 8, 0, :] = peak
-
-
-def single(number, inside, field, coef, peaks, pixels):
-    devices = peaks.shape[0]
-    operands = [inside, field, coef, peaks]
-    scratch = [VM(WIDE.shape, F32), VM(ROW, F32)]
-    if number == SUBSTEPS - 1:
-        operands += list(pixels)
-        out_shape = [OWN, jax.ShapeDtypeStruct((devices, 4, CX), F32)]
-        scratch += [VM((M, CX), F32)]
-    else:
-        out_shape = [WIDE, jax.ShapeDtypeStruct((devices, 1, CX), F32)]
+    send_row(whole_peak(peak), out_peaks)
+
+
+def single(number, inside, field, coef, peaks):
     return pl.pallas_call(
         functools.partial(single_kernel, number),
-        out_shape=out_shape,
+        out_shape=[WIDE, jax.ShapeDtypeStruct(peaks.shape, F32)],
+        in_specs=[smem()] + [vspec()] * 3,
+        out_specs=[vspec()] * 2,
+        scratch_shapes=[VM(WIDE.shape, F32), VM(ROW, F32)],
+        compiler_params=params(),
+        name=f"single_{number}",
+    )(inside, field, coef, peaks)
+
+
+def closing_kernel(
+    inside, field, coef, peaks, weight, data, out, out_changes, sums, half, above, flat
+):
+    fill_half(field, coef, half, HALO - 1, HALO + CY + 1)
+    peak = peaks[0:8, 0, :]
+    closing(
+        field, half, above, inside, weight, data, peak, jnp.zeros((8, CX), F32),
+        out, out_changes, sums, flat,
+    )
+
+
+def close(inside, field, coef, peaks, pixels):
+    operands = [inside, field, coef, peaks, *pixels]
+    return pl.pallas_call(
+        closing_kernel,
+        out_shape=[OWN, OWN, sums_shape(peaks.shape[0])],
         in_specs=[smem()] + [vspec()] * (len(operands) - 1),
-        out_specs=[vspec()] * 2,
-        scratch_shapes=scratch,
-        compiler_params=params(),
-        name=f"single_{number}",
+        out_specs=[vspec()] * 3,
+        scratch_shapes=[VM(WIDE.shape, F32), VM(ROW, F32), VM((M, CX), F32)],
+        compiler_params=params(),
+        name="closing",
     )(*operands)
 
 
@@ -729,24 +835,46 @@
     )(cell, observed, variance, noise)
 
 
-def update_kernel(sums, field, status, out, flag):
-    quad = sums[0]
-    late = quad
+def update_kernel(sums, field, changes, status, out, flag):
+    total = sums[0]
+    most = total
     for d in range(1, sums.shape[0]):
-        quad = quad + sums[d]
-        late = jnp.maximum(late, sums[d])
-    late = jnp.broadcast_to(late[0:1, 1:2], (1, CX))
+        total = total + sums[d]
+        most = jnp.maximum(most, sums[d])
+    step = step_of(jnp.broadcast_to(most[0:1, 0:1], (1, CX)))
+    late = jnp.broadcast_to(most[1:2, 1:2], (1, CX))
     bad = jnp.maximum(status[1:2, :], differs(late, status[0:1, :]))
     flag[0] = jnp.where(jnp.max(bad) > 0.0, 1, 0)
-    row = rows()
-    quad = jnp.concatenate([quad, jnp.zeros_like(quad)], axis=0)
-    pair = jnp.where(row < 4, quad, pltpu.roll(pltpu.roll(quad, 64, axis=1), 4, axis=0))
-    system = jnp.concatenate([pair, pltpu.roll(pair, CX - 32, axis=1)], axis=0)
+
     tall = lax.broadcasted_iota(jnp.int32, (M, CX), 0)
     wide = lax.broadcasted_iota(jnp.int32, (M, CX), 1)
-    system = jnp.where(tall == wide, system + (M - 1.0), system)
-    mirror = jnp.broadcast_to(system[1:2, 0:1], (M, CX))
-    system = jnp.where((tall == 0) & (wide == 1), mirror, system)
+    packed = jnp.concatenate([total, pltpu.roll(total, CX // 2, axis=1)], axis=0)
+
+    def block(at):
+        return jnp.where(wide < M, pltpu.roll(packed, (CX - M * at) % CX, axis=1), 0.0)
+
+    def whole(part):
+        rest = jnp.where(tall == 0, 0.0, part)
+        first = -jnp.sum(rest, axis=0, keepdims=True)
+        return jnp.where(tall == 0, first, rest), part[0:1, :]
+
+    def balanced(part):
+        part = jnp.where((tall == wide) | (wide >= M), 0.0, part)
+        return jnp.where(tall == wide, -jnp.sum(part, axis=1, keepdims=True), part)
+
+    corner = block(0)
+    mirror = jnp.concatenate([corner, jnp.zeros((CX - M, CX), F32)], axis=0).T[0:M, :]
+    square = balanced(jnp.where(tall < wide, corner, mirror))
+    square_c = balanced(jnp.where(tall > wide, corner, mirror))
+    mixed, mean_1 = whole(block(1))
+    data, mean_0 = whole(block(2))
+    data_c, mean_2 = whole(block(3))
+    cross = square + step * (mixed + step * square_c)
+    mean = mean_0 + step * (mean_1 + step * mean_2)
+    mean = jnp.sum(jnp.where(tall == wide, mean, 0.0), axis=1, keepdims=True)
+    target = jnp.where(wide < M, data + step * data_c - cross - mean, 0.0)
+    system = jnp.where(tall == wide, cross + (M - 1.0), cross)
+    system = system + pltpu.roll(target, M, axis=1)
     for i in range(M):
         pivot = system[i : i + 1, :]
         pivot = pivot / pivot[:, i : i + 1]
@@ -765,7 +893,7 @@
         for y in range(CY):
             part = lax.dot_general(
                 mixing,
-                field[zi, y],
+                field[zi, y] + step * changes[zi, y],
                 NT,
                 precision=lax.Precision.HIGHEST,
                 preferred_element_type=F32,
@@ -776,18 +904,18 @@
                     out[m0 : m0 + 8, 2 * group + zi, y, :] = part[at : at + 8, :]
 
 
-def update(sums, field, status):
+def update(sums, field, changes, status):
     return pl.pallas_call(
         update_kernel,
         out_shape=[
             jax.ShapeDtypeStruct((M, NZ, CY, CX), F32),
             jax.ShapeDtypeStruct((1,), jnp.int32),
         ],
-        in_specs=[vspec()] * 3,
+        in_specs=[vspec()] * 4,
         out_specs=[vspec(), smem()],
         compiler_params=params(),
         name="update",
-    )(sums, field, status)
+    )(sums, field, changes, status)
 
 
 def exchange(parts):
@@ -818,7 +946,9 @@
         [gx > 0, gx < lax.axis_size("gx") - 1, gy > 0, gy < lax.axis_size("gy") - 1]
     ).astype(F32)
     incoming = exchange(pack(owner_tile.reshape(-1), heat_input, voxel_list, devices))
-    own, turned_c, to_high, to_low = relayout(state_prior, conductivity)
+    own, turned_c, to_high, to_low, edge_left, edge_right, top, quiet = relayout(
+        state_prior, conductivity
+    )
     low, high = move(to_high, "gy", True), move(to_low, "gy", False)
     seen = pixel_sums(
         pixel_cell.reshape(1, pixels),
@@ -826,10 +956,15 @@
         pixel_variance.reshape(1, pixels),
         pixel_noise,
     )
-    incoming, own, inside, *seen = lax.optimization_barrier((incoming, own, inside, *seen))
-    heat = deposit(incoming)
+    incoming, own, top, inside, *seen = lax.optimization_barrier(
+        (incoming, own, top, inside, *seen)
+    )
+    heat, peaks = deposit(incoming, top, conductivity, quiet)
     heat_low, heat_high = move(heat, "gy", True), move(heat, "gy", False)
-    to_left, to_right = sides(own, turned_c, low, high, heat_low, heat, heat_high)
+    peaks = exchange(peaks)
+    to_left, to_right = sides(
+        edge_left, edge_right, turned_c, low, high, heat_low, heat, heat_high
+    )
     left, right = move(to_right, "gx", True), move(to_left, "gx", False)
     start, coef, changes, parts = heated(
         inside,
@@ -837,24 +972,22 @@
         (left, right),
         (heat_low, heat, heat_high),
         coefs(turned_c, low, high),
-        devices,
-    )
-    field, status = start, jnp.zeros((8, CX), F32)
-    for number in range(0, SUBSTEPS - 2, 2):
-        field, changes, parts, status = pair(
-            number, inside, field, changes, coef, exchange(parts), status
-        )
-    field, sums, status = last(inside, field, changes, coef, exchange(parts), status, seen)
-    result, flag = update(exchange(sums), field, status)
+        peaks,
+    )
+    field, changes, parts, status = pair(1, inside, start, changes, coef, exchange(parts))
+    field, changes, sums, status = last(
+        inside, field, changes, coef, exchange(parts), status, seen
+    )
+    result, flag = update(exchange(sums), field, changes, status)
 
     def again():
         peak = coef * (1.0 + start * start)
-        peak = jnp.max(peak[:, HALO : HALO + CY, 8 : XS - 8])
-        peaks = jnp.full((devices, 1, CX), peak)
+        peaks = jnp.full((devices, 1, CX), jnp.max(peak[:, HALO : HALO + CY, 8 : XS - 8]))
         field = start
-        for number in range(SUBSTEPS):
-            field, peaks = single(number, inside, field, coef, exchange(peaks), seen)
-        return update(exchange(peaks), field, jnp.ones((8, CX), F32))[0]
+        for number in range(1, SUBSTEPS - 1):
+            field, peaks = single(number, inside, field, coef, exchange(peaks))
+        field, changes, sums = close(inside, field, coef, peaks, seen)
+        return update(exchange(sums), field, changes, jnp.ones((8, CX), F32))[0]
 
     return lax.cond(flag[0] > 0, again, lambda: result)
 

time: 161 us -> 166 us (1.031)
  blocking collectives: 44.9 us -> 27.5 us
  local copies, waits for them, and re-layouts: 4.86 us -> 16.6 us
  starting transfers between devices: 31.4 us -> 40.4 us
  Pallas kernels: 46.2 us -> 48.4 us
    all_to_all x3 -> x2, blocking collectives: 44.9 us -> 27.5 us  [exchange(): return lax.all_to_all(parts, BOTH, split_axis=0, concat_axis=0, tiled=True)]
    unnamed x28 -> x62, local copies, waits for them, and re-layouts: 4.86 us -> 16.6 us
    all_to_all x2 -> x3, starting transfers between devices: 16 us -> 25.1 us  [exchange(): return lax.all_to_all(parts, BOTH, split_axis=0, concat_axis=0, tiled=True)]
    pallas_call x2 -> x1, Pallas kernels: 14.5 us -> 7.3 us  [pair(): pl.pallas_call(functools.partial(pair_kernel, number), out_shape=[WIDE, W...]
    ppermute x6, waiting for transfers between devices: 8.46 us -> 3.6 us  [move(): return lax.ppermute(part, axis, pairs)]
    all_to_all x2 -> x3, waiting for transfers between devices: 23.2 us -> 27.6 us  [exchange(): return lax.all_to_all(parts, BOTH, split_axis=0, concat_axis=0, tiled=True)]
    pallas_call x1, Pallas kernels: 5.91 us -> 9.75 us  [heated(): pl.pallas_call(heated_kernel, out_shape=[WIDE, WIDE, WIDE, jax.ShapeDtype...]
    pallas_call x2, Pallas kernels: 10 us -> 13.1 us  [the longest x1 6.61 us: deposit(): pl.pallas_call(deposit_kernel, out_shape=[jax.ShapeDtypeStruct((2, CX, CX...]
  transfers between devices with their start and end apart: 8 -> 9, of which waited for: 6 -> 5; matrix products, arithmetic and copies ran while one was open for 0% -> 0% of each run, Pallas kernels for 8% -> 9%
where the time goes in v8:
time: 166 us; the launch traced here: 165 us
  Pallas kernels  48.4 us (29%)
  starting transfers between devices  40.4 us (24%)
  waiting for transfers between devices  31.2 us (19%)
  blocking collectives  27.5 us (17%)
  local copies, waits for them, and re-layouts  16.6 us (10%)
    all_to_all x3, waiting for transfers between devices, exchange(): return lax.all_to_all(parts, BOTH, split_axis=0, concat_axis=0, tiled=True)  27.6 us
    all_to_all x2, blocking collectives, exchange(): return lax.all_to_all(parts, BOTH, split_axis=0, concat_axis=0, tiled=True)  27.5 us
    all_to_all x3, starting transfers between devices, exchange(): return lax.all_to_all(parts, BOTH, split_axis=0, concat_axis=0, tiled=True)  25.1 us
    unnamed x62, local copies, waits for them, and re-layouts  16.6 us
    ppermute x6, starting transfers between devices, move(): return lax.ppermute(part, axis, pairs)  15.4 us
    pallas_call x1, Pallas kernels, heated(): pl.pallas_call(heated_kernel, out_shape=[WIDE, WIDE, WIDE, jax.ShapeDtype...  9.75 us
    pallas_call x1, Pallas kernels, pair(): pl.pallas_call(functools.partial(pair_kernel, number), out_shape=[WIDE, W...  7.3 us
    pallas_call x1, Pallas kernels, deposit(): pl.pallas_call(deposit_kernel, out_shape=[jax.ShapeDtypeStruct((2, CX, CX...  6.61 us
  transfers between devices with their start and end apart: 9, of which 5 were waited for; matrix products, arithmetic and copies ran while one was open for 0% of the time, Pallas kernels for 9%

profile of v8, /device:TPU:1, one launch (start us, length us, event | category | flops | bytes accessed | tf_op | source)
XLA Modules:
  0.0 165.3 jit_solution(12683183424474746437)
XLA Ops:
  0.0 1.1 copy-done.12
  1.1 0.8 copy-done.17
  2.0 0.7 copy-done.26
  2.6 4.3 %pack.1 = bf16[128,40,128]{2,1,0:T(8,128)(2,1)} custom-call(s32[128]{0:T(128)S(1)} %bitcast.12, bf16[16,128,128]{2,1,0:T(8,128)(2,1)S(1)} %copy-done.12, s32[128,128]{1,0:T(8,128)S(1)} %copy-done.17), custom_call_target="tpu_custom_call" | custom-call | tf_op jit(solution)/shard_map/pack/pallas_call | solution.py:115
  6.9 11.5 %all-to-all-start.5 = ((bf16[128,40,128]{2,1,0:T(8,128)(2,1)}), bf16[128,40,128]{2,1,0:T(8,128)(2,1)S(1)}, u32[]{:S(2)}, u32[]{:S(2)}) async-start(bf16[128,40,128]{2,1,0:T(8,128)(2,1)} %pack.1), calls=%async_computation.5 | async-start | bytes 2621440 | tf_op jit(solution)/shard_map/all_to_all | solution.py:922
  18.4 2.7 %relayout.1 = (f32[2,8,128,128]{3,2,1,0:T(8,128)S(1)}, f32[16,8,128]{2,1,0:T(8,128)S(1)}, f32[208,8,128]{2,1,0:T(8,128)}, f32[208,8,128]{2,1,0:T(8,128)}, f32[16...) custom-call(f32[16,16,8,128]{3,2,1,0:T(8,128)S(1)} %copy-done.5, ...), custom_call_target="tpu_custom_call" | custom-call | tf_op jit(solution)/shard_map/relayout/pallas_call | solution.py:186
  21.1 1.0 copy-done.3
  22.1 0.6 copy-done.15
  22.7 0.6 copy-done.18
  23.3 0.6 copy-done.20
  23.9 3.5 %collective-permute-start = (f32[208,8,128]{2,1,0:T(8,128)}, f32[208,8,128]{2,1,0:T(8,128)S(1)}, u32[]{:S(2)}, u32[]{:S(2)}) collective-permute-start(f32[208,8,128]{2,1,0:T(8,128)} %get-tuple-element.76), channel_id=1, source_target_pairs={{0,1},{1,2},{2,3},{3,4},{4,5},{5,6},{6,7},{7,8},{8,9},{9,10},{10,1... | collective-permute-start | bytes 2555912 | tf_op jit(solution)/shard_map/ppermute | solution.py:928
  27.4 1.3 collective-permute-start.1
  28.7 0.0 copy-start.22
  28.8 0.7 copy-done.22
  29.5 2.4 %pixels.1 = (f32[8,128]{1,0:T(8,128)}, f32[16,8,128]{2,1,0:T(8,128)}) custom-call(s32[1,512]{1,0:T(1,128)S(1)} %bitcast.9, f32[1,512]{1,0:T(1,128)S(1)} %bitcast.10, f32[1,512]{1,0:T(1,128)S(1)} %bitcast.11, f32[16,512]{1,0:T(8,128)S(1)} %copy-done.22), custom_call_target="tpu_custom_call" | custom-call | tf_op jit(solution)/shard_map/pixels/pallas_call | solution.py:825
  31.9 0.1 add_convert_fusion.inside
  32.0 7.8 %all-to-all-done.5.incoming = bf16[128,40,128]{2,1,0:T(8,128)(2,1)S(1)} async-done(((bf16[128,40,128]{2,1,0:T(8,128)(2,1)}), bf16[128,40,128]{2,1,0:T(8,128)(2,1)S(1)}, u32[]{:S(2)}, u32[]{:S(2)}) %all-to-all-start.5) | async-done | bytes 1310752 | tf_op jit(solution)/shard_map/all_to_all | solution.py:922
  39.8 0.8 copy-done.14
  40.6 0.9 copy-done.16
  41.5 6.6 %deposit.1 = (f32[2,128,128]{2,1,0:T(8,128)S(1)}, f32[128,1,128]{2,1,0:T(1,128)}) custom-call(bf16[128,40,128]{2,1,0:T(8,128)(2,1)S(1)} %all-to-all-done.5.incoming, f32[16,2,8,128]{3,2,1,0:T(8,128)S(1)} %copy-done.16, f32[16,8,128]{2,1,0:T(8,128)S(1)} %copy-done.14, f32[8,128]{1,0:T(8,128)S(1)} %get-tuple-element.83.quiet), custom_call_target="tpu_custom_call" | custom-call | tf_op jit(solution)/shard_map/deposit/pallas_call | solution.py:324
  48.1 1.3 collective-permute-start.3
  49.4 4.0 %collective-permute-start.2 = (f32[2,128,128]{2,1,0:T(8,128)S(1)}, f32[2,128,128]{2,1,0:T(8,128)S(1)}, u32[]{:S(2)}, u32[]{:S(2)}) collective-permute-start(f32[2,128,128]{2,1,0:T(8,128)S(1)} %get-tuple-element.84.heat_own), channel_id=1, source_target_pairs={{0,1},{1,2},{2,3},{3,4},{4,5},{5,6},{6,7},{7,8},{8,9},{9,10},{10,1... | collective-permute-start | bytes 393224 | tf_op jit(solution)/shard_map/ppermute | solution.py:928
  53.4 0.0 collective-permute-done.low
  53.4 0.8 collective-permute-done.1.high
  54.2 2.8 %collective-permute-done.3.heat_high = f32[2,128,128]{2,1,0:T(8,128)S(1)} collective-permute-done((f32[2,128,128]{2,1,0:T(8,128)S(1)}, f32[2,128,128]{2,1,0:T(8,128)S(1)}, u32[]{:S(2)}, u32[]{:S(2)}) %collective-permute-start.3) | collective-permute-done | bytes 131104 | tf_op jit(solution)/shard_map/ppermute | solution.py:928
  57.0 0.9 copy-done.19
  57.9 0.8 copy-done.21
  58.8 0.8 sides.1
  59.5 0.7 copy-done.6
  60.2 3.4 %collective-permute-start.4 = (f32[49,8,128]{2,1,0:T(8,128)}, f32[49,8,128]{2,1,0:T(8,128)}, u32[]{:S(2)}, u32[]{:S(2)}) collective-permute-start(f32[49,8,128]{2,1,0:T(8,128)} %get-tuple-element.85), channel_id=1, source_target_pairs={{0,16},{16,32},{32,48},{48,64},{64,80},{80,96},{96,112},{1,17},{17... | collective-permute-start | bytes 602120 | tf_op jit(solution)/shard_map/ppermute | solution.py:928
  63.6 1.9 %collective-permute-start.5 = (f32[49,8,128]{2,1,0:T(8,128)}, f32[49,8,128]{2,1,0:T(8,128)}, u32[]{:S(2)}, u32[]{:S(2)}) collective-permute-start(f32[49,8,128]{2,1,0:T(8,128)} %get-tuple-element.86), channel_id=1, source_target_pairs={{16,0},{32,16},{48,32},{64,48},{80,64},{96,80},{112,96},{17,1},{33... | collective-permute-start | bytes 602120 | tf_op jit(solution)/shard_map/ppermute | solution.py:928
  65.6 9.1 %all-to-all-start.6 = ((f32[128,1,128]{2,1,0:T(1,128)}), f32[128,1,128]{2,1,0:T(1,128)}, u32[]{:S(2)}, u32[]{:S(2)}) async-start(f32[128,1,128]{2,1,0:T(1,128)} %get-tuple-element.87), calls=%async_computation.6 | async-start | bytes 131072 | tf_op jit(solution)/shard_map/all_to_all | solution.py:922
  74.7 1.1 copy-done.1
  75.8 2.6 %coefs.1.coef_main = f32[2,20,128,128]{3,2,1,0:T(8,128)S(1)} custom-call(f32[16,8,128]{2,1,0:T(8,128)S(1)} %get-tuple-element.80.turned_c.own, f32[208,8,128]{2,1,0:T(8,128)S(1)} %collective-permute-done.low, f32[208,8,128]{2,1,0:T(8,128)S(1)} %copy-done.1), custom_call_target="tpu_custom_call" | custom-call | tf_op jit(solution)/shard_map/coefs/pallas_call | solution.py:264
  78.4 5.9 %all-to-all-done.6.peaks = f32[128,1,128]{2,1,0:T(1,128)} async-done(((f32[128,1,128]{2,1,0:T(1,128)}), f32[128,1,128]{2,1,0:T(1,128)}, u32[]{:S(2)}, u32[]{:S(2)}) %all-to-all-start.6) | async-done | bytes 65568 | tf_op jit(solution)/shard_map/all_to_all | solution.py:922
  84.3 1.2 copy-done.2
  85.4 1.2 copy-done.4
  86.7 0.9 copy-done.7
  87.6 0.9 copy-done.9
  88.5 0.9 copy-done.11
  89.4 9.7 %heated.1 = (f32[2,20,144,128]{3,2,1,0:T(8,128)S(1)}, f32[2,20,144,128]{3,2,1,0:T(8,128)S(1)}, f32[2,20,144,128]{3,2,1,0:T(8,128)S(1)}, f32[128,1,128]{2,1,0:T(1,128)S(1)}) custom-call(f32[4]{0:T(128)S(1)} %add_convert_fusion.inside, f32[2,8,128,128]{3,2,1,0:T(8,128)S(1)} %copy-done.4, f32[208,8,128]{2,1,0:T(8,128)S(1)} %collective-permute-done.low, ...), custom_call_target="tpu_custom_call" | custom-call | tf_op jit(solution)/shard_map/heated/pallas_call | solution.py:571
  99.2 13.7 %all_to_all.50.parts = f32[128,1,128]{2,1,0:T(1,128)S(1)} all-to-all(f32[128,1,128]{2,1,0:T(1,128)S(1)} %get-tuple-element.91), channel_id=1, replica_groups=mesh['gx'=8,'gy'=16] {'gx','gy'}, dimensions={0} | all-to-all | bytes 131072 | tf_op jit(solution)/shard_map/all_to_all | solution.py:922
  112.8 7.3 %pair_1.1 = (f32[2,20,144,128]{3,2,1,0:T(8,128)S(1)}, f32[2,20,144,128]{3,2,1,0:T(8,128)S(1)}, f32[128,1,128]{2,1,0:T(1,128)S(1)}, f32[8,128]{1,0:T(8,128)S(1)}) custom-call(f32[4]{0:T(128)S(1)} %add_convert_fusion.inside, f32[2,20,144,128]{3,2,1,0:T(8,128)S(1)} %get-tuple-element.88.field, f32[2,20,144,128]{3,2,1,0:T(8,128)S(1)} %get-tuple-element.89.changes, ...), custom_call_target="tpu_custom_call" | custom-call | tf_op jit(solution)/shard_map/pair_1/pallas_call | solution.py:629
  120.1 13.9 %all_to_all.51.parts = f32[128,1,128]{2,1,0:T(1,128)S(1)} all-to-all(f32[128,1,128]{2,1,0:T(1,128)S(1)} %get-tuple-element.94), channel_id=1, replica_groups=mesh['gx'=8,'gy'=16] {'gx','gy'}, dimensions={0} | all-to-all | bytes 131072 | tf_op jit(solution)/shard_map/all_to_all | solution.py:922
  134.0 6.5 %last_pair.1 = (f32[2,8,128,128]{3,2,1,0:T(8,128)S(1)}, f32[2,8,128,128]{3,2,1,0:T(8,128)S(1)}, f32[128,8,128]{2,1,0:T(8,128)}, f32[8,128]{1,0:T(8,128)S(1)}) custom-call(f32[4]{0:T(128)S(1)} %add_convert_fusion.inside, f32[2,20,144,128]{3,2,1,0:T(8,128)S(1)} %get-tuple-element.92.field, f32[2,20,144,128]{3,2,1,0:T(8,128)S(1)} %get-tuple-element.93.changes, ...), custom_call_target="tpu_custom_call" | custom-call | tf_op jit(solution)/shard_map/last_pair/pallas_call | solution.py:733
  140.5 4.5 %all-to-all-start.9 = ((f32[128,8,128]{2,1,0:T(8,128)}), f32[128,8,128]{2,1,0:T(8,128)S(1)}, u32[]{:S(2)}, u32[]{:S(2)}) async-start(f32[128,8,128]{2,1,0:T(8,128)} %get-tuple-element.98), calls=%async_computation.9 | async-start | bytes 1048576 | tf_op jit(solution)/shard_map/all_to_all | solution.py:922
  145.0 13.9 %all-to-all-done.9.sums = f32[128,8,128]{2,1,0:T(8,128)S(1)} async-done(((f32[128,8,128]{2,1,0:T(8,128)}), f32[128,8,128]{2,1,0:T(8,128)S(1)}, u32[]{:S(2)}, u32[]{:S(2)}) %all-to-all-start.9) | async-done | bytes 524320 | tf_op jit(solution)/shard_map/all_to_all | solution.py:922
  159.0 5.5 %update.3 = (f32[16,16,8,128]{3,2,1,0:T(8,128)}, s32[1]{0:T(128)}) custom-call(f32[128,8,128]{2,1,0:T(8,128)S(1)} %all-to-all-done.9.sums, f32[2,8,128,128]{3,2,1,0:T(8,128)S(1)} %get-tuple-element.99.field, f32[2,8,128,128]{3,2,1,0:T(8,128)S(1)} %get-tuple-element.100.changes, f32[8,128]{1,0:T(8,128)S(1)} %get-tuple-element.101.status), custom_call_target="tpu_custom_call" | custom-call | tf_op jit(solution)/shard_map/update/pallas_call | solution.py:908
  (46 shorter events, 0.1 us)
Async XLA Ops:
  0.0 18.4 %copy-start.5 = (f32[16,16,8,128]{3,2,1,0:T(8,128)S(1)}, f32[16,16,8,128]{3,2,1,0:T(8,128)}, u32[]{:S(2)}) copy-start(f32[16,16,8,128]{3,2,1,0:T(8,128)} %state.1) | copy-start | bytes 3145732
  0.0 1.1 copy-start.12
  1.1 0.8 copy-start.17
  2.0 0.7 copy-start.26
  2.6 15.8 %copy-start.13 = (f32[16,8,128]{2,1,0:T(8,128)S(1)}, f32[16,8,128]{2,1,0:T(8,128)}, u32[]{:S(2)}) copy-start(f32[16,8,128]{2,1,0:T(8,128)} %conduct.3) | copy-start | bytes 196612
  2.6 26.1 %copy-start.23 = (s32[512]{0:T(512)S(1)}, s32[512]{0:T(512)}, u32[]{:S(2)}) copy-start(s32[512]{0:T(512)} %param.16) | copy-start | bytes 6148
  2.6 26.1 %copy-start.24 = (f32[512]{0:T(512)S(1)}, f32[512]{0:T(512)}, u32[]{:S(2)}) copy-start(f32[512]{0:T(512)} %param.17) | copy-start | bytes 6148
  2.6 26.1 %copy-start.25 = (f32[512]{0:T(512)S(1)}, f32[512]{0:T(512)}, u32[]{:S(2)}) copy-start(f32[512]{0:T(512)} %param.18) | copy-start | bytes 6148
  6.9 32.9 %all-to-all-start.5 = ((bf16[128,40,128]{2,1,0:T(8,128)(2,1)}), bf16[128,40,128]{2,1,0:T(8,128)(2,1)S(1)}, u32[]{:S(2)}, u32[]{:S(2)}) async-start(bf16[128,40,128]{2,1,0:T(8,128)(2,1)} %pack.1), calls=%async_computation.5 | async-start | bytes 2621440 | tf_op jit(solution)/shard_map/all_to_all | solution.py:922
  21.1 1.0 copy-start.3
  22.1 0.6 copy-start.15
  22.7 0.6 copy-start.18
  23.3 0.6 copy-start.20
  23.9 29.5 %collective-permute-start = (f32[208,8,128]{2,1,0:T(8,128)}, f32[208,8,128]{2,1,0:T(8,128)S(1)}, u32[]{:S(2)}, u32[]{:S(2)}) collective-permute-start(f32[208,8,128]{2,1,0:T(8,128)} %get-tuple-element.76), channel_id=1, source_target_pairs={{0,1},{1,2},{2,3},{3,4},{4,5},{5,6},{6,7},{7,8},{8,9},{9,10},{10,1... | collective-permute-start | bytes 2555912 | tf_op jit(solution)/shard_map/ppermute | solution.py:928
  27.4 26.8 %collective-permute-start.1 = (f32[208,8,128]{2,1,0:T(8,128)}, f32[208,8,128]{2,1,0:T(8,128)S(1)}, u32[]{:S(2)}, u32[]{:S(2)}) collective-permute-start(f32[208,8,128]{2,1,0:T(8,128)} %get-tuple-element.77), channel_id=1, source_target_pairs={{1,0},{2,1},{3,2},{4,3},{5,4},{6,5},{7,6},{8,7},{9,8},{10,9},{11,1... | collective-permute-start | bytes 2555912 | tf_op jit(solution)/shard_map/ppermute | solution.py:928
  28.7 0.8 copy-start.22
  39.8 0.8 copy-start.14
  40.6 0.9 copy-start.16
  48.1 8.9 %collective-permute-start.3 = (f32[2,128,128]{2,1,0:T(8,128)S(1)}, f32[2,128,128]{2,1,0:T(8,128)S(1)}, u32[]{:S(2)}, u32[]{:S(2)}) collective-permute-start(f32[2,128,128]{2,1,0:T(8,128)S(1)} %get-tuple-element.84.heat_own), channel_id=1, source_target_pairs={{1,0},{2,1},{3,2},{4,3},{5,4},{6,5},{7,6},{8,7},{9,8},{10,9},{11,1... | collective-permute-start | bytes 393224 | tf_op jit(solution)/shard_map/ppermute | solution.py:928
  49.4 7.6 %collective-permute-start.2 = (f32[2,128,128]{2,1,0:T(8,128)S(1)}, f32[2,128,128]{2,1,0:T(8,128)S(1)}, u32[]{:S(2)}, u32[]{:S(2)}) collective-permute-start(f32[2,128,128]{2,1,0:T(8,128)S(1)} %get-tuple-element.84.heat_own), channel_id=1, source_target_pairs={{0,1},{1,2},{2,3},{3,4},{4,5},{5,6},{6,7},{7,8},{8,9},{9,10},{10,1... | collective-permute-start | bytes 393224 | tf_op jit(solution)/shard_map/ppermute | solution.py:928
  54.2 11.4 %copy-start = (f32[208,8,128]{2,1,0:T(8,128)}, f32[208,8,128]{2,1,0:T(8,128)S(1)}, u32[]{:S(2)}) copy-start(f32[208,8,128]{2,1,0:T(8,128)S(1)} %collective-permute-done.1.high) | copy-start | bytes 2555908
  57.0 2.5 %copy-start.8 = (f32[2,128,128]{2,1,0:T(8,128)}, f32[2,128,128]{2,1,0:T(8,128)S(1)}, u32[]{:S(2)}) copy-start(f32[2,128,128]{2,1,0:T(8,128)S(1)} %collective-permute-done.3.heat_high) | copy-start | bytes 393220
  57.0 3.2 %copy-start.10 = (f32[2,128,128]{2,1,0:T(8,128)}, f32[2,128,128]{2,1,0:T(8,128)S(1)}, u32[]{:S(2)}) copy-start(f32[2,128,128]{2,1,0:T(8,128)S(1)} %collective-permute-done.2.heat_low) | copy-start | bytes 393220
  57.0 0.9 copy-start.19
  57.9 0.8 copy-start.21
  59.5 0.7 copy-start.6
  60.2 24.1 %collective-permute-start.4 = (f32[49,8,128]{2,1,0:T(8,128)}, f32[49,8,128]{2,1,0:T(8,128)}, u32[]{:S(2)}, u32[]{:S(2)}) collective-permute-start(f32[49,8,128]{2,1,0:T(8,128)} %get-tuple-element.85), channel_id=1, source_target_pairs={{0,16},{16,32},{32,48},{48,64},{64,80},{80,96},{96,112},{1,17},{17... | collective-permute-start | bytes 602120 | tf_op jit(solution)/shard_map/ppermute | solution.py:928
  63.6 20.7 %collective-permute-start.5 = (f32[49,8,128]{2,1,0:T(8,128)}, f32[49,8,128]{2,1,0:T(8,128)}, u32[]{:S(2)}, u32[]{:S(2)}) collective-permute-start(f32[49,8,128]{2,1,0:T(8,128)} %get-tuple-element.86), channel_id=1, source_target_pairs={{16,0},{32,16},{48,32},{64,48},{80,64},{96,80},{112,96},{17,1},{33... | collective-permute-start | bytes 602120 | tf_op jit(solution)/shard_map/ppermute | solution.py:928
  65.6 18.7 %all-to-all-start.6 = ((f32[128,1,128]{2,1,0:T(1,128)}), f32[128,1,128]{2,1,0:T(1,128)}, u32[]{:S(2)}, u32[]{:S(2)}) async-start(f32[128,1,128]{2,1,0:T(1,128)} %get-tuple-element.87), calls=%async_computation.6 | async-start | bytes 131072 | tf_op jit(solution)/shard_map/all_to_all | solution.py:922
  74.7 1.2 copy-start.1
  84.3 1.2 copy-start.2
  85.4 1.2 copy-start.4
  86.7 0.9 copy-start.7
  87.6 0.9 copy-start.9
  88.5 0.9 copy-start.11
  99.1 41.4 %copy-start.27 = (f32[2,20,144,128]{3,2,1,0:T(8,128)}, f32[2,20,144,128]{3,2,1,0:T(8,128)S(1)}, u32[]{:S(2)}) copy-start(f32[2,20,144,128]{3,2,1,0:T(8,128)S(1)} %get-tuple-element.90.coef) | copy-start | bytes 8847364
  99.2 41.4 %copy-start.29 = (f32[2,20,144,128]{3,2,1,0:T(8,128)}, f32[2,20,144,128]{3,2,1,0:T(8,128)S(1)}, u32[]{:S(2)}) copy-start(f32[2,20,144,128]{3,2,1,0:T(8,128)S(1)} %get-tuple-element.88.field) | copy-start | bytes 8847364
  112.8 21.2 %copy-start.30 = (f32[16,8,128]{2,1,0:T(8,128)S(1)}, f32[16,8,128]{2,1,0:T(8,128)}, u32[]{:S(2)}) copy-start(f32[16,8,128]{2,1,0:T(8,128)} %get-tuple-element.97.data) | copy-start | bytes 196612
  112.8 21.2 %copy-start.31 = (f32[8,128]{1,0:T(8,128)S(1)}, f32[8,128]{1,0:T(8,128)}, u32[]{:S(2)}) copy-start(f32[8,128]{1,0:T(8,128)} %get-tuple-element.96.weight) | copy-start | bytes 12292
  140.5 18.4 %all-to-all-start.9 = ((f32[128,8,128]{2,1,0:T(8,128)}), f32[128,8,128]{2,1,0:T(8,128)S(1)}, u32[]{:S(2)}, u32[]{:S(2)}) async-start(f32[128,8,128]{2,1,0:T(8,128)} %get-tuple-element.98), calls=%async_computation.9 | async-start | bytes 1048576 | tf_op jit(solution)/shard_map/all_to_all | solution.py:922

commit v9 on v8

--- a/solution.py
+++ b/solution.py
@@ -26,27 +26,38 @@
     return pl.BlockSpec(memory_space=pltpu.VMEM)
 
 
-def params():
-    return pltpu.CompilerParams(vmem_limit_bytes=LIMIT)
-
-
-def lanes():
-    return lax.broadcasted_iota(jnp.int32, (CY, CX), 1)
-
-
-def rows():
-    return lax.broadcasted_iota(jnp.int32, (CY, CX), 0)
-
-
-def pack_kernel(owner_far, heat_far, voxel_far, out, owner, heat, voxel, wide, high, low, inverse, sems):
+def hspec():
+    return pl.BlockSpec(memory_space=pltpu.HBM)
+
+
+def far(*arrays):
+    return [pltpu.with_memory_space_constraint(array, pltpu.HBM) for array in arrays]
+
+
+def fetch(sems, pairs):
     copies = [
-        pltpu.make_async_copy(far, near, sems.at[i])
-        for i, (far, near) in enumerate(
-            ((owner_far, owner), (heat_far, heat), (voxel_far, voxel))
-        )
+        pltpu.make_async_copy(source, target, sems.at[i])
+        for i, (source, target) in enumerate(pairs)
     ]
     for copy in copies:
         copy.start()
+    return copies
+
+
+def params():
+    return pltpu.CompilerParams(vmem_limit_bytes=LIMIT)
+
+
+def lanes():
+    return lax.broadcasted_iota(jnp.int32, (CY, CX), 1)
+
+
+def rows():
+    return lax.broadcasted_iota(jnp.int32, (CY, CX), 0)
+
+
+def pack_kernel(owner_far, heat_far, voxel_far, out, owner, heat, voxel, wide, high, low, inverse, sems):
+    copies = fetch(sems, ((owner_far, owner), (heat_far, heat), (voxel_far, voxel)))
     blocks = owner.shape[0]
     devices = out.shape[0]
 
@@ -115,7 +126,7 @@
     return pl.pallas_call(
         pack_kernel,
         out_shape=jax.ShapeDtypeStruct((devices, ROWS, CX), BF16),
-        in_specs=[pl.BlockSpec(memory_space=pltpu.HBM)] * 3,
+        in_specs=[hspec()] * 3,
         out_specs=vspec(),
         scratch_shapes=[
             pltpu.SMEM((blocks,), jnp.int32),
@@ -129,7 +140,7 @@
         ],
         compiler_params=params(),
         name="pack",
-    )(owner, heat, voxel)
+    )(*far(owner, heat, voxel))
 
 
 HALO = 6
@@ -140,7 +151,7 @@
 OWN = jax.ShapeDtypeStruct((2, CY, CX, CX), F32)
 XS = 8 * XT
 WIDE = jax.ShapeDtypeStruct((2, YS, XS, CX), F32)
-EDGE = 2 * HALO * (XT - 2)
+EDGE = 2 * HALO
 SIDE = 2 * YS
 
 
@@ -149,8 +160,8 @@
 ):
     turned = (0.5 * conduct[...].reshape(CX, CX)).T.reshape(XT - 2, 8, CX)
     turned_c[...] = turned
-    to_high[EDGE:] = turned
-    to_low[EDGE:] = turned
+    to_high[EDGE] = turned
+    to_low[EDGE] = turned
     peak = jnp.zeros((8, CX), F32)
     for zi in range(2):
         for y in range(CY):
@@ -169,11 +180,9 @@
             edge_left[zi * CY + y] = turned[0]
             edge_right[zi * CY + y] = turned[XT - 3]
             if y >= CY - HALO:
-                at = (zi * HALO + y - (CY - HALO)) * (XT - 2)
-                to_high[at : at + XT - 2] = turned
+                to_high[zi * HALO + y - (CY - HALO)] = turned
             if y < HALO:
-                at = (zi * HALO + y) * (XT - 2)
-                to_low[at : at + XT - 2] = turned
+                to_low[zi * HALO + y] = turned
     quiet[...] = peak
     for m in range(M):
         for zi in range(2):
@@ -181,7 +190,7 @@
 
 
 def relayout(state, conduct):
-    edge = jax.ShapeDtypeStruct((EDGE + XT - 2, 8, CX), F32)
+    edge = jax.ShapeDtypeStruct((EDGE + 1, XT - 2, 8, CX), F32)
     side = jax.ShapeDtypeStruct((2 * CY, 8, CX), F32)
     return pl.pallas_call(
         relayout_kernel,
@@ -203,24 +212,24 @@
 
 
 def side_kernel(
-    edge_left, edge_right, turned_c, low, high, heat_low, heat_own, heat_high, to_left, to_right
+    edge_left, edge_right, turned_c, low, high, heat_low, heat_own, heat_high,
+    to_left, to_right, sems,
 ):
+    pairs = []
     for out, edge, t in ((to_left, edge_left, 0), (to_right, edge_right, XT - 3)):
         for zi in range(2):
-            for y in range(YS):
-                if y < HALO:
-                    part = low[(zi * HALO + y) * (XT - 2) + t]
-                elif y < HALO + CY:
-                    part = edge[zi * CY + y - HALO]
-                else:
-                    part = high[(zi * HALO + y - HALO - CY) * (XT - 2) + t]
-                out[zi * YS + y] = part
-        out[SIDE] = low[EDGE + t]
-        out[SIDE + 1] = turned_c[t]
-        out[SIDE + 2] = high[EDGE + t]
-        for g, heat in enumerate((heat_low, heat_own, heat_high)):
-            for zi in range(2):
-                out[SIDE + 3 + 2 * g + zi] = heat[zi, 8 * t : 8 * t + 8, :]
+            at, rows_at = zi * YS, slice(zi * HALO, zi * HALO + HALO)
+            pairs += [
+                (low.at[rows_at, t], out.at[at : at + HALO]),
+                (edge.at[zi * CY : zi * CY + CY], out.at[at + HALO : at + HALO + CY]),
+                (high.at[rows_at, t], out.at[at + HALO + CY : at + YS]),
+            ]
+            for g, heat in enumerate((heat_low, heat_own, heat_high)):
+                pairs.append((heat.at[zi, 8 * t : 8 * t + 8, :], out.at[SIDE + 3 + 2 * g + zi]))
+        for g, part in enumerate((low.at[EDGE, t], turned_c.at[t], high.at[EDGE, t])):
+            pairs.append((part, out.at[SIDE + g]))
+    for copy in fetch(sems, pairs):
+        copy.wait()
 
 
 def sides(*operands):
@@ -228,11 +237,12 @@
     return pl.pallas_call(
         side_kernel,
         out_shape=[shape, shape],
-        in_specs=[vspec()] * len(operands),
+        in_specs=[hspec()] * len(operands),
         out_specs=[vspec()] * 2,
+        scratch_shapes=[pltpu.SemaphoreType.DMA((30,))],
         compiler_params=params(),
         name="sides",
-    )(*operands)
+    )(*far(*operands))
 
 
 def placed(strip, zi, y0):
@@ -247,10 +257,11 @@
     return row if 0 <= row < YS else None
 
 
-def coef_kernel(own, low, high, out):
-    strip = jnp.concatenate(
-        [low[EDGE:].reshape(CX, CX), own[...].reshape(CX, CX), high[EDGE:].reshape(CX, CX)], axis=0
-    )
+def coef_kernel(own, low, high, out, tiles, sems):
+    pairs = ((low.at[EDGE], tiles.at[0]), (own, tiles.at[1]), (high.at[EDGE], tiles.at[2]))
+    for copy in fetch(sems, pairs):
+        copy.wait()
+    strip = tiles[...].reshape(3 * CX, CX)
     for zi in range(2):
         for y0 in range(CY):
             part = placed(strip, zi, y0)
@@ -264,14 +275,18 @@
     return pl.pallas_call(
         coef_kernel,
         out_shape=jax.ShapeDtypeStruct((2, YS, CX, CX), F32),
-        in_specs=[vspec()] * 3,
+        in_specs=[hspec()] * 3,
         out_specs=vspec(),
+        scratch_shapes=[VM((3, XT - 2, 8, CX), F32), pltpu.SemaphoreType.DMA((3,))],
         compiler_params=params(),
         name="coefs",
-    )(own, low, high)
-
-
-def deposit_kernel(incoming, top, conduct, quiet, out, peaks, total):
+    )(*far(own, low, high))
+
+
+def deposit_kernel(
+    incoming, top_far, conduct_far, quiet_far, out, peaks, total, top, conduct, quiet, sems
+):
+    copies = fetch(sems, ((top_far, top), (conduct_far.at[0:2], conduct), (quiet_far, quiet)))
     sources = incoming.shape[0]
     group = 32
     place = lax.broadcasted_iota(jnp.int32, (CX, CX), 0).astype(F32).astype(BF16)
@@ -305,6 +320,8 @@
     lax.fori_loop(0, sources // group, one, 0)
     for zi in range(2):
         out[zi] = (0.5 * total[zi * CX : (zi + 1) * CX, :]).T
+    for copy in copies:
+        copy.wait()
     peak = quiet[...]
     for zi in range(2):
         c = 0.5 * conduct[zi]
@@ -327,12 +344,18 @@
             jax.ShapeDtypeStruct((2, CX, CX), F32),
             jax.ShapeDtypeStruct((devices, 1, CX), F32),
         ],
-        in_specs=[vspec()] * 4,
+        in_specs=[vspec()] + [hspec()] * 3,
         out_specs=[vspec()] * 2,
-        scratch_shapes=[VM((2 * CY * M, CX), F32)],
+        scratch_shapes=[
+            VM((2 * CY * M, CX), F32),
+            VM(top.shape, F32),
+            VM((2, CY, CX), F32),
+            VM(quiet.shape, F32),
+            pltpu.SemaphoreType.DMA((3,)),
+        ],
         compiler_params=params(),
         name="deposit",
-    )(incoming, top, conduct, quiet)
+    )(incoming, *far(top, conduct, quiet))
 
 
 def whole_peak(value):
@@ -496,11 +519,31 @@
 
 
 def heated_kernel(
-    inside, own, low, high, left, right,
-    heat_low, heat_own, heat_high,
-    coef_main, peaks, out, coef, changes, parts, start, half, next_half, above,
+    inside, peaks, own_far, low_far, high_far, left_far, right_far,
+    heat_low_far, heat_own_far, heat_high_far, coef_far,
+    out, coef, changes, parts, start, half, next_half, above,
+    own, low, high, left, right, heat_low, heat_own, heat_high, coef_main, sems,
 ):
+    spans = (slice(0, HALO), slice(HALO, HALO + CY), slice(HALO + CY, YS))
+    copies = fetch(
+        sems,
+        [
+            (left_far, left),
+            (right_far, right),
+            (heat_low_far, heat_low),
+            (low_far.at[0:EDGE], low),
+            (coef_far.at[:, spans[0]], coef_main.at[:, spans[0]]),
+            (heat_own_far, heat_own),
+            (own_far, own),
+            (coef_far.at[:, spans[1]], coef_main.at[:, spans[1]]),
+            (heat_high_far, heat_high),
+            (high_far.at[0:EDGE], high),
+            (coef_far.at[:, spans[2]], coef_main.at[:, spans[2]]),
+        ],
+    )
     top = lanes() < M
+    for copy in copies[0:2]:
+        copy.wait()
 
     strip = jnp.concatenate(
         [side[SIDE + g] for g in range(3) for side in (left, right)], axis=0
@@ -537,12 +580,18 @@
                 half[zi, yy, tile(t), :] = after
 
     def edge(ref, y):
-        return lambda zi, t: ref[(zi * HALO + y) * (XT - 2) + t]
-
+        return lambda zi, t: ref[zi * HALO + y, t]
+
+    for copy in copies[2:5]:
+        copy.wait()
     for y in range(HALO):
         row(0, heat_low, edge(low, y), y + CY - HALO, y)
+    for copy in copies[5:8]:
+        copy.wait()
     for y in range(CY):
         row(1, heat_own, lambda zi, t: own[zi, y, tile(t), :], y, y + HALO)
+    for copy in copies[8:11]:
+        copy.wait()
     for y in range(HALO):
         row(2, heat_high, edge(high, y), y, y + HALO + CY)
 
@@ -567,16 +616,20 @@
 
 
 def heated(inside, prior, halos, heat, coef, peaks):
-    operands = [inside, *prior, *halos, *heat, coef, peaks]
+    operands = far(*prior, *halos, *heat, coef)
+    edge = VM((EDGE, XT - 2, 8, CX), F32)
     return pl.pallas_call(
         heated_kernel,
         out_shape=[WIDE, WIDE, WIDE, jax.ShapeDtypeStruct(peaks.shape, F32)],
-        in_specs=[smem()] + [vspec()] * (len(operands) - 1),
+        in_specs=[smem(), vspec()] + [hspec()] * len(operands),
         out_specs=[vspec()] * 4,
-        scratch_shapes=[VM(WIDE.shape, F32)] * 3 + [VM(ROW, F32)],
+        scratch_shapes=[VM(WIDE.shape, F32)] * 3
+        + [VM(ROW, F32), VM(OWN.shape, F32), edge, edge]
+        + [VM(part.shape, F32) for part in (*halos, *heat, coef)]
+        + [pltpu.SemaphoreType.DMA((11,))],
         compiler_params=params(),
         name="heated",
-    )(*operands)
+    )(inside, peaks, *operands)
 
 
 def first_of_pair(field, changes, coef, step, first, end, out, half):
@@ -701,9 +754,11 @@
 
 
 def last_kernel(
-    inside, field, changes, coef, parts, status, weight, data,
-    out, out_changes, sums, out_status, middle, half, near, near_half, above, flat,
+    inside, field, changes, coef, parts, status, weight_far, data_far,
+    out, out_changes, sums, out_status,
+    middle, half, near, near_half, above, flat, weight, data, sems,
 ):
+    copies = fetch(sems, ((weight_far, weight), (data_far, data)))
     number = SUBSTEPS - 3
     now, then, late = agree(parts)
     bad = differs(late[0:1], status[0:1, :])
@@ -719,6 +774,8 @@
     peak = advance(
         middle, half, coef, above, inside, step_of(then), number + 2, YS - 2 - number, put
     )
+    for copy in copies:
+        copy.wait()
     closing(
         near, near_half, above, inside, weight, data, peak, seen, out, out_changes, sums, flat
     )
@@ -729,13 +786,16 @@
 
 
 def last(inside, field, changes, coef, parts, status, pixels):
-    operands = [inside, field, changes, coef, parts, status, *pixels]
+    operands = [inside, field, changes, coef, parts, status, *far(*pixels)]
     return pl.pallas_call(
         last_kernel,
         out_shape=[OWN, OWN, sums_shape(parts.shape[0]), STATUS],
-        in_specs=[smem()] + [vspec()] * (len(operands) - 1),
+        in_specs=[smem()] + [vspec()] * 5 + [hspec()] * 2,
         out_specs=[vspec()] * 4,
-        scratch_shapes=[VM(WIDE.shape, F32)] * 4 + [VM(ROW, F32), VM((M, CX), F32)],
+        scratch_shapes=[VM(WIDE.shape, F32)] * 4
+        + [VM(ROW, F32), VM((M, CX), F32)]
+        + [VM(part.shape, F32) for part in pixels]
+        + [pltpu.SemaphoreType.DMA((2,))],
         compiler_params=params(),
         name="last_pair",
     )(*operands)

time: 166 us -> 161 us (0.970)
  local copies, waits for them, and re-layouts: 16.6 us -> 7.65 us
  Pallas kernels: 48.4 us -> 51.4 us
    unnamed x62 -> x46, local copies, waits for them, and re-layouts: 16.6 us -> 7.65 us
    ppermute x6, waiting for transfers between devices: 3.6 us -> 5.37 us  [move(): return lax.ppermute(part, axis, pairs)]
  transfers between devices with their start and end apart: 9 -> 9, of which waited for: 5 -> 6; matrix products, arithmetic and copies ran while one was open for 0% -> 0% of each run, Pallas kernels for 9% -> 9%
where the time goes in v9:
time: 161 us; the launch traced here: 160 us
  Pallas kernels  51.4 us (32%)
  starting transfers between devices  39.8 us (25%)
  waiting for transfers between devices  31.3 us (19%)
  blocking collectives  28.5 us (18%)
  local copies, waits for them, and re-layouts  7.65 us (5%)
    all_to_all x2, blocking collectives, exchange(): return lax.all_to_all(parts, BOTH, split_axis=0, concat_axis=0, tiled=True)  28.5 us
    all_to_all x3, waiting for transfers between devices, exchange(): return lax.all_to_all(parts, BOTH, split_axis=0, concat_axis=0, tiled=True)  26 us
    all_to_all x3, starting transfers between devices, exchange(): return lax.all_to_all(parts, BOTH, split_axis=0, concat_axis=0, tiled=True)  24.6 us
    ppermute x6, starting transfers between devices, move(): return lax.ppermute(part, axis, pairs)  15.3 us
    pallas_call x1, Pallas kernels, heated(): pl.pallas_call(heated_kernel, out_shape=[WIDE, WIDE, WIDE, jax.ShapeDtype...  11.2 us
    unnamed x46, local copies, waits for them, and re-layouts  7.65 us
    pallas_call x1, Pallas kernels, pair(): pl.pallas_call(functools.partial(pair_kernel, number), out_shape=[WIDE, W...  7.35 us
    pallas_call x1, Pallas kernels, deposit(): pl.pallas_call(deposit_kernel, out_shape=[jax.ShapeDtypeStruct((2, CX, CX...  6.74 us
  transfers between devices with their start and end apart: 9, of which 6 were waited for; matrix products, arithmetic and copies ran while one was open for 0% of the time, Pallas kernels for 9%

profile of v9, /device:TPU:1, one launch (start us, length us, event | category | flops | bytes accessed | tf_op | source)
XLA Modules:
  0.0 159.9 jit_solution(10379503221693289231)
XLA Ops:
  0.0 4.5 %pack.1 = bf16[128,40,128]{2,1,0:T(8,128)(2,1)} custom-call(s32[128]{0:T(128)} %bitcast.12, bf16[16,128,128]{2,1,0:T(8,128)(2,1)} %heat_far.1, s32[128,128]{1,0:T(8,128)} %voxel_far.1), custom_call_target="tpu_custom_call" | custom-call | tf_op jit(solution)/shard_map/pack/pallas_call | solution.py:126
  4.6 11.5 %all-to-all-start.5 = ((bf16[128,40,128]{2,1,0:T(8,128)(2,1)}), bf16[128,40,128]{2,1,0:T(8,128)(2,1)S(1)}, u32[]{:S(2)}, u32[]{:S(2)}) async-start(bf16[128,40,128]{2,1,0:T(8,128)(2,1)} %pack.1), calls=%async_computation.5 | async-start | bytes 2621440 | tf_op jit(solution)/shard_map/all_to_all | solution.py:982
  16.1 0.0 copy-done.5
  16.1 0.0 copy-done.2
  16.1 2.5 %relayout.1 = (f32[2,8,128,128]{3,2,1,0:T(8,128)S(1)}, f32[16,8,128]{2,1,0:T(8,128)S(1)}, f32[13,16,8,128]{3,2,1,0:T(8,128)}, f32[13,16,8,128]{3,2,1,0:T(8,128)S...) custom-call(f32[16,16,8,128]{3,2,1,0:T(8,128)S(1)} %copy-done.2, ...), custom_call_target="tpu_custom_call" | custom-call | tf_op jit(solution)/shard_map/relayout/pallas_call | solution.py:195
  18.6 1.0 copy-done.1
  19.6 0.6 copy-done.4
  20.2 0.7 copy-done.6
  20.8 0.6 copy-done.7
  21.5 0.6 copy-done.8
  22.1 0.6 copy-done.10
  22.7 3.5 %collective-permute-start = (f32[13,16,8,128]{3,2,1,0:T(8,128)}, f32[13,16,8,128]{3,2,1,0:T(8,128)S(1)}, u32[]{:S(2)}, u32[]{:S(2)}) collective-permute-start(f32[13,16,8,128]{3,2,1,0:T(8,128)} %get-tuple-element.80), channel_id=1, source_target_pairs={{0,1},{1,2},{2,3},{3,4},{4,5},{5,6},{6,7},{7,8},{8,9},{9,10},{10,1... | collective-permute-start | bytes 2555912 | tf_op jit(solution)/shard_map/ppermute | solution.py:988
  26.1 1.3 collective-permute-start.1
  27.5 2.4 %pixels.1 = (f32[8,128]{1,0:T(8,128)}, f32[16,8,128]{2,1,0:T(8,128)}) custom-call(s32[1,512]{1,0:T(1,128)S(1)} %bitcast.9, f32[1,512]{1,0:T(1,128)S(1)} %bitcast.10, f32[1,512]{1,0:T(1,128)S(1)} %bitcast.11, f32[16,512]{1,0:T(8,128)S(1)} %copy-done.9), custom_call_target="tpu_custom_call" | custom-call | tf_op jit(solution)/shard_map/pixels/pallas_call | solution.py:885
  29.8 0.1 add_convert_fusion.inside
  29.9 7.5 %all-to-all-done.5.incoming = bf16[128,40,128]{2,1,0:T(8,128)(2,1)S(1)} async-done(((bf16[128,40,128]{2,1,0:T(8,128)(2,1)}), bf16[128,40,128]{2,1,0:T(8,128)(2,1)S(1)}, u32[]{:S(2)}, u32[]{:S(2)}) %all-to-all-start.5) | async-done | bytes 1310752 | tf_op jit(solution)/shard_map/all_to_all | solution.py:982
  37.4 6.7 %deposit.1 = (f32[2,128,128]{2,1,0:T(8,128)S(1)}, f32[128,1,128]{2,1,0:T(1,128)}) custom-call(bf16[128,40,128]{2,1,0:T(8,128)(2,1)S(1)} %all-to-all-done.5.incoming, f32[16,2,8,128]{3,2,1,0:T(8,128)} %copy-done.6, f32[16,8,128]{2,1,0:T(8,128)} %conduct_far.1, f32[8,128]{1,0:T(8,128)} %copy-done.10), custom_call_target="tpu_custom_call" | custom-call | tf_op jit(solution)/shard_map/deposit/pallas_call | solution.py:341
  44.2 1.3 collective-permute-start.3
  45.5 4.0 %collective-permute-start.2 = (f32[2,128,128]{2,1,0:T(8,128)S(1)}, f32[2,128,128]{2,1,0:T(8,128)S(1)}, u32[]{:S(2)}, u32[]{:S(2)}) collective-permute-start(f32[2,128,128]{2,1,0:T(8,128)S(1)} %get-tuple-element.85.heat_own.heat_own_far), channel_id=1, source_target_pairs={{0,1},{1,2},{2,3},{3,4},{4,5},{5,6},{6,7},{7,8},{8,9},{9,10},{10,1... | collective-permute-start | bytes 393224 | tf_op jit(solution)/shard_map/ppermute | solution.py:988
  49.5 0.6 collective-permute-done.low.low_far
  50.0 2.1 %collective-permute-done.1.high.high_far = f32[13,16,8,128]{3,2,1,0:T(8,128)} collective-permute-done((f32[13,16,8,128]{3,2,1,0:T(8,128)S(1)}, f32[13,16,8,128]{3,2,1,0:T(8,128)}, u32[]{:S(2)}, u32[]{:S(2)}) %collective-permute-start.1) | collective-permute-done | bytes 852000 | tf_op jit(solution)/shard_map/ppermute | solution.py:988
  52.1 2.7 %collective-permute-done.3.heat_high.heat_high_far = f32[2,128,128]{2,1,0:T(8,128)S(1)} collective-permute-done((f32[2,128,128]{2,1,0:T(8,128)S(1)}, f32[2,128,128]{2,1,0:T(8,128)S(1)}, u32[]{:S(2)}, u32[]{:S(2)}) %collective-permute-start.3) | collective-permute-done | bytes 131104 | tf_op jit(solution)/shard_map/ppermute | solution.py:988
  54.9 0.0 collective-permute-done.2.heat_low.heat_low_far
  54.9 0.0 copy-done.17
  54.9 0.6 copy-done.18
  55.5 0.1 copy-done.19
  55.6 1.2 sides.1
  56.8 3.3 %collective-permute-start.4 = (f32[49,8,128]{2,1,0:T(8,128)S(1)}, f32[49,8,128]{2,1,0:T(8,128)S(1)}, u32[]{:S(2)}, u32[]{:S(2)}) collective-permute-start(f32[49,8,128]{2,1,0:T(8,128)S(1)} %get-tuple-element.86), channel_id=1, source_target_pairs={{0,16},{16,32},{32,48},{48,64},{64,80},{80,96},{96,112},{1,17},{17... | collective-permute-start | bytes 602120 | tf_op jit(solution)/shard_map/ppermute | solution.py:988
  60.1 1.9 %collective-permute-start.5 = (f32[49,8,128]{2,1,0:T(8,128)S(1)}, f32[49,8,128]{2,1,0:T(8,128)S(1)}, u32[]{:S(2)}, u32[]{:S(2)}) collective-permute-start(f32[49,8,128]{2,1,0:T(8,128)S(1)} %get-tuple-element.87), channel_id=1, source_target_pairs={{16,0},{32,16},{48,32},{64,48},{80,64},{96,80},{112,96},{17,1},{33... | collective-permute-start | bytes 602120 | tf_op jit(solution)/shard_map/ppermute | solution.py:988
  62.0 8.6 %all-to-all-start.6 = ((f32[128,1,128]{2,1,0:T(1,128)}), f32[128,1,128]{2,1,0:T(1,128)S(1)}, u32[]{:S(2)}, u32[]{:S(2)}) async-start(f32[128,1,128]{2,1,0:T(1,128)} %get-tuple-element.78), calls=%async_computation.6 | async-start | bytes 131072 | tf_op jit(solution)/shard_map/all_to_all | solution.py:982
  70.6 3.5 %coefs.1.coef_far = f32[2,20,128,128]{3,2,1,0:T(8,128)S(1)} custom-call(f32[16,8,128]{2,1,0:T(8,128)} %copy-done.4, f32[13,16,8,128]{3,2,1,0:T(8,128)} %copy-done.17, f32[13,16,8,128]{3,2,1,0:T(8,128)} %collective-permute-done.1.high.high_far), custom_call_target="tpu_custom_call" | custom-call | tf_op jit(solution)/shard_map/coefs/pallas_call | solution.py:275
  74.2 1.5 copy-done
  75.7 4.5 %all-to-all-done.6.peaks = f32[128,1,128]{2,1,0:T(1,128)S(1)} async-done(((f32[128,1,128]{2,1,0:T(1,128)}), f32[128,1,128]{2,1,0:T(1,128)S(1)}, u32[]{:S(2)}, u32[]{:S(2)}) %all-to-all-start.6) | async-done | bytes 65568 | tf_op jit(solution)/shard_map/all_to_all | solution.py:982
  80.2 0.0 collective-permute-done.4.left_far
  80.2 0.0 collective-permute-done.5.right_far
  80.2 0.7 copy-done.21
  80.9 0.7 copy-done.22
  81.6 11.2 %heated.1 = (f32[2,20,144,128]{3,2,1,0:T(8,128)S(1)}, f32[2,20,144,128]{3,2,1,0:T(8,128)S(1)}, f32[2,20,144,128]{3,2,1,0:T(8,128)S(1)}, f32[128,1,128]{2,1,0:T(1,128)S(1)}) custom-call(f32[4]{0:T(128)S(1)} %add_convert_fusion.inside, f32[128,1,128]{2,1,0:T(1,128)S(1)} %all-to-all-done.6.peaks, f32[2,8,128,128]{3,2,1,0:T(8,128)} %copy-done.1, ...), custom_call_target="tpu_custom_call" | custom-call | tf_op jit(solution)/shard_map/heated/pallas_call | solution.py:621
  92.8 0.0 copy-start.16
  92.8 0.0 copy-start.14
  92.8 14.6 %all_to_all.50.parts = f32[128,1,128]{2,1,0:T(1,128)S(1)} all-to-all(f32[128,1,128]{2,1,0:T(1,128)S(1)} %get-tuple-element.91), channel_id=1, replica_groups=mesh['gx'=8,'gy'=16] {'gx','gy'}, dimensions={0} | all-to-all | bytes 131072 | tf_op jit(solution)/shard_map/all_to_all | solution.py:982
  107.4 7.3 %pair_1.1 = (f32[2,20,144,128]{3,2,1,0:T(8,128)S(1)}, f32[2,20,144,128]{3,2,1,0:T(8,128)S(1)}, f32[128,1,128]{2,1,0:T(1,128)S(1)}, f32[8,128]{1,0:T(8,128)S(1)}) custom-call(f32[4]{0:T(128)S(1)} %add_convert_fusion.inside, f32[2,20,144,128]{3,2,1,0:T(8,128)S(1)} %get-tuple-element.88.field, f32[2,20,144,128]{3,2,1,0:T(8,128)S(1)} %get-tuple-element.89.changes, ...), custom_call_target="tpu_custom_call" | custom-call | tf_op jit(solution)/shard_map/pair_1/pallas_call | solution.py:682
  114.8 13.9 %all_to_all.51.parts = f32[128,1,128]{2,1,0:T(1,128)S(1)} all-to-all(f32[128,1,128]{2,1,0:T(1,128)S(1)} %get-tuple-element.94), channel_id=1, replica_groups=mesh['gx'=8,'gy'=16] {'gx','gy'}, dimensions={0} | all-to-all | bytes 131072 | tf_op jit(solution)/shard_map/all_to_all | solution.py:982
  128.7 6.5 %last_pair.1 = (f32[2,8,128,128]{3,2,1,0:T(8,128)S(1)}, f32[2,8,128,128]{3,2,1,0:T(8,128)S(1)}, f32[128,8,128]{2,1,0:T(8,128)}, f32[8,128]{1,0:T(8,128)S(1)}) custom-call(f32[4]{0:T(128)S(1)} %add_convert_fusion.inside, f32[2,20,144,128]{3,2,1,0:T(8,128)S(1)} %get-tuple-element.92.field, f32[2,20,144,128]{3,2,1,0:T(8,128)S(1)} %get-tuple-element.93.changes, ...), custom_call_target="tpu_custom_call" | custom-call | tf_op jit(solution)/shard_map/last_pair/pallas_call | solution.py:790
  135.2 4.5 %all-to-all-start.9 = ((f32[128,8,128]{2,1,0:T(8,128)}), f32[128,8,128]{2,1,0:T(8,128)S(1)}, u32[]{:S(2)}, u32[]{:S(2)}) async-start(f32[128,8,128]{2,1,0:T(8,128)} %get-tuple-element.98), calls=%async_computation.9 | async-start | bytes 1048576 | tf_op jit(solution)/shard_map/all_to_all | solution.py:982
  139.7 13.9 %all-to-all-done.9.sums = f32[128,8,128]{2,1,0:T(8,128)S(1)} async-done(((f32[128,8,128]{2,1,0:T(8,128)}), f32[128,8,128]{2,1,0:T(8,128)S(1)}, u32[]{:S(2)}, u32[]{:S(2)}) %all-to-all-start.9) | async-done | bytes 524320 | tf_op jit(solution)/shard_map/all_to_all | solution.py:982
  153.6 5.5 %update.3 = (f32[16,16,8,128]{3,2,1,0:T(8,128)}, s32[1]{0:T(128)}) custom-call(f32[128,8,128]{2,1,0:T(8,128)S(1)} %all-to-all-done.9.sums, f32[2,8,128,128]{3,2,1,0:T(8,128)S(1)} %get-tuple-element.99.field, f32[2,8,128,128]{3,2,1,0:T(8,128)S(1)} %get-tuple-element.100.changes, f32[8,128]{1,0:T(8,128)S(1)} %get-tuple-element.101.status), custom_call_target="tpu_custom_call" | custom-call | tf_op jit(solution)/shard_map/update/pallas_call | solution.py:968
  159.7 0.0 copy-done.20
  (30 shorter events, 0.1 us)
Async XLA Ops:
  0.0 16.1 %copy-start.5 = (f32[16,8,128]{2,1,0:T(8,128)S(1)}, f32[16,8,128]{2,1,0:T(8,128)}, u32[]{:S(2)}) copy-start(f32[16,8,128]{2,1,0:T(8,128)} %conduct_far.1) | copy-start | bytes 196612
  0.0 16.1 %copy-start.2 = (f32[16,16,8,128]{3,2,1,0:T(8,128)S(1)}, f32[16,16,8,128]{3,2,1,0:T(8,128)}, u32[]{:S(2)}) copy-start(f32[16,16,8,128]{3,2,1,0:T(8,128)} %state.1) | copy-start | bytes 3145732
  0.0 27.4 %copy-start.9 = (f32[16,512]{1,0:T(8,128)S(1)}, f32[16,512]{1,0:T(8,128)}, u32[]{:S(2)}) copy-start(f32[16,512]{1,0:T(8,128)} %noise.1) | copy-start | bytes 98308
  0.0 27.4 %copy-start.13 = (f32[512]{0:T(512)S(1)}, f32[512]{0:T(512)}, u32[]{:S(2)}) copy-start(f32[512]{0:T(512)} %param.18) | copy-start | bytes 6148
  0.0 27.4 %copy-start.12 = (f32[512]{0:T(512)S(1)}, f32[512]{0:T(512)}, u32[]{:S(2)}) copy-start(f32[512]{0:T(512)} %param.17) | copy-start | bytes 6148
  0.0 27.4 %copy-start.11 = (s32[512]{0:T(512)S(1)}, s32[512]{0:T(512)}, u32[]{:S(2)}) copy-start(s32[512]{0:T(512)} %param.16) | copy-start | bytes 6148
  4.6 32.9 %all-to-all-start.5 = ((bf16[128,40,128]{2,1,0:T(8,128)(2,1)}), bf16[128,40,128]{2,1,0:T(8,128)(2,1)S(1)}, u32[]{:S(2)}, u32[]{:S(2)}) async-start(bf16[128,40,128]{2,1,0:T(8,128)(2,1)} %pack.1), calls=%async_computation.5 | async-start | bytes 2621440 | tf_op jit(solution)/shard_map/all_to_all | solution.py:982
  18.6 1.0 copy-start.1
  19.6 0.6 copy-start.4
  20.2 0.7 copy-start.6
  20.8 0.6 copy-start.7
  21.4 0.6 copy-start.8
  22.1 0.6 copy-start.10
  22.7 27.4 %collective-permute-start = (f32[13,16,8,128]{3,2,1,0:T(8,128)}, f32[13,16,8,128]{3,2,1,0:T(8,128)S(1)}, u32[]{:S(2)}, u32[]{:S(2)}) collective-permute-start(f32[13,16,8,128]{3,2,1,0:T(8,128)} %get-tuple-element.80), channel_id=1, source_target_pairs={{0,1},{1,2},{2,3},{3,4},{4,5},{5,6},{6,7},{7,8},{8,9},{9,10},{10,1... | collective-permute-start | bytes 2555912 | tf_op jit(solution)/shard_map/ppermute | solution.py:988
  26.1 26.0 %collective-permute-start.1 = (f32[13,16,8,128]{3,2,1,0:T(8,128)S(1)}, f32[13,16,8,128]{3,2,1,0:T(8,128)}, u32[]{:S(2)}, u32[]{:S(2)}) collective-permute-start(f32[13,16,8,128]{3,2,1,0:T(8,128)S(1)} %get-tuple-element.81), channel_id=1, source_target_pairs={{1,0},{2,1},{3,2},{4,3},{5,4},{6,5},{7,6},{8,7},{9,8},{10,9},{11,1... | collective-permute-start | bytes 2555912 | tf_op jit(solution)/shard_map/ppermute | solution.py:988
  44.2 10.7 %copy-start.3 = (f32[2,128,128]{2,1,0:T(8,128)}, f32[2,128,128]{2,1,0:T(8,128)S(1)}, u32[]{:S(2)}) copy-start(f32[2,128,128]{2,1,0:T(8,128)S(1)} %get-tuple-element.85.heat_own.heat_own_far) | copy-start | bytes 393220
  44.2 10.7 %collective-permute-start.3 = (f32[2,128,128]{2,1,0:T(8,128)S(1)}, f32[2,128,128]{2,1,0:T(8,128)S(1)}, u32[]{:S(2)}, u32[]{:S(2)}) collective-permute-start(f32[2,128,128]{2,1,0:T(8,128)S(1)} %get-tuple-element.85.heat_own.heat_own_far), channel_id=1, source_target_pairs={{1,0},{2,1},{3,2},{4,3},{5,4},{6,5},{7,6},{8,7},{9,8},{10,9},{11,1... | collective-permute-start | bytes 393224 | tf_op jit(solution)/shard_map/ppermute | solution.py:988
  45.5 9.4 %collective-permute-start.2 = (f32[2,128,128]{2,1,0:T(8,128)S(1)}, f32[2,128,128]{2,1,0:T(8,128)S(1)}, u32[]{:S(2)}, u32[]{:S(2)}) collective-permute-start(f32[2,128,128]{2,1,0:T(8,128)S(1)} %get-tuple-element.85.heat_own.heat_own_far), channel_id=1, source_target_pairs={{0,1},{1,2},{2,3},{3,4},{4,5},{5,6},{6,7},{7,8},{8,9},{9,10},{10,1... | collective-permute-start | bytes 393224 | tf_op jit(solution)/shard_map/ppermute | solution.py:988
  50.0 4.8 %copy-start.17 = (f32[13,16,8,128]{3,2,1,0:T(8,128)}, f32[13,16,8,128]{3,2,1,0:T(8,128)S(1)}, u32[]{:S(2)}) copy-start(f32[13,16,8,128]{3,2,1,0:T(8,128)S(1)} %collective-permute-done.low.low_far) | copy-start | bytes 2555908
  54.9 0.7 copy-start.18
  54.9 0.7 copy-start.19
  56.8 23.4 %collective-permute-start.4 = (f32[49,8,128]{2,1,0:T(8,128)S(1)}, f32[49,8,128]{2,1,0:T(8,128)S(1)}, u32[]{:S(2)}, u32[]{:S(2)}) collective-permute-start(f32[49,8,128]{2,1,0:T(8,128)S(1)} %get-tuple-element.86), channel_id=1, source_target_pairs={{0,16},{16,32},{32,48},{48,64},{64,80},{80,96},{96,112},{1,17},{17... | collective-permute-start | bytes 602120 | tf_op jit(solution)/shard_map/ppermute | solution.py:988
  60.1 20.1 %collective-permute-start.5 = (f32[49,8,128]{2,1,0:T(8,128)S(1)}, f32[49,8,128]{2,1,0:T(8,128)S(1)}, u32[]{:S(2)}, u32[]{:S(2)}) collective-permute-start(f32[49,8,128]{2,1,0:T(8,128)S(1)} %get-tuple-element.87), channel_id=1, source_target_pairs={{16,0},{32,16},{48,32},{64,48},{80,64},{96,80},{112,96},{17,1},{33... | collective-permute-start | bytes 602120 | tf_op jit(solution)/shard_map/ppermute | solution.py:988
  62.0 18.2 %all-to-all-start.6 = ((f32[128,1,128]{2,1,0:T(1,128)}), f32[128,1,128]{2,1,0:T(1,128)S(1)}, u32[]{:S(2)}, u32[]{:S(2)}) async-start(f32[128,1,128]{2,1,0:T(1,128)} %get-tuple-element.78), calls=%async_computation.6 | async-start | bytes 131072 | tf_op jit(solution)/shard_map/all_to_all | solution.py:982
  74.2 1.5 copy-start
  80.2 0.7 copy-start.21
  80.9 0.7 copy-start.22
  92.8 22.0 %copy-start.16 = (f32[2,20,144,128]{3,2,1,0:T(8,128)}, f32[2,20,144,128]{3,2,1,0:T(8,128)S(1)}, u32[]{:S(2)}) copy-start(f32[2,20,144,128]{3,2,1,0:T(8,128)S(1)} %get-tuple-element.88.field) | copy-start | bytes 8847364
  92.8 35.9 %copy-start.14 = (f32[2,20,144,128]{3,2,1,0:T(8,128)}, f32[2,20,144,128]{3,2,1,0:T(8,128)S(1)}, u32[]{:S(2)}) copy-start(f32[2,20,144,128]{3,2,1,0:T(8,128)S(1)} %get-tuple-element.90.coef) | copy-start | bytes 8847364
  135.1 24.6 %copy-start.20 = (f32[16,8,128]{2,1,0:T(8,128)S(1)}, f32[16,8,128]{2,1,0:T(8,128)}, u32[]{:S(2)}) copy-start(f32[16,8,128]{2,1,0:T(8,128)} %get-tuple-element.97.data_far) | copy-start | bytes 196612
  135.1 24.6 %copy-start.23 = (f32[8,128]{1,0:T(8,128)S(1)}, f32[8,128]{1,0:T(8,128)}, u32[]{:S(2)}) copy-start(f32[8,128]{1,0:T(8,128)} %get-tuple-element.96.weight_far) | copy-start | bytes 12292
  135.2 18.4 %all-to-all-start.9 = ((f32[128,8,128]{2,1,0:T(8,128)}), f32[128,8,128]{2,1,0:T(8,128)S(1)}, u32[]{:S(2)}, u32[]{:S(2)}) async-start(f32[128,8,128]{2,1,0:T(8,128)} %get-tuple-element.98), calls=%async_computation.9 | async-start | bytes 1048576 | tf_op jit(solution)/shard_map/all_to_all | solution.py:982

commit v10 on v9

--- a/solution.py
+++ b/solution.py
@@ -32,6 +32,10 @@
 
 def far(*arrays):
     return [pltpu.with_memory_space_constraint(array, pltpu.HBM) for array in arrays]
+
+
+def kept(shape):
+    return pltpu.HBM(tuple(shape), F32)
 
 
 def fetch(sems, pairs):
@@ -190,19 +194,19 @@
 
 
 def relayout(state, conduct):
-    edge = jax.ShapeDtypeStruct((EDGE + 1, XT - 2, 8, CX), F32)
-    side = jax.ShapeDtypeStruct((2 * CY, 8, CX), F32)
+    edge = kept((EDGE + 1, XT - 2, 8, CX))
+    side = kept((2 * CY, 8, CX))
     return pl.pallas_call(
         relayout_kernel,
         out_shape=[
-            OWN,
-            jax.ShapeDtypeStruct((XT - 2, 8, CX), F32),
+            kept(OWN.shape),
+            kept((XT - 2, 8, CX)),
             edge,
             edge,
             side,
             side,
-            jax.ShapeDtypeStruct((M, 2, CY, CX), F32),
-            jax.ShapeDtypeStruct((8, CX), F32),
+            kept((M, 2, CY, CX)),
+            kept((8, CX)),
         ],
         in_specs=[vspec()] * 2,
         out_specs=[vspec()] * 8,
@@ -341,7 +345,7 @@
     return pl.pallas_call(
         deposit_kernel,
         out_shape=[
-            jax.ShapeDtypeStruct((2, CX, CX), F32),
+            kept((2, CX, CX)),
             jax.ShapeDtypeStruct((devices, 1, CX), F32),
         ],
         in_specs=[vspec()] + [hspec()] * 3,
@@ -519,31 +523,23 @@
 
 
 def heated_kernel(
-    inside, peaks, own_far, low_far, high_far, left_far, right_far,
-    heat_low_far, heat_own_far, heat_high_far, coef_far,
+    inside, peaks, left, right, coef_main, own_far, low_far, high_far,
+    heat_low_far, heat_own_far, heat_high_far,
     out, coef, changes, parts, start, half, next_half, above,
-    own, low, high, left, right, heat_low, heat_own, heat_high, coef_main, sems,
+    own, low, high, heat_low, heat_own, heat_high, sems,
 ):
-    spans = (slice(0, HALO), slice(HALO, HALO + CY), slice(HALO + CY, YS))
     copies = fetch(
         sems,
         [
-            (left_far, left),
-            (right_far, right),
             (heat_low_far, heat_low),
             (low_far.at[0:EDGE], low),
-            (coef_far.at[:, spans[0]], coef_main.at[:, spans[0]]),
             (heat_own_far, heat_own),
             (own_far, own),
-            (coef_far.at[:, spans[1]], coef_main.at[:, spans[1]]),
             (heat_high_far, heat_high),
             (high_far.at[0:EDGE], high),
-            (coef_far.at[:, spans[2]], coef_main.at[:, spans[2]]),
         ],
     )
     top = lanes() < M
-    for copy in copies[0:2]:
-        copy.wait()
 
     strip = jnp.concatenate(
         [side[SIDE + g] for g in range(3) for side in (left, right)], axis=0
@@ -582,15 +578,15 @@
     def edge(ref, y):
         return lambda zi, t: ref[zi * HALO + y, t]
 
-    for copy in copies[2:5]:
+    for copy in copies[0:2]:
         copy.wait()
     for y in range(HALO):
         row(0, heat_low, edge(low, y), y + CY - HALO, y)
-    for copy in copies[5:8]:
+    for copy in copies[2:4]:
         copy.wait()
     for y in range(CY):
         row(1, heat_own, lambda zi, t: own[zi, y, tile(t), :], y, y + HALO)
-    for copy in copies[8:11]:
+    for copy in copies[4:6]:
         copy.wait()
     for y in range(HALO):
         row(2, heat_high, edge(high, y), y, y + HALO + CY)
@@ -616,20 +612,21 @@
 
 
 def heated(inside, prior, halos, heat, coef, peaks):
-    operands = far(*prior, *halos, *heat, coef)
+    near = [inside, peaks, *halos, coef]
+    operands = far(*prior, *heat)
     edge = VM((EDGE, XT - 2, 8, CX), F32)
     return pl.pallas_call(
         heated_kernel,
         out_shape=[WIDE, WIDE, WIDE, jax.ShapeDtypeStruct(peaks.shape, F32)],
-        in_specs=[smem(), vspec()] + [hspec()] * len(operands),
+        in_specs=[smem()] + [vspec()] * 4 + [hspec()] * len(operands),
         out_specs=[vspec()] * 4,
         scratch_shapes=[VM(WIDE.shape, F32)] * 3
         + [VM(ROW, F32), VM(OWN.shape, F32), edge, edge]
-        + [VM(part.shape, F32) for part in (*halos, *heat, coef)]
-        + [pltpu.SemaphoreType.DMA((11,))],
+        + [VM(part.shape, F32) for part in heat]
+        + [pltpu.SemaphoreType.DMA((6,))],
         compiler_params=params(),
         name="heated",
-    )(inside, peaks, *operands)
+    )(*near, *operands)
 
 
 def first_of_pair(field, changes, coef, step, first, end, out, half):
@@ -884,10 +881,7 @@
 def pixel_sums(cell, observed, variance, noise):
     return pl.pallas_call(
         pixel_kernel,
-        out_shape=[
-            jax.ShapeDtypeStruct((CY, CX), F32),
-            jax.ShapeDtypeStruct((M, CY, CX), F32),
-        ],
+        out_shape=[kept((CY, CX)), kept((M, CY, CX))],
         in_specs=[vspec()] * 4,
         out_specs=[vspec()] * 2,
         compiler_params=params(),
@@ -1021,7 +1015,9 @@
     )
     heat, peaks = deposit(incoming, top, conductivity, quiet)
     heat_low, heat_high = move(heat, "gy", True), move(heat, "gy", False)
-    peaks = exchange(peaks)
+    low, high, heat_low, heat_high, peaks = lax.optimization_barrier(
+        (low, high, heat_low, heat_high, exchange(peaks))
+    )
     to_left, to_right = sides(
         edge_left, edge_right, turned_c, low, high, heat_low, heat, heat_high
     )

time: 161 us -> 155 us (0.963)
  local copies, waits for them, and re-layouts: 7.65 us -> 0.72 us
  waiting for transfers between devices: 31.3 us -> 35.8 us
    all_to_all x3, waiting for transfers between devices: 26 us -> 34.4 us  [exchange(): return lax.all_to_all(parts, BOTH, split_axis=0, concat_axis=0, tiled=True)]
    unnamed x46 -> x28, local copies, waits for them, and re-layouts: 7.65 us -> 0.72 us
    ppermute x6, waiting for transfers between devices: 5.37 us -> 1.39 us  [move(): return lax.ppermute(part, axis, pairs)]
  transfers between devices with their start and end apart: 9 -> 9, of which waited for: 6 -> 4; matrix products, arithmetic and copies ran while one was open for 0% -> 0% of each run, Pallas kernels for 9% -> 10%
where the time goes in v10:
time: 155 us; the launch traced here: 154 us
  Pallas kernels  51.1 us (33%)
  starting transfers between devices  38.3 us (25%)
  waiting for transfers between devices  35.8 us (23%)
  blocking collectives  27.2 us (18%)
    all_to_all x3, waiting for transfers between devices, exchange(): return lax.all_to_all(parts, BOTH, split_axis=0, concat_axis=0, tiled=True)  34.4 us
    all_to_all x2, blocking collectives, exchange(): return lax.all_to_all(parts, BOTH, split_axis=0, concat_axis=0, tiled=True)  27.2 us
    all_to_all x3, starting transfers between devices, exchange(): return lax.all_to_all(parts, BOTH, split_axis=0, concat_axis=0, tiled=True)  23.1 us
    ppermute x6, starting transfers between devices, move(): return lax.ppermute(part, axis, pairs)  15.2 us
    pallas_call x1, Pallas kernels, heated(): pl.pallas_call(heated_kernel, out_shape=[WIDE, WIDE, WIDE, jax.ShapeDtype...  10.3 us
    pallas_call x1, Pallas kernels, pair(): pl.pallas_call(functools.partial(pair_kernel, number), out_shape=[WIDE, W...  7.35 us
    pallas_call x1, Pallas kernels, deposit(): pl.pallas_call(deposit_kernel, out_shape=[kept((2, CX, CX)), jax.ShapeDty...  6.76 us
    pallas_call x1, Pallas kernels, last(): pl.pallas_call(last_kernel, out_shape=[OWN, OWN, sums_shape(parts.shape[0...  6.47 us
  transfers between devices with their start and end apart: 9, of which 4 were waited for; matrix products, arithmetic and copies ran while one was open for 0% of the time, Pallas kernels for 10%

profile of v10, /device:TPU:1, one launch (start us, length us, event | category | flops | bytes accessed | tf_op | source)
XLA Modules:
  0.0 154.3 jit_solution(4082480806149444857)
XLA Ops:
  0.0 0.0 copy-start.5
  0.0 0.0 copy-start.4
  0.0 0.0 copy-start.3
  0.0 4.5 %pack.1 = bf16[128,40,128]{2,1,0:T(8,128)(2,1)} custom-call(s32[128]{0:T(128)} %bitcast.12, bf16[16,128,128]{2,1,0:T(8,128)(2,1)} %heat_far.1, s32[128,128]{1,0:T(8,128)} %voxel_far.1), custom_call_target="tpu_custom_call" | custom-call | tf_op jit(solution)/shard_map/pack/pallas_call | solution.py:130
  4.5 11.5 %all-to-all-start.5 = ((bf16[128,40,128]{2,1,0:T(8,128)(2,1)}), bf16[128,40,128]{2,1,0:T(8,128)(2,1)S(1)}, u32[]{:S(2)}, u32[]{:S(2)}) async-start(bf16[128,40,128]{2,1,0:T(8,128)(2,1)} %pack.1), calls=%async_computation.5 | async-start | bytes 2621440 | tf_op jit(solution)/shard_map/all_to_all | solution.py:976
  16.0 0.0 copy-done.1
  16.1 0.0 copy-done
  16.1 3.1 %relayout.1 = (f32[2,8,128,128]{3,2,1,0:T(8,128)}, f32[16,8,128]{2,1,0:T(8,128)}, f32[13,16,8,128]{3,2,1,0:T(8,128)}, f32[13,16,8,128]{3,2,1,0:T(8,128)}, f32[16...) custom-call(f32[16,16,8,128]{3,2,1,0:T(8,128)S(1)} %copy-done, ...), custom_call_target="tpu_custom_call" | custom-call | tf_op jit(solution)/shard_map/relayout/pallas_call | solution.py:199
  19.2 3.5 %collective-permute-start = (f32[13,16,8,128]{3,2,1,0:T(8,128)}, f32[13,16,8,128]{3,2,1,0:T(8,128)S(1)}, u32[]{:S(2)}, u32[]{:S(2)}) collective-permute-start(f32[13,16,8,128]{3,2,1,0:T(8,128)} %get-tuple-element.80), channel_id=1, source_target_pairs={{0,1},{1,2},{2,3},{3,4},{4,5},{5,6},{6,7},{7,8},{8,9},{9,10},{10,1... | collective-permute-start | bytes 2555912 | tf_op jit(solution)/shard_map/ppermute | solution.py:982
  22.6 1.3 collective-permute-start.1
  23.9 0.0 copy-done.2
  23.9 0.0 copy-done.5
  24.0 2.4 %pixels.1 = (f32[8,128]{1,0:T(8,128)}, f32[16,8,128]{2,1,0:T(8,128)}) custom-call(s32[1,512]{1,0:T(1,128)S(1)} %bitcast.9, f32[1,512]{1,0:T(1,128)S(1)} %bitcast.10, f32[1,512]{1,0:T(1,128)S(1)} %bitcast.11, f32[16,512]{1,0:T(8,128)S(1)} %copy-done.2), custom_call_target="tpu_custom_call" | custom-call | tf_op jit(solution)/shard_map/pixels/pallas_call | solution.py:882
  26.3 0.1 add_convert_fusion.inside
  26.4 11.0 %all-to-all-done.5.incoming = bf16[128,40,128]{2,1,0:T(8,128)(2,1)S(1)} async-done(((bf16[128,40,128]{2,1,0:T(8,128)(2,1)}), bf16[128,40,128]{2,1,0:T(8,128)(2,1)S(1)}, u32[]{:S(2)}, u32[]{:S(2)}) %all-to-all-start.5) | async-done | bytes 1310752 | tf_op jit(solution)/shard_map/all_to_all | solution.py:976
  37.4 6.8 %deposit.1 = (f32[2,128,128]{2,1,0:T(8,128)}, f32[128,1,128]{2,1,0:T(1,128)}) custom-call(bf16[128,40,128]{2,1,0:T(8,128)(2,1)S(1)} %all-to-all-done.5.incoming, f32[16,2,8,128]{3,2,1,0:T(8,128)} %get-tuple-element.83.top_far, f32[16,8,128]{2,1,0:T(8,128)} %conduct_far.1, f32[8,128]{1,0:T(8,128)} %get-tuple-element.84.quiet_far), custom_call_target="tpu_custom_call" | custom-call | tf_op jit(solution)/shard_map/deposit/pallas_call | solution.py:345
  44.2 1.3 collective-permute-start.3
  45.5 4.0 %collective-permute-start.2 = (f32[2,128,128]{2,1,0:T(8,128)}, f32[2,128,128]{2,1,0:T(8,128)S(1)}, u32[]{:S(2)}, u32[]{:S(2)}) collective-permute-start(f32[2,128,128]{2,1,0:T(8,128)} %get-tuple-element.85.heat_own.heat_own_far), channel_id=1, source_target_pairs={{0,1},{1,2},{2,3},{3,4},{4,5},{5,6},{6,7},{7,8},{8,9},{9,10},{10,1... | collective-permute-start | bytes 393224 | tf_op jit(solution)/shard_map/ppermute | solution.py:982
  49.5 7.1 %all-to-all-start.6 = ((f32[128,1,128]{2,1,0:T(1,128)}), f32[128,1,128]{2,1,0:T(1,128)S(1)}, u32[]{:S(2)}, u32[]{:S(2)}) async-start(f32[128,1,128]{2,1,0:T(1,128)} %get-tuple-element.86), calls=%async_computation.6 | async-start | bytes 131072 | tf_op jit(solution)/shard_map/all_to_all | solution.py:976
  56.6 0.0 collective-permute-done.low.low_far
  56.6 0.0 collective-permute-done.1.high.high_far
  56.6 0.0 copy-start.10
  56.6 9.5 %all-to-all-done.6.peaks = f32[128,1,128]{2,1,0:T(1,128)S(1)} async-done(((f32[128,1,128]{2,1,0:T(1,128)}), f32[128,1,128]{2,1,0:T(1,128)S(1)}, u32[]{:S(2)}, u32[]{:S(2)}) %all-to-all-start.6) | async-done | bytes 65568 | tf_op jit(solution)/shard_map/all_to_all | solution.py:976
  66.1 0.0 collective-permute-done.3.heat_high.heat_high_far
  66.1 0.0 collective-permute-done.2.heat_low.heat_low_far
  66.1 0.0 copy-start.12
  66.2 0.0 copy-done.9
  66.2 0.0 copy-done.10
  66.2 0.6 copy-done.11
  66.8 0.0 copy-done.12
  66.8 1.2 sides.1
  68.1 3.1 %collective-permute-start.4 = (f32[49,8,128]{2,1,0:T(8,128)S(1)}, f32[49,8,128]{2,1,0:T(8,128)S(1)}, u32[]{:S(2)}, u32[]{:S(2)}) collective-permute-start(f32[49,8,128]{2,1,0:T(8,128)S(1)} %get-tuple-element.95), channel_id=1, source_target_pairs={{0,16},{16,32},{32,48},{48,64},{64,80},{80,96},{96,112},{1,17},{17... | collective-permute-start | bytes 602120 | tf_op jit(solution)/shard_map/ppermute | solution.py:982
  71.1 2.1 %collective-permute-start.5 = (f32[49,8,128]{2,1,0:T(8,128)S(1)}, f32[49,8,128]{2,1,0:T(8,128)S(1)}, u32[]{:S(2)}, u32[]{:S(2)}) collective-permute-start(f32[49,8,128]{2,1,0:T(8,128)S(1)} %get-tuple-element.96), channel_id=1, source_target_pairs={{16,0},{32,16},{48,32},{64,48},{80,64},{96,80},{112,96},{17,1},{33... | collective-permute-start | bytes 602120 | tf_op jit(solution)/shard_map/ppermute | solution.py:982
  73.2 3.5 %coefs.1.coef_main = f32[2,20,128,128]{3,2,1,0:T(8,128)S(1)} custom-call(f32[16,8,128]{2,1,0:T(8,128)} %get-tuple-element.90.turned_c.own, f32[13,16,8,128]{3,2,1,0:T(8,128)} %copy-done.9, f32[13,16,8,128]{3,2,1,0:T(8,128)} %copy-done.10), custom_call_target="tpu_custom_call" | custom-call | tf_op jit(solution)/shard_map/coefs/pallas_call | solution.py:279
  76.8 0.0 collective-permute-done.4.left
  76.8 1.4 collective-permute-done.5.right
  78.2 10.3 %heated.1 = (f32[2,20,144,128]{3,2,1,0:T(8,128)S(1)}, f32[2,20,144,128]{3,2,1,0:T(8,128)S(1)}, f32[2,20,144,128]{3,2,1,0:T(8,128)S(1)}, f32[128,1,128]{2,1,0:T(1,128)S(1)}) custom-call(f32[4]{0:T(128)S(1)} %add_convert_fusion.inside, f32[128,1,128]{2,1,0:T(1,128)S(1)} %all-to-all-done.6.peaks, f32[49,8,128]{2,1,0:T(8,128)S(1)} %collective-permute-done.4.left, ...), custom_call_target="tpu_custom_call" | custom-call | tf_op jit(solution)/shard_map/heated/pallas_call | solution.py:618
  88.5 0.0 copy-start.8
  88.5 0.0 copy-start.6
  88.5 13.3 %all_to_all.50.parts = f32[128,1,128]{2,1,0:T(1,128)S(1)} all-to-all(f32[128,1,128]{2,1,0:T(1,128)S(1)} %get-tuple-element.101), channel_id=1, replica_groups=mesh['gx'=8,'gy'=16] {'gx','gy'}, dimensions={0} | all-to-all | bytes 131072 | tf_op jit(solution)/shard_map/all_to_all | solution.py:976
  101.8 7.3 %pair_1.1 = (f32[2,20,144,128]{3,2,1,0:T(8,128)S(1)}, f32[2,20,144,128]{3,2,1,0:T(8,128)S(1)}, f32[128,1,128]{2,1,0:T(1,128)S(1)}, f32[8,128]{1,0:T(8,128)S(1)}) custom-call(f32[4]{0:T(128)S(1)} %add_convert_fusion.inside, f32[2,20,144,128]{3,2,1,0:T(8,128)S(1)} %get-tuple-element.98.field, f32[2,20,144,128]{3,2,1,0:T(8,128)S(1)} %get-tuple-element.99.changes, ...), custom_call_target="tpu_custom_call" | custom-call | tf_op jit(solution)/shard_map/pair_1/pallas_call | solution.py:679
  109.2 13.9 %all_to_all.51.parts = f32[128,1,128]{2,1,0:T(1,128)S(1)} all-to-all(f32[128,1,128]{2,1,0:T(1,128)S(1)} %get-tuple-element.104), channel_id=1, replica_groups=mesh['gx'=8,'gy'=16] {'gx','gy'}, dimensions={0} | all-to-all | bytes 131072 | tf_op jit(solution)/shard_map/all_to_all | solution.py:976
  123.1 6.5 %last_pair.1 = (f32[2,8,128,128]{3,2,1,0:T(8,128)S(1)}, f32[2,8,128,128]{3,2,1,0:T(8,128)S(1)}, f32[128,8,128]{2,1,0:T(8,128)}, f32[8,128]{1,0:T(8,128)S(1)}) custom-call(f32[4]{0:T(128)S(1)} %add_convert_fusion.inside, f32[2,20,144,128]{3,2,1,0:T(8,128)S(1)} %get-tuple-element.102.field, f32[2,20,144,128]{3,2,1,0:T(8,128)S(1)} %get-tuple-element.103.changes, ...), custom_call_target="tpu_custom_call" | custom-call | tf_op jit(solution)/shard_map/last_pair/pallas_call | solution.py:787
  129.6 0.0 copy-start.13
  129.6 0.0 copy-start.14
  129.6 4.5 %all-to-all-start.9 = ((f32[128,8,128]{2,1,0:T(8,128)}), f32[128,8,128]{2,1,0:T(8,128)S(1)}, u32[]{:S(2)}, u32[]{:S(2)}) async-start(f32[128,8,128]{2,1,0:T(8,128)} %get-tuple-element.108), calls=%async_computation.9 | async-start | bytes 1048576 | tf_op jit(solution)/shard_map/all_to_all | solution.py:976
  134.1 13.9 %all-to-all-done.9.sums = f32[128,8,128]{2,1,0:T(8,128)S(1)} async-done(((f32[128,8,128]{2,1,0:T(8,128)}), f32[128,8,128]{2,1,0:T(8,128)S(1)}, u32[]{:S(2)}, u32[]{:S(2)}) %all-to-all-start.9) | async-done | bytes 524320 | tf_op jit(solution)/shard_map/all_to_all | solution.py:976
  148.0 5.5 %update.3 = (f32[16,16,8,128]{3,2,1,0:T(8,128)}, s32[1]{0:T(128)}) custom-call(f32[128,8,128]{2,1,0:T(8,128)S(1)} %all-to-all-done.9.sums, f32[2,8,128,128]{3,2,1,0:T(8,128)S(1)} %get-tuple-element.109.field, f32[2,8,128,128]{3,2,1,0:T(8,128)S(1)} %get-tuple-element.110.changes, f32[8,128]{1,0:T(8,128)S(1)} %get-tuple-element.111.status), custom_call_target="tpu_custom_call" | custom-call | tf_op jit(solution)/shard_map/update/pallas_call | solution.py:962
  (12 shorter events, 0.0 us)
Async XLA Ops:
  0.0 16.0 %copy-start.1 = (f32[16,8,128]{2,1,0:T(8,128)S(1)}, f32[16,8,128]{2,1,0:T(8,128)}, u32[]{:S(2)}) copy-start(f32[16,8,128]{2,1,0:T(8,128)} %conduct_far.1) | copy-start | bytes 196612
  0.0 16.1 %copy-start = (f32[16,16,8,128]{3,2,1,0:T(8,128)S(1)}, f32[16,16,8,128]{3,2,1,0:T(8,128)}, u32[]{:S(2)}) copy-start(f32[16,16,8,128]{3,2,1,0:T(8,128)} %state.1) | copy-start | bytes 3145732
  0.0 23.9 %copy-start.2 = (f32[16,512]{1,0:T(8,128)S(1)}, f32[16,512]{1,0:T(8,128)}, u32[]{:S(2)}) copy-start(f32[16,512]{1,0:T(8,128)} %noise.1) | copy-start | bytes 98308
  0.0 23.9 %copy-start.5 = (f32[512]{0:T(512)S(1)}, f32[512]{0:T(512)}, u32[]{:S(2)}) copy-start(f32[512]{0:T(512)} %param.18) | copy-start | bytes 6148
  0.0 23.9 %copy-start.4 = (f32[512]{0:T(512)S(1)}, f32[512]{0:T(512)}, u32[]{:S(2)}) copy-start(f32[512]{0:T(512)} %param.17) | copy-start | bytes 6148
  0.0 23.9 %copy-start.3 = (s32[512]{0:T(512)S(1)}, s32[512]{0:T(512)}, u32[]{:S(2)}) copy-start(s32[512]{0:T(512)} %param.16) | copy-start | bytes 6148
  4.5 32.9 %all-to-all-start.5 = ((bf16[128,40,128]{2,1,0:T(8,128)(2,1)}), bf16[128,40,128]{2,1,0:T(8,128)(2,1)S(1)}, u32[]{:S(2)}, u32[]{:S(2)}) async-start(bf16[128,40,128]{2,1,0:T(8,128)(2,1)} %pack.1), calls=%async_computation.5 | async-start | bytes 2621440 | tf_op jit(solution)/shard_map/all_to_all | solution.py:976
  19.2 37.4 %collective-permute-start = (f32[13,16,8,128]{3,2,1,0:T(8,128)}, f32[13,16,8,128]{3,2,1,0:T(8,128)S(1)}, u32[]{:S(2)}, u32[]{:S(2)}) collective-permute-start(f32[13,16,8,128]{3,2,1,0:T(8,128)} %get-tuple-element.80), channel_id=1, source_target_pairs={{0,1},{1,2},{2,3},{3,4},{4,5},{5,6},{6,7},{7,8},{8,9},{9,10},{10,1... | collective-permute-start | bytes 2555912 | tf_op jit(solution)/shard_map/ppermute | solution.py:982
  22.6 34.0 %collective-permute-start.1 = (f32[13,16,8,128]{3,2,1,0:T(8,128)}, f32[13,16,8,128]{3,2,1,0:T(8,128)S(1)}, u32[]{:S(2)}, u32[]{:S(2)}) collective-permute-start(f32[13,16,8,128]{3,2,1,0:T(8,128)} %get-tuple-element.81), channel_id=1, source_target_pairs={{1,0},{2,1},{3,2},{4,3},{5,4},{6,5},{7,6},{8,7},{9,8},{10,9},{11,1... | collective-permute-start | bytes 2555912 | tf_op jit(solution)/shard_map/ppermute | solution.py:982
  44.2 22.0 %collective-permute-start.3 = (f32[2,128,128]{2,1,0:T(8,128)}, f32[2,128,128]{2,1,0:T(8,128)S(1)}, u32[]{:S(2)}, u32[]{:S(2)}) collective-permute-start(f32[2,128,128]{2,1,0:T(8,128)} %get-tuple-element.85.heat_own.heat_own_far), channel_id=1, source_target_pairs={{1,0},{2,1},{3,2},{4,3},{5,4},{6,5},{7,6},{8,7},{9,8},{10,9},{11,1... | collective-permute-start | bytes 393224 | tf_op jit(solution)/shard_map/ppermute | solution.py:982
  45.5 20.7 %collective-permute-start.2 = (f32[2,128,128]{2,1,0:T(8,128)}, f32[2,128,128]{2,1,0:T(8,128)S(1)}, u32[]{:S(2)}, u32[]{:S(2)}) collective-permute-start(f32[2,128,128]{2,1,0:T(8,128)} %get-tuple-element.85.heat_own.heat_own_far), channel_id=1, source_target_pairs={{0,1},{1,2},{2,3},{3,4},{4,5},{5,6},{6,7},{7,8},{8,9},{9,10},{10,1... | collective-permute-start | bytes 393224 | tf_op jit(solution)/shard_map/ppermute | solution.py:982
  49.5 16.7 %all-to-all-start.6 = ((f32[128,1,128]{2,1,0:T(1,128)}), f32[128,1,128]{2,1,0:T(1,128)S(1)}, u32[]{:S(2)}, u32[]{:S(2)}) async-start(f32[128,1,128]{2,1,0:T(1,128)} %get-tuple-element.86), calls=%async_computation.6 | async-start | bytes 131072 | tf_op jit(solution)/shard_map/all_to_all | solution.py:976
  56.6 9.6 %copy-start.9 = (f32[13,16,8,128]{3,2,1,0:T(8,128)}, f32[13,16,8,128]{3,2,1,0:T(8,128)S(1)}, u32[]{:S(2)}) copy-start(f32[13,16,8,128]{3,2,1,0:T(8,128)S(1)} %collective-permute-done.low.low_far) | copy-start | bytes 2555908
  56.6 9.6 %copy-start.10 = (f32[13,16,8,128]{3,2,1,0:T(8,128)}, f32[13,16,8,128]{3,2,1,0:T(8,128)S(1)}, u32[]{:S(2)}) copy-start(f32[13,16,8,128]{3,2,1,0:T(8,128)S(1)} %collective-permute-done.1.high.high_far) | copy-start | bytes 2555908
  66.1 0.7 copy-start.11
  66.1 0.7 copy-start.12
  68.1 8.7 %collective-permute-start.4 = (f32[49,8,128]{2,1,0:T(8,128)S(1)}, f32[49,8,128]{2,1,0:T(8,128)S(1)}, u32[]{:S(2)}, u32[]{:S(2)}) collective-permute-start(f32[49,8,128]{2,1,0:T(8,128)S(1)} %get-tuple-element.95), channel_id=1, source_target_pairs={{0,16},{16,32},{32,48},{48,64},{64,80},{80,96},{96,112},{1,17},{17... | collective-permute-start | bytes 602120 | tf_op jit(solution)/shard_map/ppermute | solution.py:982
  71.1 7.0 %collective-permute-start.5 = (f32[49,8,128]{2,1,0:T(8,128)S(1)}, f32[49,8,128]{2,1,0:T(8,128)S(1)}, u32[]{:S(2)}, u32[]{:S(2)}) collective-permute-start(f32[49,8,128]{2,1,0:T(8,128)S(1)} %get-tuple-element.96), channel_id=1, source_target_pairs={{16,0},{32,16},{48,32},{64,48},{80,64},{96,80},{112,96},{17,1},{33... | collective-permute-start | bytes 602120 | tf_op jit(solution)/shard_map/ppermute | solution.py:982
  88.5 20.7 %copy-start.8 = (f32[2,20,144,128]{3,2,1,0:T(8,128)}, f32[2,20,144,128]{3,2,1,0:T(8,128)S(1)}, u32[]{:S(2)}) copy-start(f32[2,20,144,128]{3,2,1,0:T(8,128)S(1)} %get-tuple-element.98.field) | copy-start | bytes 8847364
  88.5 34.6 %copy-start.6 = (f32[2,20,144,128]{3,2,1,0:T(8,128)}, f32[2,20,144,128]{3,2,1,0:T(8,128)S(1)}, u32[]{:S(2)}) copy-start(f32[2,20,144,128]{3,2,1,0:T(8,128)S(1)} %get-tuple-element.100.coef) | copy-start | bytes 8847364
  129.6 24.5 %copy-start.13 = (f32[16,8,128]{2,1,0:T(8,128)S(1)}, f32[16,8,128]{2,1,0:T(8,128)}, u32[]{:S(2)}) copy-start(f32[16,8,128]{2,1,0:T(8,128)} %get-tuple-element.107.data_far) | copy-start | bytes 196612
  129.6 24.5 %copy-start.14 = (f32[8,128]{1,0:T(8,128)S(1)}, f32[8,128]{1,0:T(8,128)}, u32[]{:S(2)}) copy-start(f32[8,128]{1,0:T(8,128)} %get-tuple-element.106.weight_far) | copy-start | bytes 12292
  129.6 18.4 %all-to-all-start.9 = ((f32[128,8,128]{2,1,0:T(8,128)}), f32[128,8,128]{2,1,0:T(8,128)S(1)}, u32[]{:S(2)}, u32[]{:S(2)}) async-start(f32[128,8,128]{2,1,0:T(8,128)} %get-tuple-element.108), calls=%async_computation.9 | async-start | bytes 1048576 | tf_op jit(solution)/shard_map/all_to_all | solution.py:976

commit v11 on v10

--- a/solution.py
+++ b/solution.py
@@ -122,7 +122,7 @@
         out[d] = chunk.astype(BF16)
         return carry
 
-    lax.fori_loop(0, devices, emit, 0, unroll=4)
+    lax.fori_loop(0, devices, emit, 0, unroll=16)
 
 
 def pack(owner, heat, voxel, devices):
@@ -249,11 +249,21 @@
     )(*far(*operands))
 
 
-def placed(strip, zi, y0):
+def split(strip):
+    parts = []
+    for _ in range(3):
+        part = strip.astype(BF16)
+        parts.append(part)
+        strip = strip - part.astype(F32)
+    return jnp.concatenate(parts, axis=1)
+
+
+def placed(parts, zi, y0):
     source = lax.broadcasted_iota(jnp.int32, (CX, CX), 0)
     target = lax.broadcasted_iota(jnp.int32, (CX, CX), 1)
-    hot = jnp.where(source == (2 * (target >> 4) + zi) * CY + y0, 1.0, 0.0).astype(F32)
-    return jnp.dot(strip, hot, precision=lax.Precision.HIGHEST, preferred_element_type=F32)
+    hot = jnp.where(source == (2 * (target >> 4) + zi) * CY + y0, 1.0, 0.0).astype(BF16)
+    hot = jnp.concatenate([hot] * 3, axis=0)
+    return jnp.dot(parts, hot, preferred_element_type=F32)
 
 
 def halo_row(g, y0):
@@ -265,7 +275,7 @@
     pairs = ((low.at[EDGE], tiles.at[0]), (own, tiles.at[1]), (high.at[EDGE], tiles.at[2]))
     for copy in fetch(sems, pairs):
         copy.wait()
-    strip = tiles[...].reshape(3 * CX, CX)
+    strip = split(tiles[...].reshape(3 * CX, CX))
     for zi in range(2):
         for y0 in range(CY):
             part = placed(strip, zi, y0)
@@ -402,6 +412,7 @@
     last_row = row == 7
     first_row = row == 0
     inner_lane = lane < CX - M
+    outer_lane = lane >= M
     cooling = jnp.where(lane < M, COOL, 0.0)
 
     for zi in range(2):
@@ -412,7 +423,6 @@
             )
 
     def line(own, row_mask, y, state):
-        carried = [jnp.zeros((8, CX), F32)] * 2
         for t in range(XT):
             s = tile(t)
             us = [field[zi, y, s, :] for zi in range(2)]
@@ -426,10 +436,13 @@
                 else:
                     u_after = jnp.where(last_row, u, pltpu.roll(u, 7, axis=0))
                     h_after = pltpu.roll(h, 7, axis=0)
-                along = (h + h_after) * (u_after - u)
-                turned = pltpu.roll(along, 1, axis=0)
-                total = along - jnp.where(first_row, carried[zi], turned)
-                carried[zi] = turned
+                if t:
+                    before = slice(8 * t - 1, 8 * t + 7)
+                    u_before, h_before = field[zi, y, before, :], half[zi, y, before, :]
+                else:
+                    u_before = jnp.where(first_row, u, pltpu.roll(u, 1, axis=0))
+                    h_before = pltpu.roll(h, 1, axis=0)
+                total = (h + h_after) * (u_after - u) + (h + h_before) * (u_before - u)
                 across = (h + half[zi, y + 1, s, :]) * (field[zi, y + 1, s, :] - u)
                 total = total + (across - above[zi, t])
                 above[zi, t] = across
@@ -439,7 +452,9 @@
                 pltpu.roll(us[0], CX - M, axis=1) - us[1]
             )
             between = jnp.where(inner_lane, between, 0.0)
-            change[0] = change[0] + (within - pltpu.roll(between, M, axis=1)) - cooling * us[0]
+            below = (hs[0] + pltpu.roll(hs[1], M, axis=1)) * (us[0] - pltpu.roll(us[1], M, axis=1))
+            below = jnp.where(outer_lane, below, 0.0)
+            change[0] = change[0] + (within - below) - cooling * us[0]
             change[1] = change[1] + (between - within)
             state = emit(y, t, us, change, own, mask_of(inside, row_mask, t), state)
         return state
@@ -541,8 +556,8 @@
     )
     top = lanes() < M
 
-    strip = jnp.concatenate(
-        [side[SIDE + g] for g in range(3) for side in (left, right)], axis=0
+    strip = split(
+        jnp.concatenate([side[SIDE + g] for g in range(3) for side in (left, right)], axis=0)
     )
     for zi in range(2):
         for y0 in range(CY):
@@ -698,7 +713,7 @@
         return state
 
     sweep(field, half, above, inside, HALO, HALO + CY, emit, 0)
-    grams = jnp.zeros((5 * CY, 3 * M), F32)
+    lefts, rights = [], []
     for y in range(CY):
         w = weight[y : y + 1, :]
         for m in range(M):
@@ -710,11 +725,15 @@
             mean = jnp.mean(seen, axis=0, keepdims=True)
             means.append(mean)
             spreads.append(seen - mean)
-        left = jnp.concatenate(spreads + means + [jnp.zeros((6, CX), F32)], axis=0)
-        right = jnp.concatenate([part * w for part in spreads] + [flat[...]], axis=0)
-        grams = grams + lax.dot_general(
-            left, right, NT, precision=lax.Precision.HIGHEST, preferred_element_type=F32
-        )
+        lefts.append(jnp.concatenate(spreads + means + [jnp.zeros((6, CX), F32)], axis=0))
+        rights.append(jnp.concatenate([part * w for part in spreads] + [flat[...]], axis=0))
+    grams = lax.dot_general(
+        jnp.concatenate(lefts, axis=1),
+        jnp.concatenate(rights, axis=1),
+        NT,
+        precision=lax.Precision.HIGHEST,
+        preferred_element_type=F32,
+    )
     grams = jnp.concatenate([grams, jnp.zeros((5 * CY, CX - 3 * M), F32)], axis=1)
     tall = lax.broadcasted_iota(jnp.int32, (M, CX), 0)
     wide = lax.broadcasted_iota(jnp.int32, (M, CX), 1)
@@ -928,14 +947,16 @@
     mean = jnp.sum(jnp.where(tall == wide, mean, 0.0), axis=1, keepdims=True)
     target = jnp.where(wide < M, data + step * data_c - cross - mean, 0.0)
     system = jnp.where(tall == wide, cross + (M - 1.0), cross)
-    system = system + pltpu.roll(target, M, axis=1)
+    columns = [jnp.broadcast_to(system[:, i : i + 1], (M, CX)) for i in range(M)]
     for i in range(M):
-        pivot = system[i : i + 1, :]
-        pivot = pivot / pivot[:, i : i + 1]
-        factor = jnp.where(tall == i, 0.0, jnp.broadcast_to(system[:, i : i + 1], (M, CX)))
-        system = jnp.where(tall == i, pivot, system - factor * pivot)
-    mixing = system - jnp.mean(system, axis=0, keepdims=True)
-    mixing = pltpu.roll(mixing, CX - M, axis=1)
+        pivot = 1.0 / columns[i][i : i + 1, :]
+        factor = jnp.where(tall == i, 0.0, columns[i] * pivot)
+        for j in range(i + 1, M):
+            columns[j] = columns[j] - factor * columns[j][i : i + 1, :]
+        target = target - factor * target[i : i + 1, :]
+    for i in range(M):
+        target = jnp.where(tall == i, target / columns[i], target)
+    mixing = target - jnp.mean(target, axis=0, keepdims=True)
     mixing = jnp.where(wide < M, mixing + jnp.where(tall == wide, 1.0, 0.0), 0.0)
     for shift in (16, 32, 64):
         mixing = mixing + pltpu.roll(mixing, shift, axis=1)
@@ -943,13 +964,18 @@
     tall = lax.broadcasted_iota(jnp.int32, (CX, CX), 0)
     wide = lax.broadcasted_iota(jnp.int32, (CX, CX), 1)
     mixing = jnp.where((tall >> 4) == (wide >> 4), 2.0 * mixing, 0.0).T
+    mixing_high = mixing.astype(BF16)
+    mixing_low = (mixing - mixing_high.astype(F32)).astype(BF16)
+    mixing = jnp.concatenate([mixing_high, mixing_low, mixing_high], axis=1)
     for zi in range(2):
         for y in range(CY):
+            prior = field[zi, y] + step * changes[zi, y]
+            high = prior.astype(BF16)
+            low = (prior - high.astype(F32)).astype(BF16)
             part = lax.dot_general(
                 mixing,
-                field[zi, y] + step * changes[zi, y],
+                jnp.concatenate([high, high, low], axis=1),
                 NT,
-                precision=lax.Precision.HIGHEST,
                 preferred_element_type=F32,
             )
             for group in range(ZG):

time: 155 us -> 150 us (0.968)
  Pallas kernels: 51.1 us -> 44.7 us
    pallas_call x1, Pallas kernels: 5.51 us -> 3.04 us  [update(): pl.pallas_call(update_kernel, out_shape=[jax.ShapeDtypeStruct((M, NZ, CY,...]
where the time goes in v11:
time: 150 us; the launch traced here: 149 us
  Pallas kernels  44.7 us (30%)
  starting transfers between devices  38.1 us (25%)
  waiting for transfers between devices  37.2 us (25%)
  blocking collectives  27.2 us (18%)
    all_to_all x3, waiting for transfers between devices, exchange(): return lax.all_to_all(parts, BOTH, split_axis=0, concat_axis=0, tiled=True)  34.4 us
    all_to_all x2, blocking collectives, exchange(): return lax.all_to_all(parts, BOTH, split_axis=0, concat_axis=0, tiled=True)  27.2 us
    all_to_all x3, starting transfers between devices, exchange(): return lax.all_to_all(parts, BOTH, split_axis=0, concat_axis=0, tiled=True)  23.1 us
    ppermute x6, starting transfers between devices, move(): return lax.ppermute(part, axis, pairs)  15 us
    pallas_call x1, Pallas kernels, heated(): pl.pallas_call(heated_kernel, out_shape=[WIDE, WIDE, WIDE, jax.ShapeDtype...  9.31 us
    pallas_call x1, Pallas kernels, deposit(): pl.pallas_call(deposit_kernel, out_shape=[kept((2, CX, CX)), jax.ShapeDty...  6.74 us
    pallas_call x1, Pallas kernels, pair(): pl.pallas_call(functools.partial(pair_kernel, number), out_shape=[WIDE, W...  6.39 us
    pallas_call x1, Pallas kernels, last(): pl.pallas_call(last_kernel, out_shape=[OWN, OWN, sums_shape(parts.shape[0...  5.93 us
  transfers between devices with their start and end apart: 9, of which 4 were waited for; matrix products, arithmetic and copies ran while one was open for 0% of the time, Pallas kernels for 10%

profile of v11, /device:TPU:1, one launch (start us, length us, event | category | flops | bytes accessed | tf_op | source)
XLA Modules:
  0.0 149.1 jit_solution(15137731049414834754)
XLA Ops:
  0.0 0.0 copy-start.5
  0.0 0.0 copy-start.4
  0.0 0.0 copy-start.3
  0.0 4.3 %pack.1 = bf16[128,40,128]{2,1,0:T(8,128)(2,1)} custom-call(s32[128]{0:T(128)} %bitcast.12, bf16[16,128,128]{2,1,0:T(8,128)(2,1)} %heat_far.1, s32[128,128]{1,0:T(8,128)} %voxel_far.1), custom_call_target="tpu_custom_call" | custom-call | tf_op jit(solution)/shard_map/pack/pallas_call | solution.py:130
  4.3 11.5 %all-to-all-start.5 = ((bf16[128,40,128]{2,1,0:T(8,128)(2,1)}), bf16[128,40,128]{2,1,0:T(8,128)(2,1)S(1)}, u32[]{:S(2)}, u32[]{:S(2)}) async-start(bf16[128,40,128]{2,1,0:T(8,128)(2,1)} %pack.1), calls=%async_computation.5 | async-start | bytes 2621440 | tf_op jit(solution)/shard_map/all_to_all | solution.py:1002
  15.8 0.0 copy-done.1
  15.9 0.0 copy-done
  15.9 3.1 %relayout.1 = (f32[2,8,128,128]{3,2,1,0:T(8,128)}, f32[16,8,128]{2,1,0:T(8,128)}, f32[13,16,8,128]{3,2,1,0:T(8,128)}, f32[13,16,8,128]{3,2,1,0:T(8,128)}, f32[16...) custom-call(f32[16,16,8,128]{3,2,1,0:T(8,128)S(1)} %copy-done, ...), custom_call_target="tpu_custom_call" | custom-call | tf_op jit(solution)/shard_map/relayout/pallas_call | solution.py:199
  19.0 3.5 %collective-permute-start = (f32[13,16,8,128]{3,2,1,0:T(8,128)}, f32[13,16,8,128]{3,2,1,0:T(8,128)S(1)}, u32[]{:S(2)}, u32[]{:S(2)}) collective-permute-start(f32[13,16,8,128]{3,2,1,0:T(8,128)} %get-tuple-element.80), channel_id=1, source_target_pairs={{0,1},{1,2},{2,3},{3,4},{4,5},{5,6},{6,7},{7,8},{8,9},{9,10},{10,1... | collective-permute-start | bytes 2555912 | tf_op jit(solution)/shard_map/ppermute | solution.py:1008
  22.4 1.3 collective-permute-start.1
  23.7 0.0 copy-done.2
  23.7 0.0 copy-done.5
  23.8 0.0 copy-done.4
  23.8 0.0 copy-done.3
  23.8 2.4 %pixels.1 = (f32[8,128]{1,0:T(8,128)}, f32[16,8,128]{2,1,0:T(8,128)}) custom-call(s32[1,512]{1,0:T(1,128)S(1)} %bitcast.9, f32[1,512]{1,0:T(1,128)S(1)} %bitcast.10, f32[1,512]{1,0:T(1,128)S(1)} %bitcast.11, f32[16,512]{1,0:T(8,128)S(1)} %copy-done.2), custom_call_target="tpu_custom_call" | custom-call | tf_op jit(solution)/shard_map/pixels/pallas_call | solution.py:901
  26.1 0.1 add_convert_fusion.inside
  26.2 11.0 %all-to-all-done.5.incoming = bf16[128,40,128]{2,1,0:T(8,128)(2,1)S(1)} async-done(((bf16[128,40,128]{2,1,0:T(8,128)(2,1)}), bf16[128,40,128]{2,1,0:T(8,128)(2,1)S(1)}, u32[]{:S(2)}, u32[]{:S(2)}) %all-to-all-start.5) | async-done | bytes 1310752 | tf_op jit(solution)/shard_map/all_to_all | solution.py:1002
  37.2 6.7 %deposit.1 = (f32[2,128,128]{2,1,0:T(8,128)}, f32[128,1,128]{2,1,0:T(1,128)}) custom-call(bf16[128,40,128]{2,1,0:T(8,128)(2,1)S(1)} %all-to-all-done.5.incoming, f32[16,2,8,128]{3,2,1,0:T(8,128)} %get-tuple-element.83.top_far, f32[16,8,128]{2,1,0:T(8,128)} %conduct_far.1, f32[8,128]{1,0:T(8,128)} %get-tuple-element.84.quiet_far), custom_call_target="tpu_custom_call" | custom-call | tf_op jit(solution)/shard_map/deposit/pallas_call | solution.py:355
  44.0 1.3 collective-permute-start.3
  45.3 4.0 %collective-permute-start.2 = (f32[2,128,128]{2,1,0:T(8,128)}, f32[2,128,128]{2,1,0:T(8,128)S(1)}, u32[]{:S(2)}, u32[]{:S(2)}) collective-permute-start(f32[2,128,128]{2,1,0:T(8,128)} %get-tuple-element.85.heat_own.heat_own_far), channel_id=1, source_target_pairs={{0,1},{1,2},{2,3},{3,4},{4,5},{5,6},{6,7},{7,8},{8,9},{9,10},{10,1... | collective-permute-start | bytes 393224 | tf_op jit(solution)/shard_map/ppermute | solution.py:1008
  49.3 7.1 %all-to-all-start.6 = ((f32[128,1,128]{2,1,0:T(1,128)}), f32[128,1,128]{2,1,0:T(1,128)S(1)}, u32[]{:S(2)}, u32[]{:S(2)}) async-start(f32[128,1,128]{2,1,0:T(1,128)} %get-tuple-element.86), calls=%async_computation.6 | async-start | bytes 131072 | tf_op jit(solution)/shard_map/all_to_all | solution.py:1002
  56.3 0.0 collective-permute-done.low.low_far
  56.4 0.0 copy-start.9
  56.4 0.0 collective-permute-done.1.high.high_far
  56.4 0.0 copy-start.10
  56.4 9.5 %all-to-all-done.6.peaks = f32[128,1,128]{2,1,0:T(1,128)S(1)} async-done(((f32[128,1,128]{2,1,0:T(1,128)}), f32[128,1,128]{2,1,0:T(1,128)S(1)}, u32[]{:S(2)}, u32[]{:S(2)}) %all-to-all-start.6) | async-done | bytes 65568 | tf_op jit(solution)/shard_map/all_to_all | solution.py:1002
  65.9 0.0 collective-permute-done.3.heat_high.heat_high_far
  65.9 0.0 collective-permute-done.2.heat_low.heat_low_far
  65.9 0.0 copy-start.12
  66.0 0.6 copy-done.11
  66.6 0.0 copy-done.12
  66.6 1.2 sides.1
  67.9 3.1 %collective-permute-start.4 = (f32[49,8,128]{2,1,0:T(8,128)S(1)}, f32[49,8,128]{2,1,0:T(8,128)S(1)}, u32[]{:S(2)}, u32[]{:S(2)}) collective-permute-start(f32[49,8,128]{2,1,0:T(8,128)S(1)} %get-tuple-element.95), channel_id=1, source_target_pairs={{0,16},{16,32},{32,48},{48,64},{64,80},{80,96},{96,112},{1,17},{17... | collective-permute-start | bytes 602120 | tf_op jit(solution)/shard_map/ppermute | solution.py:1008
  70.9 1.9 %collective-permute-start.5 = (f32[49,8,128]{2,1,0:T(8,128)S(1)}, f32[49,8,128]{2,1,0:T(8,128)S(1)}, u32[]{:S(2)}, u32[]{:S(2)}) collective-permute-start(f32[49,8,128]{2,1,0:T(8,128)S(1)} %get-tuple-element.96), channel_id=1, source_target_pairs={{16,0},{32,16},{48,32},{64,48},{80,64},{96,80},{112,96},{17,1},{33... | collective-permute-start | bytes 602120 | tf_op jit(solution)/shard_map/ppermute | solution.py:1008
  72.9 2.3 %coefs.1.coef_main = f32[2,20,128,128]{3,2,1,0:T(8,128)S(1)} custom-call(f32[16,8,128]{2,1,0:T(8,128)} %get-tuple-element.90.turned_c.own, f32[13,16,8,128]{3,2,1,0:T(8,128)} %copy-done.9, f32[13,16,8,128]{3,2,1,0:T(8,128)} %copy-done.10), custom_call_target="tpu_custom_call" | custom-call | tf_op jit(solution)/shard_map/coefs/pallas_call | solution.py:289
  75.2 0.0 collective-permute-done.4.left
  75.2 2.8 %collective-permute-done.5.right = f32[49,8,128]{2,1,0:T(8,128)S(1)} collective-permute-done((f32[49,8,128]{2,1,0:T(8,128)S(1)}, f32[49,8,128]{2,1,0:T(8,128)S(1)}, u32[]{:S(2)}, u32[]{:S(2)}) %collective-permute-start.5) | collective-permute-done | bytes 200736 | tf_op jit(solution)/shard_map/ppermute | solution.py:1008
  78.0 9.3 %heated.1 = (f32[2,20,144,128]{3,2,1,0:T(8,128)S(1)}, f32[2,20,144,128]{3,2,1,0:T(8,128)S(1)}, f32[2,20,144,128]{3,2,1,0:T(8,128)S(1)}, f32[128,1,128]{2,1,0:T(1,128)S(1)}) custom-call(f32[4]{0:T(128)S(1)} %add_convert_fusion.inside, f32[128,1,128]{2,1,0:T(1,128)S(1)} %all-to-all-done.6.peaks, f32[49,8,128]{2,1,0:T(8,128)S(1)} %collective-permute-done.4.left, ...), custom_call_target="tpu_custom_call" | custom-call | tf_op jit(solution)/shard_map/heated/pallas_call | solution.py:633
  87.3 13.3 %all_to_all.50.parts = f32[128,1,128]{2,1,0:T(1,128)S(1)} all-to-all(f32[128,1,128]{2,1,0:T(1,128)S(1)} %get-tuple-element.101), channel_id=1, replica_groups=mesh['gx'=8,'gy'=16] {'gx','gy'}, dimensions={0} | all-to-all | bytes 131072 | tf_op jit(solution)/shard_map/all_to_all | solution.py:1002
  100.6 6.4 %pair_1.1 = (f32[2,20,144,128]{3,2,1,0:T(8,128)S(1)}, f32[2,20,144,128]{3,2,1,0:T(8,128)S(1)}, f32[128,1,128]{2,1,0:T(1,128)S(1)}, f32[8,128]{1,0:T(8,128)S(1)}) custom-call(f32[4]{0:T(128)S(1)} %add_convert_fusion.inside, f32[2,20,144,128]{3,2,1,0:T(8,128)S(1)} %get-tuple-element.98.field, f32[2,20,144,128]{3,2,1,0:T(8,128)S(1)} %get-tuple-element.99.changes, ...), custom_call_target="tpu_custom_call" | custom-call | tf_op jit(solution)/shard_map/pair_1/pallas_call | solution.py:694
  107.1 13.9 %all_to_all.51.parts = f32[128,1,128]{2,1,0:T(1,128)S(1)} all-to-all(f32[128,1,128]{2,1,0:T(1,128)S(1)} %get-tuple-element.104), channel_id=1, replica_groups=mesh['gx'=8,'gy'=16] {'gx','gy'}, dimensions={0} | all-to-all | bytes 131072 | tf_op jit(solution)/shard_map/all_to_all | solution.py:1002
  120.9 0.0 copy-done.6
  120.9 5.9 %last_pair.1 = (f32[2,8,128,128]{3,2,1,0:T(8,128)S(1)}, f32[2,8,128,128]{3,2,1,0:T(8,128)S(1)}, f32[128,8,128]{2,1,0:T(8,128)}, f32[8,128]{1,0:T(8,128)S(1)}) custom-call(f32[4]{0:T(128)S(1)} %add_convert_fusion.inside, f32[2,20,144,128]{3,2,1,0:T(8,128)S(1)} %get-tuple-element.102.field, f32[2,20,144,128]{3,2,1,0:T(8,128)S(1)} %get-tuple-element.103.changes, ...), custom_call_target="tpu_custom_call" | custom-call | tf_op jit(solution)/shard_map/last_pair/pallas_call | solution.py:806
  126.9 4.5 %all-to-all-start.9 = ((f32[128,8,128]{2,1,0:T(8,128)}), f32[128,8,128]{2,1,0:T(8,128)S(1)}, u32[]{:S(2)}, u32[]{:S(2)}) async-start(f32[128,8,128]{2,1,0:T(8,128)} %get-tuple-element.108), calls=%async_computation.9 | async-start | bytes 1048576 | tf_op jit(solution)/shard_map/all_to_all | solution.py:1002
  131.4 13.9 %all-to-all-done.9.sums = f32[128,8,128]{2,1,0:T(8,128)S(1)} async-done(((f32[128,8,128]{2,1,0:T(8,128)}), f32[128,8,128]{2,1,0:T(8,128)S(1)}, u32[]{:S(2)}, u32[]{:S(2)}) %all-to-all-start.9) | async-done | bytes 524320 | tf_op jit(solution)/shard_map/all_to_all | solution.py:1002
  145.3 3.0 %update.3 = (f32[16,16,8,128]{3,2,1,0:T(8,128)}, s32[1]{0:T(128)}) custom-call(f32[128,8,128]{2,1,0:T(8,128)S(1)} %all-to-all-done.9.sums, f32[2,8,128,128]{3,2,1,0:T(8,128)S(1)} %get-tuple-element.109.field, f32[2,8,128,128]{3,2,1,0:T(8,128)S(1)} %get-tuple-element.110.changes, f32[8,128]{1,0:T(8,128)S(1)} %get-tuple-element.111.status), custom_call_target="tpu_custom_call" | custom-call | tf_op jit(solution)/shard_map/update/pallas_call | solution.py:988
  148.9 0.0 copy-done.13
  148.9 0.0 copy-done.14
  (12 shorter events, 0.0 us)
Async XLA Ops:
  0.0 15.8 %copy-start.1 = (f32[16,8,128]{2,1,0:T(8,128)S(1)}, f32[16,8,128]{2,1,0:T(8,128)}, u32[]{:S(2)}) copy-start(f32[16,8,128]{2,1,0:T(8,128)} %conduct_far.1) | copy-start | bytes 196612
  0.0 15.9 %copy-start = (f32[16,16,8,128]{3,2,1,0:T(8,128)S(1)}, f32[16,16,8,128]{3,2,1,0:T(8,128)}, u32[]{:S(2)}) copy-start(f32[16,16,8,128]{3,2,1,0:T(8,128)} %state.1) | copy-start | bytes 3145732
  0.0 23.7 %copy-start.2 = (f32[16,512]{1,0:T(8,128)S(1)}, f32[16,512]{1,0:T(8,128)}, u32[]{:S(2)}) copy-start(f32[16,512]{1,0:T(8,128)} %noise.1) | copy-start | bytes 98308
  0.0 23.7 %copy-start.5 = (f32[512]{0:T(512)S(1)}, f32[512]{0:T(512)}, u32[]{:S(2)}) copy-start(f32[512]{0:T(512)} %param.18) | copy-start | bytes 6148
  0.0 23.7 %copy-start.4 = (f32[512]{0:T(512)S(1)}, f32[512]{0:T(512)}, u32[]{:S(2)}) copy-start(f32[512]{0:T(512)} %param.17) | copy-start | bytes 6148
  0.0 23.7 %copy-start.3 = (s32[512]{0:T(512)S(1)}, s32[512]{0:T(512)}, u32[]{:S(2)}) copy-start(s32[512]{0:T(512)} %param.16) | copy-start | bytes 6148
  4.3 32.9 %all-to-all-start.5 = ((bf16[128,40,128]{2,1,0:T(8,128)(2,1)}), bf16[128,40,128]{2,1,0:T(8,128)(2,1)S(1)}, u32[]{:S(2)}, u32[]{:S(2)}) async-start(bf16[128,40,128]{2,1,0:T(8,128)(2,1)} %pack.1), calls=%async_computation.5 | async-start | bytes 2621440 | tf_op jit(solution)/shard_map/all_to_all | solution.py:1002
  19.0 37.4 %collective-permute-start = (f32[13,16,8,128]{3,2,1,0:T(8,128)}, f32[13,16,8,128]{3,2,1,0:T(8,128)S(1)}, u32[]{:S(2)}, u32[]{:S(2)}) collective-permute-start(f32[13,16,8,128]{3,2,1,0:T(8,128)} %get-tuple-element.80), channel_id=1, source_target_pairs={{0,1},{1,2},{2,3},{3,4},{4,5},{5,6},{6,7},{7,8},{8,9},{9,10},{10,1... | collective-permute-start | bytes 2555912 | tf_op jit(solution)/shard_map/ppermute | solution.py:1008
  22.4 33.9 %collective-permute-start.1 = (f32[13,16,8,128]{3,2,1,0:T(8,128)}, f32[13,16,8,128]{3,2,1,0:T(8,128)S(1)}, u32[]{:S(2)}, u32[]{:S(2)}) collective-permute-start(f32[13,16,8,128]{3,2,1,0:T(8,128)} %get-tuple-element.81), channel_id=1, source_target_pairs={{1,0},{2,1},{3,2},{4,3},{5,4},{6,5},{7,6},{8,7},{9,8},{10,9},{11,1... | collective-permute-start | bytes 2555912 | tf_op jit(solution)/shard_map/ppermute | solution.py:1008
  44.0 22.0 %collective-permute-start.3 = (f32[2,128,128]{2,1,0:T(8,128)}, f32[2,128,128]{2,1,0:T(8,128)S(1)}, u32[]{:S(2)}, u32[]{:S(2)}) collective-permute-start(f32[2,128,128]{2,1,0:T(8,128)} %get-tuple-element.85.heat_own.heat_own_far), channel_id=1, source_target_pairs={{1,0},{2,1},{3,2},{4,3},{5,4},{6,5},{7,6},{8,7},{9,8},{10,9},{11,1... | collective-permute-start | bytes 393224 | tf_op jit(solution)/shard_map/ppermute | solution.py:1008
  45.3 20.7 %collective-permute-start.2 = (f32[2,128,128]{2,1,0:T(8,128)}, f32[2,128,128]{2,1,0:T(8,128)S(1)}, u32[]{:S(2)}, u32[]{:S(2)}) collective-permute-start(f32[2,128,128]{2,1,0:T(8,128)} %get-tuple-element.85.heat_own.heat_own_far), channel_id=1, source_target_pairs={{0,1},{1,2},{2,3},{3,4},{4,5},{5,6},{6,7},{7,8},{8,9},{9,10},{10,1... | collective-permute-start | bytes 393224 | tf_op jit(solution)/shard_map/ppermute | solution.py:1008
  49.3 16.7 %all-to-all-start.6 = ((f32[128,1,128]{2,1,0:T(1,128)}), f32[128,1,128]{2,1,0:T(1,128)S(1)}, u32[]{:S(2)}, u32[]{:S(2)}) async-start(f32[128,1,128]{2,1,0:T(1,128)} %get-tuple-element.86), calls=%async_computation.6 | async-start | bytes 131072 | tf_op jit(solution)/shard_map/all_to_all | solution.py:1002
  56.4 9.6 %copy-start.9 = (f32[13,16,8,128]{3,2,1,0:T(8,128)}, f32[13,16,8,128]{3,2,1,0:T(8,128)S(1)}, u32[]{:S(2)}) copy-start(f32[13,16,8,128]{3,2,1,0:T(8,128)S(1)} %collective-permute-done.low.low_far) | copy-start | bytes 2555908
  56.4 9.6 %copy-start.10 = (f32[13,16,8,128]{3,2,1,0:T(8,128)}, f32[13,16,8,128]{3,2,1,0:T(8,128)S(1)}, u32[]{:S(2)}) copy-start(f32[13,16,8,128]{3,2,1,0:T(8,128)S(1)} %collective-permute-done.1.high.high_far) | copy-start | bytes 2555908
  65.9 0.7 copy-start.11
  65.9 0.7 copy-start.12
  67.9 7.3 %collective-permute-start.4 = (f32[49,8,128]{2,1,0:T(8,128)S(1)}, f32[49,8,128]{2,1,0:T(8,128)S(1)}, u32[]{:S(2)}, u32[]{:S(2)}) collective-permute-start(f32[49,8,128]{2,1,0:T(8,128)S(1)} %get-tuple-element.95), channel_id=1, source_target_pairs={{0,16},{16,32},{32,48},{48,64},{64,80},{80,96},{96,112},{1,17},{17... | collective-permute-start | bytes 602120 | tf_op jit(solution)/shard_map/ppermute | solution.py:1008
  70.9 7.0 %collective-permute-start.5 = (f32[49,8,128]{2,1,0:T(8,128)S(1)}, f32[49,8,128]{2,1,0:T(8,128)S(1)}, u32[]{:S(2)}, u32[]{:S(2)}) collective-permute-start(f32[49,8,128]{2,1,0:T(8,128)S(1)} %get-tuple-element.96), channel_id=1, source_target_pairs={{16,0},{32,16},{48,32},{64,48},{80,64},{96,80},{112,96},{17,1},{33... | collective-permute-start | bytes 602120 | tf_op jit(solution)/shard_map/ppermute | solution.py:1008
  87.3 19.8 %copy-start.8 = (f32[2,20,144,128]{3,2,1,0:T(8,128)}, f32[2,20,144,128]{3,2,1,0:T(8,128)S(1)}, u32[]{:S(2)}) copy-start(f32[2,20,144,128]{3,2,1,0:T(8,128)S(1)} %get-tuple-element.98.field) | copy-start | bytes 8847364
  87.3 33.6 %copy-start.6 = (f32[2,20,144,128]{3,2,1,0:T(8,128)}, f32[2,20,144,128]{3,2,1,0:T(8,128)S(1)}, u32[]{:S(2)}) copy-start(f32[2,20,144,128]{3,2,1,0:T(8,128)S(1)} %get-tuple-element.100.coef) | copy-start | bytes 8847364
  126.9 22.1 %copy-start.13 = (f32[16,8,128]{2,1,0:T(8,128)S(1)}, f32[16,8,128]{2,1,0:T(8,128)}, u32[]{:S(2)}) copy-start(f32[16,8,128]{2,1,0:T(8,128)} %get-tuple-element.107.data_far) | copy-start | bytes 196612
  126.9 22.1 %copy-start.14 = (f32[8,128]{1,0:T(8,128)S(1)}, f32[8,128]{1,0:T(8,128)}, u32[]{:S(2)}) copy-start(f32[8,128]{1,0:T(8,128)} %get-tuple-element.106.weight_far) | copy-start | bytes 12292
  126.9 18.4 %all-to-all-start.9 = ((f32[128,8,128]{2,1,0:T(8,128)}), f32[128,8,128]{2,1,0:T(8,128)S(1)}, u32[]{:S(2)}, u32[]{:S(2)}) async-start(f32[128,8,128]{2,1,0:T(8,128)} %get-tuple-element.108), calls=%async_computation.9 | async-start | bytes 1048576 | tf_op jit(solution)/shard_map/all_to_all | solution.py:1002

commit v12 on v11

--- a/solution.py
+++ b/solution.py
@@ -60,7 +60,13 @@
     return lax.broadcasted_iota(jnp.int32, (CY, CX), 0)
 
 
-def pack_kernel(owner_far, heat_far, voxel_far, out, owner, heat, voxel, wide, high, low, inverse, sems):
+PARTS = 4
+
+
+def pack_kernel(
+    owner_far, heat_far, voxel_far, out_far,
+    out, owner, heat, voxel, wide, high, low, inverse, sems, out_sems,
+):
     copies = fetch(sems, ((owner_far, owner), (heat_far, heat), (voxel_far, voxel)))
     blocks = owner.shape[0]
     devices = out.shape[0]
@@ -122,17 +128,27 @@
         out[d] = chunk.astype(BF16)
         return carry
 
-    lax.fori_loop(0, devices, emit, 0, unroll=16)
+    share = devices // PARTS
+    sent = []
+    for part in range(PARTS):
+        lax.fori_loop(part * share, (part + 1) * share, emit, 0, unroll=16)
+        at = pl.ds(part * share, share)
+        copy = pltpu.make_async_copy(out.at[at], out_far.at[at], out_sems.at[part])
+        copy.start()
+        sent.append(copy)
+    for copy in sent:
+        copy.wait()
 
 
 def pack(owner, heat, voxel, devices):
     blocks = owner.shape[0]
     return pl.pallas_call(
         pack_kernel,
-        out_shape=jax.ShapeDtypeStruct((devices, ROWS, CX), BF16),
+        out_shape=pltpu.HBM((devices, ROWS, CX), BF16),
         in_specs=[hspec()] * 3,
-        out_specs=vspec(),
+        out_specs=hspec(),
         scratch_shapes=[
+            VM((devices, ROWS, CX), BF16),
             pltpu.SMEM((blocks,), jnp.int32),
             VM((M, blocks, CX), BF16),
             VM((blocks, CX), jnp.int32),
@@ -141,6 +157,7 @@
             VM((blocks + 8, CX), F32),
             pltpu.SMEM((devices * CAP,), jnp.int32),
             pltpu.SemaphoreType.DMA((3,)),
+            pltpu.SemaphoreType.DMA((PARTS,)),
         ],
         compiler_params=params(),
         name="pack",
@@ -159,34 +176,50 @@
 SIDE = 2 * YS
 
 
-def relayout_kernel(
-    state, conduct, own, turned_c, to_high, to_low, edge_left, edge_right, top, quiet
-):
+def layout_block(state, zi, y):
+    parts = [state[m0 : m0 + 8, 2 * group + zi, y, :] for group in range(ZG) for m0 in (0, 8)]
+    return (0.5 * jnp.concatenate(parts, axis=0)).T
+
+
+def rim_kernel(state, conduct, turned_c, to_high, to_low):
     turned = (0.5 * conduct[...].reshape(CX, CX)).T.reshape(XT - 2, 8, CX)
     turned_c[...] = turned
     to_high[EDGE] = turned
     to_low[EDGE] = turned
-    peak = jnp.zeros((8, CX), F32)
     for zi in range(2):
         for y in range(CY):
-            parts = []
-            for group in range(ZG):
-                layer = 2 * group + zi
-                c = 0.5 * conduct[layer, y : y + 1, :]
-                for m0 in (0, 8):
-                    part = 0.5 * state[m0 : m0 + 8, layer, y, :]
-                    parts.append(part)
-                    if group:
-                        peak = jnp.maximum(peak, c + c * (part * part))
-            turned = jnp.concatenate(parts, axis=0).T
-            own[zi, y] = turned
-            turned = turned.reshape(XT - 2, 8, CX)
-            edge_left[zi * CY + y] = turned[0]
-            edge_right[zi * CY + y] = turned[XT - 3]
+            turned = layout_block(state, zi, y).reshape(XT - 2, 8, CX)
             if y >= CY - HALO:
                 to_high[zi * HALO + y - (CY - HALO)] = turned
             if y < HALO:
                 to_low[zi * HALO + y] = turned
+
+
+def rims(state, conduct):
+    edge = kept((EDGE + 1, XT - 2, 8, CX))
+    return pl.pallas_call(
+        rim_kernel,
+        out_shape=[kept((XT - 2, 8, CX)), edge, edge],
+        in_specs=[vspec()] * 2,
+        out_specs=[vspec()] * 3,
+        compiler_params=params(),
+        name="rims",
+    )(state, conduct)
+
+
+def relayout_kernel(state, conduct, own, edge_left, edge_right, top, quiet):
+    peak = jnp.zeros((8, CX), F32)
+    for zi in range(2):
+        for y in range(CY):
+            turned = layout_block(state, zi, y)
+            own[zi, y] = turned
+            edge_left[zi * CY + y] = turned[0:8]
+            edge_right[zi * CY + y] = turned[CX - 8 :]
+    for z in range(2, NZ):
+        c = 0.5 * conduct[z]
+        for m in range(M):
+            value = 0.5 * state[m, z]
+            peak = jnp.maximum(peak, c + c * (value * value))
     quiet[...] = peak
     for m in range(M):
         for zi in range(2):
@@ -194,22 +227,12 @@
 
 
 def relayout(state, conduct):
-    edge = kept((EDGE + 1, XT - 2, 8, CX))
     side = kept((2 * CY, 8, CX))
     return pl.pallas_call(
         relayout_kernel,
-        out_shape=[
-            kept(OWN.shape),
-            kept((XT - 2, 8, CX)),
-            edge,
-            edge,
-            side,
-            side,
-            kept((M, 2, CY, CX)),
-            kept((8, CX)),
-        ],
+        out_shape=[kept(OWN.shape), side, side, kept((M, 2, CY, CX)), kept((8, CX))],
         in_specs=[vspec()] * 2,
-        out_specs=[vspec()] * 8,
+        out_specs=[vspec()] * 5,
         compiler_params=params(),
         name="relayout",
     )(state, conduct)
@@ -302,7 +325,7 @@
 ):
     copies = fetch(sems, ((top_far, top), (conduct_far.at[0:2], conduct), (quiet_far, quiet)))
     sources = incoming.shape[0]
-    group = 32
+    group = 64
     place = lax.broadcasted_iota(jnp.int32, (CX, CX), 0).astype(F32).astype(BF16)
     zero = jnp.zeros((M, CX), BF16)
     total[...] = jnp.zeros_like(total)
@@ -1026,10 +1049,10 @@
         [gx > 0, gx < lax.axis_size("gx") - 1, gy > 0, gy < lax.axis_size("gy") - 1]
     ).astype(F32)
     incoming = exchange(pack(owner_tile.reshape(-1), heat_input, voxel_list, devices))
-    own, turned_c, to_high, to_low, edge_left, edge_right, top, quiet = relayout(
-        state_prior, conductivity
-    )
+    turned_c, to_high, to_low = rims(state_prior, conductivity)
     low, high = move(to_high, "gy", True), move(to_low, "gy", False)
+    state_prior, turned_c = lax.optimization_barrier((state_prior, turned_c))
+    own, edge_left, edge_right, top, quiet = relayout(state_prior, conductivity)
     seen = pixel_sums(
         pixel_cell.reshape(1, pixels),
         observed.reshape(1, pixels),

time: 150 us -> 149 us (level)
    pallas_call x2 -> x3, Pallas kernels: 7.38 us -> 7.48 us  [the longest x1 3.96 us: pack(): pl.pallas_call(pack_kernel, out_shape=pltpu.HBM((devices, ROWS, CX), BF16...]
where the time goes in v12:
time: 149 us; the launch traced here: 148 us
  Pallas kernels  44 us (30%)
  starting transfers between devices  38.3 us (26%)
  waiting for transfers between devices  36.7 us (25%)
  blocking collectives  27.2 us (18%)
    all_to_all x3, waiting for transfers between devices, exchange(): return lax.all_to_all(parts, BOTH, split_axis=0, concat_axis=0, tiled=True)  34.1 us
    all_to_all x2, blocking collectives, exchange(): return lax.all_to_all(parts, BOTH, split_axis=0, concat_axis=0, tiled=True)  27.2 us
    all_to_all x3, starting transfers between devices, exchange(): return lax.all_to_all(parts, BOTH, split_axis=0, concat_axis=0, tiled=True)  23.1 us
    ppermute x6, starting transfers between devices, move(): return lax.ppermute(part, axis, pairs)  15.2 us
    pallas_call x1, Pallas kernels, heated(): pl.pallas_call(heated_kernel, out_shape=[WIDE, WIDE, WIDE, jax.ShapeDtype...  8.92 us
    pallas_call x1, Pallas kernels, deposit(): pl.pallas_call(deposit_kernel, out_shape=[kept((2, CX, CX)), jax.ShapeDty...  6.39 us
    pallas_call x1, Pallas kernels, pair(): pl.pallas_call(functools.partial(pair_kernel, number), out_shape=[WIDE, W...  6.29 us
    pallas_call x1, Pallas kernels, last(): pl.pallas_call(last_kernel, out_shape=[OWN, OWN, sums_shape(parts.shape[0...  5.93 us
  transfers between devices with their start and end apart: 9, of which 4 were waited for; matrix products, arithmetic and copies ran while one was open for 0% of the time, Pallas kernels for 10%

profile of v12, /device:TPU:1, one launch (start us, length us, event | category | flops | bytes accessed | tf_op | source)
XLA Modules:
  0.0 147.9 jit_solution(9891792459523219446)
XLA Ops:
  0.0 0.0 copy-start.3
  0.0 0.0 copy-start.4
  0.0 0.0 copy-start.5
  0.0 4.0 %pack.1 = bf16[128,40,128]{2,1,0:T(8,128)(2,1)} custom-call(s32[128]{0:T(128)} %bitcast.12, bf16[16,128,128]{2,1,0:T(8,128)(2,1)} %heat_far.1, s32[128,128]{1,0:T(8,128)} %voxel_far.1), custom_call_target="tpu_custom_call" | custom-call | tf_op jit(solution)/shard_map/pack/pallas_call | solution.py:145
  4.0 11.5 %all-to-all-start.5 = ((bf16[128,40,128]{2,1,0:T(8,128)(2,1)}), bf16[128,40,128]{2,1,0:T(8,128)(2,1)S(1)}, u32[]{:S(2)}, u32[]{:S(2)}) async-start(bf16[128,40,128]{2,1,0:T(8,128)(2,1)} %pack.1), calls=%async_computation.5 | async-start | bytes 2621440 | tf_op jit(solution)/shard_map/all_to_all | solution.py:1025
  15.5 0.0 copy-done.1
  15.5 0.0 copy-done
  15.5 1.9 %rims.1 = (f32[16,8,128]{2,1,0:T(8,128)}, f32[13,16,8,128]{3,2,1,0:T(8,128)}, f32[13,16,8,128]{3,2,1,0:T(8,128)}) custom-call(f32[16,16,8,128]{3,2,1,0:T(8,128)S(1)} %copy-done, f32[16,8,128]{2,1,0:T(8,128)S(1)} %copy-done.1), custom_call_target="tpu_custom_call" | custom-call | tf_op jit(solution)/shard_map/rims/pallas_call | solution.py:200
  17.4 3.5 %collective-permute-start = (f32[13,16,8,128]{3,2,1,0:T(8,128)}, f32[13,16,8,128]{3,2,1,0:T(8,128)S(1)}, u32[]{:S(2)}, u32[]{:S(2)}) collective-permute-start(f32[13,16,8,128]{3,2,1,0:T(8,128)} %get-tuple-element.84), channel_id=1, source_target_pairs={{0,1},{1,2},{2,3},{3,4},{4,5},{5,6},{6,7},{7,8},{8,9},{9,10},{10,1... | collective-permute-start | bytes 2555912 | tf_op jit(solution)/shard_map/ppermute | solution.py:1031
  20.9 1.3 collective-permute-start.1
  22.2 1.7 %relayout.1 = (f32[2,8,128,128]{3,2,1,0:T(8,128)}, f32[16,8,128]{2,1,0:T(8,128)}, f32[16,8,128]{2,1,0:T(8,128)}, f32[16,2,8,128]{3,2,1,0:T(8,128)}, f32[8,128]{1,0:T(8,128)}) custom-call(f32[16,16,8,128]{3,2,1,0:T(8,128)S(1)} %copy-done, f32[16,8,128]{2,1,0:T(8,128)S(1)} %copy-done.1), custom_call_target="tpu_custom_call" | custom-call | tf_op jit(solution)/shard_map/relayout/pallas_call | solution.py:231
  23.8 0.0 copy-done.2
  23.8 0.0 copy-done.3
  23.9 2.4 %pixels.1 = (f32[8,128]{1,0:T(8,128)}, f32[16,8,128]{2,1,0:T(8,128)}) custom-call(s32[1,512]{1,0:T(1,128)S(1)} %bitcast.9, f32[1,512]{1,0:T(1,128)S(1)} %bitcast.10, f32[1,512]{1,0:T(1,128)S(1)} %bitcast.11, f32[16,512]{1,0:T(8,128)S(1)} %copy-done.2), custom_call_target="tpu_custom_call" | custom-call | tf_op jit(solution)/shard_map/pixels/pallas_call | solution.py:924
  26.2 0.1 add_convert_fusion.inside
  26.3 10.6 %all-to-all-done.5.incoming = bf16[128,40,128]{2,1,0:T(8,128)(2,1)S(1)} async-done(((bf16[128,40,128]{2,1,0:T(8,128)(2,1)}), bf16[128,40,128]{2,1,0:T(8,128)(2,1)S(1)}, u32[]{:S(2)}, u32[]{:S(2)}) %all-to-all-start.5) | async-done | bytes 1310752 | tf_op jit(solution)/shard_map/all_to_all | solution.py:1025
  36.9 6.4 %deposit.1 = (f32[2,128,128]{2,1,0:T(8,128)}, f32[128,1,128]{2,1,0:T(1,128)}) custom-call(bf16[128,40,128]{2,1,0:T(8,128)(2,1)S(1)} %all-to-all-done.5.incoming, f32[16,2,8,128]{3,2,1,0:T(8,128)} %get-tuple-element.87.top_far, f32[16,8,128]{2,1,0:T(8,128)} %conduct_far.1, f32[8,128]{1,0:T(8,128)} %get-tuple-element.88.quiet_far), custom_call_target="tpu_custom_call" | custom-call | tf_op jit(solution)/shard_map/deposit/pallas_call | solution.py:378
  43.3 1.3 collective-permute-start.3
  44.6 4.0 %collective-permute-start.2 = (f32[2,128,128]{2,1,0:T(8,128)}, f32[2,128,128]{2,1,0:T(8,128)S(1)}, u32[]{:S(2)}, u32[]{:S(2)}) collective-permute-start(f32[2,128,128]{2,1,0:T(8,128)} %get-tuple-element.89.heat_own.heat_own_far), channel_id=1, source_target_pairs={{0,1},{1,2},{2,3},{3,4},{4,5},{5,6},{6,7},{7,8},{8,9},{9,10},{10,1... | collective-permute-start | bytes 393224 | tf_op jit(solution)/shard_map/ppermute | solution.py:1031
  48.6 7.1 %all-to-all-start.6 = ((f32[128,1,128]{2,1,0:T(1,128)}), f32[128,1,128]{2,1,0:T(1,128)S(1)}, u32[]{:S(2)}, u32[]{:S(2)}) async-start(f32[128,1,128]{2,1,0:T(1,128)} %get-tuple-element.90), calls=%async_computation.6 | async-start | bytes 131072 | tf_op jit(solution)/shard_map/all_to_all | solution.py:1025
  55.7 0.0 collective-permute-done.low.low_far
  55.7 0.0 collective-permute-done.1.high.high_far
  55.7 9.5 %all-to-all-done.6.peaks = f32[128,1,128]{2,1,0:T(1,128)S(1)} async-done(((f32[128,1,128]{2,1,0:T(1,128)}), f32[128,1,128]{2,1,0:T(1,128)S(1)}, u32[]{:S(2)}, u32[]{:S(2)}) %all-to-all-start.6) | async-done | bytes 65568 | tf_op jit(solution)/shard_map/all_to_all | solution.py:1025
  65.2 0.0 collective-permute-done.3.heat_high.heat_high_far
  65.2 0.0 collective-permute-done.2.heat_low.heat_low_far
  65.3 0.0 copy-start.11
  65.3 0.0 copy-done.9
  65.3 0.6 copy-done.10
  65.9 0.1 copy-done.11
  66.0 1.2 sides.1
  67.2 3.1 %collective-permute-start.4 = (f32[49,8,128]{2,1,0:T(8,128)S(1)}, f32[49,8,128]{2,1,0:T(8,128)S(1)}, u32[]{:S(2)}, u32[]{:S(2)}) collective-permute-start(f32[49,8,128]{2,1,0:T(8,128)S(1)} %get-tuple-element.99), channel_id=1, source_target_pairs={{0,16},{16,32},{32,48},{48,64},{64,80},{80,96},{96,112},{1,17},{17... | collective-permute-start | bytes 602120 | tf_op jit(solution)/shard_map/ppermute | solution.py:1031
  70.2 2.1 %collective-permute-start.5 = (f32[49,8,128]{2,1,0:T(8,128)S(1)}, f32[49,8,128]{2,1,0:T(8,128)S(1)}, u32[]{:S(2)}, u32[]{:S(2)}) collective-permute-start(f32[49,8,128]{2,1,0:T(8,128)S(1)} %get-tuple-element.100), channel_id=1, source_target_pairs={{16,0},{32,16},{48,32},{64,48},{80,64},{96,80},{112,96},{17,1},{33... | collective-permute-start | bytes 602120 | tf_op jit(solution)/shard_map/ppermute | solution.py:1031
  72.4 2.3 %coefs.1.coef_main = f32[2,20,128,128]{3,2,1,0:T(8,128)S(1)} custom-call(f32[16,8,128]{2,1,0:T(8,128)} %get-tuple-element.94.turned_c.own, f32[13,16,8,128]{3,2,1,0:T(8,128)} %copy-done.9, f32[13,16,8,128]{3,2,1,0:T(8,128)} %collective-permute-done.1.high.high_far), custom_call_target="tpu_custom_call" | custom-call | tf_op jit(solution)/shard_map/coefs/pallas_call | solution.py:312
  74.7 0.0 collective-permute-done.4.left
  74.7 2.6 %collective-permute-done.5.right = f32[49,8,128]{2,1,0:T(8,128)S(1)} collective-permute-done((f32[49,8,128]{2,1,0:T(8,128)S(1)}, f32[49,8,128]{2,1,0:T(8,128)S(1)}, u32[]{:S(2)}, u32[]{:S(2)}) %collective-permute-start.5) | collective-permute-done | bytes 200736 | tf_op jit(solution)/shard_map/ppermute | solution.py:1031
  77.3 8.9 %heated.1 = (f32[2,20,144,128]{3,2,1,0:T(8,128)S(1)}, f32[2,20,144,128]{3,2,1,0:T(8,128)S(1)}, f32[2,20,144,128]{3,2,1,0:T(8,128)S(1)}, f32[128,1,128]{2,1,0:T(1,128)S(1)}) custom-call(f32[4]{0:T(128)S(1)} %add_convert_fusion.inside, f32[128,1,128]{2,1,0:T(1,128)S(1)} %all-to-all-done.6.peaks, f32[49,8,128]{2,1,0:T(8,128)S(1)} %collective-permute-done.4.left, ...), custom_call_target="tpu_custom_call" | custom-call | tf_op jit(solution)/shard_map/heated/pallas_call | solution.py:656
  86.2 13.3 %all_to_all.50.parts = f32[128,1,128]{2,1,0:T(1,128)S(1)} all-to-all(f32[128,1,128]{2,1,0:T(1,128)S(1)} %get-tuple-element.105), channel_id=1, replica_groups=mesh['gx'=8,'gy'=16] {'gx','gy'}, dimensions={0} | all-to-all | bytes 131072 | tf_op jit(solution)/shard_map/all_to_all | solution.py:1025
  99.6 6.3 %pair_1.1 = (f32[2,20,144,128]{3,2,1,0:T(8,128)S(1)}, f32[2,20,144,128]{3,2,1,0:T(8,128)S(1)}, f32[128,1,128]{2,1,0:T(1,128)S(1)}, f32[8,128]{1,0:T(8,128)S(1)}) custom-call(f32[4]{0:T(128)S(1)} %add_convert_fusion.inside, f32[2,20,144,128]{3,2,1,0:T(8,128)S(1)} %get-tuple-element.102.field, f32[2,20,144,128]{3,2,1,0:T(8,128)S(1)} %get-tuple-element.103.changes, ...), custom_call_target="tpu_custom_call" | custom-call | tf_op jit(solution)/shard_map/pair_1/pallas_call | solution.py:717
  105.9 0.0 copy-done.8
  105.9 13.9 %all_to_all.51.parts = f32[128,1,128]{2,1,0:T(1,128)S(1)} all-to-all(f32[128,1,128]{2,1,0:T(1,128)S(1)} %get-tuple-element.108), channel_id=1, replica_groups=mesh['gx'=8,'gy'=16] {'gx','gy'}, dimensions={0} | all-to-all | bytes 131072 | tf_op jit(solution)/shard_map/all_to_all | solution.py:1025
  119.8 5.9 %last_pair.1 = (f32[2,8,128,128]{3,2,1,0:T(8,128)S(1)}, f32[2,8,128,128]{3,2,1,0:T(8,128)S(1)}, f32[128,8,128]{2,1,0:T(8,128)}, f32[8,128]{1,0:T(8,128)S(1)}) custom-call(f32[4]{0:T(128)S(1)} %add_convert_fusion.inside, f32[2,20,144,128]{3,2,1,0:T(8,128)S(1)} %get-tuple-element.106.field, f32[2,20,144,128]{3,2,1,0:T(8,128)S(1)} %get-tuple-element.107.changes, ...), custom_call_target="tpu_custom_call" | custom-call | tf_op jit(solution)/shard_map/last_pair/pallas_call | solution.py:829
  125.7 0.0 copy-start.12
  125.7 0.0 copy-start.13
  125.7 4.5 %all-to-all-start.9 = ((f32[128,8,128]{2,1,0:T(8,128)}), f32[128,8,128]{2,1,0:T(8,128)S(1)}, u32[]{:S(2)}, u32[]{:S(2)}) async-start(f32[128,8,128]{2,1,0:T(8,128)} %get-tuple-element.112), calls=%async_computation.9 | async-start | bytes 1048576 | tf_op jit(solution)/shard_map/all_to_all | solution.py:1025
  130.2 13.9 %all-to-all-done.9.sums = f32[128,8,128]{2,1,0:T(8,128)S(1)} async-done(((f32[128,8,128]{2,1,0:T(8,128)}), f32[128,8,128]{2,1,0:T(8,128)S(1)}, u32[]{:S(2)}, u32[]{:S(2)}) %all-to-all-start.9) | async-done | bytes 524320 | tf_op jit(solution)/shard_map/all_to_all | solution.py:1025
  144.1 3.0 %update.3 = (f32[16,16,8,128]{3,2,1,0:T(8,128)}, s32[1]{0:T(128)}) custom-call(f32[128,8,128]{2,1,0:T(8,128)S(1)} %all-to-all-done.9.sums, f32[2,8,128,128]{3,2,1,0:T(8,128)S(1)} %get-tuple-element.113.field, f32[2,8,128,128]{3,2,1,0:T(8,128)S(1)} %get-tuple-element.114.changes, f32[8,128]{1,0:T(8,128)S(1)} %get-tuple-element.115.status), custom_call_target="tpu_custom_call" | custom-call | tf_op jit(solution)/shard_map/update/pallas_call | solution.py:1011
  147.8 0.0 copy-done.12
  147.8 0.0 copy-done.13
  (11 shorter events, 0.0 us)
Async XLA Ops:
  0.0 15.5 %copy-start.1 = (f32[16,8,128]{2,1,0:T(8,128)S(1)}, f32[16,8,128]{2,1,0:T(8,128)}, u32[]{:S(2)}) copy-start(f32[16,8,128]{2,1,0:T(8,128)} %conduct_far.1) | copy-start | bytes 196612
  0.0 15.5 %copy-start = (f32[16,16,8,128]{3,2,1,0:T(8,128)S(1)}, f32[16,16,8,128]{3,2,1,0:T(8,128)}, u32[]{:S(2)}) copy-start(f32[16,16,8,128]{3,2,1,0:T(8,128)} %state.2) | copy-start | bytes 3145732
  0.0 23.8 %copy-start.2 = (f32[16,512]{1,0:T(8,128)S(1)}, f32[16,512]{1,0:T(8,128)}, u32[]{:S(2)}) copy-start(f32[16,512]{1,0:T(8,128)} %noise.1) | copy-start | bytes 98308
  0.0 23.8 %copy-start.3 = (s32[512]{0:T(512)S(1)}, s32[512]{0:T(512)}, u32[]{:S(2)}) copy-start(s32[512]{0:T(512)} %param.16) | copy-start | bytes 6148
  0.0 23.8 %copy-start.4 = (f32[512]{0:T(512)S(1)}, f32[512]{0:T(512)}, u32[]{:S(2)}) copy-start(f32[512]{0:T(512)} %param.17) | copy-start | bytes 6148
  0.0 23.8 %copy-start.5 = (f32[512]{0:T(512)S(1)}, f32[512]{0:T(512)}, u32[]{:S(2)}) copy-start(f32[512]{0:T(512)} %param.18) | copy-start | bytes 6148
  4.0 32.9 %all-to-all-start.5 = ((bf16[128,40,128]{2,1,0:T(8,128)(2,1)}), bf16[128,40,128]{2,1,0:T(8,128)(2,1)S(1)}, u32[]{:S(2)}, u32[]{:S(2)}) async-start(bf16[128,40,128]{2,1,0:T(8,128)(2,1)} %pack.1), calls=%async_computation.5 | async-start | bytes 2621440 | tf_op jit(solution)/shard_map/all_to_all | solution.py:1025
  17.4 38.3 %collective-permute-start = (f32[13,16,8,128]{3,2,1,0:T(8,128)}, f32[13,16,8,128]{3,2,1,0:T(8,128)S(1)}, u32[]{:S(2)}, u32[]{:S(2)}) collective-permute-start(f32[13,16,8,128]{3,2,1,0:T(8,128)} %get-tuple-element.84), channel_id=1, source_target_pairs={{0,1},{1,2},{2,3},{3,4},{4,5},{5,6},{6,7},{7,8},{8,9},{9,10},{10,1... | collective-permute-start | bytes 2555912 | tf_op jit(solution)/shard_map/ppermute | solution.py:1031
  20.9 34.8 %collective-permute-start.1 = (f32[13,16,8,128]{3,2,1,0:T(8,128)}, f32[13,16,8,128]{3,2,1,0:T(8,128)}, u32[]{:S(2)}, u32[]{:S(2)}) collective-permute-start(f32[13,16,8,128]{3,2,1,0:T(8,128)} %get-tuple-element.85), channel_id=1, source_target_pairs={{1,0},{2,1},{3,2},{4,3},{5,4},{6,5},{7,6},{8,7},{9,8},{10,9},{11,1... | collective-permute-start | bytes 2555912 | tf_op jit(solution)/shard_map/ppermute | solution.py:1031
  43.3 22.0 %collective-permute-start.3 = (f32[2,128,128]{2,1,0:T(8,128)}, f32[2,128,128]{2,1,0:T(8,128)S(1)}, u32[]{:S(2)}, u32[]{:S(2)}) collective-permute-start(f32[2,128,128]{2,1,0:T(8,128)} %get-tuple-element.89.heat_own.heat_own_far), channel_id=1, source_target_pairs={{1,0},{2,1},{3,2},{4,3},{5,4},{6,5},{7,6},{8,7},{9,8},{10,9},{11,1... | collective-permute-start | bytes 393224 | tf_op jit(solution)/shard_map/ppermute | solution.py:1031
  44.6 20.7 %collective-permute-start.2 = (f32[2,128,128]{2,1,0:T(8,128)}, f32[2,128,128]{2,1,0:T(8,128)S(1)}, u32[]{:S(2)}, u32[]{:S(2)}) collective-permute-start(f32[2,128,128]{2,1,0:T(8,128)} %get-tuple-element.89.heat_own.heat_own_far), channel_id=1, source_target_pairs={{0,1},{1,2},{2,3},{3,4},{4,5},{5,6},{6,7},{7,8},{8,9},{9,10},{10,1... | collective-permute-start | bytes 393224 | tf_op jit(solution)/shard_map/ppermute | solution.py:1031
  48.6 16.7 %all-to-all-start.6 = ((f32[128,1,128]{2,1,0:T(1,128)}), f32[128,1,128]{2,1,0:T(1,128)S(1)}, u32[]{:S(2)}, u32[]{:S(2)}) async-start(f32[128,1,128]{2,1,0:T(1,128)} %get-tuple-element.90), calls=%async_computation.6 | async-start | bytes 131072 | tf_op jit(solution)/shard_map/all_to_all | solution.py:1025
  55.7 9.6 %copy-start.9 = (f32[13,16,8,128]{3,2,1,0:T(8,128)}, f32[13,16,8,128]{3,2,1,0:T(8,128)S(1)}, u32[]{:S(2)}) copy-start(f32[13,16,8,128]{3,2,1,0:T(8,128)S(1)} %collective-permute-done.low.low_far) | copy-start | bytes 2555908
  65.2 0.6 copy-start.10
  65.3 0.7 copy-start.11
  67.2 7.5 %collective-permute-start.4 = (f32[49,8,128]{2,1,0:T(8,128)S(1)}, f32[49,8,128]{2,1,0:T(8,128)S(1)}, u32[]{:S(2)}, u32[]{:S(2)}) collective-permute-start(f32[49,8,128]{2,1,0:T(8,128)S(1)} %get-tuple-element.99), channel_id=1, source_target_pairs={{0,16},{16,32},{32,48},{48,64},{64,80},{80,96},{96,112},{1,17},{17... | collective-permute-start | bytes 602120 | tf_op jit(solution)/shard_map/ppermute | solution.py:1031
  70.2 7.0 %collective-permute-start.5 = (f32[49,8,128]{2,1,0:T(8,128)S(1)}, f32[49,8,128]{2,1,0:T(8,128)S(1)}, u32[]{:S(2)}, u32[]{:S(2)}) collective-permute-start(f32[49,8,128]{2,1,0:T(8,128)S(1)} %get-tuple-element.100), channel_id=1, source_target_pairs={{16,0},{32,16},{48,32},{64,48},{80,64},{96,80},{112,96},{17,1},{33... | collective-permute-start | bytes 602120 | tf_op jit(solution)/shard_map/ppermute | solution.py:1031
  86.2 19.7 %copy-start.8 = (f32[2,20,144,128]{3,2,1,0:T(8,128)}, f32[2,20,144,128]{3,2,1,0:T(8,128)S(1)}, u32[]{:S(2)}) copy-start(f32[2,20,144,128]{3,2,1,0:T(8,128)S(1)} %get-tuple-element.102.field) | copy-start | bytes 8847364
  86.2 33.5 %copy-start.6 = (f32[2,20,144,128]{3,2,1,0:T(8,128)}, f32[2,20,144,128]{3,2,1,0:T(8,128)S(1)}, u32[]{:S(2)}) copy-start(f32[2,20,144,128]{3,2,1,0:T(8,128)S(1)} %get-tuple-element.104.coef) | copy-start | bytes 8847364
  125.7 22.1 %copy-start.12 = (f32[16,8,128]{2,1,0:T(8,128)S(1)}, f32[16,8,128]{2,1,0:T(8,128)}, u32[]{:S(2)}) copy-start(f32[16,8,128]{2,1,0:T(8,128)} %get-tuple-element.111.data_far) | copy-start | bytes 196612
  125.7 22.1 %copy-start.13 = (f32[8,128]{1,0:T(8,128)S(1)}, f32[8,128]{1,0:T(8,128)}, u32[]{:S(2)}) copy-start(f32[8,128]{1,0:T(8,128)} %get-tuple-element.110.weight_far) | copy-start | bytes 12292
  125.7 18.4 %all-to-all-start.9 = ((f32[128,8,128]{2,1,0:T(8,128)}), f32[128,8,128]{2,1,0:T(8,128)S(1)}, u32[]{:S(2)}, u32[]{:S(2)}) async-start(f32[128,8,128]{2,1,0:T(8,128)} %get-tuple-element.112), calls=%async_computation.9 | async-start | bytes 1048576 | tf_op jit(solution)/shard_map/all_to_all | solution.py:1025

commit v13 on v12

--- a/solution.py
+++ b/solution.py
@@ -429,7 +429,7 @@
     return row_mask
 
 
-def sweep(field, half, above, inside, first, end, emit, carry):
+def sweep(field, half, above, inside, first, end, emit, carry, unroll=1):
     lane = lanes()
     row = rows()
     last_row = row == 7
@@ -483,11 +483,13 @@
         return state
 
     for start, stop, own, row_mask in segments(inside, first, end):
-        carry = lax.fori_loop(start, stop, functools.partial(line, own, row_mask), carry)
+        carry = lax.fori_loop(
+            start, stop, functools.partial(line, own, row_mask), carry, unroll=unroll
+        )
     return carry
 
 
-def advance(field, half, coef, above, inside, step, first, end, put):
+def advance(field, half, coef, above, inside, step, first, end, put, unroll=2):
     def emit(y, t, us, change, own, mask, peak):
         part = step if mask is None else step * mask
         for zi in range(2):
@@ -498,7 +500,8 @@
                 peak = jnp.maximum(peak, after)
         return peak
 
-    return sweep(field, half, above, inside, first, end, emit, jnp.zeros((8, CX), F32))
+    zero = jnp.zeros((8, CX), F32)
+    return sweep(field, half, above, inside, first, end, emit, zero, unroll=unroll)
 
 
 def propose(field, half, coef, above, inside, guess, first, end, changes, peak, late, out):
@@ -517,7 +520,8 @@
         return best
 
     best = sweep(
-        field, half, above, inside, first, end, emit, (jnp.zeros((8, CX), F32),) * 4
+        field, half, above, inside, first, end, emit, (jnp.zeros((8, CX), F32),) * 4,
+        unroll=1,
     )
     for shift, axis in ((4, 0), (2, 0), (1, 0), (64, 1), (32, 1)):
         other = tuple(pltpu.roll(part, shift, axis=axis) for part in best)
@@ -634,7 +638,7 @@
         next_half[zi, y, tile(t), :] = after
 
     step = step_of(whole_peak(largest(gather_rows(peaks))))
-    peak = advance(start, half, coef, above, inside, step, 1, YS - 1, put)
+    peak = advance(start, half, coef, above, inside, step, 1, YS - 1, put, unroll=4)
     guess = jnp.minimum(step_of(whole_peak(peak)), 2.0 * step)
     zero = jnp.zeros((8, CX), F32)
     propose(
@@ -681,7 +685,7 @@
         own = jnp.where((y >= HALO) & (y < HALO + CY), 1.0, 0.0)
         return jnp.maximum(peak, own * top)
 
-    return lax.fori_loop(first, end, line, jnp.zeros((8, CX), F32))
+    return lax.fori_loop(first, end, line, jnp.zeros((8, CX), F32), unroll=2)
 
 
 def pair_kernel(
@@ -735,7 +739,7 @@
                 out_changes[zi, y - HALO, tile(t - 1), :] = change[zi]
         return state
 
-    sweep(field, half, above, inside, HALO, HALO + CY, emit, 0)
+    sweep(field, half, above, inside, HALO, HALO + CY, emit, 0, unroll=4)
     lefts, rights = [], []
     for y in range(CY):
         w = weight[y : y + 1, :]

time: 149 us -> 147 us (0.987)
  Pallas kernels: 44 us -> 41.9 us
where the time goes in v13:
time: 147 us; the launch traced here: 146 us
  Pallas kernels  41.9 us (29%)
  starting transfers between devices  38.3 us (26%)
  waiting for transfers between devices  36.6 us (25%)
  blocking collectives  27.2 us (19%)
    all_to_all x3, waiting for transfers between devices, exchange(): return lax.all_to_all(parts, BOTH, split_axis=0, concat_axis=0, tiled=True)  34 us
    all_to_all x2, blocking collectives, exchange(): return lax.all_to_all(parts, BOTH, split_axis=0, concat_axis=0, tiled=True)  27.2 us
    all_to_all x3, starting transfers between devices, exchange(): return lax.all_to_all(parts, BOTH, split_axis=0, concat_axis=0, tiled=True)  23.1 us
    ppermute x6, starting transfers between devices, move(): return lax.ppermute(part, axis, pairs)  15.2 us
    pallas_call x1, Pallas kernels, heated(): pl.pallas_call(heated_kernel, out_shape=[WIDE, WIDE, WIDE, jax.ShapeDtype...  8.19 us
    pallas_call x1, Pallas kernels, deposit(): pl.pallas_call(deposit_kernel, out_shape=[kept((2, CX, CX)), jax.ShapeDty...  6.39 us
    pallas_call x1, Pallas kernels, pair(): pl.pallas_call(functools.partial(pair_kernel, number), out_shape=[WIDE, W...  5.66 us
    pallas_call x1, Pallas kernels, last(): pl.pallas_call(last_kernel, out_shape=[OWN, OWN, sums_shape(parts.shape[0...  5.21 us
  transfers between devices with their start and end apart: 9, of which 4 were waited for; matrix products, arithmetic and copies ran while one was open for 0% of the time, Pallas kernels for 10%

profile of v13, /device:TPU:1, one launch (start us, length us, event | category | flops | bytes accessed | tf_op | source)
XLA Modules:
  0.0 145.9 jit_solution(8736746076928572446)
XLA Ops:
  0.0 0.0 copy-start.3
  0.0 0.0 copy-start.4
  0.0 0.0 copy-start.5
  0.0 4.0 %pack.1 = bf16[128,40,128]{2,1,0:T(8,128)(2,1)} custom-call(s32[128]{0:T(128)} %bitcast.12, bf16[16,128,128]{2,1,0:T(8,128)(2,1)} %heat_far.1, s32[128,128]{1,0:T(8,128)} %voxel_far.1), custom_call_target="tpu_custom_call" | custom-call | tf_op jit(solution)/shard_map/pack/pallas_call | solution.py:145
  4.0 11.5 %all-to-all-start.5 = ((bf16[128,40,128]{2,1,0:T(8,128)(2,1)}), bf16[128,40,128]{2,1,0:T(8,128)(2,1)S(1)}, u32[]{:S(2)}, u32[]{:S(2)}) async-start(bf16[128,40,128]{2,1,0:T(8,128)(2,1)} %pack.1), calls=%async_computation.5 | async-start | bytes 2621440 | tf_op jit(solution)/shard_map/all_to_all | solution.py:1029
  15.5 0.0 copy-done.1
  15.5 0.0 copy-done
  15.5 1.9 %rims.1 = (f32[16,8,128]{2,1,0:T(8,128)}, f32[13,16,8,128]{3,2,1,0:T(8,128)}, f32[13,16,8,128]{3,2,1,0:T(8,128)}) custom-call(f32[16,16,8,128]{3,2,1,0:T(8,128)S(1)} %copy-done, f32[16,8,128]{2,1,0:T(8,128)S(1)} %copy-done.1), custom_call_target="tpu_custom_call" | custom-call | tf_op jit(solution)/shard_map/rims/pallas_call | solution.py:200
  17.4 3.5 %collective-permute-start = (f32[13,16,8,128]{3,2,1,0:T(8,128)}, f32[13,16,8,128]{3,2,1,0:T(8,128)S(1)}, u32[]{:S(2)}, u32[]{:S(2)}) collective-permute-start(f32[13,16,8,128]{3,2,1,0:T(8,128)} %get-tuple-element.84), channel_id=1, source_target_pairs={{0,1},{1,2},{2,3},{3,4},{4,5},{5,6},{6,7},{7,8},{8,9},{9,10},{10,1... | collective-permute-start | bytes 2555912 | tf_op jit(solution)/shard_map/ppermute | solution.py:1035
  20.9 1.3 collective-permute-start.1
  22.2 1.7 %relayout.1 = (f32[2,8,128,128]{3,2,1,0:T(8,128)}, f32[16,8,128]{2,1,0:T(8,128)}, f32[16,8,128]{2,1,0:T(8,128)}, f32[16,2,8,128]{3,2,1,0:T(8,128)}, f32[8,128]{1,0:T(8,128)}) custom-call(f32[16,16,8,128]{3,2,1,0:T(8,128)S(1)} %copy-done, f32[16,8,128]{2,1,0:T(8,128)S(1)} %copy-done.1), custom_call_target="tpu_custom_call" | custom-call | tf_op jit(solution)/shard_map/relayout/pallas_call | solution.py:231
  23.8 0.0 copy-done.2
  23.8 0.0 copy-done.3
  23.8 0.0 copy-done.4
  23.8 0.0 copy-done.5
  23.9 2.4 %pixels.1 = (f32[8,128]{1,0:T(8,128)}, f32[16,8,128]{2,1,0:T(8,128)}) custom-call(s32[1,512]{1,0:T(1,128)S(1)} %bitcast.9, f32[1,512]{1,0:T(1,128)S(1)} %bitcast.10, f32[1,512]{1,0:T(1,128)S(1)} %bitcast.11, f32[16,512]{1,0:T(8,128)S(1)} %copy-done.2), custom_call_target="tpu_custom_call" | custom-call | tf_op jit(solution)/shard_map/pixels/pallas_call | solution.py:928
  26.2 0.1 add_convert_fusion.inside
  26.3 10.6 %all-to-all-done.5.incoming = bf16[128,40,128]{2,1,0:T(8,128)(2,1)S(1)} async-done(((bf16[128,40,128]{2,1,0:T(8,128)(2,1)}), bf16[128,40,128]{2,1,0:T(8,128)(2,1)S(1)}, u32[]{:S(2)}, u32[]{:S(2)}) %all-to-all-start.5) | async-done | bytes 1310752 | tf_op jit(solution)/shard_map/all_to_all | solution.py:1029
  36.9 6.4 %deposit.1 = (f32[2,128,128]{2,1,0:T(8,128)}, f32[128,1,128]{2,1,0:T(1,128)}) custom-call(bf16[128,40,128]{2,1,0:T(8,128)(2,1)S(1)} %all-to-all-done.5.incoming, f32[16,2,8,128]{3,2,1,0:T(8,128)} %get-tuple-element.87.top_far, f32[16,8,128]{2,1,0:T(8,128)} %conduct_far.1, f32[8,128]{1,0:T(8,128)} %get-tuple-element.88.quiet_far), custom_call_target="tpu_custom_call" | custom-call | tf_op jit(solution)/shard_map/deposit/pallas_call | solution.py:378
  43.3 1.3 collective-permute-start.3
  44.6 4.0 %collective-permute-start.2 = (f32[2,128,128]{2,1,0:T(8,128)}, f32[2,128,128]{2,1,0:T(8,128)S(1)}, u32[]{:S(2)}, u32[]{:S(2)}) collective-permute-start(f32[2,128,128]{2,1,0:T(8,128)} %get-tuple-element.89.heat_own.heat_own_far), channel_id=1, source_target_pairs={{0,1},{1,2},{2,3},{3,4},{4,5},{5,6},{6,7},{7,8},{8,9},{9,10},{10,1... | collective-permute-start | bytes 393224 | tf_op jit(solution)/shard_map/ppermute | solution.py:1035
  48.6 7.1 %all-to-all-start.6 = ((f32[128,1,128]{2,1,0:T(1,128)}), f32[128,1,128]{2,1,0:T(1,128)S(1)}, u32[]{:S(2)}, u32[]{:S(2)}) async-start(f32[128,1,128]{2,1,0:T(1,128)} %get-tuple-element.90), calls=%async_computation.6 | async-start | bytes 131072 | tf_op jit(solution)/shard_map/all_to_all | solution.py:1029
  55.7 0.0 collective-permute-done.low.low_far
  55.7 0.0 copy-start.9
  55.7 0.0 collective-permute-done.1.high.high_far
  55.7 9.5 %all-to-all-done.6.peaks = f32[128,1,128]{2,1,0:T(1,128)S(1)} async-done(((f32[128,1,128]{2,1,0:T(1,128)}), f32[128,1,128]{2,1,0:T(1,128)S(1)}, u32[]{:S(2)}, u32[]{:S(2)}) %all-to-all-start.6) | async-done | bytes 65568 | tf_op jit(solution)/shard_map/all_to_all | solution.py:1029
  65.2 0.0 collective-permute-done.3.heat_high.heat_high_far
  65.2 0.0 collective-permute-done.2.heat_low.heat_low_far
  65.3 0.0 copy-start.11
  65.3 0.6 copy-done.10
  65.9 0.1 copy-done.11
  66.0 1.2 sides.1
  67.2 3.1 %collective-permute-start.4 = (f32[49,8,128]{2,1,0:T(8,128)S(1)}, f32[49,8,128]{2,1,0:T(8,128)S(1)}, u32[]{:S(2)}, u32[]{:S(2)}) collective-permute-start(f32[49,8,128]{2,1,0:T(8,128)S(1)} %get-tuple-element.99), channel_id=1, source_target_pairs={{0,16},{16,32},{32,48},{48,64},{64,80},{80,96},{96,112},{1,17},{17... | collective-permute-start | bytes 602120 | tf_op jit(solution)/shard_map/ppermute | solution.py:1035
  70.2 2.1 %collective-permute-start.5 = (f32[49,8,128]{2,1,0:T(8,128)S(1)}, f32[49,8,128]{2,1,0:T(8,128)S(1)}, u32[]{:S(2)}, u32[]{:S(2)}) collective-permute-start(f32[49,8,128]{2,1,0:T(8,128)S(1)} %get-tuple-element.100), channel_id=1, source_target_pairs={{16,0},{32,16},{48,32},{64,48},{80,64},{96,80},{112,96},{17,1},{33... | collective-permute-start | bytes 602120 | tf_op jit(solution)/shard_map/ppermute | solution.py:1035
  72.4 2.3 %coefs.1.coef_main = f32[2,20,128,128]{3,2,1,0:T(8,128)S(1)} custom-call(f32[16,8,128]{2,1,0:T(8,128)} %get-tuple-element.94.turned_c.own, f32[13,16,8,128]{3,2,1,0:T(8,128)} %copy-done.9, f32[13,16,8,128]{3,2,1,0:T(8,128)} %collective-permute-done.1.high.high_far), custom_call_target="tpu_custom_call" | custom-call | tf_op jit(solution)/shard_map/coefs/pallas_call | solution.py:312
  74.7 0.0 collective-permute-done.4.left
  74.7 2.6 %collective-permute-done.5.right = f32[49,8,128]{2,1,0:T(8,128)S(1)} collective-permute-done((f32[49,8,128]{2,1,0:T(8,128)S(1)}, f32[49,8,128]{2,1,0:T(8,128)S(1)}, u32[]{:S(2)}, u32[]{:S(2)}) %collective-permute-start.5) | collective-permute-done | bytes 200736 | tf_op jit(solution)/shard_map/ppermute | solution.py:1035
  77.3 8.2 %heated.1 = (f32[2,20,144,128]{3,2,1,0:T(8,128)S(1)}, f32[2,20,144,128]{3,2,1,0:T(8,128)S(1)}, f32[2,20,144,128]{3,2,1,0:T(8,128)S(1)}, f32[128,1,128]{2,1,0:T(1,128)S(1)}) custom-call(f32[4]{0:T(128)S(1)} %add_convert_fusion.inside, f32[128,1,128]{2,1,0:T(1,128)S(1)} %all-to-all-done.6.peaks, f32[49,8,128]{2,1,0:T(8,128)S(1)} %collective-permute-done.4.left, ...), custom_call_target="tpu_custom_call" | custom-call | tf_op jit(solution)/shard_map/heated/pallas_call | solution.py:660
  85.5 13.3 %all_to_all.50.parts = f32[128,1,128]{2,1,0:T(1,128)S(1)} all-to-all(f32[128,1,128]{2,1,0:T(1,128)S(1)} %get-tuple-element.105), channel_id=1, replica_groups=mesh['gx'=8,'gy'=16] {'gx','gy'}, dimensions={0} | all-to-all | bytes 131072 | tf_op jit(solution)/shard_map/all_to_all | solution.py:1029
  98.8 5.7 %pair_1.1 = (f32[2,20,144,128]{3,2,1,0:T(8,128)S(1)}, f32[2,20,144,128]{3,2,1,0:T(8,128)S(1)}, f32[128,1,128]{2,1,0:T(1,128)S(1)}, f32[8,128]{1,0:T(8,128)S(1)}) custom-call(f32[4]{0:T(128)S(1)} %add_convert_fusion.inside, f32[2,20,144,128]{3,2,1,0:T(8,128)S(1)} %get-tuple-element.102.field, f32[2,20,144,128]{3,2,1,0:T(8,128)S(1)} %get-tuple-element.103.changes, ...), custom_call_target="tpu_custom_call" | custom-call | tf_op jit(solution)/shard_map/pair_1/pallas_call | solution.py:721
  104.5 13.9 %all_to_all.51.parts = f32[128,1,128]{2,1,0:T(1,128)S(1)} all-to-all(f32[128,1,128]{2,1,0:T(1,128)S(1)} %get-tuple-element.108), channel_id=1, replica_groups=mesh['gx'=8,'gy'=16] {'gx','gy'}, dimensions={0} | all-to-all | bytes 131072 | tf_op jit(solution)/shard_map/all_to_all | solution.py:1029
  118.4 0.0 copy-done.6
  118.4 5.2 %last_pair.1 = (f32[2,8,128,128]{3,2,1,0:T(8,128)S(1)}, f32[2,8,128,128]{3,2,1,0:T(8,128)S(1)}, f32[128,8,128]{2,1,0:T(8,128)}, f32[8,128]{1,0:T(8,128)S(1)}) custom-call(f32[4]{0:T(128)S(1)} %add_convert_fusion.inside, f32[2,20,144,128]{3,2,1,0:T(8,128)S(1)} %get-tuple-element.106.field, f32[2,20,144,128]{3,2,1,0:T(8,128)S(1)} %get-tuple-element.107.changes, ...), custom_call_target="tpu_custom_call" | custom-call | tf_op jit(solution)/shard_map/last_pair/pallas_call | solution.py:833
  123.6 0.0 copy-start.12
  123.6 0.0 copy-start.13
  123.6 4.5 %all-to-all-start.9 = ((f32[128,8,128]{2,1,0:T(8,128)}), f32[128,8,128]{2,1,0:T(8,128)S(1)}, u32[]{:S(2)}, u32[]{:S(2)}) async-start(f32[128,8,128]{2,1,0:T(8,128)} %get-tuple-element.112), calls=%async_computation.9 | async-start | bytes 1048576 | tf_op jit(solution)/shard_map/all_to_all | solution.py:1029
  128.1 13.9 %all-to-all-done.9.sums = f32[128,8,128]{2,1,0:T(8,128)S(1)} async-done(((f32[128,8,128]{2,1,0:T(8,128)}), f32[128,8,128]{2,1,0:T(8,128)S(1)}, u32[]{:S(2)}, u32[]{:S(2)}) %all-to-all-start.9) | async-done | bytes 524320 | tf_op jit(solution)/shard_map/all_to_all | solution.py:1029
  142.1 3.0 %update.3 = (f32[16,16,8,128]{3,2,1,0:T(8,128)}, s32[1]{0:T(128)}) custom-call(f32[128,8,128]{2,1,0:T(8,128)S(1)} %all-to-all-done.9.sums, f32[2,8,128,128]{3,2,1,0:T(8,128)S(1)} %get-tuple-element.113.field, f32[2,8,128,128]{3,2,1,0:T(8,128)S(1)} %get-tuple-element.114.changes, f32[8,128]{1,0:T(8,128)S(1)} %get-tuple-element.115.status), custom_call_target="tpu_custom_call" | custom-call | tf_op jit(solution)/shard_map/update/pallas_call | solution.py:1015
  (11 shorter events, 0.0 us)
Async XLA Ops:
  0.0 15.5 %copy-start.1 = (f32[16,8,128]{2,1,0:T(8,128)S(1)}, f32[16,8,128]{2,1,0:T(8,128)}, u32[]{:S(2)}) copy-start(f32[16,8,128]{2,1,0:T(8,128)} %conduct_far.1) | copy-start | bytes 196612
  0.0 15.5 %copy-start = (f32[16,16,8,128]{3,2,1,0:T(8,128)S(1)}, f32[16,16,8,128]{3,2,1,0:T(8,128)}, u32[]{:S(2)}) copy-start(f32[16,16,8,128]{3,2,1,0:T(8,128)} %state.2) | copy-start | bytes 3145732
  0.0 23.8 %copy-start.2 = (f32[16,512]{1,0:T(8,128)S(1)}, f32[16,512]{1,0:T(8,128)}, u32[]{:S(2)}) copy-start(f32[16,512]{1,0:T(8,128)} %noise.1) | copy-start | bytes 98308
  0.0 23.8 %copy-start.3 = (s32[512]{0:T(512)S(1)}, s32[512]{0:T(512)}, u32[]{:S(2)}) copy-start(s32[512]{0:T(512)} %param.16) | copy-start | bytes 6148
  0.0 23.8 %copy-start.4 = (f32[512]{0:T(512)S(1)}, f32[512]{0:T(512)}, u32[]{:S(2)}) copy-start(f32[512]{0:T(512)} %param.17) | copy-start | bytes 6148
  0.0 23.8 %copy-start.5 = (f32[512]{0:T(512)S(1)}, f32[512]{0:T(512)}, u32[]{:S(2)}) copy-start(f32[512]{0:T(512)} %param.18) | copy-start | bytes 6148
  4.0 32.9 %all-to-all-start.5 = ((bf16[128,40,128]{2,1,0:T(8,128)(2,1)}), bf16[128,40,128]{2,1,0:T(8,128)(2,1)S(1)}, u32[]{:S(2)}, u32[]{:S(2)}) async-start(bf16[128,40,128]{2,1,0:T(8,128)(2,1)} %pack.1), calls=%async_computation.5 | async-start | bytes 2621440 | tf_op jit(solution)/shard_map/all_to_all | solution.py:1029
  17.4 38.3 %collective-permute-start = (f32[13,16,8,128]{3,2,1,0:T(8,128)}, f32[13,16,8,128]{3,2,1,0:T(8,128)S(1)}, u32[]{:S(2)}, u32[]{:S(2)}) collective-permute-start(f32[13,16,8,128]{3,2,1,0:T(8,128)} %get-tuple-element.84), channel_id=1, source_target_pairs={{0,1},{1,2},{2,3},{3,4},{4,5},{5,6},{6,7},{7,8},{8,9},{9,10},{10,1... | collective-permute-start | bytes 2555912 | tf_op jit(solution)/shard_map/ppermute | solution.py:1035
  20.9 34.8 %collective-permute-start.1 = (f32[13,16,8,128]{3,2,1,0:T(8,128)}, f32[13,16,8,128]{3,2,1,0:T(8,128)}, u32[]{:S(2)}, u32[]{:S(2)}) collective-permute-start(f32[13,16,8,128]{3,2,1,0:T(8,128)} %get-tuple-element.85), channel_id=1, source_target_pairs={{1,0},{2,1},{3,2},{4,3},{5,4},{6,5},{7,6},{8,7},{9,8},{10,9},{11,1... | collective-permute-start | bytes 2555912 | tf_op jit(solution)/shard_map/ppermute | solution.py:1035
  43.3 22.0 %collective-permute-start.3 = (f32[2,128,128]{2,1,0:T(8,128)}, f32[2,128,128]{2,1,0:T(8,128)S(1)}, u32[]{:S(2)}, u32[]{:S(2)}) collective-permute-start(f32[2,128,128]{2,1,0:T(8,128)} %get-tuple-element.89.heat_own.heat_own_far), channel_id=1, source_target_pairs={{1,0},{2,1},{3,2},{4,3},{5,4},{6,5},{7,6},{8,7},{9,8},{10,9},{11,1... | collective-permute-start | bytes 393224 | tf_op jit(solution)/shard_map/ppermute | solution.py:1035
  44.6 20.7 %collective-permute-start.2 = (f32[2,128,128]{2,1,0:T(8,128)}, f32[2,128,128]{2,1,0:T(8,128)S(1)}, u32[]{:S(2)}, u32[]{:S(2)}) collective-permute-start(f32[2,128,128]{2,1,0:T(8,128)} %get-tuple-element.89.heat_own.heat_own_far), channel_id=1, source_target_pairs={{0,1},{1,2},{2,3},{3,4},{4,5},{5,6},{6,7},{7,8},{8,9},{9,10},{10,1... | collective-permute-start | bytes 393224 | tf_op jit(solution)/shard_map/ppermute | solution.py:1035
  48.6 16.7 %all-to-all-start.6 = ((f32[128,1,128]{2,1,0:T(1,128)}), f32[128,1,128]{2,1,0:T(1,128)S(1)}, u32[]{:S(2)}, u32[]{:S(2)}) async-start(f32[128,1,128]{2,1,0:T(1,128)} %get-tuple-element.90), calls=%async_computation.6 | async-start | bytes 131072 | tf_op jit(solution)/shard_map/all_to_all | solution.py:1029
  55.7 9.6 %copy-start.9 = (f32[13,16,8,128]{3,2,1,0:T(8,128)}, f32[13,16,8,128]{3,2,1,0:T(8,128)S(1)}, u32[]{:S(2)}) copy-start(f32[13,16,8,128]{3,2,1,0:T(8,128)S(1)} %collective-permute-done.low.low_far) | copy-start | bytes 2555908
  65.2 0.6 copy-start.10
  65.3 0.7 copy-start.11
  67.2 7.5 %collective-permute-start.4 = (f32[49,8,128]{2,1,0:T(8,128)S(1)}, f32[49,8,128]{2,1,0:T(8,128)S(1)}, u32[]{:S(2)}, u32[]{:S(2)}) collective-permute-start(f32[49,8,128]{2,1,0:T(8,128)S(1)} %get-tuple-element.99), channel_id=1, source_target_pairs={{0,16},{16,32},{32,48},{48,64},{64,80},{80,96},{96,112},{1,17},{17... | collective-permute-start | bytes 602120 | tf_op jit(solution)/shard_map/ppermute | solution.py:1035
  70.2 7.0 %collective-permute-start.5 = (f32[49,8,128]{2,1,0:T(8,128)S(1)}, f32[49,8,128]{2,1,0:T(8,128)S(1)}, u32[]{:S(2)}, u32[]{:S(2)}) collective-permute-start(f32[49,8,128]{2,1,0:T(8,128)S(1)} %get-tuple-element.100), channel_id=1, source_target_pairs={{16,0},{32,16},{48,32},{64,48},{80,64},{96,80},{112,96},{17,1},{33... | collective-permute-start | bytes 602120 | tf_op jit(solution)/shard_map/ppermute | solution.py:1035
  85.5 19.0 %copy-start.8 = (f32[2,20,144,128]{3,2,1,0:T(8,128)}, f32[2,20,144,128]{3,2,1,0:T(8,128)S(1)}, u32[]{:S(2)}) copy-start(f32[2,20,144,128]{3,2,1,0:T(8,128)S(1)} %get-tuple-element.102.field) | copy-start | bytes 8847364
  85.5 32.9 %copy-start.6 = (f32[2,20,144,128]{3,2,1,0:T(8,128)}, f32[2,20,144,128]{3,2,1,0:T(8,128)S(1)}, u32[]{:S(2)}) copy-start(f32[2,20,144,128]{3,2,1,0:T(8,128)S(1)} %get-tuple-element.104.coef) | copy-start | bytes 8847364
  123.6 22.1 %copy-start.12 = (f32[16,8,128]{2,1,0:T(8,128)S(1)}, f32[16,8,128]{2,1,0:T(8,128)}, u32[]{:S(2)}) copy-start(f32[16,8,128]{2,1,0:T(8,128)} %get-tuple-element.111.data_far) | copy-start | bytes 196612
  123.6 22.1 %copy-start.13 = (f32[8,128]{1,0:T(8,128)S(1)}, f32[8,128]{1,0:T(8,128)}, u32[]{:S(2)}) copy-start(f32[8,128]{1,0:T(8,128)} %get-tuple-element.110.weight_far) | copy-start | bytes 12292
  123.6 18.4 %all-to-all-start.9 = ((f32[128,8,128]{2,1,0:T(8,128)}), f32[128,8,128]{2,1,0:T(8,128)S(1)}, u32[]{:S(2)}, u32[]{:S(2)}) async-start(f32[128,8,128]{2,1,0:T(8,128)} %get-tuple-element.112), calls=%async_computation.9 | async-start | bytes 1048576 | tf_op jit(solution)/shard_map/all_to_all | solution.py:1029

commit v14 on v13

--- a/solution.py
+++ b/solution.py
@@ -325,7 +325,7 @@
 ):
     copies = fetch(sems, ((top_far, top), (conduct_far.at[0:2], conduct), (quiet_far, quiet)))
     sources = incoming.shape[0]
-    group = 64
+    group = 128
     place = lax.broadcasted_iota(jnp.int32, (CX, CX), 0).astype(F32).astype(BF16)
     zero = jnp.zeros((M, CX), BF16)
     total[...] = jnp.zeros_like(total)
@@ -685,7 +685,7 @@
         own = jnp.where((y >= HALO) & (y < HALO + CY), 1.0, 0.0)
         return jnp.maximum(peak, own * top)
 
-    return lax.fori_loop(first, end, line, jnp.zeros((8, CX), F32), unroll=2)
+    return lax.fori_loop(first, end, line, jnp.zeros((8, CX), F32), unroll=4)
 
 
 def pair_kernel(

time: 147 us -> 147 us (level)
  no operation moved by 1% of the time
where the time goes in v14:
time: 147 us; the launch traced here: 146 us
  Pallas kernels  42.2 us (29%)
  starting transfers between devices  38.3 us (26%)
  waiting for transfers between devices  36.7 us (25%)
  blocking collectives  27.2 us (19%)
    all_to_all x3, waiting for transfers between devices, exchange(): return lax.all_to_all(parts, BOTH, split_axis=0, concat_axis=0, tiled=True)  34.1 us
    all_to_all x2, blocking collectives, exchange(): return lax.all_to_all(parts, BOTH, split_axis=0, concat_axis=0, tiled=True)  27.2 us
    all_to_all x3, starting transfers between devices, exchange(): return lax.all_to_all(parts, BOTH, split_axis=0, concat_axis=0, tiled=True)  23.1 us
    ppermute x6, starting transfers between devices, move(): return lax.ppermute(part, axis, pairs)  15.2 us
    pallas_call x1, Pallas kernels, heated(): pl.pallas_call(heated_kernel, out_shape=[WIDE, WIDE, WIDE, jax.ShapeDtype...  8.19 us
    pallas_call x1, Pallas kernels, deposit(): pl.pallas_call(deposit_kernel, out_shape=[kept((2, CX, CX)), jax.ShapeDty...  6.83 us
    pallas_call x1, Pallas kernels, pair(): pl.pallas_call(functools.partial(pair_kernel, number), out_shape=[WIDE, W...  5.6 us
    pallas_call x1, Pallas kernels, last(): pl.pallas_call(last_kernel, out_shape=[OWN, OWN, sums_shape(parts.shape[0...  5.17 us
  transfers between devices with their start and end apart: 9, of which 4 were waited for; matrix products, arithmetic and copies ran while one was open for 0% of the time, Pallas kernels for 10%

profile of v14, /device:TPU:1, one launch (start us, length us, event | category | flops | bytes accessed | tf_op | source)
XLA Modules:
  0.0 146.2 jit_solution(15237052859168133826)
XLA Ops:
  0.0 0.0 copy-start.3
  0.0 0.0 copy-start.4
  0.0 0.0 copy-start.5
  0.0 4.0 %pack.1 = bf16[128,40,128]{2,1,0:T(8,128)(2,1)} custom-call(s32[128]{0:T(128)} %bitcast.12, bf16[16,128,128]{2,1,0:T(8,128)(2,1)} %heat_far.1, s32[128,128]{1,0:T(8,128)} %voxel_far.1), custom_call_target="tpu_custom_call" | custom-call | tf_op jit(solution)/shard_map/pack/pallas_call | solution.py:145
  4.0 11.5 %all-to-all-start.5 = ((bf16[128,40,128]{2,1,0:T(8,128)(2,1)}), bf16[128,40,128]{2,1,0:T(8,128)(2,1)S(1)}, u32[]{:S(2)}, u32[]{:S(2)}) async-start(bf16[128,40,128]{2,1,0:T(8,128)(2,1)} %pack.1), calls=%async_computation.5 | async-start | bytes 2621440 | tf_op jit(solution)/shard_map/all_to_all | solution.py:1029
  15.5 0.0 copy-done.1
  15.5 0.0 copy-done
  15.5 1.9 %rims.1 = (f32[16,8,128]{2,1,0:T(8,128)}, f32[13,16,8,128]{3,2,1,0:T(8,128)}, f32[13,16,8,128]{3,2,1,0:T(8,128)}) custom-call(f32[16,16,8,128]{3,2,1,0:T(8,128)S(1)} %copy-done, f32[16,8,128]{2,1,0:T(8,128)S(1)} %copy-done.1), custom_call_target="tpu_custom_call" | custom-call | tf_op jit(solution)/shard_map/rims/pallas_call | solution.py:200
  17.4 3.5 %collective-permute-start = (f32[13,16,8,128]{3,2,1,0:T(8,128)}, f32[13,16,8,128]{3,2,1,0:T(8,128)S(1)}, u32[]{:S(2)}, u32[]{:S(2)}) collective-permute-start(f32[13,16,8,128]{3,2,1,0:T(8,128)} %get-tuple-element.84), channel_id=1, source_target_pairs={{0,1},{1,2},{2,3},{3,4},{4,5},{5,6},{6,7},{7,8},{8,9},{9,10},{10,1... | collective-permute-start | bytes 2555912 | tf_op jit(solution)/shard_map/ppermute | solution.py:1035
  20.9 1.3 collective-permute-start.1
  22.2 1.7 %relayout.1 = (f32[2,8,128,128]{3,2,1,0:T(8,128)}, f32[16,8,128]{2,1,0:T(8,128)}, f32[16,8,128]{2,1,0:T(8,128)}, f32[16,2,8,128]{3,2,1,0:T(8,128)}, f32[8,128]{1,0:T(8,128)}) custom-call(f32[16,16,8,128]{3,2,1,0:T(8,128)S(1)} %copy-done, f32[16,8,128]{2,1,0:T(8,128)S(1)} %copy-done.1), custom_call_target="tpu_custom_call" | custom-call | tf_op jit(solution)/shard_map/relayout/pallas_call | solution.py:231
  23.8 0.0 copy-done.2
  23.8 0.0 copy-done.3
  23.8 0.0 copy-done.4
  23.8 0.0 copy-done.5
  23.9 2.4 %pixels.1 = (f32[8,128]{1,0:T(8,128)}, f32[16,8,128]{2,1,0:T(8,128)}) custom-call(s32[1,512]{1,0:T(1,128)S(1)} %bitcast.9, f32[1,512]{1,0:T(1,128)S(1)} %bitcast.10, f32[1,512]{1,0:T(1,128)S(1)} %bitcast.11, f32[16,512]{1,0:T(8,128)S(1)} %copy-done.2), custom_call_target="tpu_custom_call" | custom-call | tf_op jit(solution)/shard_map/pixels/pallas_call | solution.py:928
  26.2 0.1 add_convert_fusion.inside
  26.3 10.6 %all-to-all-done.5.incoming = bf16[128,40,128]{2,1,0:T(8,128)(2,1)S(1)} async-done(((bf16[128,40,128]{2,1,0:T(8,128)(2,1)}), bf16[128,40,128]{2,1,0:T(8,128)(2,1)S(1)}, u32[]{:S(2)}, u32[]{:S(2)}) %all-to-all-start.5) | async-done | bytes 1310752 | tf_op jit(solution)/shard_map/all_to_all | solution.py:1029
  36.9 6.8 %deposit.1 = (f32[2,128,128]{2,1,0:T(8,128)}, f32[128,1,128]{2,1,0:T(1,128)}) custom-call(bf16[128,40,128]{2,1,0:T(8,128)(2,1)S(1)} %all-to-all-done.5.incoming, f32[16,2,8,128]{3,2,1,0:T(8,128)} %get-tuple-element.87.top_far, f32[16,8,128]{2,1,0:T(8,128)} %conduct_far.1, f32[8,128]{1,0:T(8,128)} %get-tuple-element.88.quiet_far), custom_call_target="tpu_custom_call" | custom-call | tf_op jit(solution)/shard_map/deposit/pallas_call | solution.py:378
  43.7 1.3 collective-permute-start.3
  45.0 4.0 %collective-permute-start.2 = (f32[2,128,128]{2,1,0:T(8,128)}, f32[2,128,128]{2,1,0:T(8,128)S(1)}, u32[]{:S(2)}, u32[]{:S(2)}) collective-permute-start(f32[2,128,128]{2,1,0:T(8,128)} %get-tuple-element.89.heat_own.heat_own_far), channel_id=1, source_target_pairs={{0,1},{1,2},{2,3},{3,4},{4,5},{5,6},{6,7},{7,8},{8,9},{9,10},{10,1... | collective-permute-start | bytes 393224 | tf_op jit(solution)/shard_map/ppermute | solution.py:1035
  49.0 7.1 %all-to-all-start.6 = ((f32[128,1,128]{2,1,0:T(1,128)}), f32[128,1,128]{2,1,0:T(1,128)S(1)}, u32[]{:S(2)}, u32[]{:S(2)}) async-start(f32[128,1,128]{2,1,0:T(1,128)} %get-tuple-element.90), calls=%async_computation.6 | async-start | bytes 131072 | tf_op jit(solution)/shard_map/all_to_all | solution.py:1029
  56.1 0.0 collective-permute-done.low.low_far
  56.1 0.0 copy-start.9
  56.1 0.0 collective-permute-done.1.high.high_far
  56.1 9.5 %all-to-all-done.6.peaks = f32[128,1,128]{2,1,0:T(1,128)S(1)} async-done(((f32[128,1,128]{2,1,0:T(1,128)}), f32[128,1,128]{2,1,0:T(1,128)S(1)}, u32[]{:S(2)}, u32[]{:S(2)}) %all-to-all-start.6) | async-done | bytes 65568 | tf_op jit(solution)/shard_map/all_to_all | solution.py:1029
  65.7 0.0 collective-permute-done.3.heat_high.heat_high_far
  65.7 0.0 collective-permute-done.2.heat_low.heat_low_far
  65.7 0.6 copy-done.10
  66.3 0.1 copy-done.11
  66.4 1.2 sides.1
  67.6 3.1 %collective-permute-start.4 = (f32[49,8,128]{2,1,0:T(8,128)S(1)}, f32[49,8,128]{2,1,0:T(8,128)S(1)}, u32[]{:S(2)}, u32[]{:S(2)}) collective-permute-start(f32[49,8,128]{2,1,0:T(8,128)S(1)} %get-tuple-element.99), channel_id=1, source_target_pairs={{0,16},{16,32},{32,48},{48,64},{64,80},{80,96},{96,112},{1,17},{17... | collective-permute-start | bytes 602120 | tf_op jit(solution)/shard_map/ppermute | solution.py:1035
  70.7 2.1 %collective-permute-start.5 = (f32[49,8,128]{2,1,0:T(8,128)S(1)}, f32[49,8,128]{2,1,0:T(8,128)S(1)}, u32[]{:S(2)}, u32[]{:S(2)}) collective-permute-start(f32[49,8,128]{2,1,0:T(8,128)S(1)} %get-tuple-element.100), channel_id=1, source_target_pairs={{16,0},{32,16},{48,32},{64,48},{80,64},{96,80},{112,96},{17,1},{33... | collective-permute-start | bytes 602120 | tf_op jit(solution)/shard_map/ppermute | solution.py:1035
  72.8 2.3 %coefs.1.coef_main = f32[2,20,128,128]{3,2,1,0:T(8,128)S(1)} custom-call(f32[16,8,128]{2,1,0:T(8,128)} %get-tuple-element.94.turned_c.own, f32[13,16,8,128]{3,2,1,0:T(8,128)} %copy-done.9, f32[13,16,8,128]{3,2,1,0:T(8,128)} %collective-permute-done.1.high.high_far), custom_call_target="tpu_custom_call" | custom-call | tf_op jit(solution)/shard_map/coefs/pallas_call | solution.py:312
  75.1 0.0 collective-permute-done.4.left
  75.1 2.6 %collective-permute-done.5.right = f32[49,8,128]{2,1,0:T(8,128)S(1)} collective-permute-done((f32[49,8,128]{2,1,0:T(8,128)S(1)}, f32[49,8,128]{2,1,0:T(8,128)S(1)}, u32[]{:S(2)}, u32[]{:S(2)}) %collective-permute-start.5) | collective-permute-done | bytes 200736 | tf_op jit(solution)/shard_map/ppermute | solution.py:1035
  77.7 8.2 %heated.1 = (f32[2,20,144,128]{3,2,1,0:T(8,128)S(1)}, f32[2,20,144,128]{3,2,1,0:T(8,128)S(1)}, f32[2,20,144,128]{3,2,1,0:T(8,128)S(1)}, f32[128,1,128]{2,1,0:T(1,128)S(1)}) custom-call(f32[4]{0:T(128)S(1)} %add_convert_fusion.inside, f32[128,1,128]{2,1,0:T(1,128)S(1)} %all-to-all-done.6.peaks, f32[49,8,128]{2,1,0:T(8,128)S(1)} %collective-permute-done.4.left, ...), custom_call_target="tpu_custom_call" | custom-call | tf_op jit(solution)/shard_map/heated/pallas_call | solution.py:660
  85.9 13.3 %all_to_all.50.parts = f32[128,1,128]{2,1,0:T(1,128)S(1)} all-to-all(f32[128,1,128]{2,1,0:T(1,128)S(1)} %get-tuple-element.105), channel_id=1, replica_groups=mesh['gx'=8,'gy'=16] {'gx','gy'}, dimensions={0} | all-to-all | bytes 131072 | tf_op jit(solution)/shard_map/all_to_all | solution.py:1029
  99.3 5.6 %pair_1.1 = (f32[2,20,144,128]{3,2,1,0:T(8,128)S(1)}, f32[2,20,144,128]{3,2,1,0:T(8,128)S(1)}, f32[128,1,128]{2,1,0:T(1,128)S(1)}, f32[8,128]{1,0:T(8,128)S(1)}) custom-call(f32[4]{0:T(128)S(1)} %add_convert_fusion.inside, f32[2,20,144,128]{3,2,1,0:T(8,128)S(1)} %get-tuple-element.102.field, f32[2,20,144,128]{3,2,1,0:T(8,128)S(1)} %get-tuple-element.103.changes, ...), custom_call_target="tpu_custom_call" | custom-call | tf_op jit(solution)/shard_map/pair_1/pallas_call | solution.py:721
  104.9 13.9 %all_to_all.51.parts = f32[128,1,128]{2,1,0:T(1,128)S(1)} all-to-all(f32[128,1,128]{2,1,0:T(1,128)S(1)} %get-tuple-element.108), channel_id=1, replica_groups=mesh['gx'=8,'gy'=16] {'gx','gy'}, dimensions={0} | all-to-all | bytes 131072 | tf_op jit(solution)/shard_map/all_to_all | solution.py:1029
  118.8 5.2 %last_pair.1 = (f32[2,8,128,128]{3,2,1,0:T(8,128)S(1)}, f32[2,8,128,128]{3,2,1,0:T(8,128)S(1)}, f32[128,8,128]{2,1,0:T(8,128)}, f32[8,128]{1,0:T(8,128)S(1)}) custom-call(f32[4]{0:T(128)S(1)} %add_convert_fusion.inside, f32[2,20,144,128]{3,2,1,0:T(8,128)S(1)} %get-tuple-element.106.field, f32[2,20,144,128]{3,2,1,0:T(8,128)S(1)} %get-tuple-element.107.changes, ...), custom_call_target="tpu_custom_call" | custom-call | tf_op jit(solution)/shard_map/last_pair/pallas_call | solution.py:833
  123.9 0.0 copy-start.12
  123.9 0.0 copy-start.13
  124.0 4.5 %all-to-all-start.9 = ((f32[128,8,128]{2,1,0:T(8,128)}), f32[128,8,128]{2,1,0:T(8,128)S(1)}, u32[]{:S(2)}, u32[]{:S(2)}) async-start(f32[128,8,128]{2,1,0:T(8,128)} %get-tuple-element.112), calls=%async_computation.9 | async-start | bytes 1048576 | tf_op jit(solution)/shard_map/all_to_all | solution.py:1029
  128.5 13.9 %all-to-all-done.9.sums = f32[128,8,128]{2,1,0:T(8,128)S(1)} async-done(((f32[128,8,128]{2,1,0:T(8,128)}), f32[128,8,128]{2,1,0:T(8,128)S(1)}, u32[]{:S(2)}, u32[]{:S(2)}) %all-to-all-start.9) | async-done | bytes 524320 | tf_op jit(solution)/shard_map/all_to_all | solution.py:1029
  142.4 3.0 %update.3 = (f32[16,16,8,128]{3,2,1,0:T(8,128)}, s32[1]{0:T(128)}) custom-call(f32[128,8,128]{2,1,0:T(8,128)S(1)} %all-to-all-done.9.sums, f32[2,8,128,128]{3,2,1,0:T(8,128)S(1)} %get-tuple-element.113.field, f32[2,8,128,128]{3,2,1,0:T(8,128)S(1)} %get-tuple-element.114.changes, f32[8,128]{1,0:T(8,128)S(1)} %get-tuple-element.115.status), custom_call_target="tpu_custom_call" | custom-call | tf_op jit(solution)/shard_map/update/pallas_call | solution.py:1015
  146.0 0.0 copy-done.12
  146.0 0.0 copy-done.13
  (11 shorter events, 0.0 us)
Async XLA Ops:
  0.0 15.5 %copy-start.1 = (f32[16,8,128]{2,1,0:T(8,128)S(1)}, f32[16,8,128]{2,1,0:T(8,128)}, u32[]{:S(2)}) copy-start(f32[16,8,128]{2,1,0:T(8,128)} %conduct_far.1) | copy-start | bytes 196612
  0.0 15.5 %copy-start = (f32[16,16,8,128]{3,2,1,0:T(8,128)S(1)}, f32[16,16,8,128]{3,2,1,0:T(8,128)}, u32[]{:S(2)}) copy-start(f32[16,16,8,128]{3,2,1,0:T(8,128)} %state.2) | copy-start | bytes 3145732
  0.0 23.8 %copy-start.2 = (f32[16,512]{1,0:T(8,128)S(1)}, f32[16,512]{1,0:T(8,128)}, u32[]{:S(2)}) copy-start(f32[16,512]{1,0:T(8,128)} %noise.1) | copy-start | bytes 98308
  0.0 23.8 %copy-start.3 = (s32[512]{0:T(512)S(1)}, s32[512]{0:T(512)}, u32[]{:S(2)}) copy-start(s32[512]{0:T(512)} %param.16) | copy-start | bytes 6148
  0.0 23.8 %copy-start.4 = (f32[512]{0:T(512)S(1)}, f32[512]{0:T(512)}, u32[]{:S(2)}) copy-start(f32[512]{0:T(512)} %param.17) | copy-start | bytes 6148
  0.0 23.8 %copy-start.5 = (f32[512]{0:T(512)S(1)}, f32[512]{0:T(512)}, u32[]{:S(2)}) copy-start(f32[512]{0:T(512)} %param.18) | copy-start | bytes 6148
  4.0 32.9 %all-to-all-start.5 = ((bf16[128,40,128]{2,1,0:T(8,128)(2,1)}), bf16[128,40,128]{2,1,0:T(8,128)(2,1)S(1)}, u32[]{:S(2)}, u32[]{:S(2)}) async-start(bf16[128,40,128]{2,1,0:T(8,128)(2,1)} %pack.1), calls=%async_computation.5 | async-start | bytes 2621440 | tf_op jit(solution)/shard_map/all_to_all | solution.py:1029
  17.4 38.7 %collective-permute-start = (f32[13,16,8,128]{3,2,1,0:T(8,128)}, f32[13,16,8,128]{3,2,1,0:T(8,128)S(1)}, u32[]{:S(2)}, u32[]{:S(2)}) collective-permute-start(f32[13,16,8,128]{3,2,1,0:T(8,128)} %get-tuple-element.84), channel_id=1, source_target_pairs={{0,1},{1,2},{2,3},{3,4},{4,5},{5,6},{6,7},{7,8},{8,9},{9,10},{10,1... | collective-permute-start | bytes 2555912 | tf_op jit(solution)/shard_map/ppermute | solution.py:1035
  20.9 35.3 %collective-permute-start.1 = (f32[13,16,8,128]{3,2,1,0:T(8,128)}, f32[13,16,8,128]{3,2,1,0:T(8,128)}, u32[]{:S(2)}, u32[]{:S(2)}) collective-permute-start(f32[13,16,8,128]{3,2,1,0:T(8,128)} %get-tuple-element.85), channel_id=1, source_target_pairs={{1,0},{2,1},{3,2},{4,3},{5,4},{6,5},{7,6},{8,7},{9,8},{10,9},{11,1... | collective-permute-start | bytes 2555912 | tf_op jit(solution)/shard_map/ppermute | solution.py:1035
  43.7 22.0 %collective-permute-start.3 = (f32[2,128,128]{2,1,0:T(8,128)}, f32[2,128,128]{2,1,0:T(8,128)S(1)}, u32[]{:S(2)}, u32[]{:S(2)}) collective-permute-start(f32[2,128,128]{2,1,0:T(8,128)} %get-tuple-element.89.heat_own.heat_own_far), channel_id=1, source_target_pairs={{1,0},{2,1},{3,2},{4,3},{5,4},{6,5},{7,6},{8,7},{9,8},{10,9},{11,1... | collective-permute-start | bytes 393224 | tf_op jit(solution)/shard_map/ppermute | solution.py:1035
  45.0 20.7 %collective-permute-start.2 = (f32[2,128,128]{2,1,0:T(8,128)}, f32[2,128,128]{2,1,0:T(8,128)S(1)}, u32[]{:S(2)}, u32[]{:S(2)}) collective-permute-start(f32[2,128,128]{2,1,0:T(8,128)} %get-tuple-element.89.heat_own.heat_own_far), channel_id=1, source_target_pairs={{0,1},{1,2},{2,3},{3,4},{4,5},{5,6},{6,7},{7,8},{8,9},{9,10},{10,1... | collective-permute-start | bytes 393224 | tf_op jit(solution)/shard_map/ppermute | solution.py:1035
  49.0 16.7 %all-to-all-start.6 = ((f32[128,1,128]{2,1,0:T(1,128)}), f32[128,1,128]{2,1,0:T(1,128)S(1)}, u32[]{:S(2)}, u32[]{:S(2)}) async-start(f32[128,1,128]{2,1,0:T(1,128)} %get-tuple-element.90), calls=%async_computation.6 | async-start | bytes 131072 | tf_op jit(solution)/shard_map/all_to_all | solution.py:1029
  56.1 9.6 %copy-start.9 = (f32[13,16,8,128]{3,2,1,0:T(8,128)}, f32[13,16,8,128]{3,2,1,0:T(8,128)S(1)}, u32[]{:S(2)}) copy-start(f32[13,16,8,128]{3,2,1,0:T(8,128)S(1)} %collective-permute-done.low.low_far) | copy-start | bytes 2555908
  65.7 0.6 copy-start.10
  65.7 0.7 copy-start.11
  67.6 7.5 %collective-permute-start.4 = (f32[49,8,128]{2,1,0:T(8,128)S(1)}, f32[49,8,128]{2,1,0:T(8,128)S(1)}, u32[]{:S(2)}, u32[]{:S(2)}) collective-permute-start(f32[49,8,128]{2,1,0:T(8,128)S(1)} %get-tuple-element.99), channel_id=1, source_target_pairs={{0,16},{16,32},{32,48},{48,64},{64,80},{80,96},{96,112},{1,17},{17... | collective-permute-start | bytes 602120 | tf_op jit(solution)/shard_map/ppermute | solution.py:1035
  70.7 7.0 %collective-permute-start.5 = (f32[49,8,128]{2,1,0:T(8,128)S(1)}, f32[49,8,128]{2,1,0:T(8,128)S(1)}, u32[]{:S(2)}, u32[]{:S(2)}) collective-permute-start(f32[49,8,128]{2,1,0:T(8,128)S(1)} %get-tuple-element.100), channel_id=1, source_target_pairs={{16,0},{32,16},{48,32},{64,48},{80,64},{96,80},{112,96},{17,1},{33... | collective-permute-start | bytes 602120 | tf_op jit(solution)/shard_map/ppermute | solution.py:1035
  85.9 19.0 %copy-start.8 = (f32[2,20,144,128]{3,2,1,0:T(8,128)}, f32[2,20,144,128]{3,2,1,0:T(8,128)S(1)}, u32[]{:S(2)}) copy-start(f32[2,20,144,128]{3,2,1,0:T(8,128)S(1)} %get-tuple-element.102.field) | copy-start | bytes 8847364
  85.9 32.8 %copy-start.6 = (f32[2,20,144,128]{3,2,1,0:T(8,128)}, f32[2,20,144,128]{3,2,1,0:T(8,128)S(1)}, u32[]{:S(2)}) copy-start(f32[2,20,144,128]{3,2,1,0:T(8,128)S(1)} %get-tuple-element.104.coef) | copy-start | bytes 8847364
  123.9 22.1 %copy-start.12 = (f32[16,8,128]{2,1,0:T(8,128)S(1)}, f32[16,8,128]{2,1,0:T(8,128)}, u32[]{:S(2)}) copy-start(f32[16,8,128]{2,1,0:T(8,128)} %get-tuple-element.111.data_far) | copy-start | bytes 196612
  123.9 22.1 %copy-start.13 = (f32[8,128]{1,0:T(8,128)S(1)}, f32[8,128]{1,0:T(8,128)}, u32[]{:S(2)}) copy-start(f32[8,128]{1,0:T(8,128)} %get-tuple-element.110.weight_far) | copy-start | bytes 12292
  124.0 18.4 %all-to-all-start.9 = ((f32[128,8,128]{2,1,0:T(8,128)}), f32[128,8,128]{2,1,0:T(8,128)S(1)}, u32[]{:S(2)}, u32[]{:S(2)}) async-start(f32[128,8,128]{2,1,0:T(8,128)} %get-tuple-element.112), calls=%async_computation.9 | async-start | bytes 1048576 | tf_op jit(solution)/shard_map/all_to_all | solution.py:1029
